TPU v7x, 32 devices: a whole 2x2x4 slice. The times are simulated.
32 devices in a mesh: groups: 2 (over x), role: 8 (over z, y), tp: 2 (over core).
Axes of the slice: x: 2, y: 2, z: 4, core: 2. Of those that a mesh axis runs over, the one named last changes fastest.
Arguments:
- q_lat: bfloat16 [64, 64, 576], P(('groups', 'role'), 'tp'), parts along dimension 0, may hold values from -10 to 10
- latent_cache: bfloat16 [64, 256, 576], P(('groups', 'role')), parts along dimension 0, may hold values from -16 to 16
- lengths: int32 [64], P('groups'), parts along dimension 0, may hold values from 1 to 256, 4915 in all
- placement: int32 [64], P('groups'), parts along dimension 0, may hold values from 0 to 31, each once
- tokens: bfloat16 [1536, 3584], P(('groups', 'role'), 'tp'), parts along dimension 0, may hold values from -6 to 6
- expert_ids: int32 [1536, 4], P(('groups', 'role')), parts along dimension 0, may hold values from 0 to 7, all different within a row; in each aligned block of 96 rows (0 to 95, 96 to 191, ...) at most 72 rows name the same one
- gate_weights: float32 [1536, 4], P(('groups', 'role')), parts along dimension 0, may hold values from 0.1 to 1
- w_gate: bfloat16 [8, 3584, 1024], P('role', None, 'tp'), may hold values from -0.09375 to 0.09375
- w_up: bfloat16 [8, 3584, 1024], P('role', None, 'tp'), may hold values from -0.09375 to 0.09375
- w_down: bfloat16 [8, 1024, 3584], P('role', 'tp'), may hold values from -0.1875 to 0.1875
Outputs:
- attended: bfloat16 [64, 64, 512], P(('groups', 'role'), 'tp'), parts along dimension 0
- moe_out: bfloat16 [1536, 3584], P(('groups', 'role'), 'tp'), parts along dimension 0
There are 2 independent parts, one for each index of `groups`. A program takes and returns all parts, laid end to end along the dimension named above; an argument that names none is the same for every part. Nothing has to cross between parts.
Inputs may be any that keep to these rules, and one draw needn't show every extreme that they name: `expert_ids`: the rows of one device (96 tokens in a row) name no expert more than 72 times, and in every draw some expert is named exactly 72 times by the rows of some device. `placement`: each cache slot holds exactly one request.
All inputs are finite; a program needn't handle non-finite values.
Results may differ from a plain program's by a relative error of at most 0.0066.
Values may be sent and summed in bfloat16 or wider, within the bound.
No kernel may reach another device: no remote copies, remote signals or barrier semaphores. Data moves between devices by JAX's collectives and lax.ppermute only.
A program may use at most 64 MiB of HBM per device.

v0:
```python
import jax
import jax.numpy as jnp
from jax import lax
from jax.sharding import PartitionSpec as P

KV_RANK = 512


score_scale = 192.0 ** (-0.5)


def attend_local(q_lat, latent_cache, lengths, placement):
    slot_count = q_lat.shape[0]
    offset = lax.axis_index("role") * slot_count
    slot_ids = offset + jnp.arange(slot_count, dtype=jnp.int32)
    matches = placement[None, :] == slot_ids[:, None]
    slot_length = jnp.sum(jnp.where(matches, lengths[None, :], 0), axis=1)
    scores = (
        jnp.einsum("shc,stc->sht", q_lat, latent_cache, preferred_element_type=jnp.float32)
        * score_scale
    )
    position = jnp.arange(latent_cache.shape[1], dtype=jnp.int32)
    visible = position[None, None, :] < slot_length[:, None, None]
    scores = jnp.where(visible, scores, -jnp.inf)
    highest = jnp.max(scores, axis=2, keepdims=True)
    raised = jnp.exp(scores - highest)
    attn_weights = (raised / jnp.sum(raised, axis=2, keepdims=True)).astype(jnp.bfloat16)
    values = latent_cache[:, :, :KV_RANK]
    return jnp.einsum(
        "sht,stc->shc", attn_weights, values, preferred_element_type=jnp.float32
    ).astype(jnp.bfloat16)


def shards(
    q_lat, latent_cache, lengths, placement, tokens, expert_ids, gate_weights, w_gate, w_up, w_down
):
    attended = attend_local(q_lat, latent_cache, lengths, placement)
    role_count = lax.axis_size("role")
    token_count = expert_ids.shape[0]
    route_count = expert_ids.shape[1]
    capacity = 3 * token_count * route_count // (2 * role_count)
    flat_ids = expert_ids.reshape(-1)
    onehot = (flat_ids[:, None] == jnp.arange(role_count, dtype=jnp.int32)[None, :]).astype(
        jnp.int32
    )
    earlier = jnp.cumsum(onehot, axis=0) - onehot
    slot_index = jnp.sum(earlier * onehot, axis=1)
    target = flat_ids * capacity + slot_index
    source = jnp.arange(token_count * route_count, dtype=jnp.int32) // route_count
    outgoing = lax.all_gather(tokens, "tp", axis=1, tiled=True)
    columns = outgoing.shape[1]
    buffer_rows = (
        jnp.zeros((role_count * capacity, columns), jnp.bfloat16).at[target].set(outgoing[source])
    )
    buffer_rows = buffer_rows.reshape(role_count, capacity, columns)
    gate_matrix = w_gate[0]
    up_matrix = w_up[0]
    down_matrix = w_down[0]
    received = lax.all_to_all(buffer_rows, "role", split_axis=0, concat_axis=0, tiled=True)
    item_count = received.shape[1]
    arrived = received.reshape(role_count * item_count, columns)
    gate_proj = jnp.dot(arrived, gate_matrix, preferred_element_type=jnp.float32)
    up_proj = jnp.dot(arrived, up_matrix, preferred_element_type=jnp.float32)
    expert_hidden = (jax.nn.silu(gate_proj) * up_proj).astype(jnp.bfloat16)
    partial_out = jnp.dot(expert_hidden, down_matrix, preferred_element_type=jnp.float32)
    summed = lax.psum_scatter(
        partial_out.astype(jnp.bfloat16), "tp", scatter_dimension=1, tiled=True
    )
    summed = summed.reshape(role_count, item_count, summed.shape[1])
    returned = lax.all_to_all(summed, "role", split_axis=0, concat_axis=0, tiled=True)
    half_width = returned.shape[2]
    flat_back = returned.reshape(role_count * capacity, half_width)
    chosen_rows = (
        flat_back[target].reshape(token_count, route_count, half_width).astype(jnp.float32)
    )
    moe_result = jnp.sum(chosen_rows * gate_weights[:, :, None], axis=1).astype(jnp.bfloat16)
    return (attended, moe_result)


def solution(mesh):
    return jax.shard_map(
        shards,
        mesh=mesh,
        in_specs=(
            P(("groups", "role"), "tp", None),
            P(("groups", "role"), None, None),
            P("groups"),
            P("groups"),
            P(("groups", "role"), "tp"),
            P(("groups", "role"), None),
            P(("groups", "role"), None),
            P("role", None, "tp"),
            P("role", None, "tp"),
            P("role", "tp", None),
        ),
        out_specs=(P(("groups", "role"), "tp", None), P(("groups", "role"), "tp")),
        check_vma=False,
    )
```

profile of v0, /device:TPU:0, one launch (start us, length us, event | category | flops | bytes accessed | tf_op | source)
XLA Modules:
  0.0 216.8 jit_solution(13776567959777975198)
XLA Ops:
  7.2 0.0 copy-start
  7.2 0.0 reduce-scatter.2.cloned.1.call-start
  7.2 0.8 copy.21
  8.0 0.1 eq.45
  8.1 0.1 eq.41
  8.3 0.7 broadcast_multiply_fusion
  9.0 0.9 reduce-window.6
  9.8 0.2 slice_reduce_fusion
  10.1 0.1 copy.20
  10.2 0.1 mul.48
  10.3 2.6 %all_gather.3 = bf16[96,3584]{1,0:T(8,128)(2,1)S(1)} all-gather(bf16[96,1792]{1,0:T(8,128)(2,1)} %param.14), channel_id=1, replica_groups=mesh['groups'=2,'role'=8,'tp'=2] {'tp'}, dimensions={1}, use_global_device_ids=true | all-gather | bytes 1032192 | tf_op jit(solution)/shard_map/all_gather | solution.py:50
  12.9 0.1 fusion.21
  13.0 15.1 %scatter_custom_fusion = bf16[576,3584]{1,0:T(8,128)(2,1)} fusion(s32[384]{0:T(512)S(1)} %fusion.23, bf16[96,3584]{1,0:T(8,128)(2,1)S(1)} %all_gather.3, s32[1024]{0:T(1024)S(1)} %pad_clamp_fusion.1, bf16[]{:T(256)} %constant.39.clone.1), kind=kCustom, calls=%fused_computation.10 | custom fusion | bytes 4128770 | tf_op jit(solution)/shard_map/scatter | solution.py:53
  28.1 0.0 copy-start.6
  28.1 99.6 %all_to_all.10 = bf16[8,72,3584]{2,1,0:T(8,128)(2,1)S(1)} all-to-all(bf16[8,72,3584]{2,1,0:T(8,128)(2,1)} %bitcast.34), channel_id=1, replica_groups=mesh['groups'=2,'role'=8,'tp'=2] {'role'}, dimensions={0} | all-to-all | bytes 8257536 | tf_op jit(solution)/shard_map/all_to_all | solution.py:59
  127.7 0.0 copy-done.6
  127.7 0.0 copy-start.7
  127.7 2.3 %fusion.4 = f32[576,512]{1,0:T(8,128)S(1)} fusion(bf16[576,3584]{1,0:T(8,128)(2,1)S(1)} %bitcast.35, bf16[1,3584,512]{2,1,0:T(8,128)(2,1)S(1)} %copy-done.6), kind=kOutput, calls=%fused_computation.8 | convolution fusion | flops 2113929216 | bytes 8978432 | tf_op jit(solution)/shard_map/dot_general | solution.py:62
  130.0 0.0 copy-done.7
  130.0 0.0 copy-start.8
  130.0 2.4 %fusion.12 = bf16[576,512]{1,0:T(8,128)(2,1)S(1)} fusion(bf16[576,3584]{1,0:T(8,128)(2,1)S(1)} %bitcast.36, bf16[1,3584,512]{2,1,0:T(8,128)(2,1)S(1)} %copy-done.7, f32[576,512]{1,0:T(8,128)S(1)} %fusion.4), kind=kOutput, calls=%fused_computation.15 | convolution fusion | flops 2115698688 | bytes 9568256 | tf_op jit(solution)/shard_map/dot_general | solution.py:63
  132.5 0.0 copy-done.8
  132.5 4.3 %convolution_convert_fusion = bf16[576,3584]{1,0:T(8,128)(2,1)} fusion(bf16[576,512]{1,0:T(8,128)(2,1)S(1)} %fusion.12, bf16[1,512,3584]{2,1,0:T(8,128)(2,1)S(1)} %copy-done.8), kind=kOutput, calls=%fused_computation.4 | convolution fusion | flops 2115993600 | bytes 8388608 | tf_op jit(solution)/shard_map/dot_general | solution.py:65
  136.7 0.0 reduce-scatter.2.cloned.1.call-update
  136.8 0.0 copy-start.3
  136.8 0.0 copy-start.4
  136.8 0.0 copy-start.5
  136.8 0.0 copy-start.1
  136.8 11.0 %reduce-scatter.2.cloned.1.call-done = bf16[576,1792]{1,0:T(8,128)(2,1)} async-done(((bf16[576,3584]{1,0:T(8,128)(2,1)}), bf16[576,1792]{1,0:T(8,128)(2,1)}) %reduce-scatter.2.cloned.1.call-update) | async-done | bytes 2064400 | tf_op jit(solution)/shard_map/reduce_scatter | solution.py:66
  147.8 5.9 %all-to-all-start.1 = ((bf16[8,72,1792]{2,1,0:T(8,128)(2,1)}), bf16[8,72,1792]{2,1,0:T(8,128)(2,1)S(1)}, u32[]{:S(2)}, u32[]{:S(2)}) async-start(bf16[8,72,1792]{2,1,0:T(8,128)(2,1)} %bitcast.37), calls=%async_computation.2 | async-start | bytes 4128768 | tf_op jit(solution)/shard_map/all_to_all | solution.py:70
  153.7 0.0 copy-done.3
  153.7 0.7 copy.23
  154.5 0.0 copy-done.4
  154.5 0.0 copy-done.5
  154.5 0.2 select_reduce_fusion
  154.7 0.1 iota_compare_fusion.2
  154.8 0.0 copy-done
  154.8 0.0 copy-done.1
  154.8 0.3 fusion.17
  155.1 0.2 fusion.26
  155.3 1.1 convolution_convert_fusion.1
  156.4 45.3 %all-to-all-done.1 = bf16[8,72,1792]{2,1,0:T(8,128)(2,1)S(1)} async-done(((bf16[8,72,1792]{2,1,0:T(8,128)(2,1)}), bf16[8,72,1792]{2,1,0:T(8,128)(2,1)S(1)}, u32[]{:S(2)}, u32[]{:S(2)}) %all-to-all-start.1) | async-done | bytes 2064416 | tf_op jit(solution)/shard_map/all_to_all | solution.py:70
  201.6 3.0 %gather_fusion = bf16[384,1792]{1,0:T(8,128)(2,1)} fusion(bf16[576,1792]{1,0:T(8,128)(2,1)S(1)} %bitcast.33, s32[1024]{0:T(1024)S(1)} %pad_clamp_fusion), kind=kCustom, calls=%fused_computation.1 | custom fusion | bytes 2754048 | tf_op jit(solution)/shard_map/gather | solution.py:74
  204.6 0.0 copy-start.2
  204.6 2.7 %reshape.143 = f32[96,4,1792]{2,1,0:T(4,128)S(1)} reshape(bf16[384,1792]{1,0:T(8,128)(2,1)} %gather_fusion) | data formatting | bytes 4128768 | tf_op jit(solution)/shard_map/convert_element_type | solution.py:74
  207.3 0.0 copy-done.2
  207.3 2.7 %multiply_reduce_fusion = bf16[96,1792]{1,0:T(8,128)(2,1)} fusion(f32[96,4,1792]{2,1,0:T(4,128)S(1)} %reshape.143, f32[96,4]{1,0:T(8,128)S(1)} %copy-done.2), kind=kLoop, calls=%fused_computation.12 | loop fusion | flops 1204224 | bytes 3098112 | tf_op jit(solution)/shard_map/reduce_sum | solution.py:76
  (7 shorter events, 0.1 us)
Async XLA Ops:
  7.2 147.6 %copy-start = (bf16[4,32,576]{2,1,0:T(8,128)(2,1)S(1)}, bf16[4,32,576]{2,1,0:T(8,128)(2,1)}, u32[]{:S(2)}) copy-start(bf16[4,32,576]{2,1,0:T(8,128)(2,1)} %param.10) | copy-start | bytes 442372
  7.2 140.6 %reduce-scatter.2.cloned.1.call-start = ((), (), s32[]{:S(2)}) async-start(), calls=%async_computation.3 | async-start | bytes 6193152 | tf_op jit(solution)/shard_map/reduce_scatter | solution.py:66
  28.1 99.6 %copy-start.6 = (bf16[1,3584,512]{2,1,0:T(8,128)(2,1)S(1)}, bf16[1,3584,512]{2,1,0:T(8,128)(2,1)}, u32[]{:S(2)}) copy-start(bf16[1,3584,512]{2,1,0:T(8,128)(2,1)} %param.17) | copy-start | bytes 11010052
  127.7 2.3 %copy-start.7 = (bf16[1,3584,512]{2,1,0:T(8,128)(2,1)S(1)}, bf16[1,3584,512]{2,1,0:T(8,128)(2,1)}, u32[]{:S(2)}) copy-start(bf16[1,3584,512]{2,1,0:T(8,128)(2,1)} %param.18) | copy-start | bytes 11010052
  130.0 2.4 %copy-start.8 = (bf16[1,512,3584]{2,1,0:T(8,128)(2,1)S(1)}, bf16[1,512,3584]{2,1,0:T(8,128)(2,1)}, u32[]{:S(2)}) copy-start(bf16[1,512,3584]{2,1,0:T(8,128)(2,1)} %param.19) | copy-start | bytes 11010052
  136.8 17.0 %copy-start.3 = (f32[96,4]{0,1:T(4,128)S(1)}, f32[96,4]{0,1:T(4,128)}, u32[]{:S(2)}) copy-start(f32[96,4]{0,1:T(4,128)} %param.16) | copy-start | bytes 4612
  136.8 17.7 %copy-start.4 = (s32[32]{0:T(128)S(1)}, s32[32]{0:T(128)}, u32[]{:S(2)}) copy-start(s32[32]{0:T(128)} %param.12) | copy-start | bytes 388
  136.8 17.7 %copy-start.5 = (s32[32]{0:T(128)S(1)}, s32[32]{0:T(128)}, u32[]{:S(2)}) copy-start(s32[32]{0:T(128)} %param.13) | copy-start | bytes 388
  136.8 18.0 %copy-start.1 = (bf16[4,256,576]{1,2,0:T(8,128)(2,1)S(1)}, bf16[4,256,576]{1,2,0:T(8,128)(2,1)}, u32[]{:S(2)}) copy-start(bf16[4,256,576]{1,2,0:T(8,128)(2,1)} %param.11) | copy-start | bytes 3538948
  147.8 53.8 %all-to-all-start.1 = ((bf16[8,72,1792]{2,1,0:T(8,128)(2,1)}), bf16[8,72,1792]{2,1,0:T(8,128)(2,1)S(1)}, u32[]{:S(2)}, u32[]{:S(2)}) async-start(bf16[8,72,1792]{2,1,0:T(8,128)(2,1)} %bitcast.37), calls=%async_computation.2 | async-start | bytes 4128768 | tf_op jit(solution)/shard_map/all_to_all | solution.py:70
  204.6 2.7 %copy-start.2 = (f32[96,4]{1,0:T(8,128)S(1)}, f32[96,4]{1,0:T(8,128)}, u32[]{:S(2)}) copy-start(f32[96,4]{1,0:T(8,128)} %copy.23) | copy-start | bytes 4612
Sparse Core Ops, SparseCore 0:
  136.9 10.9 reduce-scatter.1
where the time goes:
time: 217 us
  blocking collectives  102 us (47%)
  waiting for transfers between devices  56.3 us (26%)
  local copies, waits for them, and re-layouts  23 us (11%)
  between operations  14.2 us (7%)
  matrix products  10.4 us (5%)
  starting transfers between devices  5.94 us (3%)
  other arithmetic  4.89 us (2%)
    all_to_all x1, blocking collectives, shards(): lax.all_to_all(buffer_rows, 'role', split_axis=0, concat_axis=0, tiled=True)  99.6 us
    all_to_all x1, waiting for transfers between devices, shards(): lax.all_to_all(summed, 'role', split_axis=0, concat_axis=0, tiled=True)  45.3 us
    scatter x1, local copies, waits for them, and re-layouts, shards(): jnp.zeros((role_count * capacity, columns), jnp.bfloat16).at[target]  15.1 us
    reduce_scatter x1, waiting for transfers between devices, shards(): lax.psum_scatter(partial_out.astype(jnp.bfloat16), 'tp', scatter_dimensio...  11 us
    all_to_all x1, starting transfers between devices, shards(): lax.all_to_all(summed, 'role', split_axis=0, concat_axis=0, tiled=True)  5.91 us
  transfers between devices with their start and end apart: 2, of which 2 were waited for; matrix products, arithmetic and copies ran while one was open for 1% of the time, Pallas kernels for 0%

commit v1 on v0

--- a/solution.py
+++ b/solution.py
@@ -1,6 +1,10 @@
+import functools
+
 import jax
 import jax.numpy as jnp
 from jax import lax
+from jax.experimental import pallas as pl
+from jax.experimental.pallas import tpu as pltpu
 from jax.sharding import PartitionSpec as P
 
 KV_RANK = 512
@@ -31,10 +35,7 @@
     ).astype(jnp.bfloat16)
 
 
-def shards(
-    q_lat, latent_cache, lengths, placement, tokens, expert_ids, gate_weights, w_gate, w_up, w_down
-):
-    attended = attend_local(q_lat, latent_cache, lengths, placement)
+def route_all_to_all(tokens, expert_ids, gate_weights, w_gate, w_up, w_down):
     role_count = lax.axis_size("role")
     token_count = expert_ids.shape[0]
     route_count = expert_ids.shape[1]
@@ -74,7 +75,324 @@
         flat_back[target].reshape(token_count, route_count, half_width).astype(jnp.float32)
     )
     moe_result = jnp.sum(chosen_rows * gate_weights[:, :, None], axis=1).astype(jnp.bfloat16)
-    return (attended, moe_result)
+    return moe_result
+
+
+LANES = 128
+VMEM_LIMIT = 56 * 1024 * 1024
+
+
+def round_up(value, unit):
+    return -(-value // unit) * unit
+
+
+def call(kernel, out_shape, flops, moved, **kwargs):
+    return pl.pallas_call(
+        kernel,
+        out_shape=out_shape,
+        compiler_params=pltpu.CompilerParams(vmem_limit_bytes=VMEM_LIMIT),
+        cost_estimate=pl.CostEstimate(flops=flops, bytes_accessed=moved, transcendentals=0),
+        **kwargs,
+    )
+
+
+def lane_index(rows):
+    return lax.broadcasted_iota(jnp.int32, (rows, LANES), 1)
+
+
+def decode_gate(pieces, expert, expert_count):
+    lane = lane_index(pieces.shape[0])
+    wanted = lane == expert
+    for piece in (1, 2):
+        wanted = wanted | (lane == expert + piece * expert_count)
+    return jnp.sum(jnp.where(wanted, pieces, 0.0), axis=1, keepdims=True)
+
+
+def slot_matrix(gate):
+    rows = gate.shape[0]
+    named = jnp.broadcast_to((gate > 0.0).astype(jnp.float32), (rows, LANES))
+    lower = lax.broadcasted_iota(jnp.int32, (rows, rows), 0) >= lax.broadcasted_iota(
+        jnp.int32, (rows, rows), 1
+    )
+    rank = jnp.dot(
+        lower.astype(jnp.bfloat16), named.astype(jnp.bfloat16), preferred_element_type=jnp.float32
+    )
+    slot = lane_index(rows).astype(jnp.float32)
+    return jnp.where((named > 0.0) & (rank - 1.0 == slot), 1.0, 0.0).astype(jnp.bfloat16)
+
+
+def compact(gate, rows_in, capacity):
+    picked = lax.dot_general(
+        slot_matrix(gate),
+        rows_in,
+        (((0,), (0,)), ((), ())),
+        preferred_element_type=jnp.float32,
+    )
+    return picked[:capacity].astype(jnp.bfloat16)
+
+
+def prepare_kernel(expert_count, tokens_ref, ids_ref, gates_ref, wide_ref, cross_ref):
+    rows, half = tokens_ref.shape
+    lane = lane_index(rows)
+    column = lane
+    for piece in (1, 2):
+        column = jnp.where(
+            (lane >= piece * expert_count) & (lane < (piece + 1) * expert_count),
+            lane - piece * expert_count,
+            column,
+        )
+    dense = jnp.zeros((rows, LANES), jnp.float32)
+    for choice in range(ids_ref.shape[1]):
+        dense = dense + jnp.where(
+            ids_ref[:, choice : choice + 1] == column, gates_ref[:, choice : choice + 1], 0.0
+        )
+    high = dense.astype(jnp.bfloat16).astype(jnp.float32)
+    middle = (dense - high).astype(jnp.bfloat16).astype(jnp.float32)
+    low = dense - high - middle
+    pieces = jnp.where(
+        lane < expert_count,
+        high,
+        jnp.where(
+            lane < 2 * expert_count, middle, jnp.where(lane < 3 * expert_count, low, 0.0)
+        ),
+    ).astype(jnp.bfloat16)
+    wide_ref[:, :half] = tokens_ref[...]
+    wide_ref[:, half:] = pieces
+    other = lax.axis_index("role") ^ 1
+    gate = decode_gate(pieces.astype(jnp.float32), other, expert_count)
+    cross_ref[...] = compact(gate, tokens_ref[...], cross_ref.shape[0])
+
+
+def prepare(tokens, expert_ids, gate_weights, expert_count, capacity):
+    rows, half = tokens.shape
+    return call(
+        functools.partial(prepare_kernel, expert_count),
+        (
+            jax.ShapeDtypeStruct((rows, half + LANES), jnp.bfloat16),
+            jax.ShapeDtypeStruct((capacity, half), jnp.bfloat16),
+        ),
+        2 * rows * LANES * half,
+        6 * rows * half,
+        name="prepare",
+    )(tokens, expert_ids, gate_weights)
+
+
+def cross_kernel(expert_count, wide_ref, cross_ref):
+    half = cross_ref.shape[1]
+    other = lax.axis_index("role") ^ 1
+    gate = decode_gate(wide_ref[:, half:].astype(jnp.float32), other, expert_count)
+    cross_ref[...] = compact(gate, wide_ref[:, :half], cross_ref.shape[0])
+
+
+def cross_rows(wide, expert_count, capacity):
+    rows, width = wide.shape
+    half = width - LANES
+    return call(
+        functools.partial(cross_kernel, expert_count),
+        jax.ShapeDtypeStruct((capacity, half), jnp.bfloat16),
+        2 * rows * LANES * half,
+        4 * rows * half,
+        name="cross_rows",
+    )(wide)
+
+
+def expert_kernel(starts, part_count, *refs):
+    parts = refs[: 2 * part_count]
+    gate_ref, up_ref, down_ref, keep_ref, send_ref, arrived, total = refs[2 * part_count :]
+    half = keep_ref.shape[1]
+    core = lax.axis_index("tp")
+    own = pl.ds(pl.multiple_of(core * half, LANES), half)
+    sibling = pl.ds(pl.multiple_of((1 - core) * half, LANES), half)
+    step = pl.program_id(0)
+
+    @pl.when(step == 0)
+    def _():
+        for index, start in enumerate(starts):
+            near, far = parts[2 * index], parts[2 * index + 1]
+            arrived[start : start + near.shape[0], own] = near[:, :half]
+            arrived[start : start + near.shape[0], sibling] = far[:, :half]
+
+    gate_proj = jnp.dot(arrived[...], gate_ref[...], preferred_element_type=jnp.float32)
+    up_proj = jnp.dot(arrived[...], up_ref[...], preferred_element_type=jnp.float32)
+    hidden = (jax.nn.silu(gate_proj) * up_proj).astype(jnp.bfloat16)
+    width = half // 2
+    for column in range(0, 2 * half, width):
+        columns = slice(column, column + width)
+        product = jnp.dot(hidden, down_ref[:, columns], preferred_element_type=jnp.float32)
+
+        @pl.when(step == 0)
+        def _():
+            total[:, columns] = product
+
+        @pl.when(step > 0)
+        def _():
+            total[:, columns] += product
+
+    @pl.when(step == pl.num_programs(0) - 1)
+    def _():
+        keep_ref[...] = total[:, own].astype(jnp.bfloat16)
+        send_ref[...] = total[:, sibling].astype(jnp.bfloat16)
+
+
+def expert(parts, half, w_gate, w_up, w_down):
+    _, depth, hidden_count = w_gate.shape
+    starts, rows = [], 0
+    for near, _ in parts:
+        starts.append(rows)
+        rows += near.shape[0]
+    steps = 2
+    width = hidden_count // steps
+    operands = [ref for pair in parts for ref in pair]
+    shape = jax.ShapeDtypeStruct((rows, half), jnp.bfloat16)
+    whole = pl.BlockSpec((rows, half), lambda step: (0, 0))
+    return call(
+        functools.partial(expert_kernel, tuple(starts), len(parts)),
+        (shape, shape),
+        6 * rows * depth * hidden_count,
+        6 * depth * hidden_count + 8 * rows * half,
+        grid=(steps,),
+        in_specs=[pl.BlockSpec(ref.shape, lambda step: (0, 0)) for ref in operands]
+        + [
+            pl.BlockSpec((None, depth, width), lambda step: (0, 0, step)),
+            pl.BlockSpec((None, depth, width), lambda step: (0, 0, step)),
+            pl.BlockSpec((None, width, depth), lambda step: (0, step, 0)),
+        ],
+        out_specs=(whole, whole),
+        scratch_shapes=[
+            pltpu.VMEM((rows, depth), jnp.bfloat16),
+            pltpu.VMEM((rows, depth), jnp.float32),
+        ],
+        name="expert",
+    )(*operands, w_gate, w_up, w_down)
+
+
+def add_parts(keep, received):
+    return (keep.astype(jnp.float32) + received.astype(jnp.float32)).astype(jnp.bfloat16)
+
+
+def outputs_kernel(starts, keep_ref, received_ref, *out_refs):
+    for start, out_ref in zip(starts, out_refs):
+        rows = slice(start, start + out_ref.shape[0])
+        out_ref[...] = add_parts(keep_ref[rows, :], received_ref[rows, :])
+
+
+def outputs(keep, received, starts, capacity):
+    half = keep.shape[1]
+    return call(
+        functools.partial(outputs_kernel, tuple(starts)),
+        tuple(jax.ShapeDtypeStruct((capacity, half), jnp.bfloat16) for _ in starts),
+        len(starts) * capacity * half,
+        6 * len(starts) * capacity * half,
+        name="outputs",
+    )(keep, received)
+
+
+def combine_kernel(expert_count, wide_ref, keep_ref, received_ref, back_ref, *refs):
+    sums, out_ref = refs[:-1], refs[-1]
+    half = out_ref.shape[1]
+    me = lax.axis_index("role")
+    pieces = wide_ref[:, half:].astype(jnp.float32)
+    gate = decode_gate(pieces, me, expert_count)
+    gate_other = decode_gate(pieces, me ^ 1, expert_count)
+    slots = slot_matrix(gate_other)[:, : back_ref.shape[0]]
+    spread = jnp.dot(slots, back_ref[...], preferred_element_type=jnp.float32)
+    own = add_parts(keep_ref[...], received_ref[...]).astype(jnp.float32)
+    result = gate * own + gate_other * spread
+    for ref in sums:
+        result = result + ref[...].astype(jnp.float32)
+    out_ref[...] = result.astype(jnp.bfloat16)
+
+
+def combine(wide, index, keep, received, back, sums, expert_count):
+    rows = wide.shape[0]
+    half = keep.shape[1]
+    block = pl.BlockSpec((rows, half), lambda step: (index, 0))
+    plain = pl.BlockSpec((rows, half), lambda step: (0, 0))
+    return call(
+        functools.partial(combine_kernel, expert_count),
+        jax.ShapeDtypeStruct((rows, half), jnp.bfloat16),
+        2 * rows * LANES * half,
+        12 * rows * half,
+        grid=(1,),
+        in_specs=[
+            pl.BlockSpec(wide.shape, lambda step: (0, 0)),
+            block,
+            block,
+            pl.BlockSpec(back.shape, lambda step: (0, 0)),
+        ]
+        + [plain] * len(sums),
+        out_specs=plain,
+        name="combine",
+    )(wide, keep, received, back, *sums)
+
+
+def swap(array, bits):
+    count = lax.axis_size("role")
+    return lax.ppermute(array, "role", [(device, device ^ bits) for device in range(count)])
+
+
+def swap_core(array):
+    return lax.ppermute(array, "tp", [(0, 1), (1, 0)])
+
+
+def route_multicast(tokens, expert_ids, gate_weights, w_gate, w_up, w_down):
+    role_count = lax.axis_size("role")
+    token_count, route_count = expert_ids.shape
+    half = tokens.shape[1]
+    capacity = round_up(3 * token_count * route_count // (2 * role_count), 16)
+    pair, mirror, row = 2, 6, 1
+
+    wide, cross = prepare(tokens, expert_ids, gate_weights, role_count, capacity)
+    wide_mirror = swap(wide, mirror)
+    wide_pair = swap(wide, pair)
+    cross_in = swap(cross, row)
+    cross_pair_in = swap(cross_rows(wide_pair, role_count, capacity), row)
+    wide_far = swap(wide_mirror, pair)
+    cross_mirror_in = swap(cross_rows(wide_mirror, role_count, capacity), row)
+    cross_far_in = swap(cross_rows(wide_far, role_count, capacity), row)
+
+    early = [wide, wide_pair, wide_mirror, cross_in, cross_pair_in]
+    late = [wide_far, cross_mirror_in, cross_far_in]
+    weights = (w_gate, w_up, w_down)
+    keep_early, send_early = expert([(a, swap_core(a)) for a in early], half, *weights)
+    received_early = swap_core(send_early)
+    keep_late, send_late = expert([(a, swap_core(a)) for a in late], half, *weights)
+    received_late = swap_core(send_late)
+
+    after = 3 * token_count
+    back_own, back_pair = outputs(
+        keep_early, received_early, (after, after + capacity), capacity
+    )
+    after = token_count
+    back_mirror, back_far = outputs(
+        keep_late, received_late, (after, after + capacity), capacity
+    )
+    back_far = swap(back_far, row)
+    back_mirror = swap(back_mirror, row)
+    back_pair = swap(back_pair, row)
+    back_own = swap(back_own, row)
+    sum_far = combine(wide_far, 0, keep_late, received_late, back_far, (), role_count)
+    from_far = swap(sum_far, pair)
+    sum_pair = combine(wide_pair, 1, keep_early, received_early, back_pair, (), role_count)
+    from_pair = swap(sum_pair, pair)
+    sum_mirror = combine(
+        wide_mirror, 2, keep_early, received_early, back_mirror, (from_far,), role_count
+    )
+    from_mirror = swap(sum_mirror, mirror)
+    return combine(
+        wide, 0, keep_early, received_early, back_own, (from_pair, from_mirror), role_count
+    )
+
+
+def shards(
+    q_lat, latent_cache, lengths, placement, tokens, expert_ids, gate_weights, w_gate, w_up, w_down
+):
+    attended = attend_local(q_lat, latent_cache, lengths, placement)
+    if lax.axis_size("role") == 8 and lax.axis_size("tp") == 2:
+        route = route_multicast
+    else:
+        route = route_all_to_all
+    return (attended, route(tokens, expert_ids, gate_weights, w_gate, w_up, w_down))
 
 
 def solution(mesh):

time: 217 us -> 136 us (0.63)
  blocking collectives: 102 us -> 0 us
  Pallas kernels: 0 us -> 48.8 us
  starting transfers between devices: 5.94 us -> 27.4 us
  between operations: 14.2 us -> 0.81 us
  waiting for transfers between devices: 56.3 us -> 44.7 us
  local copies, waits for them, and re-layouts: 23 us -> 12.4 us
  matrix products: 10.4 us -> 1.41 us
  other arithmetic: 4.89 us -> 0.44 us
    all_to_all x1 -> x0, blocking collectives: 99.6 us -> none  [shards(): lax.all_to_all(buffer_rows, 'role', split_axis=0, concat_axis=0, tiled=True)]
    pallas_call x0 -> x12, Pallas kernels: none -> 48.8 us  [the longest x2 24 us: expert(): call(functools.partial(expert_kernel, tuple(starts), len(parts)), (shape,...]
    all_to_all x1 -> x0, waiting for transfers between devices: 45.3 us -> none  [shards(): lax.all_to_all(summed, 'role', split_axis=0, concat_axis=0, tiled=True)]
    ppermute x0 -> x24, waiting for transfers between devices: none -> 44.7 us  [the longest x14 42 us: swap(): lax.ppermute(array, 'role', [(device, device ^ bits) for device in range(...]
    ppermute x0 -> x24, starting transfers between devices: none -> 27.4 us  [the longest x14 25.7 us: swap(): lax.ppermute(array, 'role', [(device, device ^ bits) for device in range(...]
    scatter x1 -> x0, local copies, waits for them, and re-layouts: 15.1 us -> none  [shards(): jnp.zeros((role_count * capacity, columns), jnp.bfloat16).at[target]]
    reduce_scatter x1 -> x0, waiting for transfers between devices: 11 us -> none  [shards(): lax.psum_scatter(partial_out.astype(jnp.bfloat16), 'tp', scatter_dimensio...]
    unnamed x20 -> x58, local copies, waits for them, and re-layouts: 1.59 us -> 12.4 us
  transfers between devices with their start and end apart: 2 -> 24, of which waited for: 2 -> 11; matrix products, arithmetic and copies ran while one was open for 1% -> 1% of each run, Pallas kernels for 0% -> 32%
where the time goes in v1:
time: 136 us
  Pallas kernels  48.8 us (36%)
  waiting for transfers between devices  44.7 us (33%)
  starting transfers between devices  27.4 us (20%)
  local copies, waits for them, and re-layouts  12.4 us (9%)
  matrix products  1.41 us (1%)
    ppermute x14, waiting for transfers between devices, swap(): lax.ppermute(array, 'role', [(device, device ^ bits) for device in range(...  42 us
    ppermute x14, starting transfers between devices, swap(): lax.ppermute(array, 'role', [(device, device ^ bits) for device in range(...  25.7 us
    pallas_call x2, Pallas kernels, expert(): call(functools.partial(expert_kernel, tuple(starts), len(parts)), (shape,...  24 us
    unnamed x58, local copies, waits for them, and re-layouts  12.4 us
    pallas_call x4, Pallas kernels, combine(): call(functools.partial(combine_kernel, expert_count), jax.ShapeDtypeStruc...  10.4 us
    pallas_call x3, Pallas kernels, cross_rows(): call(functools.partial(cross_kernel, expert_count), jax.ShapeDtypeStruct(...  6.66 us
    pallas_call x2, Pallas kernels, outputs(): call(functools.partial(outputs_kernel, tuple(starts)), tuple((jax.ShapeDt...  5.2 us
  transfers between devices with their start and end apart: 24, of which 11 were waited for; matrix products, arithmetic and copies ran while one was open for 1% of the time, Pallas kernels for 32%

profile of v1, /device:TPU:0, one launch (start us, length us, event | category | flops | bytes accessed | tf_op | source)
XLA Modules:
  0.0 135.9 jit_solution(66197998250720517)
XLA Ops:
  0.6 0.0 copy-start
  0.6 1.4 %copy.16.ids_ref = s32[96,4]{1,0:T(8,128)} copy(s32[96,4]{0,1:T(4,128)} %param.15) | data formatting | bytes 3072 | tf_op args[5]
  2.1 1.4 %copy.17.gates_ref = f32[96,4]{1,0:T(8,128)} copy(f32[96,4]{0,1:T(4,128)} %param.16) | data formatting | bytes 3072 | tf_op args[6]
  3.5 2.5 %prepare.1 = (bf16[96,1920]{1,0:T(8,128)(2,1)}, bf16[80,1792]{1,0:T(8,128)(2,1)}) custom-call(bf16[96,1792]{1,0:T(8,128)(2,1)} %tokens_ref.1, s32[96,4]{1,0:T(8,128)} %copy.16.ids_ref, f32[96,4]{1,0:T(8,128)} %copy.17.gates_ref), custom_call_target="tpu_custom_call" | custom-call | flops 44040192 | bytes 1032192 | tf_op jit(solution)/shard_map/prepare/pallas_call | solution.py:168
  6.0 5.0 %collective-permute-start.3 = (bf16[96,1920]{1,0:T(8,128)(2,1)}, bf16[96,1920]{1,0:T(8,128)(2,1)S(1)}, u32[]{:S(2)}, u32[]{:S(2)}) collective-permute-start(bf16[96,1920]{1,0:T(8,128)(2,1)} %get-tuple-element.12.refs_0_.wide_ref), channel_id=1, source_target_pairs={{0,12},{2,14},{4,8},{6,10},{8,4},{10,6},{12,0},{14,2},{1,13},{3,15... | collective-permute-start | bytes 1105928 | tf_op jit(solution)/shard_map/ppermute | solution.py:331
  11.0 1.5 %collective-permute-start.5 = (bf16[80,1792]{1,0:T(8,128)(2,1)}, bf16[80,1792]{1,0:T(8,128)(2,1)S(1)}, u32[]{:S(2)}, u32[]{:S(2)}) collective-permute-start(bf16[80,1792]{1,0:T(8,128)(2,1)} %get-tuple-element.13), channel_id=1, source_target_pairs={{0,2},{2,0},{4,6},{6,4},{8,10},{10,8},{12,14},{14,12},{1,3},{3,1},... | collective-permute-start | bytes 860168 | tf_op jit(solution)/shard_map/ppermute | solution.py:331
  12.6 0.0 collective-permute-start
  12.6 8.2 %collective-permute-done.3.refs_4_.wide_ref = bf16[96,1920]{1,0:T(8,128)(2,1)S(1)} collective-permute-done((bf16[96,1920]{1,0:T(8,128)(2,1)}, bf16[96,1920]{1,0:T(8,128)(2,1)S(1)}, u32[]{:S(2)}, u32[]{:S(2)}) %collective-permute-start.3) | collective-permute-done | bytes 368672 | tf_op jit(solution)/shard_map/ppermute | solution.py:331
  20.8 6.7 %collective-permute-start.13 = (bf16[96,1920]{1,0:T(8,128)(2,1)S(1)}, bf16[96,1920]{1,0:T(8,128)(2,1)S(1)}, u32[]{:S(2)}, u32[]{:S(2)}) collective-permute-start(bf16[96,1920]{1,0:T(8,128)(2,1)S(1)} %collective-permute-done.3.refs_4_.wide_ref), channel_id=1, source_target_pairs={{0,4},{2,6},{4,0},{6,2},{8,12},{10,14},{12,8},{14,10},{1,5},{3,7},... | collective-permute-start | bytes 1105928 | tf_op jit(solution)/shard_map/ppermute | solution.py:331
  27.5 0.0 collective-permute-done.5.refs_6_
  27.5 0.5 collective-permute-done.1.wide_ref.refs_2_
  27.9 0.8 copy-done.5
  28.7 2.2 %cross_rows.3 = bf16[80,1792]{1,0:T(8,128)(2,1)} custom-call(bf16[96,1920]{1,0:T(8,128)(2,1)} %copy-done.5), custom_call_target="tpu_custom_call" | custom-call | flops 44040192 | bytes 688128 | tf_op jit(solution)/shard_map/cross_rows/pallas_call | solution.py:190
  30.9 1.5 %collective-permute-start.7 = (bf16[80,1792]{1,0:T(8,128)(2,1)}, bf16[80,1792]{1,0:T(8,128)(2,1)S(1)}, u32[]{:S(2)}, u32[]{:S(2)}) collective-permute-start(bf16[80,1792]{1,0:T(8,128)(2,1)} %cross_rows.3), channel_id=1, source_target_pairs={{0,2},{2,0},{4,6},{6,4},{8,10},{10,8},{12,14},{14,12},{1,3},{3,1},... | collective-permute-start | bytes 860168 | tf_op jit(solution)/shard_map/ppermute | solution.py:331
  32.4 0.0 collective-permute-done.refs_1_
  32.4 0.5 collective-permute-start.2
  33.0 2.2 %cross_rows.4 = bf16[80,1792]{1,0:T(8,128)(2,1)} custom-call(bf16[96,1920]{1,0:T(8,128)(2,1)} %copy-done.4), custom_call_target="tpu_custom_call" | custom-call | flops 44040192 | bytes 688128 | tf_op jit(solution)/shard_map/cross_rows/pallas_call | solution.py:190
  35.2 0.5 collective-permute-done.13.wide_ref.refs_0_
  35.7 1.5 %collective-permute-start.15 = (bf16[80,1792]{1,0:T(8,128)(2,1)}, bf16[80,1792]{1,0:T(8,128)(2,1)S(1)}, u32[]{:S(2)}, u32[]{:S(2)}) collective-permute-start(bf16[80,1792]{1,0:T(8,128)(2,1)} %cross_rows.4), channel_id=1, source_target_pairs={{0,2},{2,0},{4,6},{6,4},{8,10},{10,8},{12,14},{14,12},{1,3},{3,1},... | collective-permute-start | bytes 860168 | tf_op jit(solution)/shard_map/ppermute | solution.py:331
  37.3 2.2 %cross_rows.5 = bf16[80,1792]{1,0:T(8,128)(2,1)} custom-call(bf16[96,1920]{1,0:T(8,128)(2,1)} %copy-done.3), custom_call_target="tpu_custom_call" | custom-call | flops 44040192 | bytes 688128 | tf_op jit(solution)/shard_map/cross_rows/pallas_call | solution.py:190
  39.5 0.7 collective-permute-start.17
  40.2 0.6 collective-permute-done.7.refs_8_
  40.8 6.1 %collective-permute-done.15.refs_2_ = bf16[80,1792]{1,0:T(8,128)(2,1)S(1)} collective-permute-done((bf16[80,1792]{1,0:T(8,128)(2,1)}, bf16[80,1792]{1,0:T(8,128)(2,1)S(1)}, u32[]{:S(2)}, u32[]{:S(2)}) %collective-permute-start.15) | collective-permute-done | bytes 286752 | tf_op jit(solution)/shard_map/ppermute | solution.py:331
  47.0 0.5 collective-permute-start.14
  47.5 4.7 %collective-permute-done.17.refs_4_ = bf16[80,1792]{1,0:T(8,128)(2,1)S(1)} collective-permute-done((bf16[80,1792]{1,0:T(8,128)(2,1)}, bf16[80,1792]{1,0:T(8,128)(2,1)S(1)}, u32[]{:S(2)}, u32[]{:S(2)}) %collective-permute-start.17) | collective-permute-done | bytes 286752 | tf_op jit(solution)/shard_map/ppermute | solution.py:331
  52.3 0.7 copy-done.23
  53.0 0.7 copy-done.27
  53.7 13.8 %expert.2 = (bf16[448,1792]{1,0:T(8,128)(2,1)}, bf16[448,1792]{1,0:T(8,128)(2,1)}) custom-call(bf16[96,1920]{1,0:T(8,128)(2,1)} %get-tuple-element.12.refs_0_.wide_ref, bf16[96,1920]{1,0:T(8,128)(2,1)} %copy-done.21, bf16[96,1920]{1,0:T(8,128)(2,1)} %copy-done.5, bf16[96,1920]{1,0:T(8,128)(2,1)} %copy-done.23, bf16[96,1920]{1,0:T(8,128)(2,1)} %copy-done.4, ...), custom_call_target="tpu_custom_call" | custom-call | flops 4932501504 | bytes 17432576 | tf_op jit(solution)/shard_map/expert/pallas_call | solution.py:248
  67.6 0.5 collective-permute-start.9
  68.1 0.7 copy-done.14
  68.8 0.1 copy-done.7
  68.9 0.8 copy-done.16
  69.7 10.2 %expert.3 = (bf16[256,1792]{1,0:T(8,128)(2,1)}, bf16[256,1792]{1,0:T(8,128)(2,1)}) custom-call(bf16[96,1920]{1,0:T(8,128)(2,1)} %copy-done.3, bf16[96,1920]{1,0:T(8,128)(2,1)} %copy-done.7, bf16[80,1792]{1,0:T(8,128)(2,1)} %copy-done.11, bf16[80,1792]{1,0:T(8,128)(2,1)} %copy-done.14, bf16[80,1792]{1,0:T(8,128)(2,1)} %copy-done.12, ...), custom_call_target="tpu_custom_call" | custom-call | flops 2818572288 | bytes 14680064 | tf_op jit(solution)/shard_map/expert/pallas_call | solution.py:248
  79.9 0.1 collective-permute-start.19
  80.0 2.7 %collective-permute-done.19.received_ref = bf16[256,1792]{1,0:T(8,128)(2,1)S(1)} collective-permute-done((bf16[256,1792]{1,0:T(8,128)(2,1)}, bf16[256,1792]{1,0:T(8,128)(2,1)S(1)}, u32[]{:S(2)}, u32[]{:S(2)}) %collective-permute-start.19) | collective-permute-done | bytes 917536 | tf_op jit(solution)/shard_map/ppermute | solution.py:335
  82.7 1.0 copy-done.2
  83.7 2.3 %outputs.3 = (bf16[80,1792]{1,0:T(8,128)(2,1)}, bf16[80,1792]{1,0:T(8,128)(2,1)}) custom-call(bf16[256,1792]{1,0:T(8,128)(2,1)} %get-tuple-element.18.keep_ref, bf16[256,1792]{1,0:T(8,128)(2,1)} %copy-done.2), custom_call_target="tpu_custom_call" | custom-call | flops 286720 | bytes 1720320 | tf_op jit(solution)/shard_map/outputs/pallas_call | solution.py:281
  86.0 1.5 %collective-permute-start.21 = (bf16[80,1792]{1,0:T(8,128)(2,1)}, bf16[80,1792]{1,0:T(8,128)(2,1)S(1)}, u32[]{:S(2)}, u32[]{:S(2)}) collective-permute-start(bf16[80,1792]{1,0:T(8,128)(2,1)} %get-tuple-element.21), channel_id=1, source_target_pairs={{0,2},{2,0},{4,6},{6,4},{8,10},{10,8},{12,14},{14,12},{1,3},{3,1},... | collective-permute-start | bytes 860168 | tf_op jit(solution)/shard_map/ppermute | solution.py:331
  87.5 0.2 select_reduce_fusion
  87.7 0.6 collective-permute-start.20
  88.3 7.6 %collective-permute-done.21.back_ref = bf16[80,1792]{1,0:T(8,128)(2,1)S(1)} collective-permute-done((bf16[80,1792]{1,0:T(8,128)(2,1)}, bf16[80,1792]{1,0:T(8,128)(2,1)S(1)}, u32[]{:S(2)}, u32[]{:S(2)}) %collective-permute-start.21) | collective-permute-done | bytes 286752 | tf_op jit(solution)/shard_map/ppermute | solution.py:331
  95.9 0.7 copy-done.18
  96.6 2.5 %combine.5 = bf16[96,1792]{1,0:T(8,128)(2,1)} custom-call(bf16[96,1920]{1,0:T(8,128)(2,1)} %copy-done.3, bf16[256,1792]{1,0:T(8,128)(2,1)} %get-tuple-element.18.keep_ref, bf16[256,1792]{1,0:T(8,128)(2,1)} %copy-done.2, bf16[80,1792]{1,0:T(8,128)(2,1)} %copy-done.18), custom_call_target="tpu_custom_call" | custom-call | flops 44040192 | bytes 2064384 | tf_op jit(solution)/shard_map/combine/pallas_call | solution.py:311
  99.1 0.5 collective-permute-start.22
  99.6 1.2 copy-done.1
  100.8 2.9 %outputs.2 = (bf16[80,1792]{1,0:T(8,128)(2,1)}, bf16[80,1792]{1,0:T(8,128)(2,1)}) custom-call(bf16[448,1792]{1,0:T(8,128)(2,1)} %get-tuple-element.14.keep_ref, bf16[448,1792]{1,0:T(8,128)(2,1)} %copy-done.1), custom_call_target="tpu_custom_call" | custom-call | flops 286720 | bytes 1720320 | tf_op jit(solution)/shard_map/outputs/pallas_call | solution.py:281
  103.6 1.5 %collective-permute-start.11 = (bf16[80,1792]{1,0:T(8,128)(2,1)}, bf16[80,1792]{1,0:T(8,128)(2,1)S(1)}, u32[]{:S(2)}, u32[]{:S(2)}) collective-permute-start(bf16[80,1792]{1,0:T(8,128)(2,1)} %get-tuple-element.17), channel_id=1, source_target_pairs={{0,2},{2,0},{4,6},{6,4},{8,10},{10,8},{12,14},{14,12},{1,3},{3,1},... | collective-permute-start | bytes 860168 | tf_op jit(solution)/shard_map/ppermute | solution.py:331
  105.2 0.1 iota_compare_fusion
  105.3 0.3 fusion.3
  105.6 0.5 collective-permute-start.10
  106.1 7.5 %collective-permute-done.11.back_ref = bf16[80,1792]{1,0:T(8,128)(2,1)S(1)} collective-permute-done((bf16[80,1792]{1,0:T(8,128)(2,1)}, bf16[80,1792]{1,0:T(8,128)(2,1)S(1)}, u32[]{:S(2)}, u32[]{:S(2)}) %collective-permute-start.11) | collective-permute-done | bytes 286752 | tf_op jit(solution)/shard_map/ppermute | solution.py:331
  113.6 0.7 copy-done.17
  114.3 2.5 %combine.4 = bf16[96,1792]{1,0:T(8,128)(2,1)} custom-call(bf16[96,1920]{1,0:T(8,128)(2,1)} %copy-done.5, bf16[448,1792]{1,0:T(8,128)(2,1)} %get-tuple-element.14.keep_ref, bf16[448,1792]{1,0:T(8,128)(2,1)} %copy-done.1, bf16[80,1792]{1,0:T(8,128)(2,1)} %copy-done.17), custom_call_target="tpu_custom_call" | custom-call | flops 44040192 | bytes 2064384 | tf_op jit(solution)/shard_map/combine/pallas_call | solution.py:311
  116.8 1.5 %collective-permute-start.12 = (bf16[96,1792]{1,0:T(8,128)(2,1)}, bf16[96,1792]{1,0:T(8,128)(2,1)S(1)}, u32[]{:S(2)}, u32[]{:S(2)}) collective-permute-start(bf16[96,1792]{1,0:T(8,128)(2,1)} %combine.4), channel_id=1, source_target_pairs={{0,4},{2,6},{4,0},{6,2},{8,12},{10,14},{12,8},{14,10},{1,5},{3,7},... | collective-permute-start | bytes 1032200 | tf_op jit(solution)/shard_map/ppermute | solution.py:331
  118.3 0.7 copy-done.13
  119.0 0.7 copy-done.8
  119.7 2.6 %combine.6 = bf16[96,1792]{1,0:T(8,128)(2,1)} custom-call(bf16[96,1920]{1,0:T(8,128)(2,1)} %copy-done.4, bf16[448,1792]{1,0:T(8,128)(2,1)} %get-tuple-element.14.keep_ref, bf16[448,1792]{1,0:T(8,128)(2,1)} %copy-done.1, bf16[80,1792]{1,0:T(8,128)(2,1)} %copy-done.13, bf16[96,1792]{1,0:T(8,128)(2,1)} %copy-done.8), custom_call_target="tpu_custom_call" | custom-call | flops 44040192 | bytes 2064384 | tf_op jit(solution)/shard_map/combine/pallas_call | solution.py:311
  122.4 2.5 %collective-permute-start.23 = (bf16[96,1792]{1,0:T(8,128)(2,1)}, bf16[96,1792]{1,0:T(8,128)(2,1)S(1)}, u32[]{:S(2)}, u32[]{:S(2)}) collective-permute-start(bf16[96,1792]{1,0:T(8,128)(2,1)} %combine.6), channel_id=1, source_target_pairs={{0,12},{2,14},{4,8},{6,10},{8,4},{10,6},{12,0},{14,2},{1,13},{3,15... | collective-permute-start | bytes 1032200 | tf_op jit(solution)/shard_map/ppermute | solution.py:331
  124.9 0.2 fusion.7
  125.0 1.1 convolution_convert_fusion
  126.1 1.8 %collective-permute-done.12.refs_0_ = bf16[96,1792]{1,0:T(8,128)(2,1)S(1)} collective-permute-done((bf16[96,1792]{1,0:T(8,128)(2,1)}, bf16[96,1792]{1,0:T(8,128)(2,1)S(1)}, u32[]{:S(2)}, u32[]{:S(2)}) %collective-permute-start.12) | collective-permute-done | bytes 344096 | tf_op jit(solution)/shard_map/ppermute | solution.py:331
  128.0 4.4 %collective-permute-done.23.refs_1_ = bf16[96,1792]{1,0:T(8,128)(2,1)S(1)} collective-permute-done((bf16[96,1792]{1,0:T(8,128)(2,1)}, bf16[96,1792]{1,0:T(8,128)(2,1)S(1)}, u32[]{:S(2)}, u32[]{:S(2)}) %collective-permute-start.23) | collective-permute-done | bytes 344096 | tf_op jit(solution)/shard_map/ppermute | solution.py:331
  132.4 0.7 copy-done.10
  133.1 2.8 %combine.7 = bf16[96,1792]{1,0:T(8,128)(2,1)} custom-call(bf16[96,1920]{1,0:T(8,128)(2,1)} %get-tuple-element.12.refs_0_.wide_ref, bf16[448,1792]{1,0:T(8,128)(2,1)} %get-tuple-element.14.keep_ref, bf16[448,1792]{1,0:T(8,128)(2,1)} %copy-done.1, bf16[80,1792]{1,0:T(8,128)(2,1)} %copy-done.15, bf16[96,1792]{1,0:T(8,128)(2,1)} %copy-done.9, ...), custom_call_target="tpu_custom_call" | custom-call | flops 44040192 | bytes 2064384 | tf_op jit(solution)/shard_map/combine/pallas_call | solution.py:311
  (60 shorter events, 0.1 us)
Async XLA Ops:
  0.6 104.6 %copy-start = (bf16[4,32,576]{2,1,0:T(8,128)(2,1)S(1)}, bf16[4,32,576]{2,1,0:T(8,128)(2,1)}, u32[]{:S(2)}) copy-start(bf16[4,32,576]{2,1,0:T(8,128)(2,1)} %param.10) | copy-start | bytes 442372
  6.0 14.8 %collective-permute-start.3 = (bf16[96,1920]{1,0:T(8,128)(2,1)}, bf16[96,1920]{1,0:T(8,128)(2,1)S(1)}, u32[]{:S(2)}, u32[]{:S(2)}) collective-permute-start(bf16[96,1920]{1,0:T(8,128)(2,1)} %get-tuple-element.12.refs_0_.wide_ref), channel_id=1, source_target_pairs={{0,12},{2,14},{4,8},{6,10},{8,4},{10,6},{12,0},{14,2},{1,13},{3,15... | collective-permute-start | bytes 1105928 | tf_op jit(solution)/shard_map/ppermute | solution.py:331
  11.0 16.9 %collective-permute-start.1 = (bf16[96,1920]{1,0:T(8,128)(2,1)}, bf16[96,1920]{1,0:T(8,128)(2,1)S(1)}, u32[]{:S(2)}, u32[]{:S(2)}) collective-permute-start(bf16[96,1920]{1,0:T(8,128)(2,1)} %get-tuple-element.12.refs_0_.wide_ref), channel_id=1, source_target_pairs={{0,4},{2,6},{4,0},{6,2},{8,12},{10,14},{12,8},{14,10},{1,5},{3,7},... | collective-permute-start | bytes 1105928 | tf_op jit(solution)/shard_map/ppermute | solution.py:331
  11.0 16.4 %collective-permute-start.5 = (bf16[80,1792]{1,0:T(8,128)(2,1)}, bf16[80,1792]{1,0:T(8,128)(2,1)S(1)}, u32[]{:S(2)}, u32[]{:S(2)}) collective-permute-start(bf16[80,1792]{1,0:T(8,128)(2,1)} %get-tuple-element.13), channel_id=1, source_target_pairs={{0,2},{2,0},{4,6},{6,4},{8,10},{10,8},{12,14},{14,12},{1,3},{3,1},... | collective-permute-start | bytes 860168 | tf_op jit(solution)/shard_map/ppermute | solution.py:331
  12.6 19.9 %collective-permute-start = (bf16[96,1920]{1,0:T(8,128)(2,1)}, bf16[96,1920]{1,0:T(8,128)(2,1)S(1)}, u32[]{:S(2)}, u32[]{:S(2)}) collective-permute-start(bf16[96,1920]{1,0:T(8,128)(2,1)} %get-tuple-element.12.refs_0_.wide_ref), channel_id=1, source_target_pairs={{0,1},{1,0},{2,3},{3,2},{4,5},{5,4},{6,7},{7,6},{8,9},{9,8},{10,11... | collective-permute-start | bytes 1105928 | tf_op jit(solution)/shard_map/ppermute | solution.py:335
  20.8 12.2 %copy-start.4 = (bf16[96,1920]{1,0:T(8,128)(2,1)}, bf16[96,1920]{1,0:T(8,128)(2,1)S(1)}, u32[]{:S(2)}) copy-start(bf16[96,1920]{1,0:T(8,128)(2,1)S(1)} %collective-permute-done.3.refs_4_.wide_ref) | copy-start | bytes 1105924
  20.8 15.0 %collective-permute-start.13 = (bf16[96,1920]{1,0:T(8,128)(2,1)S(1)}, bf16[96,1920]{1,0:T(8,128)(2,1)S(1)}, u32[]{:S(2)}, u32[]{:S(2)}) collective-permute-start(bf16[96,1920]{1,0:T(8,128)(2,1)S(1)} %collective-permute-done.3.refs_4_.wide_ref), channel_id=1, source_target_pairs={{0,4},{2,6},{4,0},{6,2},{8,12},{10,14},{12,8},{14,10},{1,5},{3,7},... | collective-permute-start | bytes 1105928 | tf_op jit(solution)/shard_map/ppermute | solution.py:331
  27.5 24.8 %copy-start.24 = (bf16[80,1792]{1,0:T(8,128)(2,1)}, bf16[80,1792]{1,0:T(8,128)(2,1)S(1)}, u32[]{:S(2)}) copy-start(bf16[80,1792]{1,0:T(8,128)(2,1)S(1)} %collective-permute-done.5.refs_6_) | copy-start | bytes 860164
  27.5 12.0 %collective-permute-start.6 = (bf16[80,1792]{1,0:T(8,128)(2,1)S(1)}, bf16[80,1792]{1,0:T(8,128)(2,1)S(1)}, u32[]{:S(2)}, u32[]{:S(2)}) collective-permute-start(bf16[80,1792]{1,0:T(8,128)(2,1)S(1)} %collective-permute-done.5.refs_6_), channel_id=1, source_target_pairs={{0,1},{1,0},{2,3},{3,2},{4,5},{5,4},{6,7},{7,6},{8,9},{9,8},{10,11... | collective-permute-start | bytes 860168 | tf_op jit(solution)/shard_map/ppermute | solution.py:335
  27.9 0.8 copy-start.5
  30.9 9.9 %collective-permute-start.7 = (bf16[80,1792]{1,0:T(8,128)(2,1)}, bf16[80,1792]{1,0:T(8,128)(2,1)S(1)}, u32[]{:S(2)}, u32[]{:S(2)}) collective-permute-start(bf16[80,1792]{1,0:T(8,128)(2,1)} %cross_rows.3), channel_id=1, source_target_pairs={{0,2},{2,0},{4,6},{6,4},{8,10},{10,8},{12,14},{14,12},{1,3},{3,1},... | collective-permute-start | bytes 860168 | tf_op jit(solution)/shard_map/ppermute | solution.py:331
  32.4 14.5 %collective-permute-start.4 = (bf16[96,1920]{1,0:T(8,128)(2,1)S(1)}, bf16[96,1920]{1,0:T(8,128)(2,1)S(1)}, u32[]{:S(2)}, u32[]{:S(2)}) collective-permute-start(bf16[96,1920]{1,0:T(8,128)(2,1)S(1)} %collective-permute-done.3.refs_4_.wide_ref), channel_id=1, source_target_pairs={{0,1},{1,0},{2,3},{3,2},{4,5},{5,4},{6,7},{7,6},{8,9},{9,8},{10,11... | collective-permute-start | bytes 1105928 | tf_op jit(solution)/shard_map/ppermute | solution.py:335
  32.4 19.8 %copy-start.21 = (bf16[96,1920]{1,0:T(8,128)(2,1)}, bf16[96,1920]{1,0:T(8,128)(2,1)S(1)}, u32[]{:S(2)}) copy-start(bf16[96,1920]{1,0:T(8,128)(2,1)S(1)} %collective-permute-done.refs_1_) | copy-start | bytes 1105924
  32.4 19.8 %collective-permute-start.2 = (bf16[96,1920]{1,0:T(8,128)(2,1)}, bf16[96,1920]{1,0:T(8,128)(2,1)S(1)}, u32[]{:S(2)}, u32[]{:S(2)}) collective-permute-start(bf16[96,1920]{1,0:T(8,128)(2,1)} %copy-done.5), channel_id=1, source_target_pairs={{0,1},{1,0},{2,3},{3,2},{4,5},{5,4},{6,7},{7,6},{8,9},{9,8},{10,11... | collective-permute-start | bytes 1105928 | tf_op jit(solution)/shard_map/ppermute | solution.py:335
  35.7 1.5 %copy-start.3 = (bf16[96,1920]{1,0:T(8,128)(2,1)}, bf16[96,1920]{1,0:T(8,128)(2,1)S(1)}, u32[]{:S(2)}) copy-start(bf16[96,1920]{1,0:T(8,128)(2,1)S(1)} %collective-permute-done.13.wide_ref.refs_0_) | copy-start | bytes 1105924
  35.7 11.2 %collective-permute-start.15 = (bf16[80,1792]{1,0:T(8,128)(2,1)}, bf16[80,1792]{1,0:T(8,128)(2,1)S(1)}, u32[]{:S(2)}, u32[]{:S(2)}) collective-permute-start(bf16[80,1792]{1,0:T(8,128)(2,1)} %cross_rows.4), channel_id=1, source_target_pairs={{0,2},{2,0},{4,6},{6,4},{8,10},{10,8},{12,14},{14,12},{1,3},{3,1},... | collective-permute-start | bytes 860168 | tf_op jit(solution)/shard_map/ppermute | solution.py:331
  39.5 12.8 %copy-start.25 = (bf16[80,1792]{1,0:T(8,128)(2,1)}, bf16[80,1792]{1,0:T(8,128)(2,1)S(1)}, u32[]{:S(2)}) copy-start(bf16[80,1792]{1,0:T(8,128)(2,1)S(1)} %collective-permute-done.6.refs_7_) | copy-start | bytes 860164
  39.5 12.7 %collective-permute-start.17 = (bf16[80,1792]{1,0:T(8,128)(2,1)}, bf16[80,1792]{1,0:T(8,128)(2,1)S(1)}, u32[]{:S(2)}, u32[]{:S(2)}) collective-permute-start(bf16[80,1792]{1,0:T(8,128)(2,1)} %cross_rows.5), channel_id=1, source_target_pairs={{0,2},{2,0},{4,6},{6,4},{8,10},{10,8},{12,14},{14,12},{1,3},{3,1},... | collective-permute-start | bytes 860168 | tf_op jit(solution)/shard_map/ppermute | solution.py:331
  40.8 11.4 %copy-start.26 = (bf16[80,1792]{1,0:T(8,128)(2,1)}, bf16[80,1792]{1,0:T(8,128)(2,1)S(1)}, u32[]{:S(2)}) copy-start(bf16[80,1792]{1,0:T(8,128)(2,1)S(1)} %collective-permute-done.7.refs_8_) | copy-start | bytes 860164
  40.8 11.4 %collective-permute-start.8 = (bf16[80,1792]{1,0:T(8,128)(2,1)S(1)}, bf16[80,1792]{1,0:T(8,128)(2,1)S(1)}, u32[]{:S(2)}, u32[]{:S(2)}) collective-permute-start(bf16[80,1792]{1,0:T(8,128)(2,1)S(1)} %collective-permute-done.7.refs_8_), channel_id=1, source_target_pairs={{0,1},{1,0},{2,3},{3,2},{4,5},{5,4},{6,7},{7,6},{8,9},{9,8},{10,11... | collective-permute-start | bytes 860168 | tf_op jit(solution)/shard_map/ppermute | solution.py:335
  47.0 20.6 %copy-start.11 = (bf16[80,1792]{1,0:T(8,128)(2,1)}, bf16[80,1792]{1,0:T(8,128)(2,1)S(1)}, u32[]{:S(2)}) copy-start(bf16[80,1792]{1,0:T(8,128)(2,1)S(1)} %collective-permute-done.15.refs_2_) | copy-start | bytes 860164
  47.0 21.1 %collective-permute-start.16 = (bf16[80,1792]{1,0:T(8,128)(2,1)S(1)}, bf16[80,1792]{1,0:T(8,128)(2,1)S(1)}, u32[]{:S(2)}, u32[]{:S(2)}) collective-permute-start(bf16[80,1792]{1,0:T(8,128)(2,1)S(1)} %collective-permute-done.15.refs_2_), channel_id=1, source_target_pairs={{0,1},{1,0},{2,3},{3,2},{4,5},{5,4},{6,7},{7,6},{8,9},{9,8},{10,11... | collective-permute-start | bytes 860168 | tf_op jit(solution)/shard_map/ppermute | solution.py:335
  47.0 5.3 %copy-start.22 = (bf16[96,1920]{1,0:T(8,128)(2,1)}, bf16[96,1920]{1,0:T(8,128)(2,1)S(1)}, u32[]{:S(2)}) copy-start(bf16[96,1920]{1,0:T(8,128)(2,1)S(1)} %collective-permute-done.4.refs_5_) | copy-start | bytes 1105924
  47.0 21.1 %collective-permute-start.14 = (bf16[96,1920]{1,0:T(8,128)(2,1)}, bf16[96,1920]{1,0:T(8,128)(2,1)S(1)}, u32[]{:S(2)}, u32[]{:S(2)}) collective-permute-start(bf16[96,1920]{1,0:T(8,128)(2,1)} %copy-done.3), channel_id=1, source_target_pairs={{0,1},{1,0},{2,3},{3,2},{4,5},{5,4},{6,7},{7,6},{8,9},{9,8},{10,11... | collective-permute-start | bytes 1105928 | tf_op jit(solution)/shard_map/ppermute | solution.py:335
  52.2 15.4 %copy-start.12 = (bf16[80,1792]{1,0:T(8,128)(2,1)}, bf16[80,1792]{1,0:T(8,128)(2,1)S(1)}, u32[]{:S(2)}) copy-start(bf16[80,1792]{1,0:T(8,128)(2,1)S(1)} %collective-permute-done.17.refs_4_) | copy-start | bytes 860164
  52.2 15.9 %collective-permute-start.18 = (bf16[80,1792]{1,0:T(8,128)(2,1)S(1)}, bf16[80,1792]{1,0:T(8,128)(2,1)S(1)}, u32[]{:S(2)}, u32[]{:S(2)}) collective-permute-start(bf16[80,1792]{1,0:T(8,128)(2,1)S(1)} %collective-permute-done.17.refs_4_), channel_id=1, source_target_pairs={{0,1},{1,0},{2,3},{3,2},{4,5},{5,4},{6,7},{7,6},{8,9},{9,8},{10,11... | collective-permute-start | bytes 860168 | tf_op jit(solution)/shard_map/ppermute | solution.py:335
  52.2 0.8 copy-start.23
  53.0 0.7 copy-start.27
  67.6 32.1 %collective-permute-start.9 = (bf16[448,1792]{1,0:T(8,128)(2,1)}, bf16[448,1792]{1,0:T(8,128)(2,1)S(1)}, u32[]{:S(2)}, u32[]{:S(2)}) collective-permute-start(bf16[448,1792]{1,0:T(8,128)(2,1)} %get-tuple-element.15), channel_id=1, source_target_pairs={{0,1},{1,0},{2,3},{3,2},{4,5},{5,4},{6,7},{7,6},{8,9},{9,8},{10,11... | collective-permute-start | bytes 4816904 | tf_op jit(solution)/shard_map/ppermute | solution.py:335
  68.1 0.7 copy-start.14
  68.1 0.8 copy-start.7
  68.9 0.8 copy-start.16
  79.9 7.6 %copy-start.19 = (s32[32]{0:T(128)S(1)}, s32[32]{0:T(128)}, u32[]{:S(2)}) copy-start(s32[32]{0:T(128)} %param.12) | copy-start | bytes 388
  79.9 7.6 %copy-start.20 = (s32[32]{0:T(128)S(1)}, s32[32]{0:T(128)}, u32[]{:S(2)}) copy-start(s32[32]{0:T(128)} %param.13) | copy-start | bytes 388
  79.9 2.7 %collective-permute-start.19 = (bf16[256,1792]{1,0:T(8,128)(2,1)}, bf16[256,1792]{1,0:T(8,128)(2,1)S(1)}, u32[]{:S(2)}, u32[]{:S(2)}) collective-permute-start(bf16[256,1792]{1,0:T(8,128)(2,1)} %get-tuple-element.19), channel_id=1, source_target_pairs={{0,1},{1,0},{2,3},{3,2},{4,5},{5,4},{6,7},{7,6},{8,9},{9,8},{10,11... | collective-permute-start | bytes 2752520 | tf_op jit(solution)/shard_map/ppermute | solution.py:335
  82.7 1.0 copy-start.2
  86.0 9.9 %collective-permute-start.21 = (bf16[80,1792]{1,0:T(8,128)(2,1)}, bf16[80,1792]{1,0:T(8,128)(2,1)S(1)}, u32[]{:S(2)}, u32[]{:S(2)}) collective-permute-start(bf16[80,1792]{1,0:T(8,128)(2,1)} %get-tuple-element.21), channel_id=1, source_target_pairs={{0,2},{2,0},{4,6},{6,4},{8,10},{10,8},{12,14},{14,12},{1,3},{3,1},... | collective-permute-start | bytes 860168 | tf_op jit(solution)/shard_map/ppermute | solution.py:331
  87.7 30.6 %collective-permute-start.20 = (bf16[80,1792]{1,0:T(8,128)(2,1)}, bf16[80,1792]{1,0:T(8,128)(2,1)S(1)}, u32[]{:S(2)}, u32[]{:S(2)}) collective-permute-start(bf16[80,1792]{1,0:T(8,128)(2,1)} %get-tuple-element.20), channel_id=1, source_target_pairs={{0,2},{2,0},{4,6},{6,4},{8,10},{10,8},{12,14},{14,12},{1,3},{3,1},... | collective-permute-start | bytes 860168 | tf_op jit(solution)/shard_map/ppermute | solution.py:331
  95.9 0.7 copy-start.18
  99.1 19.2 %collective-permute-start.22 = (bf16[96,1792]{1,0:T(8,128)(2,1)}, bf16[96,1792]{1,0:T(8,128)(2,1)S(1)}, u32[]{:S(2)}, u32[]{:S(2)}) collective-permute-start(bf16[96,1792]{1,0:T(8,128)(2,1)} %combine.5), channel_id=1, source_target_pairs={{0,4},{2,6},{4,0},{6,2},{8,12},{10,14},{12,8},{14,10},{1,5},{3,7},... | collective-permute-start | bytes 1032200 | tf_op jit(solution)/shard_map/ppermute | solution.py:331
  99.6 1.2 copy-start.1
  100.8 4.5 %copy-start.6 = (bf16[4,256,576]{1,2,0:T(8,128)(2,1)S(1)}, bf16[4,256,576]{1,2,0:T(8,128)(2,1)}, u32[]{:S(2)}) copy-start(bf16[4,256,576]{1,2,0:T(8,128)(2,1)} %param.11) | copy-start | bytes 3538948
  103.6 10.0 %collective-permute-start.11 = (bf16[80,1792]{1,0:T(8,128)(2,1)}, bf16[80,1792]{1,0:T(8,128)(2,1)S(1)}, u32[]{:S(2)}, u32[]{:S(2)}) collective-permute-start(bf16[80,1792]{1,0:T(8,128)(2,1)} %get-tuple-element.17), channel_id=1, source_target_pairs={{0,2},{2,0},{4,6},{6,4},{8,10},{10,8},{12,14},{14,12},{1,3},{3,1},... | collective-permute-start | bytes 860168 | tf_op jit(solution)/shard_map/ppermute | solution.py:331
  105.6 20.6 %collective-permute-start.10 = (bf16[80,1792]{1,0:T(8,128)(2,1)}, bf16[80,1792]{1,0:T(8,128)(2,1)S(1)}, u32[]{:S(2)}, u32[]{:S(2)}) collective-permute-start(bf16[80,1792]{1,0:T(8,128)(2,1)} %get-tuple-element.16), channel_id=1, source_target_pairs={{0,2},{2,0},{4,6},{6,4},{8,10},{10,8},{12,14},{14,12},{1,3},{3,1},... | collective-permute-start | bytes 860168 | tf_op jit(solution)/shard_map/ppermute | solution.py:331
  113.6 0.7 copy-start.17
  116.8 11.1 %collective-permute-start.12 = (bf16[96,1792]{1,0:T(8,128)(2,1)}, bf16[96,1792]{1,0:T(8,128)(2,1)S(1)}, u32[]{:S(2)}, u32[]{:S(2)}) collective-permute-start(bf16[96,1792]{1,0:T(8,128)(2,1)} %combine.4), channel_id=1, source_target_pairs={{0,4},{2,6},{4,0},{6,2},{8,12},{10,14},{12,8},{14,10},{1,5},{3,7},... | collective-permute-start | bytes 1032200 | tf_op jit(solution)/shard_map/ppermute | solution.py:331
  118.3 0.7 copy-start.13
  119.0 0.7 copy-start.8
  122.4 10.0 %collective-permute-start.23 = (bf16[96,1792]{1,0:T(8,128)(2,1)}, bf16[96,1792]{1,0:T(8,128)(2,1)S(1)}, u32[]{:S(2)}, u32[]{:S(2)}) collective-permute-start(bf16[96,1792]{1,0:T(8,128)(2,1)} %combine.6), channel_id=1, source_target_pairs={{0,12},{2,14},{4,8},{6,10},{8,4},{10,6},{12,0},{14,2},{1,13},{3,15... | collective-permute-start | bytes 1032200 | tf_op jit(solution)/shard_map/ppermute | solution.py:331
  126.1 6.3 %copy-start.15 = (bf16[80,1792]{1,0:T(8,128)(2,1)}, bf16[80,1792]{1,0:T(8,128)(2,1)S(1)}, u32[]{:S(2)}) copy-start(bf16[80,1792]{1,0:T(8,128)(2,1)S(1)} %collective-permute-done.10.back_ref) | copy-start | bytes 860164
  128.0 4.5 %copy-start.9 = (bf16[96,1792]{1,0:T(8,128)(2,1)}, bf16[96,1792]{1,0:T(8,128)(2,1)S(1)}, u32[]{:S(2)}) copy-start(bf16[96,1792]{1,0:T(8,128)(2,1)S(1)} %collective-permute-done.12.refs_0_) | copy-start | bytes 1032196
  132.4 0.7 copy-start.10

commit v2 on v0

--- a/solution.py
+++ b/solution.py
@@ -1,6 +1,10 @@
+import functools
+
 import jax
 import jax.numpy as jnp
 from jax import lax
+from jax.experimental import pallas as pl
+from jax.experimental.pallas import tpu as pltpu
 from jax.sharding import PartitionSpec as P
 
 KV_RANK = 512
@@ -31,10 +35,7 @@
     ).astype(jnp.bfloat16)
 
 
-def shards(
-    q_lat, latent_cache, lengths, placement, tokens, expert_ids, gate_weights, w_gate, w_up, w_down
-):
-    attended = attend_local(q_lat, latent_cache, lengths, placement)
+def route_all_to_all(tokens, expert_ids, gate_weights, w_gate, w_up, w_down):
     role_count = lax.axis_size("role")
     token_count = expert_ids.shape[0]
     route_count = expert_ids.shape[1]
@@ -74,7 +75,438 @@
         flat_back[target].reshape(token_count, route_count, half_width).astype(jnp.float32)
     )
     moe_result = jnp.sum(chosen_rows * gate_weights[:, :, None], axis=1).astype(jnp.bfloat16)
+    return moe_result
+
+
+LANES = 128
+VMEM_LIMIT = 16 * 1024 * 1024
+
+
+def round_up(value, unit):
+    return -(-value // unit) * unit
+
+
+def call(kernel, operands, out_shapes, flops, name, scratch=(), types=None, last=False):
+    place = pl.BlockSpec(memory_space=pltpu.VMEM)
+    return pl.pallas_call(
+        kernel,
+        in_specs=[place] * len(operands),
+        out_specs=[place] * len(out_shapes),
+        out_shape=[
+            (jax.ShapeDtypeStruct if last else pltpu.VMEM)(
+                shape, jnp.bfloat16 if types is None else types[index]
+            )
+            for index, shape in enumerate(out_shapes)
+        ],
+        scratch_shapes=list(scratch),
+        name=name,
+        compiler_params=pltpu.CompilerParams(vmem_limit_bytes=VMEM_LIMIT),
+        cost_estimate=pl.CostEstimate(flops=0, bytes_accessed=0, transcendentals=0),
+    )(*[pltpu.with_memory_space_constraint(operand, pltpu.VMEM) for operand in operands])
+
+
+def after(value, *earlier):
+    return lax.optimization_barrier((value, *earlier))[0]
+
+
+def lane_index(rows):
+    return lax.broadcasted_iota(jnp.int32, (rows, LANES), 1)
+
+
+def decode_gate(pieces, expert, expert_count):
+    lane = lane_index(pieces.shape[0])
+    wanted = lane == expert
+    for piece in (1, 2):
+        wanted = wanted | (lane == expert + piece * expert_count)
+    return jnp.sum(jnp.where(wanted, pieces, 0.0), axis=1, keepdims=True)
+
+
+def slot_matrix(gate):
+    rows = gate.shape[0]
+    named = jnp.broadcast_to((gate > 0.0).astype(jnp.float32), (rows, LANES))
+    lower = lax.broadcasted_iota(jnp.int32, (rows, rows), 0) >= lax.broadcasted_iota(
+        jnp.int32, (rows, rows), 1
+    )
+    rank = jnp.dot(
+        lower.astype(jnp.bfloat16), named.astype(jnp.bfloat16), preferred_element_type=jnp.float32
+    )
+    slot = lane_index(rows).astype(jnp.float32)
+    return jnp.where((named > 0.0) & (rank - 1.0 == slot), 1.0, 0.0).astype(jnp.bfloat16)
+
+
+def compact(gate, rows_in, capacity):
+    picked = lax.dot_general(
+        slot_matrix(gate),
+        rows_in,
+        (((0,), (0,)), ((), ())),
+        preferred_element_type=jnp.float32,
+    )
+    return picked[:capacity].astype(jnp.bfloat16)
+
+
+def prepare_kernel(expert_count, tokens_ref, ids_ref, gates_ref, wide_ref, cross_ref):
+    rows, half = tokens_ref.shape
+    piece_rows = round_up(3 * expert_count, 16)
+    line = lax.broadcasted_iota(jnp.int32, (piece_rows, rows), 0)
+    named = line
+    for piece in (1, 2):
+        named = jnp.where(line >= piece * expert_count, line - piece * expert_count, named)
+    dense = jnp.zeros((piece_rows, rows), jnp.float32)
+    for choice in range(ids_ref.shape[0]):
+        dense = dense + jnp.where(
+            ids_ref[choice : choice + 1, :] == named, gates_ref[choice : choice + 1, :], 0.0
+        )
+    high = dense.astype(jnp.bfloat16).astype(jnp.float32)
+    middle = (dense - high).astype(jnp.bfloat16).astype(jnp.float32)
+    low = dense - high - middle
+    pieces = jnp.where(line < expert_count, high, jnp.where(line < 2 * expert_count, middle, low))
+    unit = lax.broadcasted_iota(jnp.int32, (piece_rows, LANES), 0) == lax.broadcasted_iota(
+        jnp.int32, (piece_rows, LANES), 1
+    )
+    turned = lax.dot_general(
+        pieces.astype(jnp.bfloat16),
+        unit.astype(jnp.bfloat16),
+        (((0,), (0,)), ((), ())),
+        preferred_element_type=jnp.float32,
+    )
+    wide_ref[:, :half] = tokens_ref[...]
+    wide_ref[:, half:] = turned.astype(jnp.bfloat16)
+    gate = decode_gate(turned, lax.axis_index("role") ^ 1, expert_count)
+    cross_ref[...] = compact(gate, tokens_ref[...], cross_ref.shape[0])
+
+
+def prepare(tokens, expert_ids, gate_weights, expert_count, capacity):
+    rows, half = tokens.shape
+    return call(
+        functools.partial(prepare_kernel, expert_count),
+        (tokens, expert_ids.T, gate_weights.T),
+        ((rows, half + LANES), (capacity, half)),
+        2 * rows * LANES * half,
+        "prepare",
+    )
+
+
+def cross_kernel(expert_count, wide_ref, cross_ref):
+    half = cross_ref.shape[1]
+    other = lax.axis_index("role") ^ 1
+    gate = decode_gate(wide_ref[:, half:].astype(jnp.float32), other, expert_count)
+    cross_ref[...] = compact(gate, wide_ref[:, :half], cross_ref.shape[0])
+
+
+def cross_rows(wide, expert_count, capacity):
+    rows, width = wide.shape
+    half = width - LANES
+    return call(
+        functools.partial(cross_kernel, expert_count),
+        (wide,),
+        ((capacity, half),),
+        2 * rows * LANES * half,
+        "cross_rows",
+    )[0]
+
+
+def hidden_kernel(starts, part_count, *refs):
+    parts = refs[: 2 * part_count]
+    gate_ref, up_ref, hidden_ref, arrived = refs[2 * part_count :]
+    half = arrived.shape[1] // 2
+    core = lax.axis_index("tp")
+    own = pl.multiple_of(core * half, LANES)
+    sibling = pl.multiple_of((1 - core) * half, LANES)
+    for index, start in enumerate(starts):
+        near, far = parts[2 * index], parts[2 * index + 1]
+        rows = slice(start, start + near.shape[0])
+        arrived[rows, pl.ds(own, half)] = near[:, :half]
+        arrived[rows, pl.ds(sibling, half)] = far[:, :half]
+    width = 256
+    for first in range(0, hidden_ref.shape[1], width):
+        units = slice(first, first + width)
+        gate_proj = jnp.dot(arrived[...], gate_ref[:, units], preferred_element_type=jnp.float32)
+        up_proj = jnp.dot(arrived[...], up_ref[:, units], preferred_element_type=jnp.float32)
+        hidden_ref[:, units] = (jax.nn.silu(gate_proj) * up_proj).astype(jnp.bfloat16)
+
+
+def row_starts(parts):
+    starts, rows = [], 0
+    for part in parts:
+        starts.append(rows)
+        rows += round_up(part.shape[0], 16)
+    return tuple(starts), rows
+
+
+def hidden_units(pairs, w_gate, w_up):
+    depth, hidden_count = w_gate.shape
+    starts, rows = row_starts([near for near, _ in pairs])
+    operands = [array for pair in pairs for array in pair]
+    return call(
+        functools.partial(hidden_kernel, starts, len(pairs)),
+        (*operands, w_gate, w_up),
+        ((rows, hidden_count),),
+        4 * rows * depth * hidden_count,
+        "hidden_units",
+        (pltpu.VMEM((rows, depth), jnp.bfloat16),),
+    )[0]
+
+
+def down_kernel(expert_count, starts, wide_count, *refs):
+    wides = refs[:wide_count]
+    own_ref, other_ref, down_ref, down_other_ref = refs[wide_count : wide_count + 4]
+    outs = refs[wide_count + 4 :]
+    half = down_other_ref.shape[1]
+    me = lax.axis_index("role")
+    gates = [decode_gate(ref[:, half:].astype(jnp.float32), me, expert_count) for ref in wides]
+    width = 256
+    for first in range(0, half, width):
+        columns = slice(first, first + width)
+        result = jnp.dot(
+            own_ref[...],
+            down_ref[:, columns],
+            preferred_element_type=jnp.float32,
+        ) + jnp.dot(
+            other_ref[...], down_other_ref[:, columns], preferred_element_type=jnp.float32
+        )
+        for index, (start, out_ref) in enumerate(zip(starts, outs)):
+            block = result[start : start + out_ref.shape[0]].astype(jnp.bfloat16)
+            if index < wide_count:
+                block = gates[index] * block.astype(jnp.float32)
+            out_ref[:, columns] = block
+
+
+def down(wides, cross_count, hidden, hidden_other, w_down, down_other, capacity, expert_count):
+    half = down_other.shape[1]
+    shapes = [(wide.shape[0], half) for wide in wides] + [(capacity, half)] * cross_count
+    starts, rows = [], 0
+    for shape in shapes:
+        starts.append(rows)
+        rows += round_up(shape[0], 16)
+    return call(
+        functools.partial(down_kernel, expert_count, tuple(starts), len(wides)),
+        (*wides, hidden, hidden_other, w_down, down_other),
+        tuple(shapes),
+        4 * rows * half * hidden.shape[1],
+        "down",
+        (),
+        [jnp.float32] * len(wides) + [jnp.bfloat16] * cross_count,
+    )
+
+
+def attend_kernel(query_ref, latent_ref, lengths_ref, placement_ref, out_ref):
+    slot_count, head_count, _ = query_ref.shape
+    rank, context = out_ref.shape[2], latent_ref.shape[2]
+    first = lax.axis_index("role") * slot_count
+    position = lax.broadcasted_iota(jnp.int32, (head_count, context), 1)
+    for slot in range(slot_count):
+        here = placement_ref[...] == first + slot
+        length = jnp.sum(jnp.where(here, lengths_ref[...], 0), axis=1, keepdims=True)
+        scores = (
+            jnp.dot(query_ref[slot], latent_ref[slot], preferred_element_type=jnp.float32)
+            * score_scale
+        )
+        scores = jnp.where(position < length, scores, -jnp.inf)
+        raised = jnp.exp(scores - jnp.max(scores, axis=1, keepdims=True))
+        attn_weights = (raised / jnp.sum(raised, axis=1, keepdims=True)).astype(jnp.bfloat16)
+        out_ref[slot] = lax.dot_general(
+            attn_weights,
+            latent_ref[slot, :rank, :],
+            (((1,), (1,)), ((), ())),
+            preferred_element_type=jnp.float32,
+        ).astype(jnp.bfloat16)
+
+
+def attend(q_lat, latent_cache, lengths, placement):
+    slot_count, head_count, _ = q_lat.shape
+    return pl.pallas_call(
+        attend_kernel,
+        out_shape=jax.ShapeDtypeStruct((slot_count, head_count, KV_RANK), jnp.bfloat16),
+        name="attend",
+        compiler_params=pltpu.CompilerParams(vmem_limit_bytes=VMEM_LIMIT),
+        cost_estimate=pl.CostEstimate(flops=0, bytes_accessed=0, transcendentals=0),
+    )(q_lat, latent_cache.transpose(0, 2, 1), lengths[None, :], placement[None, :])
+
+
+def fetch_kernel(down_hbm, _, down_ref, away_ref, sems):
+    half = down_ref.shape[1]
+    core = lax.axis_index("tp")
+    own = pl.multiple_of(core * half, LANES)
+    sibling = pl.multiple_of((1 - core) * half, LANES)
+    copies = [
+        pltpu.make_async_copy(down_hbm.at[0, :, pl.ds(sibling, half)], away_ref, sems.at[0]),
+        pltpu.make_async_copy(down_hbm.at[0, :, pl.ds(own, half)], down_ref, sems.at[1]),
+    ]
+    for copy in copies:
+        copy.start()
+    for copy in copies:
+        copy.wait()
+
+
+def fetch(w_down, earlier):
+    _, hidden_count, depth = w_down.shape
+    half = depth // 2
+    shapes = [(hidden_count, half)] * 2
+    return pl.pallas_call(
+        fetch_kernel,
+        in_specs=[pl.BlockSpec(memory_space=pltpu.HBM), pl.BlockSpec(memory_space=pl.ANY)],
+        out_specs=[pl.BlockSpec(memory_space=pltpu.VMEM)] * 2,
+        out_shape=[pltpu.VMEM(shape, jnp.bfloat16) for shape in shapes],
+        scratch_shapes=[pltpu.SemaphoreType.DMA((2,))],
+        name="fetch",
+        compiler_params=pltpu.CompilerParams(vmem_limit_bytes=VMEM_LIMIT),
+        cost_estimate=pl.CostEstimate(flops=0, bytes_accessed=0, transcendentals=0),
+    )(pltpu.with_memory_space_constraint(w_down, pltpu.HBM), earlier)
+
+
+def combine_kernel(expert_count, wide_ref, own_ref, back_ref, *refs):
+    sums, out_ref = refs[:-1], refs[-1]
+    half = out_ref.shape[1]
+    other = lax.axis_index("role") ^ 1
+    gate = decode_gate(wide_ref[:, half:].astype(jnp.float32), other, expert_count)
+    slots = slot_matrix(gate)[:, : back_ref.shape[0]]
+    width = 256
+    for first in range(0, half, width):
+        columns = slice(first, first + width)
+        spread = jnp.dot(slots, back_ref[:, columns], preferred_element_type=jnp.float32)
+        result = own_ref[:, columns] + gate * spread
+        for ref in sums:
+            result = result + ref[:, columns].astype(jnp.float32)
+        out_ref[:, columns] = result.astype(jnp.bfloat16)
+
+
+def combine(wide, own, back, sums, expert_count, last=False):
+    rows, half = own.shape
+    return call(
+        functools.partial(combine_kernel, expert_count),
+        (wide, own, back, *sums),
+        ((rows, half),),
+        2 * rows * LANES * half,
+        "combine",
+        last=last,
+    )[0]
+
+
+def swap(array, bits):
+    count = lax.axis_size("role")
+    return lax.ppermute(array, "role", [(device, device ^ bits) for device in range(count)])
+
+
+def swap_core(array):
+    return lax.ppermute(array, "tp", [(0, 1), (1, 0)])
+
+
+def route_multicast(
+    q_lat, latent_cache, lengths, placement, tokens, expert_ids, gate_weights, w_gate, w_up, w_down
+):
+    role_count = lax.axis_size("role")
+    token_count, route_count = expert_ids.shape
+    half = tokens.shape[1]
+    capacity = 3 * token_count * route_count // (2 * role_count)
+    pair, mirror, row = 2, 6, 1
+
+    wide, cross = prepare(tokens, expert_ids, gate_weights, role_count, capacity)
+    wide_mirror = swap(wide, mirror)
+    wide_pair = swap(wide, pair)
+    cross_in = swap(cross, row)
+    wide_other = swap_core(wide)
+    w_gate, w_up = w_gate[0], w_up[0]
+    w_down, down_away = fetch(w_down, wide)
+    attended = attend(after(q_lat, down_away), latent_cache, lengths, placement)
+    cross_in = after(cross_in, attended)
+    wide_pair = after(wide_pair, cross_in, wide_other)
+    cross_pair = cross_rows(wide_pair, role_count, capacity)
+    cross_pair_in = swap(cross_pair, row)
+    wide_pair_other = swap_core(wide_pair)
+
+    wide_mirror = after(wide_mirror, cross_pair)
+    wide_far = swap(wide_mirror, pair)
+    cross_mirror = cross_rows(wide_mirror, role_count, capacity)
+    cross_mirror_in = swap(cross_mirror, row)
+    wide_mirror_other = swap_core(wide_mirror)
+
+    cross_pair_in = after(cross_pair_in, cross_mirror)
+    cross_in_other = swap_core(cross_in)
+    cross_pair_in_other = swap_core(cross_pair_in)
+
+    wide_far = after(
+        wide_far,
+        wide_pair_other,
+        wide_mirror_other,
+        cross_in_other,
+        cross_pair_in_other,
+        cross_mirror_in,
+    )
+    cross_far = cross_rows(wide_far, role_count, capacity)
+    cross_far_in = swap(cross_far, row)
+    cross_mirror_in_other = swap_core(after(cross_mirror_in, cross_far))
+    down_other = swap_core(after(down_away, cross_far))
+    wide_far_other = swap_core(wide_far)
+    hidden = hidden_units(
+        [
+            (wide, wide_other),
+            (wide_pair, wide_pair_other),
+            (wide_mirror, wide_mirror_other),
+            (wide_far, wide_far_other),
+            (cross_in, cross_in_other),
+            (cross_pair_in, cross_pair_in_other),
+            (cross_mirror_in, cross_mirror_in_other),
+        ],
+        w_gate,
+        w_up,
+    )
+    hidden_other = swap_core(hidden)
+    cross_far_in = after(cross_far_in, hidden)
+    hidden_far = hidden_units([(cross_far_in, swap_core(cross_far_in))], w_gate, w_up)
+    hidden_far_other = swap_core(hidden_far)
+    (back_far,) = down(
+        (), 1, hidden_far, hidden_far_other, w_down, down_other, capacity, role_count
+    )
+    blocks = (wide, wide_pair, wide_mirror, wide_far)
+    own, own_pair, own_mirror, own_far, back, back_pair, back_mirror = down(
+        blocks,
+        3,
+        hidden,
+        after(hidden_other, back_far),
+        w_down,
+        down_other,
+        capacity,
+        role_count,
+    )
+    back_far = swap(back_far, row)
+    back_mirror = swap(back_mirror, row)
+    back_pair = swap(back_pair, row)
+    back = swap(back, row)
+
+    sum_far = combine(wide_far, own_far, back_far, (), role_count)
+    from_far = swap(sum_far, pair)
+    back_mirror = after(back_mirror, sum_far)
+    sum_mirror = combine(wide_mirror, own_mirror, back_mirror, (from_far,), role_count)
+    from_mirror = swap(sum_mirror, mirror)
+    back_pair = after(back_pair, sum_mirror)
+    sum_pair = combine(wide_pair, own_pair, back_pair, (), role_count)
+    from_pair = swap(sum_pair, pair)
+    back = after(back, sum_pair)
+    moe_result = combine(
+        wide, own, back, (from_pair, from_mirror), role_count, last=True
+    )
     return (attended, moe_result)
+
+
+def shards(
+    q_lat, latent_cache, lengths, placement, tokens, expert_ids, gate_weights, w_gate, w_up, w_down
+):
+    if lax.axis_size("role") == 8 and lax.axis_size("tp") == 2:
+        return route_multicast(
+            q_lat,
+            latent_cache,
+            lengths,
+            placement,
+            tokens,
+            expert_ids,
+            gate_weights,
+            w_gate,
+            w_up,
+            w_down,
+        )
+    attended = attend_local(q_lat, latent_cache, lengths, placement)
+    routed = route_all_to_all(tokens, expert_ids, gate_weights, w_gate, w_up, w_down)
+    return (attended, routed)
 
 
 def solution(mesh):

time: 217 us -> 97.7 us (0.45)
  blocking collectives: 102 us -> 0 us
  starting transfers between devices: 5.94 us -> 25.3 us
  local copies, waits for them, and re-layouts: 23 us -> 4.37 us
  Pallas kernels: 0 us -> 18.6 us
  between operations: 14.2 us -> 0.81 us
  matrix products: 10.4 us -> 0 us
  waiting for transfers between devices: 56.3 us -> 48.5 us
  other arithmetic: 4.89 us -> 0 us
    all_to_all x1 -> x0, blocking collectives: 99.6 us -> none  [shards(): lax.all_to_all(buffer_rows, 'role', split_axis=0, concat_axis=0, tiled=True)]
    ppermute x0 -> x25, waiting for transfers between devices: none -> 48.5 us  [the longest x14 42.7 us: swap(): lax.ppermute(array, 'role', [(device, device ^ bits) for device in range(...]
    all_to_all x1 -> x0, waiting for transfers between devices: 45.3 us -> none  [shards(): lax.all_to_all(summed, 'role', split_axis=0, concat_axis=0, tiled=True)]
    ppermute x0 -> x25, starting transfers between devices: none -> 25.3 us  [the longest x14 23.1 us: swap(): lax.ppermute(array, 'role', [(device, device ^ bits) for device in range(...]
    pallas_call x0 -> x14, Pallas kernels: none -> 18.6 us  [the longest x12 14.3 us: call(): pl.pallas_call(kernel, in_specs=[place] * len(operands), out_specs=[place...]
    scatter x1 -> x0, local copies, waits for them, and re-layouts: 15.1 us -> none  [shards(): jnp.zeros((role_count * capacity, columns), jnp.bfloat16).at[target]]
    reduce_scatter x1 -> x0, waiting for transfers between devices: 11 us -> none  [shards(): lax.psum_scatter(partial_out.astype(jnp.bfloat16), 'tp', scatter_dimensio...]
    dot_general x5 -> x0, matrix products: 10.4 us -> none  [the longest x1 4.27 us: shards(): jnp.dot(expert_hidden, down_matrix, preferred_element_type=jnp.float32)]
  transfers between devices with their start and end apart: 2 -> 25, of which waited for: 2 -> 10; matrix products, arithmetic and copies ran while one was open for 1% -> 0% of each run, Pallas kernels for 0% -> 16%
where the time goes in v2:
time: 97.7 us; the launch traced here: 97.5 us
  waiting for transfers between devices  48.5 us (50%)
  starting transfers between devices  25.3 us (26%)
  Pallas kernels  18.6 us (19%)
  local copies, waits for them, and re-layouts  4.37 us (4%)
    ppermute x14, waiting for transfers between devices, swap(): lax.ppermute(array, 'role', [(device, device ^ bits) for device in range(...  42.7 us
    ppermute x14, starting transfers between devices, swap(): lax.ppermute(array, 'role', [(device, device ^ bits) for device in range(...  23.1 us
    pallas_call x12, Pallas kernels, call(): pl.pallas_call(kernel, in_specs=[place] * len(operands), out_specs=[place...  14.3 us
    ppermute x11, waiting for transfers between devices, swap_core(): return lax.ppermute(array, 'tp', [(0, 1), (1, 0)])  5.75 us
    unnamed x18, local copies, waits for them, and re-layouts  4.37 us
    pallas_call x1, Pallas kernels, fetch(): pl.pallas_call(fetch_kernel, in_specs=[pl.BlockSpec(memory_space=pltpu.HB...  2.22 us
    ppermute x11, starting transfers between devices, swap_core(): return lax.ppermute(array, 'tp', [(0, 1), (1, 0)])  2.18 us
    pallas_call x1, Pallas kernels, attend(): pl.pallas_call(attend_kernel, out_shape=jax.ShapeDtypeStruct((slot_count,...  2.05 us
  transfers between devices with their start and end apart: 25, of which 10 were waited for; matrix products, arithmetic and copies ran while one was open for 0% of the time, Pallas kernels for 16%

profile of v2, /device:TPU:0, one launch (start us, length us, event | category | flops | bytes accessed | tf_op | source)
XLA Modules:
  0.0 97.5 jit_solution(11587701902384798429)
XLA Ops:
  0.6 1.0 copy-done.3
  1.6 0.7 copy-done.5
  2.3 0.7 copy-done.6
  3.0 0.7 prepare.1
  3.7 0.5 collective-permute-start.2
  4.2 2.6 %collective-permute-start = (bf16[96,1920]{1,0:T(8,128)(2,1)S(1)}, bf16[96,1920]{1,0:T(8,128)(2,1)S(1)}, u32[]{:S(2)}, u32[]{:S(2)}) collective-permute-start(bf16[96,1920]{1,0:T(8,128)(2,1)S(1)} %get-tuple-element.26._.refs_0_.wide_ref), channel_id=1, source_target_pairs={{0,4},{2,6},{4,0},{6,2},{8,12},{10,14},{12,8},{14,10},{1,5},{3,7},... | collective-permute-start | bytes 1105928 | tf_op jit(solution)/shard_map/ppermute | solution.py:387
  6.9 1.5 %collective-permute-start.1 = (bf16[72,1792]{1,0:T(8,128)(2,1)S(1)}, bf16[72,1792]{1,0:T(8,128)(2,1)S(1)}, u32[]{:S(2)}, u32[]{:S(2)}) collective-permute-start(bf16[72,1792]{1,0:T(8,128)(2,1)S(1)} %get-tuple-element.29), channel_id=1, source_target_pairs={{0,2},{2,0},{4,6},{6,4},{8,10},{10,8},{12,14},{14,12},{1,3},{3,1},... | collective-permute-start | bytes 774152 | tf_op jit(solution)/shard_map/ppermute | solution.py:387
  8.4 2.5 %collective-permute-start.3 = (bf16[96,1920]{1,0:T(8,128)(2,1)S(1)}, bf16[96,1920]{1,0:T(8,128)(2,1)S(1)}, u32[]{:S(2)}, u32[]{:S(2)}) collective-permute-start(bf16[96,1920]{1,0:T(8,128)(2,1)S(1)} %get-tuple-element.26._.refs_0_.wide_ref), channel_id=1, source_target_pairs={{0,12},{2,14},{4,8},{6,10},{8,4},{10,6},{12,0},{14,2},{1,13},{3,15... | collective-permute-start | bytes 1105928 | tf_op jit(solution)/shard_map/ppermute | solution.py:387
  10.9 2.2 %fetch.1 = (bf16[512,1792]{1,0:T(8,128)(2,1)S(1)}, bf16[512,1792]{1,0:T(8,128)(2,1)S(1)}) custom-call(bf16[1,512,3584]{2,1,0:T(8,128)(2,1)} %down_hbm.1, bf16[96,1920]{1,0:T(8,128)(2,1)S(1)} %get-tuple-element.26._.refs_0_.wide_ref), custom_call_target="tpu_custom_call" | custom-call | tf_op jit(solution)/shard_map/fetch/pallas_call | solution.py:345
  13.1 0.0 copy-start.2
  13.1 2.0 %copy-done.2 = bf16[4,256,576]{1,2,0:T(8,128)(2,1)S(1)} copy-done((bf16[4,256,576]{1,2,0:T(8,128)(2,1)S(1)}, bf16[4,256,576]{1,2,0:T(8,128)(2,1)}, u32[]{:S(2)}) %copy-start.2) | copy-done | bytes 1179672
  15.1 2.0 %attend.1 = bf16[4,32,512]{2,1,0:T(8,128)(2,1)} custom-call(bf16[4,32,576]{2,1,0:T(8,128)(2,1)S(1)} %copy-done.4, bf16[4,576,256]{2,1,0:T(8,128)(2,1)S(1)} %bitcast.11, s32[1,32]{1,0:T(1,128)S(1)} %bitcast.14, s32[1,32]{1,0:T(1,128)S(1)} %bitcast.15), custom_call_target="tpu_custom_call" | custom-call | tf_op jit(solution)/shard_map/attend/pallas_call | solution.py:317
  17.2 0.0 collective-permute-done.1.refs_8_
  17.2 0.0 collective-permute-done.2.refs_1_
  17.2 0.0 collective-permute-done.wide_ref.refs_2_.refs_1_
  17.2 0.5 cross_rows.3
  17.7 0.6 collective-permute-start.8
  18.3 0.0 collective-permute-start.7
  18.3 7.9 %collective-permute-done.3.wide_ref.refs_4_.refs_2_ = bf16[96,1920]{1,0:T(8,128)(2,1)S(1)} collective-permute-done((bf16[96,1920]{1,0:T(8,128)(2,1)S(1)}, bf16[96,1920]{1,0:T(8,128)(2,1)S(1)}, u32[]{:S(2)}, u32[]{:S(2)}) %collective-permute-start.3) | collective-permute-done | bytes 368672 | tf_op jit(solution)/shard_map/ppermute | solution.py:387
  26.2 0.0 collective-permute-start.6
  26.2 1.8 %collective-permute-start.4 = (bf16[96,1920]{1,0:T(8,128)(2,1)S(1)}, bf16[96,1920]{1,0:T(8,128)(2,1)S(1)}, u32[]{:S(2)}, u32[]{:S(2)}) collective-permute-start(bf16[96,1920]{1,0:T(8,128)(2,1)S(1)} %collective-permute-done.3.wide_ref.refs_4_.refs_2_), channel_id=1, source_target_pairs={{0,4},{2,6},{4,0},{6,2},{8,12},{10,14},{12,8},{14,10},{1,5},{3,7},... | collective-permute-start | bytes 1105928 | tf_op jit(solution)/shard_map/ppermute | solution.py:387
  28.1 0.2 collective-permute-start.5
  28.3 0.5 cross_rows.4
  28.8 0.6 collective-permute-start.10
  29.4 0.0 collective-permute-start.9
  29.4 7.9 %collective-permute-done.10.refs_12_ = bf16[72,1792]{1,0:T(8,128)(2,1)S(1)} collective-permute-done((bf16[72,1792]{1,0:T(8,128)(2,1)S(1)}, bf16[72,1792]{1,0:T(8,128)(2,1)S(1)}, u32[]{:S(2)}, u32[]{:S(2)}) %collective-permute-start.10) | collective-permute-done | bytes 258080 | tf_op jit(solution)/shard_map/ppermute | solution.py:387
  37.3 0.0 collective-permute-done.6.refs_5_
  37.3 0.0 collective-permute-done.4.wide_ref.refs_6_.refs_3_
  37.3 0.0 collective-permute-done.5.refs_3_
  37.3 0.0 collective-permute-done.9.refs_11_
  37.3 0.5 cross_rows.5
  37.9 0.1 collective-permute-start.17
  38.0 0.5 collective-permute-start.11
  38.4 0.1 collective-permute-start.12
  38.5 1.4 %collective-permute-start.14 = (bf16[72,1792]{1,0:T(8,128)(2,1)S(1)}, bf16[72,1792]{1,0:T(8,128)(2,1)S(1)}, u32[]{:S(2)}, u32[]{:S(2)}) collective-permute-start(bf16[72,1792]{1,0:T(8,128)(2,1)S(1)} %cross_rows.5), channel_id=1, source_target_pairs={{0,2},{2,0},{4,6},{6,4},{8,10},{10,8},{12,14},{14,12},{1,3},{3,1},... | collective-permute-start | bytes 774152 | tf_op jit(solution)/shard_map/ppermute | solution.py:387
  40.0 2.7 %collective-permute-done.12.refs_13_ = bf16[72,1792]{1,0:T(8,128)(2,1)S(1)} collective-permute-done((bf16[72,1792]{1,0:T(8,128)(2,1)S(1)}, bf16[72,1792]{1,0:T(8,128)(2,1)S(1)}, u32[]{:S(2)}, u32[]{:S(2)}) %collective-permute-start.12) | collective-permute-done | bytes 258080 | tf_op jit(solution)/shard_map/ppermute | solution.py:391
  42.6 4.9 %hidden_units.2.refs_4_ = bf16[624,512]{1,0:T(8,128)(2,1)S(1)} custom-call(bf16[96,1920]{1,0:T(8,128)(2,1)S(1)} %get-tuple-element.26._.refs_0_.wide_ref, bf16[96,1920]{1,0:T(8,128)(2,1)S(1)} %collective-permute-done.2.refs_1_, bf16[96,1920]{1,0:T(8,128)(2,1)S(1)} %collective-permute-done.wide_ref.refs_2_.refs_1_, ...), custom_call_target="tpu_custom_call" | custom-call | tf_op jit(solution)/shard_map/hidden_units/pallas_call | solution.py:91
  47.5 0.2 collective-permute-start.13
  47.7 0.4 collective-permute-start.15
  48.1 1.9 %collective-permute-done.15.refs_1_ = bf16[72,1792]{1,0:T(8,128)(2,1)S(1)} collective-permute-done((bf16[72,1792]{1,0:T(8,128)(2,1)S(1)}, bf16[72,1792]{1,0:T(8,128)(2,1)S(1)}, u32[]{:S(2)}, u32[]{:S(2)}) %collective-permute-start.15) | collective-permute-done | bytes 258080 | tf_op jit(solution)/shard_map/ppermute | solution.py:391
  50.0 1.4 %hidden_units.3.refs_0_ = bf16[80,512]{1,0:T(8,128)(2,1)S(1)} custom-call(bf16[72,1792]{1,0:T(8,128)(2,1)S(1)} %collective-permute-done.14.refs_0_, bf16[72,1792]{1,0:T(8,128)(2,1)S(1)} %collective-permute-done.15.refs_1_, bf16[3584,512]{1,0:T(8,128)(2,1)S(1)} %bitcast.8, bf16[3584,512]{1,0:T(8,128)(2,1)S(1)} %bitcast.10), custom_call_target="tpu_custom_call" | custom-call | tf_op jit(solution)/shard_map/hidden_units/pallas_call | solution.py:91
  51.4 0.2 collective-permute-start.16
  51.6 1.1 %collective-permute-done.16.refs_1_ = bf16[80,512]{1,0:T(8,128)(2,1)S(1)} collective-permute-done((bf16[80,512]{1,0:T(8,128)(2,1)S(1)}, bf16[80,512]{1,0:T(8,128)(2,1)S(1)}, u32[]{:S(2)}, u32[]{:S(2)}) %collective-permute-start.16) | collective-permute-done | bytes 81952 | tf_op jit(solution)/shard_map/ppermute | solution.py:391
  52.8 0.0 collective-permute-done.17.refs_3_.refs_7_
  52.8 0.8 down.2
  53.5 1.5 %collective-permute-start.21 = (bf16[72,1792]{1,0:T(8,128)(2,1)S(1)}, bf16[72,1792]{1,0:T(8,128)(2,1)S(1)}, u32[]{:S(2)}, u32[]{:S(2)}) collective-permute-start(bf16[72,1792]{1,0:T(8,128)(2,1)S(1)} %down.2), channel_id=1, source_target_pairs={{0,2},{2,0},{4,6},{6,4},{8,10},{10,8},{12,14},{14,12},{1,3},{3,1},... | collective-permute-start | bytes 774152 | tf_op jit(solution)/shard_map/ppermute | solution.py:387
  55.0 0.0 collective-permute-done.13.refs_5_
  55.0 2.5 %down.3 = (f32[96,1792]{1,0:T(8,128)S(1)}, f32[96,1792]{1,0:T(8,128)S(1)}, f32[96,1792]{1,0:T(8,128)S(1)}, f32[96,1792]{1,0:T(8,128)S(1)}, bf16[72,1792]{1,0:T(8...) custom-call(bf16[96,1920]{1,0:T(8,128)(2,1)S(1)} %get-tuple-element.26._.refs_0_.wide_ref, ...), custom_call_target="tpu_custom_call" | custom-call | tf_op jit(solution)/shard_map/down/pallas_call | solution.py:91
  57.5 4.4 %collective-permute-done.21.back_ref = bf16[72,1792]{1,0:T(8,128)(2,1)S(1)} collective-permute-done((bf16[72,1792]{1,0:T(8,128)(2,1)S(1)}, bf16[72,1792]{1,0:T(8,128)(2,1)S(1)}, u32[]{:S(2)}, u32[]{:S(2)}) %collective-permute-start.21) | collective-permute-done | bytes 258080 | tf_op jit(solution)/shard_map/ppermute | solution.py:387
  61.9 0.4 combine.4
  62.3 1.8 %collective-permute-start.22 = (bf16[96,1792]{1,0:T(8,128)(2,1)S(1)}, bf16[96,1792]{1,0:T(8,128)(2,1)S(1)}, u32[]{:S(2)}, u32[]{:S(2)}) collective-permute-start(bf16[96,1792]{1,0:T(8,128)(2,1)S(1)} %combine.4), channel_id=1, source_target_pairs={{0,4},{2,6},{4,0},{6,2},{8,12},{10,14},{12,8},{14,10},{1,5},{3,7},... | collective-permute-start | bytes 1032200 | tf_op jit(solution)/shard_map/ppermute | solution.py:387
  64.1 0.5 collective-permute-start.20
  64.6 1.5 %collective-permute-start.19 = (bf16[72,1792]{1,0:T(8,128)(2,1)S(1)}, bf16[72,1792]{1,0:T(8,128)(2,1)S(1)}, u32[]{:S(2)}, u32[]{:S(2)}) collective-permute-start(bf16[72,1792]{1,0:T(8,128)(2,1)S(1)} %get-tuple-element.43), channel_id=1, source_target_pairs={{0,2},{2,0},{4,6},{6,4},{8,10},{10,8},{12,14},{14,12},{1,3},{3,1},... | collective-permute-start | bytes 774152 | tf_op jit(solution)/shard_map/ppermute | solution.py:387
  66.1 7.1 %collective-permute-done.20.back_ref = bf16[72,1792]{1,0:T(8,128)(2,1)S(1)} collective-permute-done((bf16[72,1792]{1,0:T(8,128)(2,1)S(1)}, bf16[72,1792]{1,0:T(8,128)(2,1)S(1)}, u32[]{:S(2)}, u32[]{:S(2)}) %collective-permute-start.20) | collective-permute-done | bytes 258080 | tf_op jit(solution)/shard_map/ppermute | solution.py:387
  73.3 0.0 collective-permute-done.22.refs_0_
  73.3 0.5 combine.5
  73.7 3.1 %collective-permute-done.19.back_ref = bf16[72,1792]{1,0:T(8,128)(2,1)S(1)} collective-permute-done((bf16[72,1792]{1,0:T(8,128)(2,1)S(1)}, bf16[72,1792]{1,0:T(8,128)(2,1)S(1)}, u32[]{:S(2)}, u32[]{:S(2)}) %collective-permute-start.19) | collective-permute-done | bytes 258080 | tf_op jit(solution)/shard_map/ppermute | solution.py:387
  76.8 0.4 combine.6
  77.3 0.4 collective-permute-start.23
  77.7 4.8 %collective-permute-start.24 = (bf16[96,1792]{1,0:T(8,128)(2,1)S(1)}, bf16[96,1792]{1,0:T(8,128)(2,1)S(1)}, u32[]{:S(2)}, u32[]{:S(2)}) collective-permute-start(bf16[96,1792]{1,0:T(8,128)(2,1)S(1)} %combine.5), channel_id=1, source_target_pairs={{0,12},{2,14},{4,8},{6,10},{8,4},{10,6},{12,0},{14,2},{1,13},{3,15... | collective-permute-start | bytes 1032200 | tf_op jit(solution)/shard_map/ppermute | solution.py:387
  82.5 1.4 %collective-permute-start.18 = (bf16[72,1792]{1,0:T(8,128)(2,1)S(1)}, bf16[72,1792]{1,0:T(8,128)(2,1)S(1)}, u32[]{:S(2)}, u32[]{:S(2)}) collective-permute-start(bf16[72,1792]{1,0:T(8,128)(2,1)S(1)} %get-tuple-element.41), channel_id=1, source_target_pairs={{0,2},{2,0},{4,6},{6,4},{8,10},{10,8},{12,14},{14,12},{1,3},{3,1},... | collective-permute-start | bytes 774152 | tf_op jit(solution)/shard_map/ppermute | solution.py:387
  84.0 4.9 %collective-permute-done.18.back_ref = bf16[72,1792]{1,0:T(8,128)(2,1)S(1)} collective-permute-done((bf16[72,1792]{1,0:T(8,128)(2,1)S(1)}, bf16[72,1792]{1,0:T(8,128)(2,1)S(1)}, u32[]{:S(2)}, u32[]{:S(2)}) %collective-permute-start.18) | collective-permute-done | bytes 258080 | tf_op jit(solution)/shard_map/ppermute | solution.py:387
  88.9 7.4 %collective-permute-done.24.refs_1_ = bf16[96,1792]{1,0:T(8,128)(2,1)S(1)} collective-permute-done((bf16[96,1792]{1,0:T(8,128)(2,1)S(1)}, bf16[96,1792]{1,0:T(8,128)(2,1)S(1)}, u32[]{:S(2)}, u32[]{:S(2)}) %collective-permute-start.24) | collective-permute-done | bytes 344096 | tf_op jit(solution)/shard_map/ppermute | solution.py:387
  96.3 1.2 %combine.7 = bf16[96,1792]{1,0:T(8,128)(2,1)} custom-call(bf16[96,1920]{1,0:T(8,128)(2,1)S(1)} %get-tuple-element.26._.refs_0_.wide_ref, f32[96,1792]{1,0:T(8,128)S(1)} %get-tuple-element.40.own_ref, bf16[72,1792]{1,0:T(8,128)(2,1)S(1)} %collective-permute-done.18.back_ref, bf16[96,1792]{1,0:T(8,128)(2,1)S(1)} %collective-permute-done.23.refs_0_, ...), custom_call_target="tpu_custom_call" | custom-call | tf_op jit(solution)/shard_map/combine/pallas_call | solution.py:91
  (18 shorter events, 0.0 us)
Async XLA Ops:
  0.6 1.0 %copy-start.3 = (bf16[96,1792]{1,0:T(8,128)(2,1)S(1)}, bf16[96,1792]{1,0:T(8,128)(2,1)}, u32[]{:S(2)}) copy-start(bf16[96,1792]{1,0:T(8,128)(2,1)} %tokens_ref.1) | copy-start | bytes 1032196
  1.6 0.7 copy-start.5
  2.3 0.7 copy-start.6
  3.0 10.1 %copy-start.4 = (bf16[4,32,576]{2,1,0:T(8,128)(2,1)S(1)}, bf16[4,32,576]{2,1,0:T(8,128)(2,1)}, u32[]{:S(2)}) copy-start(bf16[4,32,576]{2,1,0:T(8,128)(2,1)} %query_ref) | copy-start | bytes 442372
  3.7 13.5 %collective-permute-start.2 = (bf16[96,1920]{1,0:T(8,128)(2,1)S(1)}, bf16[96,1920]{1,0:T(8,128)(2,1)S(1)}, u32[]{:S(2)}, u32[]{:S(2)}) collective-permute-start(bf16[96,1920]{1,0:T(8,128)(2,1)S(1)} %get-tuple-element.26._.refs_0_.wide_ref), channel_id=1, source_target_pairs={{0,1},{1,0},{2,3},{3,2},{4,5},{5,4},{6,7},{7,6},{8,9},{9,8},{10,11... | collective-permute-start | bytes 1105928 | tf_op jit(solution)/shard_map/ppermute | solution.py:391
  4.2 13.0 %collective-permute-start = (bf16[96,1920]{1,0:T(8,128)(2,1)S(1)}, bf16[96,1920]{1,0:T(8,128)(2,1)S(1)}, u32[]{:S(2)}, u32[]{:S(2)}) collective-permute-start(bf16[96,1920]{1,0:T(8,128)(2,1)S(1)} %get-tuple-element.26._.refs_0_.wide_ref), channel_id=1, source_target_pairs={{0,4},{2,6},{4,0},{6,2},{8,12},{10,14},{12,8},{14,10},{1,5},{3,7},... | collective-permute-start | bytes 1105928 | tf_op jit(solution)/shard_map/ppermute | solution.py:387
  6.9 6.2 %copy-start.7 = (s32[32]{0:T(128)S(1)}, s32[32]{0:T(128)}, u32[]{:S(2)}) copy-start(s32[32]{0:T(128)} %param.12) | copy-start | bytes 388
  6.9 6.2 %copy-start.8 = (s32[32]{0:T(128)S(1)}, s32[32]{0:T(128)}, u32[]{:S(2)}) copy-start(s32[32]{0:T(128)} %param.13) | copy-start | bytes 388
  6.9 10.3 %collective-permute-start.1 = (bf16[72,1792]{1,0:T(8,128)(2,1)S(1)}, bf16[72,1792]{1,0:T(8,128)(2,1)S(1)}, u32[]{:S(2)}, u32[]{:S(2)}) collective-permute-start(bf16[72,1792]{1,0:T(8,128)(2,1)S(1)} %get-tuple-element.29), channel_id=1, source_target_pairs={{0,2},{2,0},{4,6},{6,4},{8,10},{10,8},{12,14},{14,12},{1,3},{3,1},... | collective-permute-start | bytes 774152 | tf_op jit(solution)/shard_map/ppermute | solution.py:387
  8.4 17.9 %collective-permute-start.3 = (bf16[96,1920]{1,0:T(8,128)(2,1)S(1)}, bf16[96,1920]{1,0:T(8,128)(2,1)S(1)}, u32[]{:S(2)}, u32[]{:S(2)}) collective-permute-start(bf16[96,1920]{1,0:T(8,128)(2,1)S(1)} %get-tuple-element.26._.refs_0_.wide_ref), channel_id=1, source_target_pairs={{0,12},{2,14},{4,8},{6,10},{8,4},{10,6},{12,0},{14,2},{1,13},{3,15... | collective-permute-start | bytes 1105928 | tf_op jit(solution)/shard_map/ppermute | solution.py:387
  10.8 31.8 %copy-start = (bf16[1,3584,512]{2,1,0:T(8,128)(2,1)S(1)}, bf16[1,3584,512]{2,1,0:T(8,128)(2,1)}, u32[]{:S(2)}) copy-start(bf16[1,3584,512]{2,1,0:T(8,128)(2,1)} %param.17) | copy-start | bytes 11010052
  10.9 31.8 %copy-start.1 = (bf16[1,3584,512]{2,1,0:T(8,128)(2,1)S(1)}, bf16[1,3584,512]{2,1,0:T(8,128)(2,1)}, u32[]{:S(2)}) copy-start(bf16[1,3584,512]{2,1,0:T(8,128)(2,1)} %param.18) | copy-start | bytes 11010052
  13.1 2.0 %copy-start.2 = (bf16[4,256,576]{1,2,0:T(8,128)(2,1)S(1)}, bf16[4,256,576]{1,2,0:T(8,128)(2,1)}, u32[]{:S(2)}) copy-start(bf16[4,256,576]{1,2,0:T(8,128)(2,1)} %param.11) | copy-start | bytes 3538948
  17.7 11.1 %collective-permute-start.8 = (bf16[72,1792]{1,0:T(8,128)(2,1)S(1)}, bf16[72,1792]{1,0:T(8,128)(2,1)S(1)}, u32[]{:S(2)}, u32[]{:S(2)}) collective-permute-start(bf16[72,1792]{1,0:T(8,128)(2,1)S(1)} %cross_rows.3), channel_id=1, source_target_pairs={{0,2},{2,0},{4,6},{6,4},{8,10},{10,8},{12,14},{14,12},{1,3},{3,1},... | collective-permute-start | bytes 774152 | tf_op jit(solution)/shard_map/ppermute | solution.py:387
  18.3 11.1 %collective-permute-start.7 = (bf16[72,1792]{1,0:T(8,128)(2,1)S(1)}, bf16[72,1792]{1,0:T(8,128)(2,1)S(1)}, u32[]{:S(2)}, u32[]{:S(2)}) collective-permute-start(bf16[72,1792]{1,0:T(8,128)(2,1)S(1)} %collective-permute-done.1.refs_8_), channel_id=1, source_target_pairs={{0,1},{1,0},{2,3},{3,2},{4,5},{5,4},{6,7},{7,6},{8,9},{9,8},{10,11... | collective-permute-start | bytes 774152 | tf_op jit(solution)/shard_map/ppermute | solution.py:391
  26.2 11.1 %collective-permute-start.6 = (bf16[96,1920]{1,0:T(8,128)(2,1)S(1)}, bf16[96,1920]{1,0:T(8,128)(2,1)S(1)}, u32[]{:S(2)}, u32[]{:S(2)}) collective-permute-start(bf16[96,1920]{1,0:T(8,128)(2,1)S(1)} %collective-permute-done.3.wide_ref.refs_4_.refs_2_), channel_id=1, source_target_pairs={{0,1},{1,0},{2,3},{3,2},{4,5},{5,4},{6,7},{7,6},{8,9},{9,8},{10,11... | collective-permute-start | bytes 1105928 | tf_op jit(solution)/shard_map/ppermute | solution.py:391
  26.2 11.1 %collective-permute-start.4 = (bf16[96,1920]{1,0:T(8,128)(2,1)S(1)}, bf16[96,1920]{1,0:T(8,128)(2,1)S(1)}, u32[]{:S(2)}, u32[]{:S(2)}) collective-permute-start(bf16[96,1920]{1,0:T(8,128)(2,1)S(1)} %collective-permute-done.3.wide_ref.refs_4_.refs_2_), channel_id=1, source_target_pairs={{0,4},{2,6},{4,0},{6,2},{8,12},{10,14},{12,8},{14,10},{1,5},{3,7},... | collective-permute-start | bytes 1105928 | tf_op jit(solution)/shard_map/ppermute | solution.py:387
  28.1 9.3 %collective-permute-start.5 = (bf16[96,1920]{1,0:T(8,128)(2,1)S(1)}, bf16[96,1920]{1,0:T(8,128)(2,1)S(1)}, u32[]{:S(2)}, u32[]{:S(2)}) collective-permute-start(bf16[96,1920]{1,0:T(8,128)(2,1)S(1)} %collective-permute-done.wide_ref.refs_2_.refs_1_), channel_id=1, source_target_pairs={{0,1},{1,0},{2,3},{3,2},{4,5},{5,4},{6,7},{7,6},{8,9},{9,8},{10,11... | collective-permute-start | bytes 1105928 | tf_op jit(solution)/shard_map/ppermute | solution.py:391
  28.8 8.5 %collective-permute-start.10 = (bf16[72,1792]{1,0:T(8,128)(2,1)S(1)}, bf16[72,1792]{1,0:T(8,128)(2,1)S(1)}, u32[]{:S(2)}, u32[]{:S(2)}) collective-permute-start(bf16[72,1792]{1,0:T(8,128)(2,1)S(1)} %cross_rows.4), channel_id=1, source_target_pairs={{0,2},{2,0},{4,6},{6,4},{8,10},{10,8},{12,14},{14,12},{1,3},{3,1},... | collective-permute-start | bytes 774152 | tf_op jit(solution)/shard_map/ppermute | solution.py:387
  29.4 7.9 %collective-permute-start.9 = (bf16[72,1792]{1,0:T(8,128)(2,1)S(1)}, bf16[72,1792]{1,0:T(8,128)(2,1)S(1)}, u32[]{:S(2)}, u32[]{:S(2)}) collective-permute-start(bf16[72,1792]{1,0:T(8,128)(2,1)S(1)} %collective-permute-done.8.refs_10_), channel_id=1, source_target_pairs={{0,1},{1,0},{2,3},{3,2},{4,5},{5,4},{6,7},{7,6},{8,9},{9,8},{10,11... | collective-permute-start | bytes 774152 | tf_op jit(solution)/shard_map/ppermute | solution.py:391
  37.9 14.9 %collective-permute-start.17 = (bf16[512,1792]{1,0:T(8,128)(2,1)S(1)}, bf16[512,1792]{1,0:T(8,128)(2,1)S(1)}, u32[]{:S(2)}, u32[]{:S(2)}) collective-permute-start(bf16[512,1792]{1,0:T(8,128)(2,1)S(1)} %get-tuple-element.38), channel_id=1, source_target_pairs={{0,1},{1,0},{2,3},{3,2},{4,5},{5,4},{6,7},{7,6},{8,9},{9,8},{10,11... | collective-permute-start | bytes 5505032 | tf_op jit(solution)/shard_map/ppermute | solution.py:391
  38.0 4.7 %collective-permute-start.11 = (bf16[96,1920]{1,0:T(8,128)(2,1)S(1)}, bf16[96,1920]{1,0:T(8,128)(2,1)S(1)}, u32[]{:S(2)}, u32[]{:S(2)}) collective-permute-start(bf16[96,1920]{1,0:T(8,128)(2,1)S(1)} %collective-permute-done.4.wide_ref.refs_6_.refs_3_), channel_id=1, source_target_pairs={{0,1},{1,0},{2,3},{3,2},{4,5},{5,4},{6,7},{7,6},{8,9},{9,8},{10,11... | collective-permute-start | bytes 1105928 | tf_op jit(solution)/shard_map/ppermute | solution.py:391
  38.4 4.2 %collective-permute-start.12 = (bf16[72,1792]{1,0:T(8,128)(2,1)S(1)}, bf16[72,1792]{1,0:T(8,128)(2,1)S(1)}, u32[]{:S(2)}, u32[]{:S(2)}) collective-permute-start(bf16[72,1792]{1,0:T(8,128)(2,1)S(1)} %collective-permute-done.10.refs_12_), channel_id=1, source_target_pairs={{0,1},{1,0},{2,3},{3,2},{4,5},{5,4},{6,7},{7,6},{8,9},{9,8},{10,11... | collective-permute-start | bytes 774152 | tf_op jit(solution)/shard_map/ppermute | solution.py:391
  38.5 9.2 %collective-permute-start.14 = (bf16[72,1792]{1,0:T(8,128)(2,1)S(1)}, bf16[72,1792]{1,0:T(8,128)(2,1)S(1)}, u32[]{:S(2)}, u32[]{:S(2)}) collective-permute-start(bf16[72,1792]{1,0:T(8,128)(2,1)S(1)} %cross_rows.5), channel_id=1, source_target_pairs={{0,2},{2,0},{4,6},{6,4},{8,10},{10,8},{12,14},{14,12},{1,3},{3,1},... | collective-permute-start | bytes 774152 | tf_op jit(solution)/shard_map/ppermute | solution.py:387
  47.5 7.5 %collective-permute-start.13 = (bf16[624,512]{1,0:T(8,128)(2,1)S(1)}, bf16[624,512]{1,0:T(8,128)(2,1)S(1)}, u32[]{:S(2)}, u32[]{:S(2)}) collective-permute-start(bf16[624,512]{1,0:T(8,128)(2,1)S(1)} %hidden_units.2.refs_4_), channel_id=1, source_target_pairs={{0,1},{1,0},{2,3},{3,2},{4,5},{5,4},{6,7},{7,6},{8,9},{9,8},{10,11... | collective-permute-start | bytes 1916936 | tf_op jit(solution)/shard_map/ppermute | solution.py:391
  47.7 2.3 %collective-permute-start.15 = (bf16[72,1792]{1,0:T(8,128)(2,1)S(1)}, bf16[72,1792]{1,0:T(8,128)(2,1)S(1)}, u32[]{:S(2)}, u32[]{:S(2)}) collective-permute-start(bf16[72,1792]{1,0:T(8,128)(2,1)S(1)} %collective-permute-done.14.refs_0_), channel_id=1, source_target_pairs={{0,1},{1,0},{2,3},{3,2},{4,5},{5,4},{6,7},{7,6},{8,9},{9,8},{10,11... | collective-permute-start | bytes 774152 | tf_op jit(solution)/shard_map/ppermute | solution.py:391
  51.4 1.3 %collective-permute-start.16 = (bf16[80,512]{1,0:T(8,128)(2,1)S(1)}, bf16[80,512]{1,0:T(8,128)(2,1)S(1)}, u32[]{:S(2)}, u32[]{:S(2)}) collective-permute-start(bf16[80,512]{1,0:T(8,128)(2,1)S(1)} %hidden_units.3.refs_0_), channel_id=1, source_target_pairs={{0,1},{1,0},{2,3},{3,2},{4,5},{5,4},{6,7},{7,6},{8,9},{9,8},{10,11... | collective-permute-start | bytes 245768 | tf_op jit(solution)/shard_map/ppermute | solution.py:391
  53.5 8.3 %collective-permute-start.21 = (bf16[72,1792]{1,0:T(8,128)(2,1)S(1)}, bf16[72,1792]{1,0:T(8,128)(2,1)S(1)}, u32[]{:S(2)}, u32[]{:S(2)}) collective-permute-start(bf16[72,1792]{1,0:T(8,128)(2,1)S(1)} %down.2), channel_id=1, source_target_pairs={{0,2},{2,0},{4,6},{6,4},{8,10},{10,8},{12,14},{14,12},{1,3},{3,1},... | collective-permute-start | bytes 774152 | tf_op jit(solution)/shard_map/ppermute | solution.py:387
  62.3 11.0 %collective-permute-start.22 = (bf16[96,1792]{1,0:T(8,128)(2,1)S(1)}, bf16[96,1792]{1,0:T(8,128)(2,1)S(1)}, u32[]{:S(2)}, u32[]{:S(2)}) collective-permute-start(bf16[96,1792]{1,0:T(8,128)(2,1)S(1)} %combine.4), channel_id=1, source_target_pairs={{0,4},{2,6},{4,0},{6,2},{8,12},{10,14},{12,8},{14,10},{1,5},{3,7},... | collective-permute-start | bytes 1032200 | tf_op jit(solution)/shard_map/ppermute | solution.py:387
  64.1 9.2 %collective-permute-start.20 = (bf16[72,1792]{1,0:T(8,128)(2,1)S(1)}, bf16[72,1792]{1,0:T(8,128)(2,1)S(1)}, u32[]{:S(2)}, u32[]{:S(2)}) collective-permute-start(bf16[72,1792]{1,0:T(8,128)(2,1)S(1)} %get-tuple-element.45), channel_id=1, source_target_pairs={{0,2},{2,0},{4,6},{6,4},{8,10},{10,8},{12,14},{14,12},{1,3},{3,1},... | collective-permute-start | bytes 774152 | tf_op jit(solution)/shard_map/ppermute | solution.py:387
  64.6 12.2 %collective-permute-start.19 = (bf16[72,1792]{1,0:T(8,128)(2,1)S(1)}, bf16[72,1792]{1,0:T(8,128)(2,1)S(1)}, u32[]{:S(2)}, u32[]{:S(2)}) collective-permute-start(bf16[72,1792]{1,0:T(8,128)(2,1)S(1)} %get-tuple-element.43), channel_id=1, source_target_pairs={{0,2},{2,0},{4,6},{6,4},{8,10},{10,8},{12,14},{14,12},{1,3},{3,1},... | collective-permute-start | bytes 774152 | tf_op jit(solution)/shard_map/ppermute | solution.py:387
  77.3 11.6 %collective-permute-start.23 = (bf16[96,1792]{1,0:T(8,128)(2,1)S(1)}, bf16[96,1792]{1,0:T(8,128)(2,1)S(1)}, u32[]{:S(2)}, u32[]{:S(2)}) collective-permute-start(bf16[96,1792]{1,0:T(8,128)(2,1)S(1)} %combine.6), channel_id=1, source_target_pairs={{0,4},{2,6},{4,0},{6,2},{8,12},{10,14},{12,8},{14,10},{1,5},{3,7},... | collective-permute-start | bytes 1032200 | tf_op jit(solution)/shard_map/ppermute | solution.py:387
  77.7 18.6 %collective-permute-start.24 = (bf16[96,1792]{1,0:T(8,128)(2,1)S(1)}, bf16[96,1792]{1,0:T(8,128)(2,1)S(1)}, u32[]{:S(2)}, u32[]{:S(2)}) collective-permute-start(bf16[96,1792]{1,0:T(8,128)(2,1)S(1)} %combine.5), channel_id=1, source_target_pairs={{0,12},{2,14},{4,8},{6,10},{8,4},{10,6},{12,0},{14,2},{1,13},{3,15... | collective-permute-start | bytes 1032200 | tf_op jit(solution)/shard_map/ppermute | solution.py:387
  82.5 6.3 %collective-permute-start.18 = (bf16[72,1792]{1,0:T(8,128)(2,1)S(1)}, bf16[72,1792]{1,0:T(8,128)(2,1)S(1)}, u32[]{:S(2)}, u32[]{:S(2)}) collective-permute-start(bf16[72,1792]{1,0:T(8,128)(2,1)S(1)} %get-tuple-element.41), channel_id=1, source_target_pairs={{0,2},{2,0},{4,6},{6,4},{8,10},{10,8},{12,14},{14,12},{1,3},{3,1},... | collective-permute-start | bytes 774152 | tf_op jit(solution)/shard_map/ppermute | solution.py:387

commit v3 on v2

--- a/solution.py
+++ b/solution.py
@@ -144,8 +144,29 @@
     return picked[:capacity].astype(jnp.bfloat16)
 
 
-def prepare_kernel(expert_count, tokens_ref, ids_ref, gates_ref, wide_ref, cross_ref):
-    rows, half = tokens_ref.shape
+def split_of(width):
+    return round_up(3 * width // 4, LANES)
+
+
+def prepare_kernel(
+    expert_count,
+    tokens_hbm,
+    down_hbm,
+    ids_ref,
+    gates_ref,
+    wide_ref,
+    left_ref,
+    right_ref,
+    cross_ref,
+    away_ref,
+    sems,
+):
+    rows, half = tokens_hbm.shape
+    copy = pltpu.make_async_copy(tokens_hbm, wide_ref.at[:, :half], sems.at[0])
+    copy.start()
+    sibling = pl.multiple_of((1 - lax.axis_index("tp")) * half, LANES)
+    away = pltpu.make_async_copy(down_hbm.at[0, :, pl.ds(sibling, half)], away_ref, sems.at[1])
+    away.start()
     piece_rows = round_up(3 * expert_count, 16)
     line = lax.broadcasted_iota(jnp.int32, (piece_rows, rows), 0)
     named = line
@@ -169,20 +190,41 @@
         (((0,), (0,)), ((), ())),
         preferred_element_type=jnp.float32,
     )
-    wide_ref[:, :half] = tokens_ref[...]
     wide_ref[:, half:] = turned.astype(jnp.bfloat16)
+    copy.wait()
+    split = left_ref.shape[1]
+    left_ref[...] = wide_ref[:, :split]
+    right_ref[...] = wide_ref[:, split:]
     gate = decode_gate(turned, lax.axis_index("role") ^ 1, expert_count)
-    cross_ref[...] = compact(gate, tokens_ref[...], cross_ref.shape[0])
-
-
-def prepare(tokens, expert_ids, gate_weights, expert_count, capacity):
+    cross_ref[...] = compact(gate, wide_ref[:, :half], cross_ref.shape[0])
+    away.wait()
+
+
+def prepare(tokens, w_down, expert_ids, gate_weights, expert_count, capacity):
     rows, half = tokens.shape
-    return call(
+    split = split_of(half)
+    shapes = [
+        (rows, half + LANES),
+        (rows, split),
+        (rows, half + LANES - split),
+        (capacity, half),
+        (w_down.shape[1], half),
+    ]
+    whole = pl.BlockSpec(memory_space=pltpu.VMEM)
+    return pl.pallas_call(
         functools.partial(prepare_kernel, expert_count),
-        (tokens, expert_ids.T, gate_weights.T),
-        ((rows, half + LANES), (capacity, half)),
-        2 * rows * LANES * half,
-        "prepare",
+        in_specs=[pl.BlockSpec(memory_space=pltpu.HBM)] * 2 + [whole, whole],
+        out_specs=[whole] * len(shapes),
+        out_shape=[pltpu.VMEM(shape, jnp.bfloat16) for shape in shapes],
+        scratch_shapes=[pltpu.SemaphoreType.DMA((2,))],
+        name="prepare",
+        compiler_params=pltpu.CompilerParams(vmem_limit_bytes=VMEM_LIMIT),
+        cost_estimate=pl.CostEstimate(flops=0, bytes_accessed=0, transcendentals=0),
+    )(
+        pltpu.with_memory_space_constraint(tokens, pltpu.HBM),
+        pltpu.with_memory_space_constraint(w_down, pltpu.HBM),
+        expert_ids.T,
+        gate_weights.T,
     )
 
 
@@ -205,45 +247,69 @@
     )[0]
 
 
-def hidden_kernel(starts, part_count, *refs):
-    parts = refs[: 2 * part_count]
-    gate_ref, up_ref, hidden_ref, arrived = refs[2 * part_count :]
-    half = arrived.shape[1] // 2
+def joined_cross_kernel(expert_count, left_ref, right_ref, wide_ref, cross_ref):
+    split = left_ref.shape[1]
+    wide_ref[:, :split] = left_ref[...]
+    wide_ref[:, split:] = right_ref[...]
+    cross_kernel(expert_count, wide_ref, cross_ref)
+
+
+def joined_cross_rows(left, right, expert_count, capacity):
+    rows, width = left.shape[0], left.shape[1] + right.shape[1]
+    half = width - LANES
+    return call(
+        functools.partial(joined_cross_kernel, expert_count),
+        (left, right),
+        ((rows, width), (capacity, half)),
+        2 * rows * LANES * half,
+        "joined_cross_rows",
+    )
+
+
+def row_starts(blocks):
+    starts, rows = [], 0
+    for block in blocks:
+        starts.append(rows)
+        rows += round_up(block.shape[0], 16)
+    return tuple(starts), rows
+
+
+def pack_kernel(starts, *refs):
+    out_ref = refs[-1]
+    for start, ref in zip(starts, refs):
+        out_ref[start : start + ref.shape[0], :] = ref[:, : out_ref.shape[1]]
+
+
+def pack(blocks, half):
+    starts, rows = row_starts(blocks)
+    return call(
+        functools.partial(pack_kernel, starts), blocks, ((rows, half),), 0, "pack_rows"
+    )[0]
+
+
+def hidden_kernel(near_ref, far_ref, gate_ref, up_ref, hidden_ref):
+    half = near_ref.shape[1]
     core = lax.axis_index("tp")
-    own = pl.multiple_of(core * half, LANES)
-    sibling = pl.multiple_of((1 - core) * half, LANES)
-    for index, start in enumerate(starts):
-        near, far = parts[2 * index], parts[2 * index + 1]
-        rows = slice(start, start + near.shape[0])
-        arrived[rows, pl.ds(own, half)] = near[:, :half]
-        arrived[rows, pl.ds(sibling, half)] = far[:, :half]
+    own = pl.ds(pl.multiple_of(core * half, LANES), half)
+    sibling = pl.ds(pl.multiple_of((1 - core) * half, LANES), half)
     width = 256
     for first in range(0, hidden_ref.shape[1], width):
         units = slice(first, first + width)
-        gate_proj = jnp.dot(arrived[...], gate_ref[:, units], preferred_element_type=jnp.float32)
-        up_proj = jnp.dot(arrived[...], up_ref[:, units], preferred_element_type=jnp.float32)
+        gate_proj, up_proj = (
+            jnp.dot(near_ref[...], ref[own, units], preferred_element_type=jnp.float32)
+            + jnp.dot(far_ref[...], ref[sibling, units], preferred_element_type=jnp.float32)
+            for ref in (gate_ref, up_ref)
+        )
         hidden_ref[:, units] = (jax.nn.silu(gate_proj) * up_proj).astype(jnp.bfloat16)
 
 
-def row_starts(parts):
-    starts, rows = [], 0
-    for part in parts:
-        starts.append(rows)
-        rows += round_up(part.shape[0], 16)
-    return tuple(starts), rows
-
-
-def hidden_units(pairs, w_gate, w_up):
-    depth, hidden_count = w_gate.shape
-    starts, rows = row_starts([near for near, _ in pairs])
-    operands = [array for pair in pairs for array in pair]
+def hidden_units(near, far, w_gate, w_up):
     return call(
-        functools.partial(hidden_kernel, starts, len(pairs)),
-        (*operands, w_gate, w_up),
-        ((rows, hidden_count),),
-        4 * rows * depth * hidden_count,
+        hidden_kernel,
+        (near, far, w_gate, w_up),
+        ((near.shape[0], w_gate.shape[1]),),
+        0,
         "hidden_units",
-        (pltpu.VMEM((rows, depth), jnp.bfloat16),),
     )[0]
 
 
@@ -253,13 +319,14 @@
     outs = refs[wide_count + 4 :]
     half = down_other_ref.shape[1]
     me = lax.axis_index("role")
+    base = pl.multiple_of(lax.axis_index("tp") * half, LANES)
     gates = [decode_gate(ref[:, half:].astype(jnp.float32), me, expert_count) for ref in wides]
     width = 256
     for first in range(0, half, width):
         columns = slice(first, first + width)
         result = jnp.dot(
             own_ref[...],
-            down_ref[:, columns],
+            down_ref[0, :, pl.ds(pl.multiple_of(base + first, LANES), width)],
             preferred_element_type=jnp.float32,
         ) + jnp.dot(
             other_ref[...], down_other_ref[:, columns], preferred_element_type=jnp.float32
@@ -323,63 +390,49 @@
     )(q_lat, latent_cache.transpose(0, 2, 1), lengths[None, :], placement[None, :])
 
 
-def fetch_kernel(down_hbm, _, down_ref, away_ref, sems):
-    half = down_ref.shape[1]
-    core = lax.axis_index("tp")
-    own = pl.multiple_of(core * half, LANES)
-    sibling = pl.multiple_of((1 - core) * half, LANES)
-    copies = [
-        pltpu.make_async_copy(down_hbm.at[0, :, pl.ds(sibling, half)], away_ref, sems.at[0]),
-        pltpu.make_async_copy(down_hbm.at[0, :, pl.ds(own, half)], down_ref, sems.at[1]),
-    ]
-    for copy in copies:
-        copy.start()
-    for copy in copies:
-        copy.wait()
-
-
-def fetch(w_down, earlier):
-    _, hidden_count, depth = w_down.shape
-    half = depth // 2
-    shapes = [(hidden_count, half)] * 2
-    return pl.pallas_call(
-        fetch_kernel,
-        in_specs=[pl.BlockSpec(memory_space=pltpu.HBM), pl.BlockSpec(memory_space=pl.ANY)],
-        out_specs=[pl.BlockSpec(memory_space=pltpu.VMEM)] * 2,
-        out_shape=[pltpu.VMEM(shape, jnp.bfloat16) for shape in shapes],
-        scratch_shapes=[pltpu.SemaphoreType.DMA((2,))],
-        name="fetch",
-        compiler_params=pltpu.CompilerParams(vmem_limit_bytes=VMEM_LIMIT),
-        cost_estimate=pl.CostEstimate(flops=0, bytes_accessed=0, transcendentals=0),
-    )(pltpu.with_memory_space_constraint(w_down, pltpu.HBM), earlier)
-
-
-def combine_kernel(expert_count, wide_ref, own_ref, back_ref, *refs):
-    sums, out_ref = refs[:-1], refs[-1]
-    half = out_ref.shape[1]
+def combine_kernel(expert_count, first, sum_count, wide_ref, own_ref, back_ref, *refs):
+    sums, outs = refs[:sum_count], refs[sum_count:]
+    half = own_ref.shape[1]
     other = lax.axis_index("role") ^ 1
     gate = decode_gate(wide_ref[:, half:].astype(jnp.float32), other, expert_count)
     slots = slot_matrix(gate)[:, : back_ref.shape[0]]
-    width = 256
-    for first in range(0, half, width):
-        columns = slice(first, first + width)
-        spread = jnp.dot(slots, back_ref[:, columns], preferred_element_type=jnp.float32)
-        result = own_ref[:, columns] + gate * spread
-        for ref in sums:
-            result = result + ref[:, columns].astype(jnp.float32)
-        out_ref[:, columns] = result.astype(jnp.bfloat16)
-
-
-def combine(wide, own, back, sums, expert_count, last=False):
-    rows, half = own.shape
+    width = LANES
+    for out_ref in outs:
+        for column in range(0, out_ref.shape[1], width):
+            columns = slice(first + column, first + column + width)
+            spread = jnp.dot(slots, back_ref[:, columns], preferred_element_type=jnp.float32)
+            result = own_ref[:, columns] + gate * spread
+            for ref in sums:
+                result = result + ref[:, column : column + width].astype(jnp.float32)
+            out_ref[:, column : column + width] = result.astype(out_ref.dtype)
+        first += out_ref.shape[1]
+
+
+def combine(wide, own, back, sums, expert_count, first, widths, dtype=jnp.bfloat16):
+    rows = own.shape[0]
     return call(
-        functools.partial(combine_kernel, expert_count),
+        functools.partial(combine_kernel, expert_count, first, len(sums)),
         (wide, own, back, *sums),
-        ((rows, half),),
-        2 * rows * LANES * half,
+        tuple((rows, width) for width in widths),
+        0,
         "combine",
-        last=last,
-    )[0]
+        types=(dtype,) * len(widths),
+    )
+
+
+def add_kernel(*refs):
+    out_ref = refs[-1]
+    count = len(refs) // 2
+    first = 0
+    for total_ref, part_ref in zip(refs[:count], refs[count:-1]):
+        result = total_ref[...] + part_ref[...].astype(jnp.float32)
+        out_ref[:, first : first + part_ref.shape[1]] = result.astype(jnp.bfloat16)
+        first += part_ref.shape[1]
+
+
+def add_last(totals, parts):
+    shape = (parts[0].shape[0], sum(part.shape[1] for part in parts))
+    return call(add_kernel, (*totals, *parts), (shape,), 0, "add_last", last=True)[0]
 
 
 def swap(array, bits):
@@ -400,67 +453,54 @@
     capacity = 3 * token_count * route_count // (2 * role_count)
     pair, mirror, row = 2, 6, 1
 
-    wide, cross = prepare(tokens, expert_ids, gate_weights, role_count, capacity)
-    wide_mirror = swap(wide, mirror)
+    wide, own_left, own_right, cross, down_away = prepare(
+        tokens, w_down, expert_ids, gate_weights, role_count, capacity
+    )
+    mirror_left = swap(own_left, mirror)
+    mirror_right = swap(own_right, mirror)
     wide_pair = swap(wide, pair)
     cross_in = swap(cross, row)
-    wide_other = swap_core(wide)
     w_gate, w_up = w_gate[0], w_up[0]
-    w_down, down_away = fetch(w_down, wide)
-    attended = attend(after(q_lat, down_away), latent_cache, lengths, placement)
+    down_other = swap_core(down_away)
+    attended = attend(after(q_lat, wide), latent_cache, lengths, placement)
     cross_in = after(cross_in, attended)
-    wide_pair = after(wide_pair, cross_in, wide_other)
+    mirror_left = after(mirror_left, cross_in, down_other)
+    far_left = swap(mirror_left, pair)
+    wide_pair = after(wide_pair, mirror_left)
     cross_pair = cross_rows(wide_pair, role_count, capacity)
     cross_pair_in = swap(cross_pair, row)
-    wide_pair_other = swap_core(wide_pair)
-
-    wide_mirror = after(wide_mirror, cross_pair)
-    wide_far = swap(wide_mirror, pair)
-    cross_mirror = cross_rows(wide_mirror, role_count, capacity)
+    mirror_right = after(mirror_right, cross_pair)
+    far_right = swap(mirror_right, pair)
+    wide_mirror, cross_mirror = joined_cross_rows(
+        mirror_left, mirror_right, role_count, capacity
+    )
     cross_mirror_in = swap(cross_mirror, row)
-    wide_mirror_other = swap_core(wide_mirror)
-
     cross_pair_in = after(cross_pair_in, cross_mirror)
-    cross_in_other = swap_core(cross_in)
-    cross_pair_in_other = swap_core(cross_pair_in)
-
-    wide_far = after(
-        wide_far,
-        wide_pair_other,
-        wide_mirror_other,
-        cross_in_other,
-        cross_pair_in_other,
-        cross_mirror_in,
-    )
-    cross_far = cross_rows(wide_far, role_count, capacity)
+    far_left = after(far_left, cross_pair_in)
+    far_right = after(far_right, far_left)
+    cross_mirror_in = after(cross_mirror_in, far_right)
+    far_right = after(far_right, cross_mirror_in)
+    wide_far, cross_far = joined_cross_rows(far_left, far_right, role_count, capacity)
     cross_far_in = swap(cross_far, row)
-    cross_mirror_in_other = swap_core(after(cross_mirror_in, cross_far))
-    down_other = swap_core(after(down_away, cross_far))
-    wide_far_other = swap_core(wide_far)
-    hidden = hidden_units(
-        [
-            (wide, wide_other),
-            (wide_pair, wide_pair_other),
-            (wide_mirror, wide_mirror_other),
-            (wide_far, wide_far_other),
-            (cross_in, cross_in_other),
-            (cross_pair_in, cross_pair_in_other),
-            (cross_mirror_in, cross_mirror_in_other),
-        ],
-        w_gate,
-        w_up,
-    )
+    near_first = pack((after(wide, cross_far), wide_pair, wide_mirror, cross_in), half)
+    far_first = swap_core(near_first)
+    near_second = pack((wide_far, cross_pair_in, cross_mirror_in), half)
+    far_second = swap_core(near_second)
+    hidden = hidden_units(near_first, after(far_first, near_second), w_gate, w_up)
     hidden_other = swap_core(hidden)
     cross_far_in = after(cross_far_in, hidden)
-    hidden_far = hidden_units([(cross_far_in, swap_core(cross_far_in))], w_gate, w_up)
-    hidden_far_other = swap_core(hidden_far)
+    hidden_second = hidden_units(near_second, after(far_second, cross_far_in), w_gate, w_up)
+    hidden_second_other = swap_core(hidden_second)
+    far_third = swap_core(cross_far_in)
+    far_third = after(far_third, hidden_second)
+    hidden_third = hidden_units(cross_far_in, far_third, w_gate, w_up)
+    hidden_third_other = swap_core(hidden_third)
     (back_far,) = down(
-        (), 1, hidden_far, hidden_far_other, w_down, down_other, capacity, role_count
-    )
-    blocks = (wide, wide_pair, wide_mirror, wide_far)
-    own, own_pair, own_mirror, own_far, back, back_pair, back_mirror = down(
-        blocks,
-        3,
+        (), 1, hidden_third, hidden_third_other, w_down, down_other, capacity, role_count
+    )
+    own, own_pair, own_mirror, back_own = down(
+        (wide, wide_pair, wide_mirror),
+        1,
         hidden,
         after(hidden_other, back_far),
         w_down,
@@ -468,23 +508,57 @@
         capacity,
         role_count,
     )
+    own_far, back_pair, back_mirror = down(
+        (wide_far,),
+        2,
+        hidden_second,
+        after(hidden_second_other, back_far),
+        w_down,
+        down_other,
+        capacity,
+        role_count,
+    )
     back_far = swap(back_far, row)
     back_mirror = swap(back_mirror, row)
     back_pair = swap(back_pair, row)
-    back = swap(back, row)
-
-    sum_far = combine(wide_far, own_far, back_far, (), role_count)
-    from_far = swap(sum_far, pair)
-    back_mirror = after(back_mirror, sum_far)
-    sum_mirror = combine(wide_mirror, own_mirror, back_mirror, (from_far,), role_count)
-    from_mirror = swap(sum_mirror, mirror)
-    back_pair = after(back_pair, sum_mirror)
-    sum_pair = combine(wide_pair, own_pair, back_pair, (), role_count)
-    from_pair = swap(sum_pair, pair)
-    back = after(back, sum_pair)
-    moe_result = combine(
-        wide, own, back, (from_pair, from_mirror), role_count, last=True
-    )
+    back_own = swap(back_own, row)
+
+    split = half // 2
+    widths = (split, half - split)
+    back_far = after(back_far, own, own_far)
+    sum_far_left, sum_far_right = combine(
+        wide_far, own_far, back_far, (), role_count, 0, widths
+    )
+    from_far_left = swap(sum_far_left, pair)
+    from_far_right = swap(sum_far_right, pair)
+    back_mirror = after(back_mirror, sum_far_left)
+    from_far_left = after(from_far_left, back_mirror)
+    (sum_mirror_left,) = combine(
+        wide_mirror, own_mirror, back_mirror, (from_far_left,), role_count, 0, widths[:1]
+    )
+    from_mirror_left = swap(sum_mirror_left, mirror)
+    from_far_right = after(from_far_right, sum_mirror_left)
+    (sum_mirror_right,) = combine(
+        wide_mirror, own_mirror, back_mirror, (from_far_right,), role_count, split, widths[1:]
+    )
+    from_mirror_right = swap(sum_mirror_right, mirror)
+    back_pair = after(back_pair, sum_mirror_right)
+    sum_pair_left, sum_pair_right = combine(
+        wide_pair, own_pair, back_pair, (), role_count, 0, widths
+    )
+    from_pair_left = swap(sum_pair_left, pair)
+    from_pair_right = swap(sum_pair_right, pair)
+    back_own = after(back_own, sum_pair_left)
+    from_mirror_left = after(from_mirror_left, back_own)
+    (sum_left,) = combine(
+        wide, own, back_own, (from_mirror_left,), role_count, 0, widths[:1], jnp.float32
+    )
+    from_mirror_right = after(from_mirror_right, sum_left)
+    (sum_right,) = combine(
+        wide, own, back_own, (from_mirror_right,), role_count, split, widths[1:], jnp.float32
+    )
+    from_pair_left = after(from_pair_left, sum_right)
+    moe_result = add_last((sum_left, sum_right), (from_pair_left, from_pair_right))
     return (attended, moe_result)
 
 

time: 97.7 us -> 89.4 us (0.915)
  waiting for transfers between devices: 48.5 us -> 39.1 us
  starting transfers between devices: 25.3 us -> 28 us
  local copies, waits for them, and re-layouts: 4.37 us -> 2.65 us
    ppermute x14 -> x19, waiting for transfers between devices: 42.7 us -> 37.3 us  [swap(): lax.ppermute(array, 'role', [(device, device ^ bits) for device in range(...]
    ppermute x11 -> x7, waiting for transfers between devices: 5.75 us -> 1.81 us  [swap_core(): return lax.ppermute(array, 'tp', [(0, 1), (1, 0)])]
    ppermute x14 -> x19, starting transfers between devices: 23.1 us -> 25.7 us  [swap(): lax.ppermute(array, 'role', [(device, device ^ bits) for device in range(...]
    unnamed x18, local copies, waits for them, and re-layouts: 4.37 us -> 2.65 us
    pallas_call x12 -> x18, Pallas kernels: 14.3 us -> 14.8 us  [call(): pl.pallas_call(kernel, in_specs=[place] * len(operands), out_specs=[place...]
    ppermute x11 -> x7, starting transfers between devices: 2.18 us -> 2.27 us  [swap_core(): return lax.ppermute(array, 'tp', [(0, 1), (1, 0)])]
  transfers between devices with their start and end apart: 25 -> 26, of which waited for: 10 -> 16; matrix products, arithmetic and copies ran while one was open for 0% -> 0% of each run, Pallas kernels for 16% -> 17%
where the time goes in v3:
time: 89.4 us; the launch traced here: 89.2 us
  waiting for transfers between devices  39.1 us (44%)
  starting transfers between devices  28 us (31%)
  Pallas kernels  18.6 us (21%)
  local copies, waits for them, and re-layouts  2.65 us (3%)
    ppermute x19, waiting for transfers between devices, swap(): lax.ppermute(array, 'role', [(device, device ^ bits) for device in range(...  37.3 us
    ppermute x19, starting transfers between devices, swap(): lax.ppermute(array, 'role', [(device, device ^ bits) for device in range(...  25.7 us
    pallas_call x18, Pallas kernels, call(): pl.pallas_call(kernel, in_specs=[place] * len(operands), out_specs=[place...  14.8 us
    unnamed x18, local copies, waits for them, and re-layouts  2.65 us
    ppermute x7, starting transfers between devices, swap_core(): return lax.ppermute(array, 'tp', [(0, 1), (1, 0)])  2.27 us
    pallas_call x1, Pallas kernels, attend(): pl.pallas_call(attend_kernel, out_shape=jax.ShapeDtypeStruct((slot_count,...  2.05 us
    ppermute x7, waiting for transfers between devices, swap_core(): return lax.ppermute(array, 'tp', [(0, 1), (1, 0)])  1.81 us
  transfers between devices with their start and end apart: 26, of which 16 were waited for; matrix products, arithmetic and copies ran while one was open for 0% of the time, Pallas kernels for 17%

profile of v3, /device:TPU:0, one launch (start us, length us, event | category | flops | bytes accessed | tf_op | source)
XLA Modules:
  0.0 89.2 jit_solution(16829065743771885718)
XLA Ops:
  0.6 0.7 copy-done.5
  1.3 0.7 copy-done.6
  2.0 1.8 %prepare.1 = (bf16[96,1920]{1,0:T(8,128)(2,1)S(1)}, bf16[96,1408]{1,0:T(8,128)(2,1)S(1)}, bf16[96,512]{1,0:T(8,128)(2,1)S(1)}, bf16[72,1792]{1,0:T(8,128)(2,1)S(1)}, bf16[512,1792]{1,0:T(8,128)(2,1)S(1)}) custom-call(bf16[96,1792]{1,0:T(8,128)(2,1)} %tokens_hbm.1, bf16[1,512,3584]{2,1,0:T(8,128)(2,1)} %refs_3_.1, s32[4,96]{1,0:T(4,128)S(1)} %bitcast.14, ...), custom_call_target="tpu_custom_call" | custom-call | tf_op jit(solution)/shard_map/prepare/pallas_call | solution.py:214
  3.8 0.5 collective-permute-start.3
  4.3 2.6 %collective-permute-start = (bf16[96,1920]{1,0:T(8,128)(2,1)S(1)}, bf16[96,1920]{1,0:T(8,128)(2,1)S(1)}, u32[]{:S(2)}, u32[]{:S(2)}) collective-permute-start(bf16[96,1920]{1,0:T(8,128)(2,1)S(1)} %get-tuple-element.66.refs_0_.wide_ref), channel_id=1, source_target_pairs={{0,4},{2,6},{4,0},{6,2},{8,12},{10,14},{12,8},{14,10},{1,5},{3,7},... | collective-permute-start | bytes 1105928 | tf_op jit(solution)/shard_map/ppermute | solution.py:440
  7.0 2.5 %collective-permute-start.1 = (bf16[96,1408]{1,0:T(8,128)(2,1)S(1)}, bf16[96,1408]{1,0:T(8,128)(2,1)S(1)}, u32[]{:S(2)}, u32[]{:S(2)}) collective-permute-start(bf16[96,1408]{1,0:T(8,128)(2,1)S(1)} %get-tuple-element.50), channel_id=1, source_target_pairs={{0,12},{2,14},{4,8},{6,10},{8,4},{10,6},{12,0},{14,2},{1,13},{3,15... | collective-permute-start | bytes 811016 | tf_op jit(solution)/shard_map/ppermute | solution.py:440
  9.4 1.5 %collective-permute-start.2 = (bf16[72,1792]{1,0:T(8,128)(2,1)S(1)}, bf16[72,1792]{1,0:T(8,128)(2,1)S(1)}, u32[]{:S(2)}, u32[]{:S(2)}) collective-permute-start(bf16[72,1792]{1,0:T(8,128)(2,1)S(1)} %get-tuple-element.51), channel_id=1, source_target_pairs={{0,2},{2,0},{4,6},{6,4},{8,10},{10,8},{12,14},{14,12},{1,3},{3,1},... | collective-permute-start | bytes 774152 | tf_op jit(solution)/shard_map/ppermute | solution.py:440
  11.0 1.3 %collective-permute-start.4 = (bf16[96,512]{1,0:T(8,128)(2,1)S(1)}, bf16[96,512]{1,0:T(8,128)(2,1)S(1)}, u32[]{:S(2)}, u32[]{:S(2)}) collective-permute-start(bf16[96,512]{1,0:T(8,128)(2,1)S(1)} %get-tuple-element.56), channel_id=1, source_target_pairs={{0,12},{2,14},{4,8},{6,10},{8,4},{10,6},{12,0},{14,2},{1,13},{3,15... | collective-permute-start | bytes 294920 | tf_op jit(solution)/shard_map/ppermute | solution.py:440
  12.3 1.3 %copy-done.3 = bf16[4,256,576]{1,2,0:T(8,128)(2,1)S(1)} copy-done((bf16[4,256,576]{1,2,0:T(8,128)(2,1)S(1)}, bf16[4,256,576]{1,2,0:T(8,128)(2,1)}, u32[]{:S(2)}) %copy-start.3) | copy-done | bytes 1179672
  13.6 2.1 %attend.1 = bf16[4,32,512]{2,1,0:T(8,128)(2,1)} custom-call(bf16[4,32,576]{2,1,0:T(8,128)(2,1)S(1)} %copy-done.4, bf16[4,576,256]{2,1,0:T(8,128)(2,1)S(1)} %bitcast.13, s32[1,32]{1,0:T(1,128)S(1)} %bitcast.16, s32[1,32]{1,0:T(1,128)S(1)} %bitcast.17), custom_call_target="tpu_custom_call" | custom-call | tf_op jit(solution)/shard_map/attend/pallas_call | solution.py:384
  15.6 1.8 %collective-permute-done.2.refs_3_ = bf16[72,1792]{1,0:T(8,128)(2,1)S(1)} collective-permute-done((bf16[72,1792]{1,0:T(8,128)(2,1)S(1)}, bf16[72,1792]{1,0:T(8,128)(2,1)S(1)}, u32[]{:S(2)}, u32[]{:S(2)}) %collective-permute-start.2) | collective-permute-done | bytes 258080 | tf_op jit(solution)/shard_map/ppermute | solution.py:440
  17.4 7.2 %collective-permute-done.1.left_ref = bf16[96,1408]{1,0:T(8,128)(2,1)S(1)} collective-permute-done((bf16[96,1408]{1,0:T(8,128)(2,1)S(1)}, bf16[96,1408]{1,0:T(8,128)(2,1)S(1)}, u32[]{:S(2)}, u32[]{:S(2)}) %collective-permute-start.1) | collective-permute-done | bytes 270368 | tf_op jit(solution)/shard_map/ppermute | solution.py:440
  24.7 0.5 cross_rows.1
  25.2 1.6 %collective-permute-start.6 = (bf16[72,1792]{1,0:T(8,128)(2,1)S(1)}, bf16[72,1792]{1,0:T(8,128)(2,1)S(1)}, u32[]{:S(2)}, u32[]{:S(2)}) collective-permute-start(bf16[72,1792]{1,0:T(8,128)(2,1)S(1)} %cross_rows.1), channel_id=1, source_target_pairs={{0,2},{2,0},{4,6},{6,4},{8,10},{10,8},{12,14},{14,12},{1,3},{3,1},... | collective-permute-start | bytes 774152 | tf_op jit(solution)/shard_map/ppermute | solution.py:440
  26.8 0.5 joined_cross_rows.2
  27.4 1.2 %collective-permute-start.8 = (bf16[72,1792]{1,0:T(8,128)(2,1)S(1)}, bf16[72,1792]{1,0:T(8,128)(2,1)S(1)}, u32[]{:S(2)}, u32[]{:S(2)}) collective-permute-start(bf16[72,1792]{1,0:T(8,128)(2,1)S(1)} %get-tuple-element.59), channel_id=1, source_target_pairs={{0,2},{2,0},{4,6},{6,4},{8,10},{10,8},{12,14},{14,12},{1,3},{3,1},... | collective-permute-start | bytes 774152 | tf_op jit(solution)/shard_map/ppermute | solution.py:440
  28.6 1.4 %collective-permute-start.7 = (bf16[96,512]{1,0:T(8,128)(2,1)S(1)}, bf16[96,512]{1,0:T(8,128)(2,1)S(1)}, u32[]{:S(2)}, u32[]{:S(2)}) collective-permute-start(bf16[96,512]{1,0:T(8,128)(2,1)S(1)} %collective-permute-done.4.right_ref), channel_id=1, source_target_pairs={{0,4},{2,6},{4,0},{6,2},{8,12},{10,14},{12,8},{14,10},{1,5},{3,7},... | collective-permute-start | bytes 294920 | tf_op jit(solution)/shard_map/ppermute | solution.py:440
  30.0 4.5 %collective-permute-done.6.refs_1_ = bf16[72,1792]{1,0:T(8,128)(2,1)S(1)} collective-permute-done((bf16[72,1792]{1,0:T(8,128)(2,1)S(1)}, bf16[72,1792]{1,0:T(8,128)(2,1)S(1)}, u32[]{:S(2)}, u32[]{:S(2)}) %collective-permute-start.6) | collective-permute-done | bytes 258080 | tf_op jit(solution)/shard_map/ppermute | solution.py:440
  34.5 3.6 %collective-permute-done.8.refs_2_ = bf16[72,1792]{1,0:T(8,128)(2,1)S(1)} collective-permute-done((bf16[72,1792]{1,0:T(8,128)(2,1)S(1)}, bf16[72,1792]{1,0:T(8,128)(2,1)S(1)}, u32[]{:S(2)}, u32[]{:S(2)}) %collective-permute-start.8) | collective-permute-done | bytes 258080 | tf_op jit(solution)/shard_map/ppermute | solution.py:440
  38.1 0.5 joined_cross_rows.3
  38.6 0.0 copy-start.1
  38.6 0.1 pack_rows.2.near_ref
  38.7 0.1 collective-permute-start.9
  38.8 0.1 pack_rows.3.near_ref
  38.9 0.6 collective-permute-start.13
  39.4 1.5 %collective-permute-start.11 = (bf16[72,1792]{1,0:T(8,128)(2,1)S(1)}, bf16[72,1792]{1,0:T(8,128)(2,1)S(1)}, u32[]{:S(2)}, u32[]{:S(2)}) collective-permute-start(bf16[72,1792]{1,0:T(8,128)(2,1)S(1)} %get-tuple-element.65), channel_id=1, source_target_pairs={{0,2},{2,0},{4,6},{6,4},{8,10},{10,8},{12,14},{14,12},{1,3},{3,1},... | collective-permute-start | bytes 774152 | tf_op jit(solution)/shard_map/ppermute | solution.py:440
  41.0 0.9 collective-permute-done.9.far_ref
  41.9 2.9 %hidden_units.3.refs_3_ = bf16[368,512]{1,0:T(8,128)(2,1)S(1)} custom-call(bf16[368,1792]{1,0:T(8,128)(2,1)S(1)} %pack_rows.2.near_ref, bf16[368,1792]{1,0:T(8,128)(2,1)S(1)} %collective-permute-done.9.far_ref, bf16[3584,512]{1,0:T(8,128)(2,1)S(1)} %bitcast.7, bf16[3584,512]{1,0:T(8,128)(2,1)S(1)} %bitcast.10), custom_call_target="tpu_custom_call" | custom-call | tf_op jit(solution)/shard_map/hidden_units/pallas_call | solution.py:91
  44.8 2.9 %collective-permute-done.11.near_ref = bf16[72,1792]{1,0:T(8,128)(2,1)S(1)} collective-permute-done((bf16[72,1792]{1,0:T(8,128)(2,1)S(1)}, bf16[72,1792]{1,0:T(8,128)(2,1)S(1)}, u32[]{:S(2)}, u32[]{:S(2)}) %collective-permute-start.11) | collective-permute-done | bytes 258080 | tf_op jit(solution)/shard_map/ppermute | solution.py:440
  47.6 0.5 collective-permute-start.10
  48.2 2.1 %hidden_units.4.refs_1_ = bf16[256,512]{1,0:T(8,128)(2,1)S(1)} custom-call(bf16[256,1792]{1,0:T(8,128)(2,1)S(1)} %pack_rows.3.near_ref, bf16[256,1792]{1,0:T(8,128)(2,1)S(1)} %collective-permute-done.13.far_ref, bf16[3584,512]{1,0:T(8,128)(2,1)S(1)} %bitcast.8, bf16[3584,512]{1,0:T(8,128)(2,1)S(1)} %bitcast.11), custom_call_target="tpu_custom_call" | custom-call | tf_op jit(solution)/shard_map/hidden_units/pallas_call | solution.py:91
  50.2 0.1 collective-permute-start.16
  50.3 1.4 %hidden_units.5.refs_0_ = bf16[72,512]{1,0:T(8,128)(2,1)S(1)} custom-call(bf16[72,1792]{1,0:T(8,128)(2,1)S(1)} %collective-permute-done.11.near_ref, bf16[72,1792]{1,0:T(8,128)(2,1)S(1)} %collective-permute-done.12.far_ref, bf16[3584,512]{1,0:T(8,128)(2,1)S(1)} %bitcast.9, bf16[3584,512]{1,0:T(8,128)(2,1)S(1)} %bitcast.12), custom_call_target="tpu_custom_call" | custom-call | tf_op jit(solution)/shard_map/hidden_units/pallas_call | solution.py:91
  51.7 0.5 collective-permute-start.14
  52.3 0.9 %collective-permute-done.14.refs_1_ = bf16[72,512]{1,0:T(8,128)(2,1)S(1)} collective-permute-done((bf16[72,512]{1,0:T(8,128)(2,1)S(1)}, bf16[72,512]{1,0:T(8,128)(2,1)S(1)}, u32[]{:S(2)}, u32[]{:S(2)}) %collective-permute-start.14) | collective-permute-done | bytes 73760 | tf_op jit(solution)/shard_map/ppermute | solution.py:444
  53.2 0.7 down.3
  53.9 1.6 %collective-permute-start.19 = (bf16[72,1792]{1,0:T(8,128)(2,1)S(1)}, bf16[72,1792]{1,0:T(8,128)(2,1)S(1)}, u32[]{:S(2)}, u32[]{:S(2)}) collective-permute-start(bf16[72,1792]{1,0:T(8,128)(2,1)S(1)} %down.3), channel_id=1, source_target_pairs={{0,2},{2,0},{4,6},{6,4},{8,10},{10,8},{12,14},{14,12},{1,3},{3,1},... | collective-permute-start | bytes 774152 | tf_op jit(solution)/shard_map/ppermute | solution.py:440
  55.5 1.1 %down.5 = (f32[96,1792]{1,0:T(8,128)S(1)}, bf16[72,1792]{1,0:T(8,128)(2,1)S(1)}, bf16[72,1792]{1,0:T(8,128)(2,1)S(1)}) custom-call(bf16[96,1920]{1,0:T(8,128)(2,1)S(1)} %get-tuple-element.67.refs_0_.wide_ref, bf16[256,512]{1,0:T(8,128)(2,1)S(1)} %hidden_units.4.refs_1_, bf16[256,512]{1,0:T(8,128)(2,1)S(1)} %collective-permute-done.16.refs_2_, ...), custom_call_target="tpu_custom_call" | custom-call | tf_op jit(solution)/shard_map/down/pallas_call | solution.py:91
  56.6 0.6 collective-permute-start.18
  57.2 1.5 %collective-permute-start.17 = (bf16[72,1792]{1,0:T(8,128)(2,1)S(1)}, bf16[72,1792]{1,0:T(8,128)(2,1)S(1)}, u32[]{:S(2)}, u32[]{:S(2)}) collective-permute-start(bf16[72,1792]{1,0:T(8,128)(2,1)S(1)} %get-tuple-element.77), channel_id=1, source_target_pairs={{0,2},{2,0},{4,6},{6,4},{8,10},{10,8},{12,14},{14,12},{1,3},{3,1},... | collective-permute-start | bytes 774152 | tf_op jit(solution)/shard_map/ppermute | solution.py:440
  58.7 1.5 %down.4 = (f32[96,1792]{1,0:T(8,128)S(1)}, f32[96,1792]{1,0:T(8,128)S(1)}, f32[96,1792]{1,0:T(8,128)S(1)}, bf16[72,1792]{1,0:T(8,128)(2,1)S(1)}) custom-call(bf16[96,1920]{1,0:T(8,128)(2,1)S(1)} %get-tuple-element.66.refs_0_.wide_ref, bf16[96,1920]{1,0:T(8,128)(2,1)S(1)} %collective-permute-done.wide_ref.refs_1_, ...), custom_call_target="tpu_custom_call" | custom-call | tf_op jit(solution)/shard_map/down/pallas_call | solution.py:91
  60.3 2.7 %collective-permute-done.19.back_ref = bf16[72,1792]{1,0:T(8,128)(2,1)S(1)} collective-permute-done((bf16[72,1792]{1,0:T(8,128)(2,1)S(1)}, bf16[72,1792]{1,0:T(8,128)(2,1)S(1)}, u32[]{:S(2)}, u32[]{:S(2)}) %collective-permute-start.19) | collective-permute-done | bytes 258080 | tf_op jit(solution)/shard_map/ppermute | solution.py:440
  63.0 0.5 combine.6
  63.5 1.8 %collective-permute-start.21 = (bf16[96,896]{1,0:T(8,128)(2,1)S(1)}, bf16[96,896]{1,0:T(8,128)(2,1)S(1)}, u32[]{:S(2)}, u32[]{:S(2)}) collective-permute-start(bf16[96,896]{1,0:T(8,128)(2,1)S(1)} %get-tuple-element.82), channel_id=1, source_target_pairs={{0,4},{2,6},{4,0},{6,2},{8,12},{10,14},{12,8},{14,10},{1,5},{3,7},... | collective-permute-start | bytes 516104 | tf_op jit(solution)/shard_map/ppermute | solution.py:440
  65.3 0.3 collective-permute-start.20
  65.6 1.5 %collective-permute-start.15 = (bf16[72,1792]{1,0:T(8,128)(2,1)S(1)}, bf16[72,1792]{1,0:T(8,128)(2,1)S(1)}, u32[]{:S(2)}, u32[]{:S(2)}) collective-permute-start(bf16[72,1792]{1,0:T(8,128)(2,1)S(1)} %get-tuple-element.74), channel_id=1, source_target_pairs={{0,2},{2,0},{4,6},{6,4},{8,10},{10,8},{12,14},{14,12},{1,3},{3,1},... | collective-permute-start | bytes 774152 | tf_op jit(solution)/shard_map/ppermute | solution.py:440
  67.1 1.4 %collective-permute-done.18.back_ref = bf16[72,1792]{1,0:T(8,128)(2,1)S(1)} collective-permute-done((bf16[72,1792]{1,0:T(8,128)(2,1)S(1)}, bf16[72,1792]{1,0:T(8,128)(2,1)S(1)}, u32[]{:S(2)}, u32[]{:S(2)}) %collective-permute-start.18) | collective-permute-done | bytes 258080 | tf_op jit(solution)/shard_map/ppermute | solution.py:440
  68.5 2.1 %collective-permute-done.21.refs_0_ = bf16[96,896]{1,0:T(8,128)(2,1)S(1)} collective-permute-done((bf16[96,896]{1,0:T(8,128)(2,1)S(1)}, bf16[96,896]{1,0:T(8,128)(2,1)S(1)}, u32[]{:S(2)}, u32[]{:S(2)}) %collective-permute-start.21) | collective-permute-done | bytes 172064 | tf_op jit(solution)/shard_map/ppermute | solution.py:440
  70.7 0.4 combine.7
  71.1 1.4 %collective-permute-start.22 = (bf16[96,896]{1,0:T(8,128)(2,1)S(1)}, bf16[96,896]{1,0:T(8,128)(2,1)S(1)}, u32[]{:S(2)}, u32[]{:S(2)}) collective-permute-start(bf16[96,896]{1,0:T(8,128)(2,1)S(1)} %combine.7), channel_id=1, source_target_pairs={{0,12},{2,14},{4,8},{6,10},{8,4},{10,6},{12,0},{14,2},{1,13},{3,15... | collective-permute-start | bytes 516104 | tf_op jit(solution)/shard_map/ppermute | solution.py:440
  72.5 1.3 %collective-permute-done.20.refs_0_ = bf16[96,896]{1,0:T(8,128)(2,1)S(1)} collective-permute-done((bf16[96,896]{1,0:T(8,128)(2,1)S(1)}, bf16[96,896]{1,0:T(8,128)(2,1)S(1)}, u32[]{:S(2)}, u32[]{:S(2)}) %collective-permute-start.20) | collective-permute-done | bytes 172064 | tf_op jit(solution)/shard_map/ppermute | solution.py:440
  73.8 0.4 combine.8
  74.2 1.2 %collective-permute-start.23 = (bf16[96,896]{1,0:T(8,128)(2,1)S(1)}, bf16[96,896]{1,0:T(8,128)(2,1)S(1)}, u32[]{:S(2)}, u32[]{:S(2)}) collective-permute-start(bf16[96,896]{1,0:T(8,128)(2,1)S(1)} %combine.8), channel_id=1, source_target_pairs={{0,12},{2,14},{4,8},{6,10},{8,4},{10,6},{12,0},{14,2},{1,13},{3,15... | collective-permute-start | bytes 516104 | tf_op jit(solution)/shard_map/ppermute | solution.py:440
  75.4 0.5 combine.9
  75.9 1.4 %collective-permute-start.24 = (bf16[96,896]{1,0:T(8,128)(2,1)S(1)}, bf16[96,896]{1,0:T(8,128)(2,1)S(1)}, u32[]{:S(2)}, u32[]{:S(2)}) collective-permute-start(bf16[96,896]{1,0:T(8,128)(2,1)S(1)} %get-tuple-element.88), channel_id=1, source_target_pairs={{0,4},{2,6},{4,0},{6,2},{8,12},{10,14},{12,8},{14,10},{1,5},{3,7},... | collective-permute-start | bytes 516104 | tf_op jit(solution)/shard_map/ppermute | solution.py:440
  77.3 0.7 collective-permute-start.25
  78.0 1.0 %collective-permute-done.15.back_ref = bf16[72,1792]{1,0:T(8,128)(2,1)S(1)} collective-permute-done((bf16[72,1792]{1,0:T(8,128)(2,1)S(1)}, bf16[72,1792]{1,0:T(8,128)(2,1)S(1)}, u32[]{:S(2)}, u32[]{:S(2)}) %collective-permute-start.15) | collective-permute-done | bytes 258080 | tf_op jit(solution)/shard_map/ppermute | solution.py:440
  79.0 1.1 %collective-permute-done.22.refs_0_ = bf16[96,896]{1,0:T(8,128)(2,1)S(1)} collective-permute-done((bf16[96,896]{1,0:T(8,128)(2,1)S(1)}, bf16[96,896]{1,0:T(8,128)(2,1)S(1)}, u32[]{:S(2)}, u32[]{:S(2)}) %collective-permute-start.22) | collective-permute-done | bytes 172064 | tf_op jit(solution)/shard_map/ppermute | solution.py:440
  80.2 0.4 combine.10.refs_0_
  80.6 3.3 %collective-permute-done.23.refs_0_ = bf16[96,896]{1,0:T(8,128)(2,1)S(1)} collective-permute-done((bf16[96,896]{1,0:T(8,128)(2,1)S(1)}, bf16[96,896]{1,0:T(8,128)(2,1)S(1)}, u32[]{:S(2)}, u32[]{:S(2)}) %collective-permute-start.23) | collective-permute-done | bytes 172064 | tf_op jit(solution)/shard_map/ppermute | solution.py:440
  83.9 0.4 combine.11.refs_1_
  84.3 1.2 %collective-permute-done.24.refs_2_ = bf16[96,896]{1,0:T(8,128)(2,1)S(1)} collective-permute-done((bf16[96,896]{1,0:T(8,128)(2,1)S(1)}, bf16[96,896]{1,0:T(8,128)(2,1)S(1)}, u32[]{:S(2)}, u32[]{:S(2)}) %collective-permute-start.24) | collective-permute-done | bytes 172064 | tf_op jit(solution)/shard_map/ppermute | solution.py:440
  85.4 3.0 %collective-permute-done.25.refs_3_ = bf16[96,896]{1,0:T(8,128)(2,1)S(1)} collective-permute-done((bf16[96,896]{1,0:T(8,128)(2,1)S(1)}, bf16[96,896]{1,0:T(8,128)(2,1)S(1)}, u32[]{:S(2)}, u32[]{:S(2)}) %collective-permute-start.25) | collective-permute-done | bytes 172064 | tf_op jit(solution)/shard_map/ppermute | solution.py:440
  88.4 0.8 add_last.1
  (26 shorter events, 0.1 us)
Async XLA Ops:
  0.6 0.7 copy-start.5
  1.3 0.7 copy-start.6
  2.0 10.3 %copy-start.4 = (bf16[4,32,576]{2,1,0:T(8,128)(2,1)S(1)}, bf16[4,32,576]{2,1,0:T(8,128)(2,1)}, u32[]{:S(2)}) copy-start(bf16[4,32,576]{2,1,0:T(8,128)(2,1)} %query_ref) | copy-start | bytes 442372
  2.0 10.3 %copy-start.7 = (s32[32]{0:T(128)S(1)}, s32[32]{0:T(128)}, u32[]{:S(2)}) copy-start(s32[32]{0:T(128)} %param.12) | copy-start | bytes 388
  2.0 10.3 %copy-start.8 = (s32[32]{0:T(128)S(1)}, s32[32]{0:T(128)}, u32[]{:S(2)}) copy-start(s32[32]{0:T(128)} %param.13) | copy-start | bytes 388
  2.0 39.9 %copy-start.2 = (bf16[1,3584,512]{2,1,0:T(8,128)(2,1)S(1)}, bf16[1,3584,512]{2,1,0:T(8,128)(2,1)}, u32[]{:S(2)}) copy-start(bf16[1,3584,512]{2,1,0:T(8,128)(2,1)} %param.18) | copy-start | bytes 11010052
  3.8 20.9 %collective-permute-start.3 = (bf16[512,1792]{1,0:T(8,128)(2,1)S(1)}, bf16[512,1792]{1,0:T(8,128)(2,1)S(1)}, u32[]{:S(2)}, u32[]{:S(2)}) collective-permute-start(bf16[512,1792]{1,0:T(8,128)(2,1)S(1)} %get-tuple-element.53), channel_id=1, source_target_pairs={{0,1},{1,0},{2,3},{3,2},{4,5},{5,4},{6,7},{7,6},{8,9},{9,8},{10,11... | collective-permute-start | bytes 5505032 | tf_op jit(solution)/shard_map/ppermute | solution.py:444
  4.3 20.4 %collective-permute-start = (bf16[96,1920]{1,0:T(8,128)(2,1)S(1)}, bf16[96,1920]{1,0:T(8,128)(2,1)S(1)}, u32[]{:S(2)}, u32[]{:S(2)}) collective-permute-start(bf16[96,1920]{1,0:T(8,128)(2,1)S(1)} %get-tuple-element.66.refs_0_.wide_ref), channel_id=1, source_target_pairs={{0,4},{2,6},{4,0},{6,2},{8,12},{10,14},{12,8},{14,10},{1,5},{3,7},... | collective-permute-start | bytes 1105928 | tf_op jit(solution)/shard_map/ppermute | solution.py:440
  7.0 17.7 %collective-permute-start.1 = (bf16[96,1408]{1,0:T(8,128)(2,1)S(1)}, bf16[96,1408]{1,0:T(8,128)(2,1)S(1)}, u32[]{:S(2)}, u32[]{:S(2)}) collective-permute-start(bf16[96,1408]{1,0:T(8,128)(2,1)S(1)} %get-tuple-element.50), channel_id=1, source_target_pairs={{0,12},{2,14},{4,8},{6,10},{8,4},{10,6},{12,0},{14,2},{1,13},{3,15... | collective-permute-start | bytes 811016 | tf_op jit(solution)/shard_map/ppermute | solution.py:440
  9.4 8.0 %collective-permute-start.2 = (bf16[72,1792]{1,0:T(8,128)(2,1)S(1)}, bf16[72,1792]{1,0:T(8,128)(2,1)S(1)}, u32[]{:S(2)}, u32[]{:S(2)}) collective-permute-start(bf16[72,1792]{1,0:T(8,128)(2,1)S(1)} %get-tuple-element.51), channel_id=1, source_target_pairs={{0,2},{2,0},{4,6},{6,4},{8,10},{10,8},{12,14},{14,12},{1,3},{3,1},... | collective-permute-start | bytes 774152 | tf_op jit(solution)/shard_map/ppermute | solution.py:440
  11.0 15.9 %collective-permute-start.4 = (bf16[96,512]{1,0:T(8,128)(2,1)S(1)}, bf16[96,512]{1,0:T(8,128)(2,1)S(1)}, u32[]{:S(2)}, u32[]{:S(2)}) collective-permute-start(bf16[96,512]{1,0:T(8,128)(2,1)S(1)} %get-tuple-element.56), channel_id=1, source_target_pairs={{0,12},{2,14},{4,8},{6,10},{8,4},{10,6},{12,0},{14,2},{1,13},{3,15... | collective-permute-start | bytes 294920 | tf_op jit(solution)/shard_map/ppermute | solution.py:440
  12.3 1.3 %copy-start.3 = (bf16[4,256,576]{1,2,0:T(8,128)(2,1)S(1)}, bf16[4,256,576]{1,2,0:T(8,128)(2,1)}, u32[]{:S(2)}) copy-start(bf16[4,256,576]{1,2,0:T(8,128)(2,1)} %param.11) | copy-start | bytes 3538948
  24.7 9.8 %collective-permute-start.5 = (bf16[96,1408]{1,0:T(8,128)(2,1)S(1)}, bf16[96,1408]{1,0:T(8,128)(2,1)S(1)}, u32[]{:S(2)}, u32[]{:S(2)}) collective-permute-start(bf16[96,1408]{1,0:T(8,128)(2,1)S(1)} %collective-permute-done.1.left_ref), channel_id=1, source_target_pairs={{0,4},{2,6},{4,0},{6,2},{8,12},{10,14},{12,8},{14,10},{1,5},{3,7},... | collective-permute-start | bytes 811016 | tf_op jit(solution)/shard_map/ppermute | solution.py:440
  25.2 9.2 %collective-permute-start.6 = (bf16[72,1792]{1,0:T(8,128)(2,1)S(1)}, bf16[72,1792]{1,0:T(8,128)(2,1)S(1)}, u32[]{:S(2)}, u32[]{:S(2)}) collective-permute-start(bf16[72,1792]{1,0:T(8,128)(2,1)S(1)} %cross_rows.1), channel_id=1, source_target_pairs={{0,2},{2,0},{4,6},{6,4},{8,10},{10,8},{12,14},{14,12},{1,3},{3,1},... | collective-permute-start | bytes 774152 | tf_op jit(solution)/shard_map/ppermute | solution.py:440
  27.4 10.8 %collective-permute-start.8 = (bf16[72,1792]{1,0:T(8,128)(2,1)S(1)}, bf16[72,1792]{1,0:T(8,128)(2,1)S(1)}, u32[]{:S(2)}, u32[]{:S(2)}) collective-permute-start(bf16[72,1792]{1,0:T(8,128)(2,1)S(1)} %get-tuple-element.59), channel_id=1, source_target_pairs={{0,2},{2,0},{4,6},{6,4},{8,10},{10,8},{12,14},{14,12},{1,3},{3,1},... | collective-permute-start | bytes 774152 | tf_op jit(solution)/shard_map/ppermute | solution.py:440
  28.6 5.9 %collective-permute-start.7 = (bf16[96,512]{1,0:T(8,128)(2,1)S(1)}, bf16[96,512]{1,0:T(8,128)(2,1)S(1)}, u32[]{:S(2)}, u32[]{:S(2)}) collective-permute-start(bf16[96,512]{1,0:T(8,128)(2,1)S(1)} %collective-permute-done.4.right_ref), channel_id=1, source_target_pairs={{0,4},{2,6},{4,0},{6,2},{8,12},{10,14},{12,8},{14,10},{1,5},{3,7},... | collective-permute-start | bytes 294920 | tf_op jit(solution)/shard_map/ppermute | solution.py:440
  38.6 3.2 %copy-start.1 = (bf16[1,3584,512]{2,1,0:T(8,128)(2,1)S(1)}, bf16[1,3584,512]{2,1,0:T(8,128)(2,1)}, u32[]{:S(2)}) copy-start(bf16[1,3584,512]{2,1,0:T(8,128)(2,1)} %param.17) | copy-start | bytes 11010052
  38.7 3.1 %collective-permute-start.9 = (bf16[368,1792]{1,0:T(8,128)(2,1)S(1)}, bf16[368,1792]{1,0:T(8,128)(2,1)S(1)}, u32[]{:S(2)}, u32[]{:S(2)}) collective-permute-start(bf16[368,1792]{1,0:T(8,128)(2,1)S(1)} %pack_rows.2.near_ref), channel_id=1, source_target_pairs={{0,1},{1,0},{2,3},{3,2},{4,5},{5,4},{6,7},{7,6},{8,9},{9,8},{10,11... | collective-permute-start | bytes 3956744 | tf_op jit(solution)/shard_map/ppermute | solution.py:444
  38.9 9.3 %collective-permute-start.13 = (bf16[256,1792]{1,0:T(8,128)(2,1)S(1)}, bf16[256,1792]{1,0:T(8,128)(2,1)S(1)}, u32[]{:S(2)}, u32[]{:S(2)}) collective-permute-start(bf16[256,1792]{1,0:T(8,128)(2,1)S(1)} %pack_rows.3.near_ref), channel_id=1, source_target_pairs={{0,1},{1,0},{2,3},{3,2},{4,5},{5,4},{6,7},{7,6},{8,9},{9,8},{10,11... | collective-permute-start | bytes 2752520 | tf_op jit(solution)/shard_map/ppermute | solution.py:444
  39.4 8.2 %collective-permute-start.11 = (bf16[72,1792]{1,0:T(8,128)(2,1)S(1)}, bf16[72,1792]{1,0:T(8,128)(2,1)S(1)}, u32[]{:S(2)}, u32[]{:S(2)}) collective-permute-start(bf16[72,1792]{1,0:T(8,128)(2,1)S(1)} %get-tuple-element.65), channel_id=1, source_target_pairs={{0,2},{2,0},{4,6},{6,4},{8,10},{10,8},{12,14},{14,12},{1,3},{3,1},... | collective-permute-start | bytes 774152 | tf_op jit(solution)/shard_map/ppermute | solution.py:440
  47.6 2.7 %collective-permute-start.12 = (bf16[72,1792]{1,0:T(8,128)(2,1)S(1)}, bf16[72,1792]{1,0:T(8,128)(2,1)S(1)}, u32[]{:S(2)}, u32[]{:S(2)}) collective-permute-start(bf16[72,1792]{1,0:T(8,128)(2,1)S(1)} %collective-permute-done.11.near_ref), channel_id=1, source_target_pairs={{0,1},{1,0},{2,3},{3,2},{4,5},{5,4},{6,7},{7,6},{8,9},{9,8},{10,11... | collective-permute-start | bytes 774152 | tf_op jit(solution)/shard_map/ppermute | solution.py:444
  47.6 11.1 %collective-permute-start.10 = (bf16[368,512]{1,0:T(8,128)(2,1)S(1)}, bf16[368,512]{1,0:T(8,128)(2,1)S(1)}, u32[]{:S(2)}, u32[]{:S(2)}) collective-permute-start(bf16[368,512]{1,0:T(8,128)(2,1)S(1)} %hidden_units.3.refs_3_), channel_id=1, source_target_pairs={{0,1},{1,0},{2,3},{3,2},{4,5},{5,4},{6,7},{7,6},{8,9},{9,8},{10,11... | collective-permute-start | bytes 1130504 | tf_op jit(solution)/shard_map/ppermute | solution.py:444
  50.2 5.3 %collective-permute-start.16 = (bf16[256,512]{1,0:T(8,128)(2,1)S(1)}, bf16[256,512]{1,0:T(8,128)(2,1)S(1)}, u32[]{:S(2)}, u32[]{:S(2)}) collective-permute-start(bf16[256,512]{1,0:T(8,128)(2,1)S(1)} %hidden_units.4.refs_1_), channel_id=1, source_target_pairs={{0,1},{1,0},{2,3},{3,2},{4,5},{5,4},{6,7},{7,6},{8,9},{9,8},{10,11... | collective-permute-start | bytes 786440 | tf_op jit(solution)/shard_map/ppermute | solution.py:444
  50.3 2.9 %copy-start = (bf16[1,512,3584]{2,1,0:T(8,128)(2,1)S(1)}, bf16[1,512,3584]{2,1,0:T(8,128)(2,1)}, u32[]{:S(2)}) copy-start(bf16[1,512,3584]{2,1,0:T(8,128)(2,1)} %refs_3_.1) | copy-start | bytes 11010052
  51.7 1.5 %collective-permute-start.14 = (bf16[72,512]{1,0:T(8,128)(2,1)S(1)}, bf16[72,512]{1,0:T(8,128)(2,1)S(1)}, u32[]{:S(2)}, u32[]{:S(2)}) collective-permute-start(bf16[72,512]{1,0:T(8,128)(2,1)S(1)} %hidden_units.5.refs_0_), channel_id=1, source_target_pairs={{0,1},{1,0},{2,3},{3,2},{4,5},{5,4},{6,7},{7,6},{8,9},{9,8},{10,11... | collective-permute-start | bytes 221192 | tf_op jit(solution)/shard_map/ppermute | solution.py:444
  53.9 9.1 %collective-permute-start.19 = (bf16[72,1792]{1,0:T(8,128)(2,1)S(1)}, bf16[72,1792]{1,0:T(8,128)(2,1)S(1)}, u32[]{:S(2)}, u32[]{:S(2)}) collective-permute-start(bf16[72,1792]{1,0:T(8,128)(2,1)S(1)} %down.3), channel_id=1, source_target_pairs={{0,2},{2,0},{4,6},{6,4},{8,10},{10,8},{12,14},{14,12},{1,3},{3,1},... | collective-permute-start | bytes 774152 | tf_op jit(solution)/shard_map/ppermute | solution.py:440
  56.6 11.9 %collective-permute-start.18 = (bf16[72,1792]{1,0:T(8,128)(2,1)S(1)}, bf16[72,1792]{1,0:T(8,128)(2,1)S(1)}, u32[]{:S(2)}, u32[]{:S(2)}) collective-permute-start(bf16[72,1792]{1,0:T(8,128)(2,1)S(1)} %get-tuple-element.79), channel_id=1, source_target_pairs={{0,2},{2,0},{4,6},{6,4},{8,10},{10,8},{12,14},{14,12},{1,3},{3,1},... | collective-permute-start | bytes 774152 | tf_op jit(solution)/shard_map/ppermute | solution.py:440
  57.2 18.2 %collective-permute-start.17 = (bf16[72,1792]{1,0:T(8,128)(2,1)S(1)}, bf16[72,1792]{1,0:T(8,128)(2,1)S(1)}, u32[]{:S(2)}, u32[]{:S(2)}) collective-permute-start(bf16[72,1792]{1,0:T(8,128)(2,1)S(1)} %get-tuple-element.77), channel_id=1, source_target_pairs={{0,2},{2,0},{4,6},{6,4},{8,10},{10,8},{12,14},{14,12},{1,3},{3,1},... | collective-permute-start | bytes 774152 | tf_op jit(solution)/shard_map/ppermute | solution.py:440
  63.5 7.2 %collective-permute-start.21 = (bf16[96,896]{1,0:T(8,128)(2,1)S(1)}, bf16[96,896]{1,0:T(8,128)(2,1)S(1)}, u32[]{:S(2)}, u32[]{:S(2)}) collective-permute-start(bf16[96,896]{1,0:T(8,128)(2,1)S(1)} %get-tuple-element.82), channel_id=1, source_target_pairs={{0,4},{2,6},{4,0},{6,2},{8,12},{10,14},{12,8},{14,10},{1,5},{3,7},... | collective-permute-start | bytes 516104 | tf_op jit(solution)/shard_map/ppermute | solution.py:440
  65.3 8.5 %collective-permute-start.20 = (bf16[96,896]{1,0:T(8,128)(2,1)S(1)}, bf16[96,896]{1,0:T(8,128)(2,1)S(1)}, u32[]{:S(2)}, u32[]{:S(2)}) collective-permute-start(bf16[96,896]{1,0:T(8,128)(2,1)S(1)} %get-tuple-element.84), channel_id=1, source_target_pairs={{0,4},{2,6},{4,0},{6,2},{8,12},{10,14},{12,8},{14,10},{1,5},{3,7},... | collective-permute-start | bytes 516104 | tf_op jit(solution)/shard_map/ppermute | solution.py:440
  65.6 13.5 %collective-permute-start.15 = (bf16[72,1792]{1,0:T(8,128)(2,1)S(1)}, bf16[72,1792]{1,0:T(8,128)(2,1)S(1)}, u32[]{:S(2)}, u32[]{:S(2)}) collective-permute-start(bf16[72,1792]{1,0:T(8,128)(2,1)S(1)} %get-tuple-element.74), channel_id=1, source_target_pairs={{0,2},{2,0},{4,6},{6,4},{8,10},{10,8},{12,14},{14,12},{1,3},{3,1},... | collective-permute-start | bytes 774152 | tf_op jit(solution)/shard_map/ppermute | solution.py:440
  71.1 9.1 %collective-permute-start.22 = (bf16[96,896]{1,0:T(8,128)(2,1)S(1)}, bf16[96,896]{1,0:T(8,128)(2,1)S(1)}, u32[]{:S(2)}, u32[]{:S(2)}) collective-permute-start(bf16[96,896]{1,0:T(8,128)(2,1)S(1)} %combine.7), channel_id=1, source_target_pairs={{0,12},{2,14},{4,8},{6,10},{8,4},{10,6},{12,0},{14,2},{1,13},{3,15... | collective-permute-start | bytes 516104 | tf_op jit(solution)/shard_map/ppermute | solution.py:440
  74.2 9.7 %collective-permute-start.23 = (bf16[96,896]{1,0:T(8,128)(2,1)S(1)}, bf16[96,896]{1,0:T(8,128)(2,1)S(1)}, u32[]{:S(2)}, u32[]{:S(2)}) collective-permute-start(bf16[96,896]{1,0:T(8,128)(2,1)S(1)} %combine.8), channel_id=1, source_target_pairs={{0,12},{2,14},{4,8},{6,10},{8,4},{10,6},{12,0},{14,2},{1,13},{3,15... | collective-permute-start | bytes 516104 | tf_op jit(solution)/shard_map/ppermute | solution.py:440
  75.9 9.5 %collective-permute-start.24 = (bf16[96,896]{1,0:T(8,128)(2,1)S(1)}, bf16[96,896]{1,0:T(8,128)(2,1)S(1)}, u32[]{:S(2)}, u32[]{:S(2)}) collective-permute-start(bf16[96,896]{1,0:T(8,128)(2,1)S(1)} %get-tuple-element.88), channel_id=1, source_target_pairs={{0,4},{2,6},{4,0},{6,2},{8,12},{10,14},{12,8},{14,10},{1,5},{3,7},... | collective-permute-start | bytes 516104 | tf_op jit(solution)/shard_map/ppermute | solution.py:440
  77.3 11.1 %collective-permute-start.25 = (bf16[96,896]{1,0:T(8,128)(2,1)S(1)}, bf16[96,896]{1,0:T(8,128)(2,1)S(1)}, u32[]{:S(2)}, u32[]{:S(2)}) collective-permute-start(bf16[96,896]{1,0:T(8,128)(2,1)S(1)} %get-tuple-element.93), channel_id=1, source_target_pairs={{0,4},{2,6},{4,0},{6,2},{8,12},{10,14},{12,8},{14,10},{1,5},{3,7},... | collective-permute-start | bytes 516104 | tf_op jit(solution)/shard_map/ppermute | solution.py:440

commit v4 on v3

--- a/solution.py
+++ b/solution.py
@@ -86,7 +86,7 @@
     return -(-value // unit) * unit
 
 
-def call(kernel, operands, out_shapes, flops, name, scratch=(), types=None, last=False):
+def call(kernel, operands, out_shapes, flops, name, scratch=(), types=None, last=False, hint=0):
     place = pl.BlockSpec(memory_space=pltpu.VMEM)
     return pl.pallas_call(
         kernel,
@@ -101,7 +101,7 @@
         scratch_shapes=list(scratch),
         name=name,
         compiler_params=pltpu.CompilerParams(vmem_limit_bytes=VMEM_LIMIT),
-        cost_estimate=pl.CostEstimate(flops=0, bytes_accessed=0, transcendentals=0),
+        cost_estimate=pl.CostEstimate(flops=hint, bytes_accessed=0, transcendentals=0),
     )(*[pltpu.with_memory_space_constraint(operand, pltpu.VMEM) for operand in operands])
 
 
@@ -142,10 +142,6 @@
         preferred_element_type=jnp.float32,
     )
     return picked[:capacity].astype(jnp.bfloat16)
-
-
-def split_of(width):
-    return round_up(3 * width // 4, LANES)
 
 
 def prepare_kernel(
@@ -155,8 +151,6 @@
     ids_ref,
     gates_ref,
     wide_ref,
-    left_ref,
-    right_ref,
     cross_ref,
     away_ref,
     sems,
@@ -192,9 +186,6 @@
     )
     wide_ref[:, half:] = turned.astype(jnp.bfloat16)
     copy.wait()
-    split = left_ref.shape[1]
-    left_ref[...] = wide_ref[:, :split]
-    right_ref[...] = wide_ref[:, split:]
     gate = decode_gate(turned, lax.axis_index("role") ^ 1, expert_count)
     cross_ref[...] = compact(gate, wide_ref[:, :half], cross_ref.shape[0])
     away.wait()
@@ -202,11 +193,8 @@
 
 def prepare(tokens, w_down, expert_ids, gate_weights, expert_count, capacity):
     rows, half = tokens.shape
-    split = split_of(half)
     shapes = [
         (rows, half + LANES),
-        (rows, split),
-        (rows, half + LANES - split),
         (capacity, half),
         (w_down.shape[1], half),
     ]
@@ -247,22 +235,34 @@
     )[0]
 
 
-def joined_cross_kernel(expert_count, left_ref, right_ref, wide_ref, cross_ref):
-    split = left_ref.shape[1]
-    wide_ref[:, :split] = left_ref[...]
-    wide_ref[:, split:] = right_ref[...]
+def is_inner():
+    place = lax.axis_index("role") // 2
+    return (place == 1) | (place == 2)
+
+
+def picked_cross_kernel(expert_count, inner_ref, outer_ref, wide_ref, cross_ref):
+    inner = is_inner()
+
+    @pl.when(inner)
+    def _():
+        wide_ref[...] = inner_ref[...]
+
+    @pl.when(jnp.logical_not(inner))
+    def _():
+        wide_ref[...] = outer_ref[...]
+
     cross_kernel(expert_count, wide_ref, cross_ref)
 
 
-def joined_cross_rows(left, right, expert_count, capacity):
-    rows, width = left.shape[0], left.shape[1] + right.shape[1]
-    half = width - LANES
+def picked_cross_rows(inner, outer, expert_count, capacity, hint=0):
+    rows, width = inner.shape
     return call(
-        functools.partial(joined_cross_kernel, expert_count),
-        (left, right),
-        ((rows, width), (capacity, half)),
-        2 * rows * LANES * half,
-        "joined_cross_rows",
+        functools.partial(picked_cross_kernel, expert_count),
+        (inner, outer),
+        ((rows, width), (capacity, width - LANES)),
+        0,
+        "picked_cross_rows",
+        hint=hint,
     )
 
 
@@ -390,54 +390,51 @@
     )(q_lat, latent_cache.transpose(0, 2, 1), lengths[None, :], placement[None, :])
 
 
-def combine_kernel(expert_count, first, sum_count, wide_ref, own_ref, back_ref, *refs):
+def combine_kernel(expert_count, sum_count, wide_ref, own_ref, back_ref, *refs):
     sums, outs = refs[:sum_count], refs[sum_count:]
     half = own_ref.shape[1]
     other = lax.axis_index("role") ^ 1
     gate = decode_gate(wide_ref[:, half:].astype(jnp.float32), other, expert_count)
     slots = slot_matrix(gate)[:, : back_ref.shape[0]]
-    width = LANES
-    for out_ref in outs:
-        for column in range(0, out_ref.shape[1], width):
-            columns = slice(first + column, first + column + width)
-            spread = jnp.dot(slots, back_ref[:, columns], preferred_element_type=jnp.float32)
-            result = own_ref[:, columns] + gate * spread
-            for ref in sums:
-                result = result + ref[:, column : column + width].astype(jnp.float32)
-            out_ref[:, column : column + width] = result.astype(out_ref.dtype)
-        first += out_ref.shape[1]
-
-
-def combine(wide, own, back, sums, expert_count, first, widths, dtype=jnp.bfloat16):
-    rows = own.shape[0]
+    width = 256
+    for first in range(0, half, width):
+        columns = slice(first, first + width)
+        spread = jnp.dot(slots, back_ref[:, columns], preferred_element_type=jnp.float32)
+        result = own_ref[:, columns] + gate * spread
+        for ref in sums:
+            result = result + ref[:, columns].astype(jnp.float32)
+        for out_ref in outs:
+            out_ref[:, columns] = result.astype(out_ref.dtype)
+
+
+def combine(wide, own, back, sums, expert_count, types, hint=0):
     return call(
-        functools.partial(combine_kernel, expert_count, first, len(sums)),
+        functools.partial(combine_kernel, expert_count, len(sums)),
         (wide, own, back, *sums),
-        tuple((rows, width) for width in widths),
+        (own.shape,) * len(types),
         0,
         "combine",
-        types=(dtype,) * len(widths),
+        types=types,
+        hint=hint,
     )
 
 
 def add_kernel(*refs):
     out_ref = refs[-1]
-    count = len(refs) // 2
-    first = 0
-    for total_ref, part_ref in zip(refs[:count], refs[count:-1]):
-        result = total_ref[...] + part_ref[...].astype(jnp.float32)
-        out_ref[:, first : first + part_ref.shape[1]] = result.astype(jnp.bfloat16)
-        first += part_ref.shape[1]
-
-
-def add_last(totals, parts):
-    shape = (parts[0].shape[0], sum(part.shape[1] for part in parts))
-    return call(add_kernel, (*totals, *parts), (shape,), 0, "add_last", last=True)[0]
-
-
-def swap(array, bits):
+    result = refs[0][...]
+    for ref in refs[1:-1]:
+        result = result + ref[...].astype(jnp.float32)
+    out_ref[...] = result.astype(out_ref.dtype)
+
+
+def add_all(total, parts, last=False):
+    return call(add_kernel, (total, *parts), (total.shape,), 0, "add_all", last=last)[0]
+
+
+def swap(array, bits, places=(0, 1, 2, 3)):
     count = lax.axis_size("role")
-    return lax.ppermute(array, "role", [(device, device ^ bits) for device in range(count)])
+    pairs = [(device, device ^ bits) for device in range(count) if device // 2 in places]
+    return lax.ppermute(array, "role", pairs)
 
 
 def swap_core(array):
@@ -452,113 +449,100 @@
     half = tokens.shape[1]
     capacity = 3 * token_count * route_count // (2 * role_count)
     pair, mirror, row = 2, 6, 1
-
-    wide, own_left, own_right, cross, down_away = prepare(
+    inner, outer = (1, 2), (0, 3)
+    narrow, exact = jnp.bfloat16, jnp.float32
+
+    wide, cross, down_away = prepare(
         tokens, w_down, expert_ids, gate_weights, role_count, capacity
     )
-    mirror_left = swap(own_left, mirror)
-    mirror_right = swap(own_right, mirror)
     wide_pair = swap(wide, pair)
+    mirror_inner = swap(wide, mirror, inner)
+    mirror_outer = swap(wide, mirror, outer)
     cross_in = swap(cross, row)
     w_gate, w_up = w_gate[0], w_up[0]
     down_other = swap_core(down_away)
     attended = attend(after(q_lat, wide), latent_cache, lengths, placement)
     cross_in = after(cross_in, attended)
-    mirror_left = after(mirror_left, cross_in, down_other)
-    far_left = swap(mirror_left, pair)
-    wide_pair = after(wide_pair, mirror_left)
+    wide_pair = after(wide_pair, cross_in, down_other)
     cross_pair = cross_rows(wide_pair, role_count, capacity)
     cross_pair_in = swap(cross_pair, row)
-    mirror_right = after(mirror_right, cross_pair)
-    far_right = swap(mirror_right, pair)
-    wide_mirror, cross_mirror = joined_cross_rows(
-        mirror_left, mirror_right, role_count, capacity
+    far_inner = swap(wide_pair, mirror, inner)
+    mirror_inner = after(mirror_inner, cross_pair)
+    far_outer = swap(mirror_inner, pair, inner)
+    mirror_outer = after(mirror_outer, mirror_inner)
+    mirror_outer = after(mirror_outer, cross_pair_in)
+    wide_mirror, cross_mirror = picked_cross_rows(
+        mirror_inner, mirror_outer, role_count, capacity
     )
     cross_mirror_in = swap(cross_mirror, row)
-    cross_pair_in = after(cross_pair_in, cross_mirror)
-    far_left = after(far_left, cross_pair_in)
-    far_right = after(far_right, far_left)
-    cross_mirror_in = after(cross_mirror_in, far_right)
-    far_right = after(far_right, cross_mirror_in)
-    wide_far, cross_far = joined_cross_rows(far_left, far_right, role_count, capacity)
+    near_first = pack((wide, wide_pair, wide_mirror, cross_in), half)
+    far_first = swap_core(near_first)
+    far_inner = after(far_inner, near_first)
+    far_outer = after(far_outer, far_inner)
+    cross_mirror_in = after(cross_mirror_in, far_outer)
+    far_outer = after(far_outer, cross_mirror_in)
+    wide_far, cross_far = picked_cross_rows(
+        far_inner, far_outer, role_count, capacity, 10**10
+    )
     cross_far_in = swap(cross_far, row)
-    near_first = pack((after(wide, cross_far), wide_pair, wide_mirror, cross_in), half)
-    far_first = swap_core(near_first)
     near_second = pack((wide_far, cross_pair_in, cross_mirror_in), half)
     far_second = swap_core(near_second)
     hidden = hidden_units(near_first, after(far_first, near_second), w_gate, w_up)
     hidden_other = swap_core(hidden)
-    cross_far_in = after(cross_far_in, hidden)
-    hidden_second = hidden_units(near_second, after(far_second, cross_far_in), w_gate, w_up)
+    hidden_second = hidden_units(near_second, after(far_second, hidden), w_gate, w_up)
     hidden_second_other = swap_core(hidden_second)
+    cross_far_in = after(cross_far_in, hidden_second)
     far_third = swap_core(cross_far_in)
-    far_third = after(far_third, hidden_second)
-    hidden_third = hidden_units(cross_far_in, far_third, w_gate, w_up)
-    hidden_third_other = swap_core(hidden_third)
-    (back_far,) = down(
-        (), 1, hidden_third, hidden_third_other, w_down, down_other, capacity, role_count
-    )
+    down_weights = (w_down, down_other)
+    hidden_other = after(hidden_other, cross_far_in)
     own, own_pair, own_mirror, back_own = down(
         (wide, wide_pair, wide_mirror),
         1,
         hidden,
-        after(hidden_other, back_far),
-        w_down,
-        down_other,
+        hidden_other,
+        *down_weights,
         capacity,
         role_count,
     )
+    far_third = after(far_third, own)
+    hidden_third = hidden_units(cross_far_in, far_third, w_gate, w_up)
+    hidden_third_other = swap_core(hidden_third)
+    hidden_second_other = after(hidden_second_other, hidden_third)
     own_far, back_pair, back_mirror = down(
-        (wide_far,),
-        2,
-        hidden_second,
-        after(hidden_second_other, back_far),
-        w_down,
-        down_other,
-        capacity,
-        role_count,
+        (wide_far,), 2, hidden_second, hidden_second_other, *down_weights, capacity, role_count
+    )
+    hidden_third_other = after(hidden_third_other, own_far)
+    (back_far,) = down(
+        (), 1, hidden_third, hidden_third_other, *down_weights, capacity, role_count
     )
     back_far = swap(back_far, row)
     back_mirror = swap(back_mirror, row)
     back_pair = swap(back_pair, row)
     back_own = swap(back_own, row)
 
-    split = half // 2
-    widths = (split, half - split)
-    back_far = after(back_far, own, own_far)
-    sum_far_left, sum_far_right = combine(
-        wide_far, own_far, back_far, (), role_count, 0, widths
-    )
-    from_far_left = swap(sum_far_left, pair)
-    from_far_right = swap(sum_far_right, pair)
-    back_mirror = after(back_mirror, sum_far_left)
-    from_far_left = after(from_far_left, back_mirror)
-    (sum_mirror_left,) = combine(
-        wide_mirror, own_mirror, back_mirror, (from_far_left,), role_count, 0, widths[:1]
-    )
-    from_mirror_left = swap(sum_mirror_left, mirror)
-    from_far_right = after(from_far_right, sum_mirror_left)
-    (sum_mirror_right,) = combine(
-        wide_mirror, own_mirror, back_mirror, (from_far_right,), role_count, split, widths[1:]
-    )
-    from_mirror_right = swap(sum_mirror_right, mirror)
-    back_pair = after(back_pair, sum_mirror_right)
-    sum_pair_left, sum_pair_right = combine(
-        wide_pair, own_pair, back_pair, (), role_count, 0, widths
-    )
-    from_pair_left = swap(sum_pair_left, pair)
-    from_pair_right = swap(sum_pair_right, pair)
-    back_own = after(back_own, sum_pair_left)
-    from_mirror_left = after(from_mirror_left, back_own)
-    (sum_left,) = combine(
-        wide, own, back_own, (from_mirror_left,), role_count, 0, widths[:1], jnp.float32
-    )
-    from_mirror_right = after(from_mirror_right, sum_left)
-    (sum_right,) = combine(
-        wide, own, back_own, (from_mirror_right,), role_count, split, widths[1:], jnp.float32
-    )
-    from_pair_left = after(from_pair_left, sum_right)
-    moe_result = add_last((sum_left, sum_right), (from_pair_left, from_pair_right))
+    (sum_far,) = combine(wide_far, own_far, back_far, (), role_count, (narrow,))
+    from_far_outer = swap(sum_far, pair, outer)
+    from_far_inner = swap(sum_far, mirror, inner)
+    back_mirror = after(back_mirror, sum_far)
+    sum_mirror, sum_mirror_sent = combine(
+        wide_mirror, own_mirror, back_mirror, (), role_count, (exact, narrow), 10**10
+    )
+    from_mirror_outer = swap(sum_mirror_sent, mirror, outer)
+    from_far_outer = after(from_far_outer, sum_mirror)
+    sum_mirror_far = add_all(sum_mirror, (from_far_outer,))
+    from_mirror_inner = swap(sum_mirror_far, mirror, inner)
+    back_pair = after(back_pair, sum_mirror_far)
+    from_far_inner = after(from_far_inner, back_pair)
+    (sum_pair,) = combine(
+        wide_pair, own_pair, back_pair, (from_far_inner,), role_count, (narrow,)
+    )
+    from_pair = swap(sum_pair, pair)
+    back_own = after(back_own, sum_pair)
+    (sum_own,) = combine(wide, own, back_own, (), role_count, (exact,))
+    from_mirror_outer = after(from_mirror_outer, sum_own)
+    moe_result = add_all(
+        sum_own, (from_mirror_outer, from_mirror_inner, from_pair), last=True
+    )
     return (attended, moe_result)
 
 

time: 89.4 us -> 91.9 us (1.028)
  starting transfers between devices: 28 us -> 34 us
  waiting for transfers between devices: 39.1 us -> 35.3 us
    ppermute x19 -> x18, starting transfers between devices: 25.7 us -> 32.7 us  [swap(): return lax.ppermute(array, 'role', pairs)]
    ppermute x19 -> x18, waiting for transfers between devices: 37.3 us -> 35.2 us  [swap(): return lax.ppermute(array, 'role', pairs)]
    ppermute x7, waiting for transfers between devices: 1.81 us -> 0.12 us  [swap_core(): return lax.ppermute(array, 'tp', [(0, 1), (1, 0)])]
    ppermute x7, starting transfers between devices: 2.27 us -> 1.31 us  [swap_core(): return lax.ppermute(array, 'tp', [(0, 1), (1, 0)])]
    pallas_call x18 -> x17, Pallas kernels: 14.8 us -> 14.3 us  [call(): pl.pallas_call(kernel, in_specs=[place] * len(operands), out_specs=[place...]
  transfers between devices with their start and end apart: 26 -> 25, of which waited for: 16 -> 9; matrix products, arithmetic and copies ran while one was open for 0% -> 0% of each run, Pallas kernels for 17% -> 16%
where the time goes in v4:
time: 91.9 us; the launch traced here: 91.6 us
  waiting for transfers between devices  35.3 us (38%)
  starting transfers between devices  34 us (37%)
  Pallas kernels  18 us (20%)
  local copies, waits for them, and re-layouts  3.25 us (4%)
  between operations  1 us (1%)
    ppermute x18, waiting for transfers between devices, swap(): return lax.ppermute(array, 'role', pairs)  35.2 us
    ppermute x18, starting transfers between devices, swap(): return lax.ppermute(array, 'role', pairs)  32.7 us
    pallas_call x17, Pallas kernels, call(): pl.pallas_call(kernel, in_specs=[place] * len(operands), out_specs=[place...  14.3 us
    unnamed x18, local copies, waits for them, and re-layouts  3.25 us
    pallas_call x1, Pallas kernels, attend(): pl.pallas_call(attend_kernel, out_shape=jax.ShapeDtypeStruct((slot_count,...  2.05 us
  transfers between devices with their start and end apart: 25, of which 9 were waited for; matrix products, arithmetic and copies ran while one was open for 0% of the time, Pallas kernels for 16%

profile of v4, /device:TPU:0, one launch (start us, length us, event | category | flops | bytes accessed | tf_op | source)
XLA Modules:
  0.0 91.6 jit_solution(14230954393596521331)
XLA Ops:
  0.6 0.7 copy-done.5
  1.3 0.7 copy-done.6
  2.0 1.7 %prepare.1 = (bf16[96,1920]{1,0:T(8,128)(2,1)S(1)}, bf16[72,1792]{1,0:T(8,128)(2,1)S(1)}, bf16[512,1792]{1,0:T(8,128)(2,1)S(1)}) custom-call(bf16[96,1792]{1,0:T(8,128)(2,1)} %tokens_hbm.1, bf16[1,512,3584]{2,1,0:T(8,128)(2,1)} %refs_2_.1, s32[4,96]{1,0:T(4,128)S(1)} %bitcast.14, f32[4,96]{1,0:T(4,128)S(1)} %bitcast.15), custom_call_target="tpu_custom_call" | custom-call | tf_op jit(solution)/shard_map/prepare/pallas_call | solution.py:202
  3.7 0.5 collective-permute-start.2
  4.3 2.6 %collective-permute-start = (bf16[96,1920]{1,0:T(8,128)(2,1)S(1)}, bf16[96,1920]{1,0:T(8,128)(2,1)S(1)}, u32[]{:S(2)}, u32[]{:S(2)}) collective-permute-start(bf16[96,1920]{1,0:T(8,128)(2,1)S(1)} %get-tuple-element.41.refs_0_.wide_ref), channel_id=1, source_target_pairs={{0,4},{2,6},{4,0},{6,2},{8,12},{10,14},{12,8},{14,10},{1,5},{3,7},... | collective-permute-start | bytes 1105928 | tf_op jit(solution)/shard_map/ppermute | solution.py:437
  6.9 1.5 %collective-permute-start.1 = (bf16[72,1792]{1,0:T(8,128)(2,1)S(1)}, bf16[72,1792]{1,0:T(8,128)(2,1)S(1)}, u32[]{:S(2)}, u32[]{:S(2)}) collective-permute-start(bf16[72,1792]{1,0:T(8,128)(2,1)S(1)} %get-tuple-element.43), channel_id=1, source_target_pairs={{0,2},{2,0},{4,6},{6,4},{8,10},{10,8},{12,14},{14,12},{1,3},{3,1},... | collective-permute-start | bytes 774152 | tf_op jit(solution)/shard_map/ppermute | solution.py:437
  8.4 0.7 collective-permute-start.3
  9.1 4.4 %collective-permute-start.4 = (bf16[96,1920]{1,0:T(8,128)(2,1)S(1)}, bf16[96,1920]{1,0:T(8,128)(2,1)S(1)}, u32[]{:S(2)}, u32[]{:S(2)}) collective-permute-start(bf16[96,1920]{1,0:T(8,128)(2,1)S(1)} %get-tuple-element.41.refs_0_.wide_ref), channel_id=1, source_target_pairs={{0,12},{2,14},{12,0},{14,2},{1,13},{3,15},{13,1},{15,3},{16,28},{1... | collective-permute-start | bytes 1105928 | tf_op jit(solution)/shard_map/ppermute | solution.py:437
  13.5 2.0 %attend.1 = bf16[4,32,512]{2,1,0:T(8,128)(2,1)} custom-call(bf16[4,32,576]{2,1,0:T(8,128)(2,1)S(1)} %copy-done.4, bf16[4,576,256]{2,1,0:T(8,128)(2,1)S(1)} %bitcast.13, s32[1,32]{1,0:T(1,128)S(1)} %bitcast.16, s32[1,32]{1,0:T(1,128)S(1)} %bitcast.17), custom_call_target="tpu_custom_call" | custom-call | tf_op jit(solution)/shard_map/attend/pallas_call | solution.py:384
  15.6 0.5 collective-permute-done.wide_ref.refs_1_
  16.1 0.5 cross_rows.1
  16.6 1.8 %collective-permute-start.5 = (bf16[72,1792]{1,0:T(8,128)(2,1)S(1)}, bf16[72,1792]{1,0:T(8,128)(2,1)S(1)}, u32[]{:S(2)}, u32[]{:S(2)}) collective-permute-start(bf16[72,1792]{1,0:T(8,128)(2,1)S(1)} %cross_rows.1), channel_id=1, source_target_pairs={{0,2},{2,0},{4,6},{6,4},{8,10},{10,8},{12,14},{14,12},{1,3},{3,1},... | collective-permute-start | bytes 774152 | tf_op jit(solution)/shard_map/ppermute | solution.py:437
  18.4 0.7 collective-permute-start.7
  19.1 1.3 %collective-permute-start.8 = (bf16[96,1920]{1,0:T(8,128)(2,1)S(1)}, bf16[96,1920]{1,0:T(8,128)(2,1)S(1)}, u32[]{:S(2)}, u32[]{:S(2)}) collective-permute-start(bf16[96,1920]{1,0:T(8,128)(2,1)S(1)} %collective-permute-done.3.inner_ref), channel_id=1, source_target_pairs={{4,0},{6,2},{8,12},{10,14},{5,1},{7,3},{9,13},{11,15},{20,16},{22,... | collective-permute-start | bytes 1105928 | tf_op jit(solution)/shard_map/ppermute | solution.py:437
  20.4 5.9 %collective-permute-done.4.outer_ref = bf16[96,1920]{1,0:T(8,128)(2,1)S(1)} collective-permute-done((bf16[96,1920]{1,0:T(8,128)(2,1)S(1)}, bf16[96,1920]{1,0:T(8,128)(2,1)S(1)}, u32[]{:S(2)}, u32[]{:S(2)}) %collective-permute-start.4) | collective-permute-done | bytes 368672 | tf_op jit(solution)/shard_map/ppermute | solution.py:437
  26.3 0.0 collective-permute-done.5.refs_1_
  26.3 0.5 picked_cross_rows.2
  26.9 1.6 %collective-permute-start.9 = (bf16[72,1792]{1,0:T(8,128)(2,1)S(1)}, bf16[72,1792]{1,0:T(8,128)(2,1)S(1)}, u32[]{:S(2)}, u32[]{:S(2)}) collective-permute-start(bf16[72,1792]{1,0:T(8,128)(2,1)S(1)} %get-tuple-element.53), channel_id=1, source_target_pairs={{0,2},{2,0},{4,6},{6,4},{8,10},{10,8},{12,14},{14,12},{1,3},{3,1},... | collective-permute-start | bytes 774152 | tf_op jit(solution)/shard_map/ppermute | solution.py:437
  28.4 0.1 pack_rows.2.near_ref
  28.5 0.1 collective-permute-start.6
  28.6 0.0 collective-permute-done.7.inner_ref
  28.6 10.7 %collective-permute-done.8.outer_ref = bf16[96,1920]{1,0:T(8,128)(2,1)S(1)} collective-permute-done((bf16[96,1920]{1,0:T(8,128)(2,1)S(1)}, bf16[96,1920]{1,0:T(8,128)(2,1)S(1)}, u32[]{:S(2)}, u32[]{:S(2)}) %collective-permute-start.8) | collective-permute-done | bytes 368672 | tf_op jit(solution)/shard_map/ppermute | solution.py:437
  39.4 0.0 collective-permute-done.9.refs_2_
  39.4 0.6 picked_cross_rows.3
  39.9 0.1 pack_rows.3.near_ref
  40.0 0.1 collective-permute-start.12
  40.1 0.6 collective-permute-start.11
  40.7 0.8 copy-done.1
  41.4 1.1 %copy-done.2 = bf16[1,3584,512]{2,1,0:T(8,128)(2,1)S(1)} copy-done((bf16[1,3584,512]{2,1,0:T(8,128)(2,1)S(1)}, bf16[1,3584,512]{2,1,0:T(8,128)(2,1)}, u32[]{:S(2)}) %copy-start.2) | copy-done | bytes 3670040
  42.5 2.9 %hidden_units.3.refs_3_ = bf16[368,512]{1,0:T(8,128)(2,1)S(1)} custom-call(bf16[368,1792]{1,0:T(8,128)(2,1)S(1)} %pack_rows.2.near_ref, bf16[368,1792]{1,0:T(8,128)(2,1)S(1)} %collective-permute-done.6.far_ref, bf16[3584,512]{1,0:T(8,128)(2,1)S(1)} %bitcast.7, bf16[3584,512]{1,0:T(8,128)(2,1)S(1)} %bitcast.10), custom_call_target="tpu_custom_call" | custom-call | tf_op jit(solution)/shard_map/hidden_units/pallas_call | solution.py:91
  45.4 0.1 collective-permute-start.10
  45.5 0.0 copy-start
  45.5 2.1 %hidden_units.4.refs_1_ = bf16[256,512]{1,0:T(8,128)(2,1)S(1)} custom-call(bf16[256,1792]{1,0:T(8,128)(2,1)S(1)} %pack_rows.3.near_ref, bf16[256,1792]{1,0:T(8,128)(2,1)S(1)} %collective-permute-done.12.far_ref, bf16[3584,512]{1,0:T(8,128)(2,1)S(1)} %bitcast.8, bf16[3584,512]{1,0:T(8,128)(2,1)S(1)} %bitcast.11), custom_call_target="tpu_custom_call" | custom-call | tf_op jit(solution)/shard_map/hidden_units/pallas_call | solution.py:91
  47.6 1.1 %collective-permute-done.11.near_ref = bf16[72,1792]{1,0:T(8,128)(2,1)S(1)} collective-permute-done((bf16[72,1792]{1,0:T(8,128)(2,1)S(1)}, bf16[72,1792]{1,0:T(8,128)(2,1)S(1)}, u32[]{:S(2)}, u32[]{:S(2)}) %collective-permute-start.11) | collective-permute-done | bytes 258080 | tf_op jit(solution)/shard_map/ppermute | solution.py:437
  48.7 0.0 collective-permute-start.15
  48.7 0.5 collective-permute-start.14
  49.2 1.5 %down.3 = (f32[96,1792]{1,0:T(8,128)S(1)}, f32[96,1792]{1,0:T(8,128)S(1)}, f32[96,1792]{1,0:T(8,128)S(1)}, bf16[72,1792]{1,0:T(8,128)(2,1)S(1)}) custom-call(bf16[96,1920]{1,0:T(8,128)(2,1)S(1)} %get-tuple-element.41.refs_0_.wide_ref, bf16[96,1920]{1,0:T(8,128)(2,1)S(1)} %collective-permute-done.wide_ref.refs_1_, ...), custom_call_target="tpu_custom_call" | custom-call | tf_op jit(solution)/shard_map/down/pallas_call | solution.py:91
  50.8 1.4 %hidden_units.5.refs_0_ = bf16[72,512]{1,0:T(8,128)(2,1)S(1)} custom-call(bf16[72,1792]{1,0:T(8,128)(2,1)S(1)} %collective-permute-done.11.near_ref, bf16[72,1792]{1,0:T(8,128)(2,1)S(1)} %collective-permute-done.15.far_ref, bf16[3584,512]{1,0:T(8,128)(2,1)S(1)} %bitcast.9, bf16[3584,512]{1,0:T(8,128)(2,1)S(1)} %bitcast.12), custom_call_target="tpu_custom_call" | custom-call | tf_op jit(solution)/shard_map/hidden_units/pallas_call | solution.py:91
  52.2 0.1 collective-permute-start.18
  52.3 0.0 collective-permute-done.14.refs_2_
  52.3 1.1 %down.4 = (f32[96,1792]{1,0:T(8,128)S(1)}, bf16[72,1792]{1,0:T(8,128)(2,1)S(1)}, bf16[72,1792]{1,0:T(8,128)(2,1)S(1)}) custom-call(bf16[96,1920]{1,0:T(8,128)(2,1)S(1)} %get-tuple-element.56.refs_0_.wide_ref, bf16[256,512]{1,0:T(8,128)(2,1)S(1)} %hidden_units.4.refs_1_, bf16[256,512]{1,0:T(8,128)(2,1)S(1)} %collective-permute-done.14.refs_2_, ...), custom_call_target="tpu_custom_call" | custom-call | tf_op jit(solution)/shard_map/down/pallas_call | solution.py:91
  53.4 0.1 collective-permute-done.18.refs_1_
  53.5 0.7 down.5
  54.2 0.6 collective-permute-start.19
  54.8 1.5 %collective-permute-start.17 = (bf16[72,1792]{1,0:T(8,128)(2,1)S(1)}, bf16[72,1792]{1,0:T(8,128)(2,1)S(1)}, u32[]{:S(2)}, u32[]{:S(2)}) collective-permute-start(bf16[72,1792]{1,0:T(8,128)(2,1)S(1)} %get-tuple-element.69), channel_id=1, source_target_pairs={{0,2},{2,0},{4,6},{6,4},{8,10},{10,8},{12,14},{14,12},{1,3},{3,1},... | collective-permute-start | bytes 774152 | tf_op jit(solution)/shard_map/ppermute | solution.py:437
  56.4 0.5 collective-permute-start.16
  56.9 6.5 %collective-permute-done.19.back_ref = bf16[72,1792]{1,0:T(8,128)(2,1)S(1)} collective-permute-done((bf16[72,1792]{1,0:T(8,128)(2,1)S(1)}, bf16[72,1792]{1,0:T(8,128)(2,1)S(1)}, u32[]{:S(2)}, u32[]{:S(2)}) %collective-permute-start.19) | collective-permute-done | bytes 258080 | tf_op jit(solution)/shard_map/ppermute | solution.py:437
  63.4 0.5 combine.4
  63.8 2.0 %collective-permute-start.20 = (bf16[96,1792]{1,0:T(8,128)(2,1)S(1)}, bf16[96,1792]{1,0:T(8,128)(2,1)S(1)}, u32[]{:S(2)}, u32[]{:S(2)}) collective-permute-start(bf16[96,1792]{1,0:T(8,128)(2,1)S(1)} %combine.4), channel_id=1, source_target_pairs={{0,4},{2,6},{12,8},{14,10},{1,5},{3,7},{13,9},{15,11},{16,20},{18,... | collective-permute-start | bytes 1032200 | tf_op jit(solution)/shard_map/ppermute | solution.py:437
  65.8 0.7 collective-permute-start.21
  66.5 2.4 %collective-permute-done.17.back_ref = bf16[72,1792]{1,0:T(8,128)(2,1)S(1)} collective-permute-done((bf16[72,1792]{1,0:T(8,128)(2,1)S(1)}, bf16[72,1792]{1,0:T(8,128)(2,1)S(1)}, u32[]{:S(2)}, u32[]{:S(2)}) %collective-permute-start.17) | collective-permute-done | bytes 258080 | tf_op jit(solution)/shard_map/ppermute | solution.py:437
  68.9 0.4 combine.5
  69.3 5.5 %collective-permute-start.22 = (bf16[96,1792]{1,0:T(8,128)(2,1)S(1)}, bf16[96,1792]{1,0:T(8,128)(2,1)S(1)}, u32[]{:S(2)}, u32[]{:S(2)}) collective-permute-start(bf16[96,1792]{1,0:T(8,128)(2,1)S(1)} %get-tuple-element.78), channel_id=1, source_target_pairs={{0,12},{2,14},{12,0},{14,2},{1,13},{3,15},{13,1},{15,3},{16,28},{1... | collective-permute-start | bytes 1032200 | tf_op jit(solution)/shard_map/ppermute | solution.py:437
  74.8 0.0 collective-permute-done.20.refs_1_
  74.8 0.1 add_all.2
  74.9 0.7 collective-permute-start.23
  75.6 0.0 collective-permute-done.16.back_ref
  75.6 0.5 combine.6
  76.1 4.6 %collective-permute-start.24 = (bf16[96,1792]{1,0:T(8,128)(2,1)S(1)}, bf16[96,1792]{1,0:T(8,128)(2,1)S(1)}, u32[]{:S(2)}, u32[]{:S(2)}) collective-permute-start(bf16[96,1792]{1,0:T(8,128)(2,1)S(1)} %combine.6), channel_id=1, source_target_pairs={{0,4},{2,6},{4,0},{6,2},{8,12},{10,14},{12,8},{14,10},{1,5},{3,7},... | collective-permute-start | bytes 1032200 | tf_op jit(solution)/shard_map/ppermute | solution.py:437
  80.7 1.5 %collective-permute-start.13 = (bf16[72,1792]{1,0:T(8,128)(2,1)S(1)}, bf16[72,1792]{1,0:T(8,128)(2,1)S(1)}, u32[]{:S(2)}, u32[]{:S(2)}) collective-permute-start(bf16[72,1792]{1,0:T(8,128)(2,1)S(1)} %get-tuple-element.63), channel_id=1, source_target_pairs={{0,2},{2,0},{4,6},{6,4},{8,10},{10,8},{12,14},{14,12},{1,3},{3,1},... | collective-permute-start | bytes 774152 | tf_op jit(solution)/shard_map/ppermute | solution.py:437
  82.2 4.8 %collective-permute-done.13.back_ref = bf16[72,1792]{1,0:T(8,128)(2,1)S(1)} collective-permute-done((bf16[72,1792]{1,0:T(8,128)(2,1)S(1)}, bf16[72,1792]{1,0:T(8,128)(2,1)S(1)}, u32[]{:S(2)}, u32[]{:S(2)}) %collective-permute-start.13) | collective-permute-done | bytes 258080 | tf_op jit(solution)/shard_map/ppermute | solution.py:437
  87.0 0.5 combine.7.refs_0_
  87.5 3.2 %collective-permute-done.24.refs_3_ = bf16[96,1792]{1,0:T(8,128)(2,1)S(1)} collective-permute-done((bf16[96,1792]{1,0:T(8,128)(2,1)S(1)}, bf16[96,1792]{1,0:T(8,128)(2,1)S(1)}, u32[]{:S(2)}, u32[]{:S(2)}) %collective-permute-start.24) | collective-permute-done | bytes 344096 | tf_op jit(solution)/shard_map/ppermute | solution.py:437
  90.7 0.9 add_all.3
  (23 shorter events, 0.0 us)
Async XLA Ops:
  0.6 0.7 copy-start.5
  1.3 0.7 copy-start.6
  2.0 11.5 %copy-start.3 = (bf16[4,256,576]{1,2,0:T(8,128)(2,1)S(1)}, bf16[4,256,576]{1,2,0:T(8,128)(2,1)}, u32[]{:S(2)}) copy-start(bf16[4,256,576]{1,2,0:T(8,128)(2,1)} %param.11) | copy-start | bytes 3538948
  2.0 11.5 %copy-start.4 = (bf16[4,32,576]{2,1,0:T(8,128)(2,1)S(1)}, bf16[4,32,576]{2,1,0:T(8,128)(2,1)}, u32[]{:S(2)}) copy-start(bf16[4,32,576]{2,1,0:T(8,128)(2,1)} %query_ref) | copy-start | bytes 442372
  2.0 11.5 %copy-start.7 = (s32[32]{0:T(128)S(1)}, s32[32]{0:T(128)}, u32[]{:S(2)}) copy-start(s32[32]{0:T(128)} %param.12) | copy-start | bytes 388
  2.0 11.5 %copy-start.8 = (s32[32]{0:T(128)S(1)}, s32[32]{0:T(128)}, u32[]{:S(2)}) copy-start(s32[32]{0:T(128)} %param.13) | copy-start | bytes 388
  3.7 12.4 %collective-permute-start.2 = (bf16[512,1792]{1,0:T(8,128)(2,1)S(1)}, bf16[512,1792]{1,0:T(8,128)(2,1)S(1)}, u32[]{:S(2)}, u32[]{:S(2)}) collective-permute-start(bf16[512,1792]{1,0:T(8,128)(2,1)S(1)} %get-tuple-element.45), channel_id=1, source_target_pairs={{0,1},{1,0},{2,3},{3,2},{4,5},{5,4},{6,7},{7,6},{8,9},{9,8},{10,11... | collective-permute-start | bytes 5505032 | tf_op jit(solution)/shard_map/ppermute | solution.py:441
  4.3 11.8 %collective-permute-start = (bf16[96,1920]{1,0:T(8,128)(2,1)S(1)}, bf16[96,1920]{1,0:T(8,128)(2,1)S(1)}, u32[]{:S(2)}, u32[]{:S(2)}) collective-permute-start(bf16[96,1920]{1,0:T(8,128)(2,1)S(1)} %get-tuple-element.41.refs_0_.wide_ref), channel_id=1, source_target_pairs={{0,4},{2,6},{4,0},{6,2},{8,12},{10,14},{12,8},{14,10},{1,5},{3,7},... | collective-permute-start | bytes 1105928 | tf_op jit(solution)/shard_map/ppermute | solution.py:437
  6.9 8.7 %collective-permute-start.1 = (bf16[72,1792]{1,0:T(8,128)(2,1)S(1)}, bf16[72,1792]{1,0:T(8,128)(2,1)S(1)}, u32[]{:S(2)}, u32[]{:S(2)}) collective-permute-start(bf16[72,1792]{1,0:T(8,128)(2,1)S(1)} %get-tuple-element.43), channel_id=1, source_target_pairs={{0,2},{2,0},{4,6},{6,4},{8,10},{10,8},{12,14},{14,12},{1,3},{3,1},... | collective-permute-start | bytes 774152 | tf_op jit(solution)/shard_map/ppermute | solution.py:437
  8.4 10.6 %collective-permute-start.3 = (bf16[96,1920]{1,0:T(8,128)(2,1)S(1)}, bf16[96,1920]{1,0:T(8,128)(2,1)S(1)}, u32[]{:S(2)}, u32[]{:S(2)}) collective-permute-start(bf16[96,1920]{1,0:T(8,128)(2,1)S(1)} %get-tuple-element.41.refs_0_.wide_ref), channel_id=1, source_target_pairs={{4,8},{6,10},{8,4},{10,6},{5,9},{7,11},{9,5},{11,7},{20,24},{22,26... | collective-permute-start | bytes 1105928 | tf_op jit(solution)/shard_map/ppermute | solution.py:437
  9.1 17.2 %collective-permute-start.4 = (bf16[96,1920]{1,0:T(8,128)(2,1)S(1)}, bf16[96,1920]{1,0:T(8,128)(2,1)S(1)}, u32[]{:S(2)}, u32[]{:S(2)}) collective-permute-start(bf16[96,1920]{1,0:T(8,128)(2,1)S(1)} %get-tuple-element.41.refs_0_.wide_ref), channel_id=1, source_target_pairs={{0,12},{2,14},{12,0},{14,2},{1,13},{3,15},{13,1},{15,3},{16,28},{1... | collective-permute-start | bytes 1105928 | tf_op jit(solution)/shard_map/ppermute | solution.py:437
  16.6 9.7 %collective-permute-start.5 = (bf16[72,1792]{1,0:T(8,128)(2,1)S(1)}, bf16[72,1792]{1,0:T(8,128)(2,1)S(1)}, u32[]{:S(2)}, u32[]{:S(2)}) collective-permute-start(bf16[72,1792]{1,0:T(8,128)(2,1)S(1)} %cross_rows.1), channel_id=1, source_target_pairs={{0,2},{2,0},{4,6},{6,4},{8,10},{10,8},{12,14},{14,12},{1,3},{3,1},... | collective-permute-start | bytes 774152 | tf_op jit(solution)/shard_map/ppermute | solution.py:437
  18.4 10.2 %collective-permute-start.7 = (bf16[96,1920]{1,0:T(8,128)(2,1)S(1)}, bf16[96,1920]{1,0:T(8,128)(2,1)S(1)}, u32[]{:S(2)}, u32[]{:S(2)}) collective-permute-start(bf16[96,1920]{1,0:T(8,128)(2,1)S(1)} %collective-permute-done.wide_ref.refs_1_), channel_id=1, source_target_pairs={{4,8},{6,10},{8,4},{10,6},{5,9},{7,11},{9,5},{11,7},{20,24},{22,26... | collective-permute-start | bytes 1105928 | tf_op jit(solution)/shard_map/ppermute | solution.py:437
  19.1 20.3 %collective-permute-start.8 = (bf16[96,1920]{1,0:T(8,128)(2,1)S(1)}, bf16[96,1920]{1,0:T(8,128)(2,1)S(1)}, u32[]{:S(2)}, u32[]{:S(2)}) collective-permute-start(bf16[96,1920]{1,0:T(8,128)(2,1)S(1)} %collective-permute-done.3.inner_ref), channel_id=1, source_target_pairs={{4,0},{6,2},{8,12},{10,14},{5,1},{7,3},{9,13},{11,15},{20,16},{22,... | collective-permute-start | bytes 1105928 | tf_op jit(solution)/shard_map/ppermute | solution.py:437
  26.9 12.5 %collective-permute-start.9 = (bf16[72,1792]{1,0:T(8,128)(2,1)S(1)}, bf16[72,1792]{1,0:T(8,128)(2,1)S(1)}, u32[]{:S(2)}, u32[]{:S(2)}) collective-permute-start(bf16[72,1792]{1,0:T(8,128)(2,1)S(1)} %get-tuple-element.53), channel_id=1, source_target_pairs={{0,2},{2,0},{4,6},{6,4},{8,10},{10,8},{12,14},{14,12},{1,3},{3,1},... | collective-permute-start | bytes 774152 | tf_op jit(solution)/shard_map/ppermute | solution.py:437
  28.5 12.1 %collective-permute-start.6 = (bf16[368,1792]{1,0:T(8,128)(2,1)S(1)}, bf16[368,1792]{1,0:T(8,128)(2,1)S(1)}, u32[]{:S(2)}, u32[]{:S(2)}) collective-permute-start(bf16[368,1792]{1,0:T(8,128)(2,1)S(1)} %pack_rows.2.near_ref), channel_id=1, source_target_pairs={{0,1},{1,0},{2,3},{3,2},{4,5},{5,4},{6,7},{7,6},{8,9},{9,8},{10,11... | collective-permute-start | bytes 3956744 | tf_op jit(solution)/shard_map/ppermute | solution.py:441
  39.4 2.0 %copy-start.1 = (bf16[1,3584,512]{2,1,0:T(8,128)(2,1)S(1)}, bf16[1,3584,512]{2,1,0:T(8,128)(2,1)}, u32[]{:S(2)}) copy-start(bf16[1,3584,512]{2,1,0:T(8,128)(2,1)} %param.17) | copy-start | bytes 11010052
  39.4 3.2 %copy-start.2 = (bf16[1,3584,512]{2,1,0:T(8,128)(2,1)S(1)}, bf16[1,3584,512]{2,1,0:T(8,128)(2,1)}, u32[]{:S(2)}) copy-start(bf16[1,3584,512]{2,1,0:T(8,128)(2,1)} %param.18) | copy-start | bytes 11010052
  40.0 5.5 %collective-permute-start.12 = (bf16[256,1792]{1,0:T(8,128)(2,1)S(1)}, bf16[256,1792]{1,0:T(8,128)(2,1)S(1)}, u32[]{:S(2)}, u32[]{:S(2)}) collective-permute-start(bf16[256,1792]{1,0:T(8,128)(2,1)S(1)} %pack_rows.3.near_ref), channel_id=1, source_target_pairs={{0,1},{1,0},{2,3},{3,2},{4,5},{5,4},{6,7},{7,6},{8,9},{9,8},{10,11... | collective-permute-start | bytes 2752520 | tf_op jit(solution)/shard_map/ppermute | solution.py:441
  40.1 8.6 %collective-permute-start.11 = (bf16[72,1792]{1,0:T(8,128)(2,1)S(1)}, bf16[72,1792]{1,0:T(8,128)(2,1)S(1)}, u32[]{:S(2)}, u32[]{:S(2)}) collective-permute-start(bf16[72,1792]{1,0:T(8,128)(2,1)S(1)} %get-tuple-element.58), channel_id=1, source_target_pairs={{0,2},{2,0},{4,6},{6,4},{8,10},{10,8},{12,14},{14,12},{1,3},{3,1},... | collective-permute-start | bytes 774152 | tf_op jit(solution)/shard_map/ppermute | solution.py:437
  45.4 3.8 %collective-permute-start.10 = (bf16[368,512]{1,0:T(8,128)(2,1)S(1)}, bf16[368,512]{1,0:T(8,128)(2,1)S(1)}, u32[]{:S(2)}, u32[]{:S(2)}) collective-permute-start(bf16[368,512]{1,0:T(8,128)(2,1)S(1)} %hidden_units.3.refs_3_), channel_id=1, source_target_pairs={{0,1},{1,0},{2,3},{3,2},{4,5},{5,4},{6,7},{7,6},{8,9},{9,8},{10,11... | collective-permute-start | bytes 1130504 | tf_op jit(solution)/shard_map/ppermute | solution.py:441
  45.5 3.7 %copy-start = (bf16[1,512,3584]{2,1,0:T(8,128)(2,1)S(1)}, bf16[1,512,3584]{2,1,0:T(8,128)(2,1)}, u32[]{:S(2)}) copy-start(bf16[1,512,3584]{2,1,0:T(8,128)(2,1)} %refs_2_.1) | copy-start | bytes 11010052
  48.7 2.1 %collective-permute-start.15 = (bf16[72,1792]{1,0:T(8,128)(2,1)S(1)}, bf16[72,1792]{1,0:T(8,128)(2,1)S(1)}, u32[]{:S(2)}, u32[]{:S(2)}) collective-permute-start(bf16[72,1792]{1,0:T(8,128)(2,1)S(1)} %collective-permute-done.11.near_ref), channel_id=1, source_target_pairs={{0,1},{1,0},{2,3},{3,2},{4,5},{5,4},{6,7},{7,6},{8,9},{9,8},{10,11... | collective-permute-start | bytes 774152 | tf_op jit(solution)/shard_map/ppermute | solution.py:441
  48.7 3.6 %collective-permute-start.14 = (bf16[256,512]{1,0:T(8,128)(2,1)S(1)}, bf16[256,512]{1,0:T(8,128)(2,1)S(1)}, u32[]{:S(2)}, u32[]{:S(2)}) collective-permute-start(bf16[256,512]{1,0:T(8,128)(2,1)S(1)} %hidden_units.4.refs_1_), channel_id=1, source_target_pairs={{0,1},{1,0},{2,3},{3,2},{4,5},{5,4},{6,7},{7,6},{8,9},{9,8},{10,11... | collective-permute-start | bytes 786440 | tf_op jit(solution)/shard_map/ppermute | solution.py:441
  52.2 1.3 %collective-permute-start.18 = (bf16[72,512]{1,0:T(8,128)(2,1)S(1)}, bf16[72,512]{1,0:T(8,128)(2,1)S(1)}, u32[]{:S(2)}, u32[]{:S(2)}) collective-permute-start(bf16[72,512]{1,0:T(8,128)(2,1)S(1)} %hidden_units.5.refs_0_), channel_id=1, source_target_pairs={{0,1},{1,0},{2,3},{3,2},{4,5},{5,4},{6,7},{7,6},{8,9},{9,8},{10,11... | collective-permute-start | bytes 221192 | tf_op jit(solution)/shard_map/ppermute | solution.py:441
  54.2 9.1 %collective-permute-start.19 = (bf16[72,1792]{1,0:T(8,128)(2,1)S(1)}, bf16[72,1792]{1,0:T(8,128)(2,1)S(1)}, u32[]{:S(2)}, u32[]{:S(2)}) collective-permute-start(bf16[72,1792]{1,0:T(8,128)(2,1)S(1)} %down.5), channel_id=1, source_target_pairs={{0,2},{2,0},{4,6},{6,4},{8,10},{10,8},{12,14},{14,12},{1,3},{3,1},... | collective-permute-start | bytes 774152 | tf_op jit(solution)/shard_map/ppermute | solution.py:437
  54.8 14.1 %collective-permute-start.17 = (bf16[72,1792]{1,0:T(8,128)(2,1)S(1)}, bf16[72,1792]{1,0:T(8,128)(2,1)S(1)}, u32[]{:S(2)}, u32[]{:S(2)}) collective-permute-start(bf16[72,1792]{1,0:T(8,128)(2,1)S(1)} %get-tuple-element.69), channel_id=1, source_target_pairs={{0,2},{2,0},{4,6},{6,4},{8,10},{10,8},{12,14},{14,12},{1,3},{3,1},... | collective-permute-start | bytes 774152 | tf_op jit(solution)/shard_map/ppermute | solution.py:437
  56.4 19.2 %collective-permute-start.16 = (bf16[72,1792]{1,0:T(8,128)(2,1)S(1)}, bf16[72,1792]{1,0:T(8,128)(2,1)S(1)}, u32[]{:S(2)}, u32[]{:S(2)}) collective-permute-start(bf16[72,1792]{1,0:T(8,128)(2,1)S(1)} %get-tuple-element.67), channel_id=1, source_target_pairs={{0,2},{2,0},{4,6},{6,4},{8,10},{10,8},{12,14},{14,12},{1,3},{3,1},... | collective-permute-start | bytes 774152 | tf_op jit(solution)/shard_map/ppermute | solution.py:437
  63.8 11.0 %collective-permute-start.20 = (bf16[96,1792]{1,0:T(8,128)(2,1)S(1)}, bf16[96,1792]{1,0:T(8,128)(2,1)S(1)}, u32[]{:S(2)}, u32[]{:S(2)}) collective-permute-start(bf16[96,1792]{1,0:T(8,128)(2,1)S(1)} %combine.4), channel_id=1, source_target_pairs={{0,4},{2,6},{12,8},{14,10},{1,5},{3,7},{13,9},{15,11},{16,20},{18,... | collective-permute-start | bytes 1032200 | tf_op jit(solution)/shard_map/ppermute | solution.py:437
  65.8 9.8 %collective-permute-start.21 = (bf16[96,1792]{1,0:T(8,128)(2,1)S(1)}, bf16[96,1792]{1,0:T(8,128)(2,1)S(1)}, u32[]{:S(2)}, u32[]{:S(2)}) collective-permute-start(bf16[96,1792]{1,0:T(8,128)(2,1)S(1)} %combine.4), channel_id=1, source_target_pairs={{4,8},{6,10},{8,4},{10,6},{5,9},{7,11},{9,5},{11,7},{20,24},{22,26... | collective-permute-start | bytes 1032200 | tf_op jit(solution)/shard_map/ppermute | solution.py:437
  69.3 18.2 %collective-permute-start.22 = (bf16[96,1792]{1,0:T(8,128)(2,1)S(1)}, bf16[96,1792]{1,0:T(8,128)(2,1)S(1)}, u32[]{:S(2)}, u32[]{:S(2)}) collective-permute-start(bf16[96,1792]{1,0:T(8,128)(2,1)S(1)} %get-tuple-element.78), channel_id=1, source_target_pairs={{0,12},{2,14},{12,0},{14,2},{1,13},{3,15},{13,1},{15,3},{16,28},{1... | collective-permute-start | bytes 1032200 | tf_op jit(solution)/shard_map/ppermute | solution.py:437
  74.9 12.6 %collective-permute-start.23 = (bf16[96,1792]{1,0:T(8,128)(2,1)S(1)}, bf16[96,1792]{1,0:T(8,128)(2,1)S(1)}, u32[]{:S(2)}, u32[]{:S(2)}) collective-permute-start(bf16[96,1792]{1,0:T(8,128)(2,1)S(1)} %add_all.2), channel_id=1, source_target_pairs={{4,8},{6,10},{8,4},{10,6},{5,9},{7,11},{9,5},{11,7},{20,24},{22,26... | collective-permute-start | bytes 1032200 | tf_op jit(solution)/shard_map/ppermute | solution.py:437
  76.1 14.6 %collective-permute-start.24 = (bf16[96,1792]{1,0:T(8,128)(2,1)S(1)}, bf16[96,1792]{1,0:T(8,128)(2,1)S(1)}, u32[]{:S(2)}, u32[]{:S(2)}) collective-permute-start(bf16[96,1792]{1,0:T(8,128)(2,1)S(1)} %combine.6), channel_id=1, source_target_pairs={{0,4},{2,6},{4,0},{6,2},{8,12},{10,14},{12,8},{14,10},{1,5},{3,7},... | collective-permute-start | bytes 1032200 | tf_op jit(solution)/shard_map/ppermute | solution.py:437
  80.7 6.3 %collective-permute-start.13 = (bf16[72,1792]{1,0:T(8,128)(2,1)S(1)}, bf16[72,1792]{1,0:T(8,128)(2,1)S(1)}, u32[]{:S(2)}, u32[]{:S(2)}) collective-permute-start(bf16[72,1792]{1,0:T(8,128)(2,1)S(1)} %get-tuple-element.63), channel_id=1, source_target_pairs={{0,2},{2,0},{4,6},{6,4},{8,10},{10,8},{12,14},{14,12},{1,3},{3,1},... | collective-permute-start | bytes 774152 | tf_op jit(solution)/shard_map/ppermute | solution.py:437

commit v5 on v3

--- a/solution.py
+++ b/solution.py
@@ -86,7 +86,7 @@
     return -(-value // unit) * unit
 
 
-def call(kernel, operands, out_shapes, flops, name, scratch=(), types=None, last=False):
+def call(kernel, operands, out_shapes, flops, name, scratch=(), types=None, last=False, hint=0):
     place = pl.BlockSpec(memory_space=pltpu.VMEM)
     return pl.pallas_call(
         kernel,
@@ -101,7 +101,7 @@
         scratch_shapes=list(scratch),
         name=name,
         compiler_params=pltpu.CompilerParams(vmem_limit_bytes=VMEM_LIMIT),
-        cost_estimate=pl.CostEstimate(flops=0, bytes_accessed=0, transcendentals=0),
+        cost_estimate=pl.CostEstimate(flops=hint, bytes_accessed=0, transcendentals=0),
     )(*[pltpu.with_memory_space_constraint(operand, pltpu.VMEM) for operand in operands])
 
 
@@ -144,29 +144,33 @@
     return picked[:capacity].astype(jnp.bfloat16)
 
 
-def split_of(width):
-    return round_up(3 * width // 4, LANES)
-
-
 def prepare_kernel(
     expert_count,
     tokens_hbm,
     down_hbm,
+    ids_hbm,
+    gates_hbm,
+    wide_ref,
+    cross_ref,
+    away_ref,
     ids_ref,
     gates_ref,
-    wide_ref,
-    left_ref,
-    right_ref,
-    cross_ref,
-    away_ref,
     sems,
 ):
     rows, half = tokens_hbm.shape
     copy = pltpu.make_async_copy(tokens_hbm, wide_ref.at[:, :half], sems.at[0])
+    first = [
+        pltpu.make_async_copy(ids_hbm, ids_ref, sems.at[2]),
+        pltpu.make_async_copy(gates_hbm, gates_ref, sems.at[3]),
+    ]
+    for part in first:
+        part.start()
     copy.start()
     sibling = pl.multiple_of((1 - lax.axis_index("tp")) * half, LANES)
     away = pltpu.make_async_copy(down_hbm.at[0, :, pl.ds(sibling, half)], away_ref, sems.at[1])
     away.start()
+    for part in first:
+        part.wait()
     piece_rows = round_up(3 * expert_count, 16)
     line = lax.broadcasted_iota(jnp.int32, (piece_rows, rows), 0)
     named = line
@@ -192,9 +196,6 @@
     )
     wide_ref[:, half:] = turned.astype(jnp.bfloat16)
     copy.wait()
-    split = left_ref.shape[1]
-    left_ref[...] = wide_ref[:, :split]
-    right_ref[...] = wide_ref[:, split:]
     gate = decode_gate(turned, lax.axis_index("role") ^ 1, expert_count)
     cross_ref[...] = compact(gate, wide_ref[:, :half], cross_ref.shape[0])
     away.wait()
@@ -202,29 +203,30 @@
 
 def prepare(tokens, w_down, expert_ids, gate_weights, expert_count, capacity):
     rows, half = tokens.shape
-    split = split_of(half)
     shapes = [
         (rows, half + LANES),
-        (rows, split),
-        (rows, half + LANES - split),
         (capacity, half),
         (w_down.shape[1], half),
     ]
     whole = pl.BlockSpec(memory_space=pltpu.VMEM)
     return pl.pallas_call(
         functools.partial(prepare_kernel, expert_count),
-        in_specs=[pl.BlockSpec(memory_space=pltpu.HBM)] * 2 + [whole, whole],
+        in_specs=[pl.BlockSpec(memory_space=pltpu.HBM)] * 4,
         out_specs=[whole] * len(shapes),
         out_shape=[pltpu.VMEM(shape, jnp.bfloat16) for shape in shapes],
-        scratch_shapes=[pltpu.SemaphoreType.DMA((2,))],
+        scratch_shapes=[
+            pltpu.VMEM(expert_ids.shape[::-1], jnp.int32),
+            pltpu.VMEM(gate_weights.shape[::-1], jnp.float32),
+            pltpu.SemaphoreType.DMA((4,)),
+        ],
         name="prepare",
         compiler_params=pltpu.CompilerParams(vmem_limit_bytes=VMEM_LIMIT),
         cost_estimate=pl.CostEstimate(flops=0, bytes_accessed=0, transcendentals=0),
     )(
         pltpu.with_memory_space_constraint(tokens, pltpu.HBM),
         pltpu.with_memory_space_constraint(w_down, pltpu.HBM),
-        expert_ids.T,
-        gate_weights.T,
+        pltpu.with_memory_space_constraint(expert_ids.T, pltpu.HBM),
+        pltpu.with_memory_space_constraint(gate_weights.T, pltpu.HBM),
     )
 
 
@@ -235,35 +237,17 @@
     cross_ref[...] = compact(gate, wide_ref[:, :half], cross_ref.shape[0])
 
 
-def cross_rows(wide, expert_count, capacity):
+def cross_rows(wide, expert_count, capacity, hint=0):
     rows, width = wide.shape
     half = width - LANES
     return call(
         functools.partial(cross_kernel, expert_count),
         (wide,),
         ((capacity, half),),
-        2 * rows * LANES * half,
+        0,
         "cross_rows",
+        hint=hint,
     )[0]
-
-
-def joined_cross_kernel(expert_count, left_ref, right_ref, wide_ref, cross_ref):
-    split = left_ref.shape[1]
-    wide_ref[:, :split] = left_ref[...]
-    wide_ref[:, split:] = right_ref[...]
-    cross_kernel(expert_count, wide_ref, cross_ref)
-
-
-def joined_cross_rows(left, right, expert_count, capacity):
-    rows, width = left.shape[0], left.shape[1] + right.shape[1]
-    half = width - LANES
-    return call(
-        functools.partial(joined_cross_kernel, expert_count),
-        (left, right),
-        ((rows, width), (capacity, half)),
-        2 * rows * LANES * half,
-        "joined_cross_rows",
-    )
 
 
 def row_starts(blocks):
@@ -435,9 +419,10 @@
     return call(add_kernel, (*totals, *parts), (shape,), 0, "add_last", last=True)[0]
 
 
-def swap(array, bits):
+def swap(array, bits, places=(0, 1, 2, 3)):
     count = lax.axis_size("role")
-    return lax.ppermute(array, "role", [(device, device ^ bits) for device in range(count)])
+    pairs = [(device, device ^ bits) for device in range(count) if device // 2 in places]
+    return lax.ppermute(array, "role", pairs)
 
 
 def swap_core(array):
@@ -453,70 +438,60 @@
     capacity = 3 * token_count * route_count // (2 * role_count)
     pair, mirror, row = 2, 6, 1
 
-    wide, own_left, own_right, cross, down_away = prepare(
+    wide, cross, down_away = prepare(
         tokens, w_down, expert_ids, gate_weights, role_count, capacity
     )
-    mirror_left = swap(own_left, mirror)
-    mirror_right = swap(own_right, mirror)
+    wide_mirror = swap(wide, mirror)
     wide_pair = swap(wide, pair)
     cross_in = swap(cross, row)
     w_gate, w_up = w_gate[0], w_up[0]
     down_other = swap_core(down_away)
     attended = attend(after(q_lat, wide), latent_cache, lengths, placement)
-    cross_in = after(cross_in, attended)
-    mirror_left = after(mirror_left, cross_in, down_other)
-    far_left = swap(mirror_left, pair)
-    wide_pair = after(wide_pair, mirror_left)
+    wide_pair = after(wide_pair, attended, down_other)
     cross_pair = cross_rows(wide_pair, role_count, capacity)
     cross_pair_in = swap(cross_pair, row)
-    mirror_right = after(mirror_right, cross_pair)
-    far_right = swap(mirror_right, pair)
-    wide_mirror, cross_mirror = joined_cross_rows(
-        mirror_left, mirror_right, role_count, capacity
-    )
+    cross_in = after(cross_in, cross_pair)
+    wide_mirror = after(wide_mirror, cross_in)
+    wide_far = swap(wide_mirror, pair)
+    wide_mirror_ready = after(wide_mirror, cross_pair_in)
+    cross_mirror = cross_rows(wide_mirror_ready, role_count, capacity)
     cross_mirror_in = swap(cross_mirror, row)
-    cross_pair_in = after(cross_pair_in, cross_mirror)
-    far_left = after(far_left, cross_pair_in)
-    far_right = after(far_right, far_left)
-    cross_mirror_in = after(cross_mirror_in, far_right)
-    far_right = after(far_right, cross_mirror_in)
-    wide_far, cross_far = joined_cross_rows(far_left, far_right, role_count, capacity)
+    near_first = pack((wide, wide_pair, after(wide_mirror, cross_mirror), cross_in), half)
+    far_first = swap_core(near_first)
+    wide_far = after(wide_far, near_first)
+    cross_mirror_in = after(cross_mirror_in, wide_far)
+    wide_far = after(wide_far, cross_mirror_in)
+    cross_far = cross_rows(wide_far, role_count, capacity, 10**10)
     cross_far_in = swap(cross_far, row)
-    near_first = pack((after(wide, cross_far), wide_pair, wide_mirror, cross_in), half)
-    far_first = swap_core(near_first)
     near_second = pack((wide_far, cross_pair_in, cross_mirror_in), half)
     far_second = swap_core(near_second)
     hidden = hidden_units(near_first, after(far_first, near_second), w_gate, w_up)
     hidden_other = swap_core(hidden)
-    cross_far_in = after(cross_far_in, hidden)
-    hidden_second = hidden_units(near_second, after(far_second, cross_far_in), w_gate, w_up)
+    hidden_second = hidden_units(near_second, after(far_second, hidden), w_gate, w_up)
     hidden_second_other = swap_core(hidden_second)
+    cross_far_in = after(cross_far_in, hidden_second)
     far_third = swap_core(cross_far_in)
-    far_third = after(far_third, hidden_second)
-    hidden_third = hidden_units(cross_far_in, far_third, w_gate, w_up)
-    hidden_third_other = swap_core(hidden_third)
-    (back_far,) = down(
-        (), 1, hidden_third, hidden_third_other, w_down, down_other, capacity, role_count
-    )
+    down_weights = (w_down, down_other)
+    hidden_other = after(hidden_other, cross_far_in)
     own, own_pair, own_mirror, back_own = down(
         (wide, wide_pair, wide_mirror),
         1,
         hidden,
-        after(hidden_other, back_far),
-        w_down,
-        down_other,
+        hidden_other,
+        *down_weights,
         capacity,
         role_count,
     )
+    far_third = after(far_third, own)
+    hidden_third = hidden_units(cross_far_in, far_third, w_gate, w_up)
+    hidden_third_other = swap_core(hidden_third)
+    hidden_second_other = after(hidden_second_other, hidden_third)
     own_far, back_pair, back_mirror = down(
-        (wide_far,),
-        2,
-        hidden_second,
-        after(hidden_second_other, back_far),
-        w_down,
-        down_other,
-        capacity,
-        role_count,
+        (wide_far,), 2, hidden_second, hidden_second_other, *down_weights, capacity, role_count
+    )
+    hidden_third_other = after(hidden_third_other, own_far)
+    (back_far,) = down(
+        (), 1, hidden_third, hidden_third_other, *down_weights, capacity, role_count
     )
     back_far = swap(back_far, row)
     back_mirror = swap(back_mirror, row)
@@ -525,7 +500,6 @@
 
     split = half // 2
     widths = (split, half - split)
-    back_far = after(back_far, own, own_far)
     sum_far_left, sum_far_right = combine(
         wide_far, own_far, back_far, (), role_count, 0, widths
     )

time: 89.4 us -> 90.5 us (1.012)
  starting transfers between devices: 28 us -> 32.6 us
  waiting for transfers between devices: 39.1 us -> 37.2 us
  local copies, waits for them, and re-layouts: 2.65 us -> 1.05 us
    ppermute x19 -> x17, starting transfers between devices: 25.7 us -> 30.8 us  [swap(): return lax.ppermute(array, 'role', pairs)]
    ppermute x7, waiting for transfers between devices: 1.81 us -> 0.12 us  [swap_core(): return lax.ppermute(array, 'tp', [(0, 1), (1, 0)])]
    unnamed x18 -> x14, local copies, waits for them, and re-layouts: 2.65 us -> 1.05 us
    ppermute x19 -> x17, waiting for transfers between devices: 37.3 us -> 37.1 us  [swap(): return lax.ppermute(array, 'role', pairs)]
  transfers between devices with their start and end apart: 26 -> 24, of which waited for: 16 -> 12; matrix products, arithmetic and copies ran while one was open for 0% -> 0% of each run, Pallas kernels for 17% -> 17%
where the time goes in v5:
time: 90.5 us; the launch traced here: 90.3 us
  waiting for transfers between devices  37.2 us (41%)
  starting transfers between devices  32.6 us (36%)
  Pallas kernels  18.6 us (21%)
  local copies, waits for them, and re-layouts  1.05 us (1%)
    ppermute x17, waiting for transfers between devices, swap(): return lax.ppermute(array, 'role', pairs)  37.1 us
    ppermute x17, starting transfers between devices, swap(): return lax.ppermute(array, 'role', pairs)  30.8 us
    pallas_call x18, Pallas kernels, call(): pl.pallas_call(kernel, in_specs=[place] * len(operands), out_specs=[place...  14.7 us
    pallas_call x1, Pallas kernels, attend(): pl.pallas_call(attend_kernel, out_shape=jax.ShapeDtypeStruct((slot_count,...  2.05 us
  transfers between devices with their start and end apart: 24, of which 12 were waited for; matrix products, arithmetic and copies ran while one was open for 0% of the time, Pallas kernels for 17%

profile of v5, /device:TPU:0, one launch (start us, length us, event | category | flops | bytes accessed | tf_op | source)
XLA Modules:
  0.0 90.3 jit_solution(1693729494722892991)
XLA Ops:
  0.7 1.8 %prepare.1 = (bf16[96,1920]{1,0:T(8,128)(2,1)S(1)}, bf16[72,1792]{1,0:T(8,128)(2,1)S(1)}, bf16[512,1792]{1,0:T(8,128)(2,1)S(1)}) custom-call(bf16[96,1792]{1,0:T(8,128)(2,1)} %tokens_hbm.1, bf16[1,512,3584]{2,1,0:T(8,128)(2,1)} %refs_2_.1, s32[4,96]{1,0:T(4,128)} %bitcast.16, f32[4,96]{1,0:T(4,128)} %bitcast.17), custom_call_target="tpu_custom_call" | custom-call | tf_op jit(solution)/shard_map/prepare/pallas_call | solution.py:212
  2.4 0.5 collective-permute-start.1
  3.0 2.6 %collective-permute-start = (bf16[96,1920]{1,0:T(8,128)(2,1)S(1)}, bf16[96,1920]{1,0:T(8,128)(2,1)S(1)}, u32[]{:S(2)}, u32[]{:S(2)}) collective-permute-start(bf16[96,1920]{1,0:T(8,128)(2,1)S(1)} %get-tuple-element.40.refs_0_.wide_ref), channel_id=1, source_target_pairs={{0,4},{2,6},{4,0},{6,2},{8,12},{10,14},{12,8},{14,10},{1,5},{3,7},... | collective-permute-start | bytes 1105928 | tf_op jit(solution)/shard_map/ppermute | solution.py:425
  5.6 2.5 %collective-permute-start.2 = (bf16[96,1920]{1,0:T(8,128)(2,1)S(1)}, bf16[96,1920]{1,0:T(8,128)(2,1)S(1)}, u32[]{:S(2)}, u32[]{:S(2)}) collective-permute-start(bf16[96,1920]{1,0:T(8,128)(2,1)S(1)} %get-tuple-element.40.refs_0_.wide_ref), channel_id=1, source_target_pairs={{0,12},{2,14},{4,8},{6,10},{8,4},{10,6},{12,0},{14,2},{1,13},{3,15... | collective-permute-start | bytes 1105928 | tf_op jit(solution)/shard_map/ppermute | solution.py:425
  8.1 1.5 %collective-permute-start.3 = (bf16[72,1792]{1,0:T(8,128)(2,1)S(1)}, bf16[72,1792]{1,0:T(8,128)(2,1)S(1)}, u32[]{:S(2)}, u32[]{:S(2)}) collective-permute-start(bf16[72,1792]{1,0:T(8,128)(2,1)S(1)} %get-tuple-element.44), channel_id=1, source_target_pairs={{0,2},{2,0},{4,6},{6,4},{8,10},{10,8},{12,14},{14,12},{1,3},{3,1},... | collective-permute-start | bytes 774152 | tf_op jit(solution)/shard_map/ppermute | solution.py:425
  9.6 2.1 %attend.1 = bf16[4,32,512]{2,1,0:T(8,128)(2,1)} custom-call(bf16[4,32,576]{2,1,0:T(8,128)(2,1)S(1)} %copy-done.4, bf16[4,576,256]{2,1,0:T(8,128)(2,1)S(1)} %bitcast.13, s32[1,32]{1,0:T(1,128)S(1)} %bitcast.14, s32[1,32]{1,0:T(1,128)S(1)} %bitcast.15), custom_call_target="tpu_custom_call" | custom-call | tf_op jit(solution)/shard_map/attend/pallas_call | solution.py:368
  11.7 3.1 %collective-permute-done.wide_ref.refs_1_ = bf16[96,1920]{1,0:T(8,128)(2,1)S(1)} collective-permute-done((bf16[96,1920]{1,0:T(8,128)(2,1)S(1)}, bf16[96,1920]{1,0:T(8,128)(2,1)S(1)}, u32[]{:S(2)}, u32[]{:S(2)}) %collective-permute-start) | collective-permute-done | bytes 368672 | tf_op jit(solution)/shard_map/ppermute | solution.py:425
  14.8 0.5 cross_rows.3
  15.3 1.8 %collective-permute-start.4 = (bf16[72,1792]{1,0:T(8,128)(2,1)S(1)}, bf16[72,1792]{1,0:T(8,128)(2,1)S(1)}, u32[]{:S(2)}, u32[]{:S(2)}) collective-permute-start(bf16[72,1792]{1,0:T(8,128)(2,1)S(1)} %cross_rows.3), channel_id=1, source_target_pairs={{0,2},{2,0},{4,6},{6,4},{8,10},{10,8},{12,14},{14,12},{1,3},{3,1},... | collective-permute-start | bytes 774152 | tf_op jit(solution)/shard_map/ppermute | solution.py:425
  17.1 0.0 collective-permute-done.3.refs_3_
  17.1 7.9 %collective-permute-done.2.wide_ref.refs_2_ = bf16[96,1920]{1,0:T(8,128)(2,1)S(1)} collective-permute-done((bf16[96,1920]{1,0:T(8,128)(2,1)S(1)}, bf16[96,1920]{1,0:T(8,128)(2,1)S(1)}, u32[]{:S(2)}, u32[]{:S(2)}) %collective-permute-start.2) | collective-permute-done | bytes 368672 | tf_op jit(solution)/shard_map/ppermute | solution.py:425
  25.0 0.6 collective-permute-start.6
  25.6 0.5 cross_rows.4
  26.1 1.6 %collective-permute-start.7 = (bf16[72,1792]{1,0:T(8,128)(2,1)S(1)}, bf16[72,1792]{1,0:T(8,128)(2,1)S(1)}, u32[]{:S(2)}, u32[]{:S(2)}) collective-permute-start(bf16[72,1792]{1,0:T(8,128)(2,1)S(1)} %cross_rows.4), channel_id=1, source_target_pairs={{0,2},{2,0},{4,6},{6,4},{8,10},{10,8},{12,14},{14,12},{1,3},{3,1},... | collective-permute-start | bytes 774152 | tf_op jit(solution)/shard_map/ppermute | solution.py:425
  27.7 0.1 pack_rows.2.near_ref
  27.8 0.1 collective-permute-start.5
  27.9 7.2 %collective-permute-done.6.refs_0_.wide_ref = bf16[96,1920]{1,0:T(8,128)(2,1)S(1)} collective-permute-done((bf16[96,1920]{1,0:T(8,128)(2,1)S(1)}, bf16[96,1920]{1,0:T(8,128)(2,1)S(1)}, u32[]{:S(2)}, u32[]{:S(2)}) %collective-permute-start.6) | collective-permute-done | bytes 368672 | tf_op jit(solution)/shard_map/ppermute | solution.py:425
  35.1 0.0 collective-permute-done.7.refs_2_
  35.1 0.1 pack_rows.3.near_ref
  35.2 0.1 collective-permute-start.10
  35.2 0.0 copy-start.1
  35.3 0.0 copy-start.2
  35.3 0.5 cross_rows.5
  35.8 1.6 %collective-permute-start.9 = (bf16[72,1792]{1,0:T(8,128)(2,1)S(1)}, bf16[72,1792]{1,0:T(8,128)(2,1)S(1)}, u32[]{:S(2)}, u32[]{:S(2)}) collective-permute-start(bf16[72,1792]{1,0:T(8,128)(2,1)S(1)} %cross_rows.5), channel_id=1, source_target_pairs={{0,2},{2,0},{4,6},{6,4},{8,10},{10,8},{12,14},{14,12},{1,3},{3,1},... | collective-permute-start | bytes 774152 | tf_op jit(solution)/shard_map/ppermute | solution.py:425
  37.4 0.0 collective-permute-done.5.far_ref
  37.4 1.0 %copy-done.2 = bf16[1,3584,512]{2,1,0:T(8,128)(2,1)S(1)} copy-done((bf16[1,3584,512]{2,1,0:T(8,128)(2,1)S(1)}, bf16[1,3584,512]{2,1,0:T(8,128)(2,1)}, u32[]{:S(2)}) %copy-start.2) | copy-done | bytes 3670040
  38.4 2.9 %hidden_units.3.refs_3_ = bf16[368,512]{1,0:T(8,128)(2,1)S(1)} custom-call(bf16[368,1792]{1,0:T(8,128)(2,1)S(1)} %pack_rows.2.near_ref, bf16[368,1792]{1,0:T(8,128)(2,1)S(1)} %collective-permute-done.5.far_ref, bf16[3584,512]{1,0:T(8,128)(2,1)S(1)} %bitcast.7, bf16[3584,512]{1,0:T(8,128)(2,1)S(1)} %bitcast.10), custom_call_target="tpu_custom_call" | custom-call | tf_op jit(solution)/shard_map/hidden_units/pallas_call | solution.py:91
  41.3 0.6 collective-permute-start.8
  41.9 0.0 collective-permute-done.10.far_ref
  41.9 2.1 %hidden_units.4.refs_1_ = bf16[256,512]{1,0:T(8,128)(2,1)S(1)} custom-call(bf16[256,1792]{1,0:T(8,128)(2,1)S(1)} %pack_rows.3.near_ref, bf16[256,1792]{1,0:T(8,128)(2,1)S(1)} %collective-permute-done.10.far_ref, bf16[3584,512]{1,0:T(8,128)(2,1)S(1)} %bitcast.8, bf16[3584,512]{1,0:T(8,128)(2,1)S(1)} %bitcast.11), custom_call_target="tpu_custom_call" | custom-call | tf_op jit(solution)/shard_map/hidden_units/pallas_call | solution.py:91
  43.9 0.5 collective-permute-done.9.near_ref
  44.5 0.0 collective-permute-start.13
  44.5 0.5 collective-permute-start.12
  45.0 1.5 %down.3 = (f32[96,1792]{1,0:T(8,128)S(1)}, f32[96,1792]{1,0:T(8,128)S(1)}, f32[96,1792]{1,0:T(8,128)S(1)}, bf16[72,1792]{1,0:T(8,128)(2,1)S(1)}) custom-call(bf16[96,1920]{1,0:T(8,128)(2,1)S(1)} %get-tuple-element.40.refs_0_.wide_ref, bf16[96,1920]{1,0:T(8,128)(2,1)S(1)} %collective-permute-done.wide_ref.refs_1_, ...), custom_call_target="tpu_custom_call" | custom-call | tf_op jit(solution)/shard_map/down/pallas_call | solution.py:91
  46.5 1.4 %hidden_units.5.refs_0_ = bf16[72,512]{1,0:T(8,128)(2,1)S(1)} custom-call(bf16[72,1792]{1,0:T(8,128)(2,1)S(1)} %collective-permute-done.9.near_ref, bf16[72,1792]{1,0:T(8,128)(2,1)S(1)} %collective-permute-done.13.far_ref, bf16[3584,512]{1,0:T(8,128)(2,1)S(1)} %bitcast.9, bf16[3584,512]{1,0:T(8,128)(2,1)S(1)} %bitcast.12), custom_call_target="tpu_custom_call" | custom-call | tf_op jit(solution)/shard_map/hidden_units/pallas_call | solution.py:91
  47.9 0.1 collective-permute-start.16
  48.0 0.0 collective-permute-done.12.refs_2_
  48.0 1.1 %down.4 = (f32[96,1792]{1,0:T(8,128)S(1)}, bf16[72,1792]{1,0:T(8,128)(2,1)S(1)}, bf16[72,1792]{1,0:T(8,128)(2,1)S(1)}) custom-call(bf16[96,1920]{1,0:T(8,128)(2,1)S(1)} %collective-permute-done.6.refs_0_.wide_ref, bf16[256,512]{1,0:T(8,128)(2,1)S(1)} %hidden_units.4.refs_1_, bf16[256,512]{1,0:T(8,128)(2,1)S(1)} %collective-permute-done.12.refs_2_, ...), custom_call_target="tpu_custom_call" | custom-call | tf_op jit(solution)/shard_map/down/pallas_call | solution.py:91
  49.2 0.1 collective-permute-done.16.refs_1_
  49.3 0.7 down.5
  50.0 1.6 %collective-permute-start.17 = (bf16[72,1792]{1,0:T(8,128)(2,1)S(1)}, bf16[72,1792]{1,0:T(8,128)(2,1)S(1)}, u32[]{:S(2)}, u32[]{:S(2)}) collective-permute-start(bf16[72,1792]{1,0:T(8,128)(2,1)S(1)} %down.5), channel_id=1, source_target_pairs={{0,2},{2,0},{4,6},{6,4},{8,10},{10,8},{12,14},{14,12},{1,3},{3,1},... | collective-permute-start | bytes 774152 | tf_op jit(solution)/shard_map/ppermute | solution.py:425
  51.6 0.5 collective-permute-start.15
  52.1 1.5 %collective-permute-start.14 = (bf16[72,1792]{1,0:T(8,128)(2,1)S(1)}, bf16[72,1792]{1,0:T(8,128)(2,1)S(1)}, u32[]{:S(2)}, u32[]{:S(2)}) collective-permute-start(bf16[72,1792]{1,0:T(8,128)(2,1)S(1)} %get-tuple-element.61), channel_id=1, source_target_pairs={{0,2},{2,0},{4,6},{6,4},{8,10},{10,8},{12,14},{14,12},{1,3},{3,1},... | collective-permute-start | bytes 774152 | tf_op jit(solution)/shard_map/ppermute | solution.py:425
  53.6 5.5 %collective-permute-done.17.back_ref = bf16[72,1792]{1,0:T(8,128)(2,1)S(1)} collective-permute-done((bf16[72,1792]{1,0:T(8,128)(2,1)S(1)}, bf16[72,1792]{1,0:T(8,128)(2,1)S(1)}, u32[]{:S(2)}, u32[]{:S(2)}) %collective-permute-start.17) | collective-permute-done | bytes 258080 | tf_op jit(solution)/shard_map/ppermute | solution.py:425
  59.1 0.4 combine.6
  59.6 0.4 collective-permute-start.19
  59.9 1.7 %collective-permute-start.18 = (bf16[96,896]{1,0:T(8,128)(2,1)S(1)}, bf16[96,896]{1,0:T(8,128)(2,1)S(1)}, u32[]{:S(2)}, u32[]{:S(2)}) collective-permute-start(bf16[96,896]{1,0:T(8,128)(2,1)S(1)} %get-tuple-element.68), channel_id=1, source_target_pairs={{0,4},{2,6},{4,0},{6,2},{8,12},{10,14},{12,8},{14,10},{1,5},{3,7},... | collective-permute-start | bytes 516104 | tf_op jit(solution)/shard_map/ppermute | solution.py:425
  61.7 1.5 %collective-permute-start.11 = (bf16[72,1792]{1,0:T(8,128)(2,1)S(1)}, bf16[72,1792]{1,0:T(8,128)(2,1)S(1)}, u32[]{:S(2)}, u32[]{:S(2)}) collective-permute-start(bf16[72,1792]{1,0:T(8,128)(2,1)S(1)} %get-tuple-element.57), channel_id=1, source_target_pairs={{0,2},{2,0},{4,6},{6,4},{8,10},{10,8},{12,14},{14,12},{1,3},{3,1},... | collective-permute-start | bytes 774152 | tf_op jit(solution)/shard_map/ppermute | solution.py:425
  63.2 1.5 %collective-permute-done.15.back_ref = bf16[72,1792]{1,0:T(8,128)(2,1)S(1)} collective-permute-done((bf16[72,1792]{1,0:T(8,128)(2,1)S(1)}, bf16[72,1792]{1,0:T(8,128)(2,1)S(1)}, u32[]{:S(2)}, u32[]{:S(2)}) %collective-permute-start.15) | collective-permute-done | bytes 258080 | tf_op jit(solution)/shard_map/ppermute | solution.py:425
  64.6 2.1 %collective-permute-done.19.refs_0_ = bf16[96,896]{1,0:T(8,128)(2,1)S(1)} collective-permute-done((bf16[96,896]{1,0:T(8,128)(2,1)S(1)}, bf16[96,896]{1,0:T(8,128)(2,1)S(1)}, u32[]{:S(2)}, u32[]{:S(2)}) %collective-permute-start.19) | collective-permute-done | bytes 172064 | tf_op jit(solution)/shard_map/ppermute | solution.py:425
  66.8 0.4 combine.7
  67.2 7.9 %collective-permute-start.20 = (bf16[96,896]{1,0:T(8,128)(2,1)S(1)}, bf16[96,896]{1,0:T(8,128)(2,1)S(1)}, u32[]{:S(2)}, u32[]{:S(2)}) collective-permute-start(bf16[96,896]{1,0:T(8,128)(2,1)S(1)} %combine.7), channel_id=1, source_target_pairs={{0,12},{2,14},{4,8},{6,10},{8,4},{10,6},{12,0},{14,2},{1,13},{3,15... | collective-permute-start | bytes 516104 | tf_op jit(solution)/shard_map/ppermute | solution.py:425
  75.1 0.4 combine.8
  75.5 1.4 %collective-permute-start.21 = (bf16[96,896]{1,0:T(8,128)(2,1)S(1)}, bf16[96,896]{1,0:T(8,128)(2,1)S(1)}, u32[]{:S(2)}, u32[]{:S(2)}) collective-permute-start(bf16[96,896]{1,0:T(8,128)(2,1)S(1)} %combine.8), channel_id=1, source_target_pairs={{0,12},{2,14},{4,8},{6,10},{8,4},{10,6},{12,0},{14,2},{1,13},{3,15... | collective-permute-start | bytes 516104 | tf_op jit(solution)/shard_map/ppermute | solution.py:425
  76.9 0.5 combine.9
  77.4 1.2 %collective-permute-start.22 = (bf16[96,896]{1,0:T(8,128)(2,1)S(1)}, bf16[96,896]{1,0:T(8,128)(2,1)S(1)}, u32[]{:S(2)}, u32[]{:S(2)}) collective-permute-start(bf16[96,896]{1,0:T(8,128)(2,1)S(1)} %get-tuple-element.72), channel_id=1, source_target_pairs={{0,4},{2,6},{4,0},{6,2},{8,12},{10,14},{12,8},{14,10},{1,5},{3,7},... | collective-permute-start | bytes 516104 | tf_op jit(solution)/shard_map/ppermute | solution.py:425
  78.6 0.9 %collective-permute-start.23 = (bf16[96,896]{1,0:T(8,128)(2,1)S(1)}, bf16[96,896]{1,0:T(8,128)(2,1)S(1)}, u32[]{:S(2)}, u32[]{:S(2)}) collective-permute-start(bf16[96,896]{1,0:T(8,128)(2,1)S(1)} %get-tuple-element.77), channel_id=1, source_target_pairs={{0,4},{2,6},{4,0},{6,2},{8,12},{10,14},{12,8},{14,10},{1,5},{3,7},... | collective-permute-start | bytes 516104 | tf_op jit(solution)/shard_map/ppermute | solution.py:425
  79.5 1.0 %collective-permute-done.20.refs_0_ = bf16[96,896]{1,0:T(8,128)(2,1)S(1)} collective-permute-done((bf16[96,896]{1,0:T(8,128)(2,1)S(1)}, bf16[96,896]{1,0:T(8,128)(2,1)S(1)}, u32[]{:S(2)}, u32[]{:S(2)}) %collective-permute-start.20) | collective-permute-done | bytes 172064 | tf_op jit(solution)/shard_map/ppermute | solution.py:425
  80.4 0.4 combine.10.refs_0_
  80.8 3.8 %collective-permute-done.21.refs_0_ = bf16[96,896]{1,0:T(8,128)(2,1)S(1)} collective-permute-done((bf16[96,896]{1,0:T(8,128)(2,1)S(1)}, bf16[96,896]{1,0:T(8,128)(2,1)S(1)}, u32[]{:S(2)}, u32[]{:S(2)}) %collective-permute-start.21) | collective-permute-done | bytes 172064 | tf_op jit(solution)/shard_map/ppermute | solution.py:425
  84.7 0.4 combine.11.refs_1_
  85.1 1.5 %collective-permute-done.22.refs_2_ = bf16[96,896]{1,0:T(8,128)(2,1)S(1)} collective-permute-done((bf16[96,896]{1,0:T(8,128)(2,1)S(1)}, bf16[96,896]{1,0:T(8,128)(2,1)S(1)}, u32[]{:S(2)}, u32[]{:S(2)}) %collective-permute-start.22) | collective-permute-done | bytes 172064 | tf_op jit(solution)/shard_map/ppermute | solution.py:425
  86.6 3.0 %collective-permute-done.23.refs_3_ = bf16[96,896]{1,0:T(8,128)(2,1)S(1)} collective-permute-done((bf16[96,896]{1,0:T(8,128)(2,1)S(1)}, bf16[96,896]{1,0:T(8,128)(2,1)S(1)}, u32[]{:S(2)}, u32[]{:S(2)}) %collective-permute-start.23) | collective-permute-done | bytes 172064 | tf_op jit(solution)/shard_map/ppermute | solution.py:425
  89.5 0.8 add_last.1
  (18 shorter events, 0.0 us)
Async XLA Ops:
  0.6 9.0 %copy-start.3 = (bf16[4,256,576]{1,2,0:T(8,128)(2,1)S(1)}, bf16[4,256,576]{1,2,0:T(8,128)(2,1)}, u32[]{:S(2)}) copy-start(bf16[4,256,576]{1,2,0:T(8,128)(2,1)} %param.11) | copy-start | bytes 3538948
  0.6 9.0 %copy-start.4 = (bf16[4,32,576]{2,1,0:T(8,128)(2,1)S(1)}, bf16[4,32,576]{2,1,0:T(8,128)(2,1)}, u32[]{:S(2)}) copy-start(bf16[4,32,576]{2,1,0:T(8,128)(2,1)} %query_ref) | copy-start | bytes 442372
  0.7 9.0 %copy-start.5 = (s32[32]{0:T(128)S(1)}, s32[32]{0:T(128)}, u32[]{:S(2)}) copy-start(s32[32]{0:T(128)} %param.12) | copy-start | bytes 388
  0.7 9.0 %copy-start.6 = (s32[32]{0:T(128)S(1)}, s32[32]{0:T(128)}, u32[]{:S(2)}) copy-start(s32[32]{0:T(128)} %param.13) | copy-start | bytes 388
  2.4 12.4 %collective-permute-start.1 = (bf16[512,1792]{1,0:T(8,128)(2,1)S(1)}, bf16[512,1792]{1,0:T(8,128)(2,1)S(1)}, u32[]{:S(2)}, u32[]{:S(2)}) collective-permute-start(bf16[512,1792]{1,0:T(8,128)(2,1)S(1)} %get-tuple-element.42), channel_id=1, source_target_pairs={{0,1},{1,0},{2,3},{3,2},{4,5},{5,4},{6,7},{7,6},{8,9},{9,8},{10,11... | collective-permute-start | bytes 5505032 | tf_op jit(solution)/shard_map/ppermute | solution.py:429
  3.0 11.8 %collective-permute-start = (bf16[96,1920]{1,0:T(8,128)(2,1)S(1)}, bf16[96,1920]{1,0:T(8,128)(2,1)S(1)}, u32[]{:S(2)}, u32[]{:S(2)}) collective-permute-start(bf16[96,1920]{1,0:T(8,128)(2,1)S(1)} %get-tuple-element.40.refs_0_.wide_ref), channel_id=1, source_target_pairs={{0,4},{2,6},{4,0},{6,2},{8,12},{10,14},{12,8},{14,10},{1,5},{3,7},... | collective-permute-start | bytes 1105928 | tf_op jit(solution)/shard_map/ppermute | solution.py:425
  5.6 19.4 %collective-permute-start.2 = (bf16[96,1920]{1,0:T(8,128)(2,1)S(1)}, bf16[96,1920]{1,0:T(8,128)(2,1)S(1)}, u32[]{:S(2)}, u32[]{:S(2)}) collective-permute-start(bf16[96,1920]{1,0:T(8,128)(2,1)S(1)} %get-tuple-element.40.refs_0_.wide_ref), channel_id=1, source_target_pairs={{0,12},{2,14},{4,8},{6,10},{8,4},{10,6},{12,0},{14,2},{1,13},{3,15... | collective-permute-start | bytes 1105928 | tf_op jit(solution)/shard_map/ppermute | solution.py:425
  8.1 9.0 %collective-permute-start.3 = (bf16[72,1792]{1,0:T(8,128)(2,1)S(1)}, bf16[72,1792]{1,0:T(8,128)(2,1)S(1)}, u32[]{:S(2)}, u32[]{:S(2)}) collective-permute-start(bf16[72,1792]{1,0:T(8,128)(2,1)S(1)} %get-tuple-element.44), channel_id=1, source_target_pairs={{0,2},{2,0},{4,6},{6,4},{8,10},{10,8},{12,14},{14,12},{1,3},{3,1},... | collective-permute-start | bytes 774152 | tf_op jit(solution)/shard_map/ppermute | solution.py:425
  15.3 10.3 %collective-permute-start.4 = (bf16[72,1792]{1,0:T(8,128)(2,1)S(1)}, bf16[72,1792]{1,0:T(8,128)(2,1)S(1)}, u32[]{:S(2)}, u32[]{:S(2)}) collective-permute-start(bf16[72,1792]{1,0:T(8,128)(2,1)S(1)} %cross_rows.3), channel_id=1, source_target_pairs={{0,2},{2,0},{4,6},{6,4},{8,10},{10,8},{12,14},{14,12},{1,3},{3,1},... | collective-permute-start | bytes 774152 | tf_op jit(solution)/shard_map/ppermute | solution.py:425
  25.0 10.1 %collective-permute-start.6 = (bf16[96,1920]{1,0:T(8,128)(2,1)S(1)}, bf16[96,1920]{1,0:T(8,128)(2,1)S(1)}, u32[]{:S(2)}, u32[]{:S(2)}) collective-permute-start(bf16[96,1920]{1,0:T(8,128)(2,1)S(1)} %collective-permute-done.2.wide_ref.refs_2_), channel_id=1, source_target_pairs={{0,4},{2,6},{4,0},{6,2},{8,12},{10,14},{12,8},{14,10},{1,5},{3,7},... | collective-permute-start | bytes 1105928 | tf_op jit(solution)/shard_map/ppermute | solution.py:425
  26.1 9.0 %collective-permute-start.7 = (bf16[72,1792]{1,0:T(8,128)(2,1)S(1)}, bf16[72,1792]{1,0:T(8,128)(2,1)S(1)}, u32[]{:S(2)}, u32[]{:S(2)}) collective-permute-start(bf16[72,1792]{1,0:T(8,128)(2,1)S(1)} %cross_rows.4), channel_id=1, source_target_pairs={{0,2},{2,0},{4,6},{6,4},{8,10},{10,8},{12,14},{14,12},{1,3},{3,1},... | collective-permute-start | bytes 774152 | tf_op jit(solution)/shard_map/ppermute | solution.py:425
  27.8 9.6 %collective-permute-start.5 = (bf16[368,1792]{1,0:T(8,128)(2,1)S(1)}, bf16[368,1792]{1,0:T(8,128)(2,1)S(1)}, u32[]{:S(2)}, u32[]{:S(2)}) collective-permute-start(bf16[368,1792]{1,0:T(8,128)(2,1)S(1)} %pack_rows.2.near_ref), channel_id=1, source_target_pairs={{0,1},{1,0},{2,3},{3,2},{4,5},{5,4},{6,7},{7,6},{8,9},{9,8},{10,11... | collective-permute-start | bytes 3956744 | tf_op jit(solution)/shard_map/ppermute | solution.py:429
  35.2 6.7 %collective-permute-start.10 = (bf16[256,1792]{1,0:T(8,128)(2,1)S(1)}, bf16[256,1792]{1,0:T(8,128)(2,1)S(1)}, u32[]{:S(2)}, u32[]{:S(2)}) collective-permute-start(bf16[256,1792]{1,0:T(8,128)(2,1)S(1)} %pack_rows.3.near_ref), channel_id=1, source_target_pairs={{0,1},{1,0},{2,3},{3,2},{4,5},{5,4},{6,7},{7,6},{8,9},{9,8},{10,11... | collective-permute-start | bytes 2752520 | tf_op jit(solution)/shard_map/ppermute | solution.py:429
  35.2 2.1 %copy-start.1 = (bf16[1,3584,512]{2,1,0:T(8,128)(2,1)S(1)}, bf16[1,3584,512]{2,1,0:T(8,128)(2,1)}, u32[]{:S(2)}) copy-start(bf16[1,3584,512]{2,1,0:T(8,128)(2,1)} %param.17) | copy-start | bytes 11010052
  35.3 3.2 %copy-start.2 = (bf16[1,3584,512]{2,1,0:T(8,128)(2,1)S(1)}, bf16[1,3584,512]{2,1,0:T(8,128)(2,1)}, u32[]{:S(2)}) copy-start(bf16[1,3584,512]{2,1,0:T(8,128)(2,1)} %param.18) | copy-start | bytes 11010052
  35.8 8.7 %collective-permute-start.9 = (bf16[72,1792]{1,0:T(8,128)(2,1)S(1)}, bf16[72,1792]{1,0:T(8,128)(2,1)S(1)}, u32[]{:S(2)}, u32[]{:S(2)}) collective-permute-start(bf16[72,1792]{1,0:T(8,128)(2,1)S(1)} %cross_rows.5), channel_id=1, source_target_pairs={{0,2},{2,0},{4,6},{6,4},{8,10},{10,8},{12,14},{14,12},{1,3},{3,1},... | collective-permute-start | bytes 774152 | tf_op jit(solution)/shard_map/ppermute | solution.py:425
  41.3 3.7 %collective-permute-start.8 = (bf16[368,512]{1,0:T(8,128)(2,1)S(1)}, bf16[368,512]{1,0:T(8,128)(2,1)S(1)}, u32[]{:S(2)}, u32[]{:S(2)}) collective-permute-start(bf16[368,512]{1,0:T(8,128)(2,1)S(1)} %hidden_units.3.refs_3_), channel_id=1, source_target_pairs={{0,1},{1,0},{2,3},{3,2},{4,5},{5,4},{6,7},{7,6},{8,9},{9,8},{10,11... | collective-permute-start | bytes 1130504 | tf_op jit(solution)/shard_map/ppermute | solution.py:429
  41.9 3.1 %copy-start = (bf16[1,512,3584]{2,1,0:T(8,128)(2,1)S(1)}, bf16[1,512,3584]{2,1,0:T(8,128)(2,1)}, u32[]{:S(2)}) copy-start(bf16[1,512,3584]{2,1,0:T(8,128)(2,1)} %refs_2_.1) | copy-start | bytes 11010052
  44.5 2.1 %collective-permute-start.13 = (bf16[72,1792]{1,0:T(8,128)(2,1)S(1)}, bf16[72,1792]{1,0:T(8,128)(2,1)S(1)}, u32[]{:S(2)}, u32[]{:S(2)}) collective-permute-start(bf16[72,1792]{1,0:T(8,128)(2,1)S(1)} %collective-permute-done.9.near_ref), channel_id=1, source_target_pairs={{0,1},{1,0},{2,3},{3,2},{4,5},{5,4},{6,7},{7,6},{8,9},{9,8},{10,11... | collective-permute-start | bytes 774152 | tf_op jit(solution)/shard_map/ppermute | solution.py:429
  44.5 3.6 %collective-permute-start.12 = (bf16[256,512]{1,0:T(8,128)(2,1)S(1)}, bf16[256,512]{1,0:T(8,128)(2,1)S(1)}, u32[]{:S(2)}, u32[]{:S(2)}) collective-permute-start(bf16[256,512]{1,0:T(8,128)(2,1)S(1)} %hidden_units.4.refs_1_), channel_id=1, source_target_pairs={{0,1},{1,0},{2,3},{3,2},{4,5},{5,4},{6,7},{7,6},{8,9},{9,8},{10,11... | collective-permute-start | bytes 786440 | tf_op jit(solution)/shard_map/ppermute | solution.py:429
  47.9 1.3 %collective-permute-start.16 = (bf16[72,512]{1,0:T(8,128)(2,1)S(1)}, bf16[72,512]{1,0:T(8,128)(2,1)S(1)}, u32[]{:S(2)}, u32[]{:S(2)}) collective-permute-start(bf16[72,512]{1,0:T(8,128)(2,1)S(1)} %hidden_units.5.refs_0_), channel_id=1, source_target_pairs={{0,1},{1,0},{2,3},{3,2},{4,5},{5,4},{6,7},{7,6},{8,9},{9,8},{10,11... | collective-permute-start | bytes 221192 | tf_op jit(solution)/shard_map/ppermute | solution.py:429
  50.0 9.1 %collective-permute-start.17 = (bf16[72,1792]{1,0:T(8,128)(2,1)S(1)}, bf16[72,1792]{1,0:T(8,128)(2,1)S(1)}, u32[]{:S(2)}, u32[]{:S(2)}) collective-permute-start(bf16[72,1792]{1,0:T(8,128)(2,1)S(1)} %down.5), channel_id=1, source_target_pairs={{0,2},{2,0},{4,6},{6,4},{8,10},{10,8},{12,14},{14,12},{1,3},{3,1},... | collective-permute-start | bytes 774152 | tf_op jit(solution)/shard_map/ppermute | solution.py:425
  51.6 13.0 %collective-permute-start.15 = (bf16[72,1792]{1,0:T(8,128)(2,1)S(1)}, bf16[72,1792]{1,0:T(8,128)(2,1)S(1)}, u32[]{:S(2)}, u32[]{:S(2)}) collective-permute-start(bf16[72,1792]{1,0:T(8,128)(2,1)S(1)} %get-tuple-element.63), channel_id=1, source_target_pairs={{0,2},{2,0},{4,6},{6,4},{8,10},{10,8},{12,14},{14,12},{1,3},{3,1},... | collective-permute-start | bytes 774152 | tf_op jit(solution)/shard_map/ppermute | solution.py:425
  52.1 24.8 %collective-permute-start.14 = (bf16[72,1792]{1,0:T(8,128)(2,1)S(1)}, bf16[72,1792]{1,0:T(8,128)(2,1)S(1)}, u32[]{:S(2)}, u32[]{:S(2)}) collective-permute-start(bf16[72,1792]{1,0:T(8,128)(2,1)S(1)} %get-tuple-element.61), channel_id=1, source_target_pairs={{0,2},{2,0},{4,6},{6,4},{8,10},{10,8},{12,14},{14,12},{1,3},{3,1},... | collective-permute-start | bytes 774152 | tf_op jit(solution)/shard_map/ppermute | solution.py:425
  59.6 7.2 %collective-permute-start.19 = (bf16[96,896]{1,0:T(8,128)(2,1)S(1)}, bf16[96,896]{1,0:T(8,128)(2,1)S(1)}, u32[]{:S(2)}, u32[]{:S(2)}) collective-permute-start(bf16[96,896]{1,0:T(8,128)(2,1)S(1)} %get-tuple-element.66), channel_id=1, source_target_pairs={{0,4},{2,6},{4,0},{6,2},{8,12},{10,14},{12,8},{14,10},{1,5},{3,7},... | collective-permute-start | bytes 516104 | tf_op jit(solution)/shard_map/ppermute | solution.py:425
  59.9 15.1 %collective-permute-start.18 = (bf16[96,896]{1,0:T(8,128)(2,1)S(1)}, bf16[96,896]{1,0:T(8,128)(2,1)S(1)}, u32[]{:S(2)}, u32[]{:S(2)}) collective-permute-start(bf16[96,896]{1,0:T(8,128)(2,1)S(1)} %get-tuple-element.68), channel_id=1, source_target_pairs={{0,4},{2,6},{4,0},{6,2},{8,12},{10,14},{12,8},{14,10},{1,5},{3,7},... | collective-permute-start | bytes 516104 | tf_op jit(solution)/shard_map/ppermute | solution.py:425
  61.7 17.8 %collective-permute-start.11 = (bf16[72,1792]{1,0:T(8,128)(2,1)S(1)}, bf16[72,1792]{1,0:T(8,128)(2,1)S(1)}, u32[]{:S(2)}, u32[]{:S(2)}) collective-permute-start(bf16[72,1792]{1,0:T(8,128)(2,1)S(1)} %get-tuple-element.57), channel_id=1, source_target_pairs={{0,2},{2,0},{4,6},{6,4},{8,10},{10,8},{12,14},{14,12},{1,3},{3,1},... | collective-permute-start | bytes 774152 | tf_op jit(solution)/shard_map/ppermute | solution.py:425
  67.2 13.3 %collective-permute-start.20 = (bf16[96,896]{1,0:T(8,128)(2,1)S(1)}, bf16[96,896]{1,0:T(8,128)(2,1)S(1)}, u32[]{:S(2)}, u32[]{:S(2)}) collective-permute-start(bf16[96,896]{1,0:T(8,128)(2,1)S(1)} %combine.7), channel_id=1, source_target_pairs={{0,12},{2,14},{4,8},{6,10},{8,4},{10,6},{12,0},{14,2},{1,13},{3,15... | collective-permute-start | bytes 516104 | tf_op jit(solution)/shard_map/ppermute | solution.py:425
  75.5 9.2 %collective-permute-start.21 = (bf16[96,896]{1,0:T(8,128)(2,1)S(1)}, bf16[96,896]{1,0:T(8,128)(2,1)S(1)}, u32[]{:S(2)}, u32[]{:S(2)}) collective-permute-start(bf16[96,896]{1,0:T(8,128)(2,1)S(1)} %combine.8), channel_id=1, source_target_pairs={{0,12},{2,14},{4,8},{6,10},{8,4},{10,6},{12,0},{14,2},{1,13},{3,15... | collective-permute-start | bytes 516104 | tf_op jit(solution)/shard_map/ppermute | solution.py:425
  77.4 9.2 %collective-permute-start.22 = (bf16[96,896]{1,0:T(8,128)(2,1)S(1)}, bf16[96,896]{1,0:T(8,128)(2,1)S(1)}, u32[]{:S(2)}, u32[]{:S(2)}) collective-permute-start(bf16[96,896]{1,0:T(8,128)(2,1)S(1)} %get-tuple-element.72), channel_id=1, source_target_pairs={{0,4},{2,6},{4,0},{6,2},{8,12},{10,14},{12,8},{14,10},{1,5},{3,7},... | collective-permute-start | bytes 516104 | tf_op jit(solution)/shard_map/ppermute | solution.py:425
  78.6 11.0 %collective-permute-start.23 = (bf16[96,896]{1,0:T(8,128)(2,1)S(1)}, bf16[96,896]{1,0:T(8,128)(2,1)S(1)}, u32[]{:S(2)}, u32[]{:S(2)}) collective-permute-start(bf16[96,896]{1,0:T(8,128)(2,1)S(1)} %get-tuple-element.77), channel_id=1, source_target_pairs={{0,4},{2,6},{4,0},{6,2},{8,12},{10,14},{12,8},{14,10},{1,5},{3,7},... | collective-permute-start | bytes 516104 | tf_op jit(solution)/shard_map/ppermute | solution.py:425

commit v6 on v5

--- a/solution.py
+++ b/solution.py
@@ -447,11 +447,11 @@
     w_gate, w_up = w_gate[0], w_up[0]
     down_other = swap_core(down_away)
     attended = attend(after(q_lat, wide), latent_cache, lengths, placement)
-    wide_pair = after(wide_pair, attended, down_other)
+    cross_in = after(cross_in, attended)
+    wide_pair = after(wide_pair, cross_in, down_other)
     cross_pair = cross_rows(wide_pair, role_count, capacity)
     cross_pair_in = swap(cross_pair, row)
-    cross_in = after(cross_in, cross_pair)
-    wide_mirror = after(wide_mirror, cross_in)
+    wide_mirror = after(wide_mirror, cross_pair)
     wide_far = swap(wide_mirror, pair)
     wide_mirror_ready = after(wide_mirror, cross_pair_in)
     cross_mirror = cross_rows(wide_mirror_ready, role_count, capacity)

time: 90.5 us -> 90.2 us (level)
  transfers between devices with their start and end apart: 24 -> 24, of which waited for: 12 -> 13; matrix products, arithmetic and copies ran while one was open for 0% -> 0% of each run, Pallas kernels for 17% -> 17%
where the time goes in v6:
time: 90.2 us; the launch traced here: 90.1 us
  waiting for transfers between devices  37 us (41%)
  starting transfers between devices  32.6 us (36%)
  Pallas kernels  18.6 us (21%)
  local copies, waits for them, and re-layouts  1.04 us (1%)
    ppermute x17, waiting for transfers between devices, swap(): return lax.ppermute(array, 'role', pairs)  36.9 us
    ppermute x17, starting transfers between devices, swap(): return lax.ppermute(array, 'role', pairs)  30.8 us
    pallas_call x18, Pallas kernels, call(): pl.pallas_call(kernel, in_specs=[place] * len(operands), out_specs=[place...  14.7 us
    pallas_call x1, Pallas kernels, attend(): pl.pallas_call(attend_kernel, out_shape=jax.ShapeDtypeStruct((slot_count,...  2.05 us
    ppermute x7, starting transfers between devices, swap_core(): return lax.ppermute(array, 'tp', [(0, 1), (1, 0)])  1.8 us
  transfers between devices with their start and end apart: 24, of which 13 were waited for; matrix products, arithmetic and copies ran while one was open for 0% of the time, Pallas kernels for 17%

profile of v6, /device:TPU:0, one launch (start us, length us, event | category | flops | bytes accessed | tf_op | source)
XLA Modules:
  0.0 90.1 jit_solution(5862310998027778870)
XLA Ops:
  0.7 1.8 %prepare.1 = (bf16[96,1920]{1,0:T(8,128)(2,1)S(1)}, bf16[72,1792]{1,0:T(8,128)(2,1)S(1)}, bf16[512,1792]{1,0:T(8,128)(2,1)S(1)}) custom-call(bf16[96,1792]{1,0:T(8,128)(2,1)} %tokens_hbm.1, bf16[1,512,3584]{2,1,0:T(8,128)(2,1)} %refs_2_.1, s32[4,96]{1,0:T(4,128)} %bitcast.16, f32[4,96]{1,0:T(4,128)} %bitcast.17), custom_call_target="tpu_custom_call" | custom-call | tf_op jit(solution)/shard_map/prepare/pallas_call | solution.py:212
  2.4 0.5 collective-permute-start.2
  3.0 2.6 %collective-permute-start = (bf16[96,1920]{1,0:T(8,128)(2,1)S(1)}, bf16[96,1920]{1,0:T(8,128)(2,1)S(1)}, u32[]{:S(2)}, u32[]{:S(2)}) collective-permute-start(bf16[96,1920]{1,0:T(8,128)(2,1)S(1)} %get-tuple-element.40.refs_0_.wide_ref), channel_id=1, source_target_pairs={{0,4},{2,6},{4,0},{6,2},{8,12},{10,14},{12,8},{14,10},{1,5},{3,7},... | collective-permute-start | bytes 1105928 | tf_op jit(solution)/shard_map/ppermute | solution.py:425
  5.6 1.5 %collective-permute-start.1 = (bf16[72,1792]{1,0:T(8,128)(2,1)S(1)}, bf16[72,1792]{1,0:T(8,128)(2,1)S(1)}, u32[]{:S(2)}, u32[]{:S(2)}) collective-permute-start(bf16[72,1792]{1,0:T(8,128)(2,1)S(1)} %get-tuple-element.42), channel_id=1, source_target_pairs={{0,2},{2,0},{4,6},{6,4},{8,10},{10,8},{12,14},{14,12},{1,3},{3,1},... | collective-permute-start | bytes 774152 | tf_op jit(solution)/shard_map/ppermute | solution.py:425
  7.1 2.5 %collective-permute-start.3 = (bf16[96,1920]{1,0:T(8,128)(2,1)S(1)}, bf16[96,1920]{1,0:T(8,128)(2,1)S(1)}, u32[]{:S(2)}, u32[]{:S(2)}) collective-permute-start(bf16[96,1920]{1,0:T(8,128)(2,1)S(1)} %get-tuple-element.40.refs_0_.wide_ref), channel_id=1, source_target_pairs={{0,12},{2,14},{4,8},{6,10},{8,4},{10,6},{12,0},{14,2},{1,13},{3,15... | collective-permute-start | bytes 1105928 | tf_op jit(solution)/shard_map/ppermute | solution.py:425
  9.6 2.1 %attend.1 = bf16[4,32,512]{2,1,0:T(8,128)(2,1)} custom-call(bf16[4,32,576]{2,1,0:T(8,128)(2,1)S(1)} %copy-done.4, bf16[4,576,256]{2,1,0:T(8,128)(2,1)S(1)} %bitcast.13, s32[1,32]{1,0:T(1,128)S(1)} %bitcast.14, s32[1,32]{1,0:T(1,128)S(1)} %bitcast.15), custom_call_target="tpu_custom_call" | custom-call | tf_op jit(solution)/shard_map/attend/pallas_call | solution.py:368
  11.7 2.2 %collective-permute-done.1.refs_3_ = bf16[72,1792]{1,0:T(8,128)(2,1)S(1)} collective-permute-done((bf16[72,1792]{1,0:T(8,128)(2,1)S(1)}, bf16[72,1792]{1,0:T(8,128)(2,1)S(1)}, u32[]{:S(2)}, u32[]{:S(2)}) %collective-permute-start.1) | collective-permute-done | bytes 258080 | tf_op jit(solution)/shard_map/ppermute | solution.py:425
  13.9 0.9 collective-permute-done.wide_ref.refs_1_
  14.8 0.5 cross_rows.3
  15.3 1.8 %collective-permute-start.4 = (bf16[72,1792]{1,0:T(8,128)(2,1)S(1)}, bf16[72,1792]{1,0:T(8,128)(2,1)S(1)}, u32[]{:S(2)}, u32[]{:S(2)}) collective-permute-start(bf16[72,1792]{1,0:T(8,128)(2,1)S(1)} %cross_rows.3), channel_id=1, source_target_pairs={{0,2},{2,0},{4,6},{6,4},{8,10},{10,8},{12,14},{14,12},{1,3},{3,1},... | collective-permute-start | bytes 774152 | tf_op jit(solution)/shard_map/ppermute | solution.py:425
  17.1 7.9 %collective-permute-done.3.wide_ref.refs_2_ = bf16[96,1920]{1,0:T(8,128)(2,1)S(1)} collective-permute-done((bf16[96,1920]{1,0:T(8,128)(2,1)S(1)}, bf16[96,1920]{1,0:T(8,128)(2,1)S(1)}, u32[]{:S(2)}, u32[]{:S(2)}) %collective-permute-start.3) | collective-permute-done | bytes 368672 | tf_op jit(solution)/shard_map/ppermute | solution.py:425
  25.0 1.8 %collective-permute-start.6 = (bf16[96,1920]{1,0:T(8,128)(2,1)S(1)}, bf16[96,1920]{1,0:T(8,128)(2,1)S(1)}, u32[]{:S(2)}, u32[]{:S(2)}) collective-permute-start(bf16[96,1920]{1,0:T(8,128)(2,1)S(1)} %collective-permute-done.3.wide_ref.refs_2_), channel_id=1, source_target_pairs={{0,4},{2,6},{4,0},{6,2},{8,12},{10,14},{12,8},{14,10},{1,5},{3,7},... | collective-permute-start | bytes 1105928 | tf_op jit(solution)/shard_map/ppermute | solution.py:425
  26.8 0.0 collective-permute-done.4.refs_1_
  26.8 0.5 cross_rows.4
  27.4 0.6 collective-permute-start.7
  27.9 0.1 pack_rows.2.near_ref
  28.0 0.1 collective-permute-start.5
  28.1 7.0 %collective-permute-done.6.refs_0_.wide_ref = bf16[96,1920]{1,0:T(8,128)(2,1)S(1)} collective-permute-done((bf16[96,1920]{1,0:T(8,128)(2,1)S(1)}, bf16[96,1920]{1,0:T(8,128)(2,1)S(1)}, u32[]{:S(2)}, u32[]{:S(2)}) %collective-permute-start.6) | collective-permute-done | bytes 368672 | tf_op jit(solution)/shard_map/ppermute | solution.py:425
  35.1 0.1 pack_rows.3.near_ref
  35.2 0.1 collective-permute-start.10
  35.2 0.0 copy-start.1
  35.3 0.0 copy-start.2
  35.3 0.5 cross_rows.5
  35.8 1.6 %collective-permute-start.9 = (bf16[72,1792]{1,0:T(8,128)(2,1)S(1)}, bf16[72,1792]{1,0:T(8,128)(2,1)S(1)}, u32[]{:S(2)}, u32[]{:S(2)}) collective-permute-start(bf16[72,1792]{1,0:T(8,128)(2,1)S(1)} %cross_rows.5), channel_id=1, source_target_pairs={{0,2},{2,0},{4,6},{6,4},{8,10},{10,8},{12,14},{14,12},{1,3},{3,1},... | collective-permute-start | bytes 774152 | tf_op jit(solution)/shard_map/ppermute | solution.py:425
  37.4 0.0 collective-permute-done.5.far_ref
  37.4 1.0 %copy-done.2 = bf16[1,3584,512]{2,1,0:T(8,128)(2,1)S(1)} copy-done((bf16[1,3584,512]{2,1,0:T(8,128)(2,1)S(1)}, bf16[1,3584,512]{2,1,0:T(8,128)(2,1)}, u32[]{:S(2)}) %copy-start.2) | copy-done | bytes 3670040
  38.4 2.9 %hidden_units.3.refs_3_ = bf16[368,512]{1,0:T(8,128)(2,1)S(1)} custom-call(bf16[368,1792]{1,0:T(8,128)(2,1)S(1)} %pack_rows.2.near_ref, bf16[368,1792]{1,0:T(8,128)(2,1)S(1)} %collective-permute-done.5.far_ref, bf16[3584,512]{1,0:T(8,128)(2,1)S(1)} %bitcast.7, bf16[3584,512]{1,0:T(8,128)(2,1)S(1)} %bitcast.10), custom_call_target="tpu_custom_call" | custom-call | tf_op jit(solution)/shard_map/hidden_units/pallas_call | solution.py:91
  41.3 0.6 collective-permute-start.8
  41.9 2.1 %hidden_units.4.refs_1_ = bf16[256,512]{1,0:T(8,128)(2,1)S(1)} custom-call(bf16[256,1792]{1,0:T(8,128)(2,1)S(1)} %pack_rows.3.near_ref, bf16[256,1792]{1,0:T(8,128)(2,1)S(1)} %collective-permute-done.10.far_ref, bf16[3584,512]{1,0:T(8,128)(2,1)S(1)} %bitcast.8, bf16[3584,512]{1,0:T(8,128)(2,1)S(1)} %bitcast.11), custom_call_target="tpu_custom_call" | custom-call | tf_op jit(solution)/shard_map/hidden_units/pallas_call | solution.py:91
  43.9 0.5 collective-permute-done.9.near_ref
  44.5 0.5 collective-permute-start.12
  45.0 0.0 collective-permute-done.8.refs_4_
  45.0 1.5 %down.3 = (f32[96,1792]{1,0:T(8,128)S(1)}, f32[96,1792]{1,0:T(8,128)S(1)}, f32[96,1792]{1,0:T(8,128)S(1)}, bf16[72,1792]{1,0:T(8,128)(2,1)S(1)}) custom-call(bf16[96,1920]{1,0:T(8,128)(2,1)S(1)} %get-tuple-element.40.refs_0_.wide_ref, bf16[96,1920]{1,0:T(8,128)(2,1)S(1)} %collective-permute-done.wide_ref.refs_1_, ...), custom_call_target="tpu_custom_call" | custom-call | tf_op jit(solution)/shard_map/down/pallas_call | solution.py:91
  46.5 0.0 collective-permute-done.13.far_ref
  46.5 1.4 %hidden_units.5.refs_0_ = bf16[72,512]{1,0:T(8,128)(2,1)S(1)} custom-call(bf16[72,1792]{1,0:T(8,128)(2,1)S(1)} %collective-permute-done.9.near_ref, bf16[72,1792]{1,0:T(8,128)(2,1)S(1)} %collective-permute-done.13.far_ref, bf16[3584,512]{1,0:T(8,128)(2,1)S(1)} %bitcast.9, bf16[3584,512]{1,0:T(8,128)(2,1)S(1)} %bitcast.12), custom_call_target="tpu_custom_call" | custom-call | tf_op jit(solution)/shard_map/hidden_units/pallas_call | solution.py:91
  47.9 0.1 collective-permute-start.16
  48.0 1.1 %down.4 = (f32[96,1792]{1,0:T(8,128)S(1)}, bf16[72,1792]{1,0:T(8,128)(2,1)S(1)}, bf16[72,1792]{1,0:T(8,128)(2,1)S(1)}) custom-call(bf16[96,1920]{1,0:T(8,128)(2,1)S(1)} %collective-permute-done.6.refs_0_.wide_ref, bf16[256,512]{1,0:T(8,128)(2,1)S(1)} %hidden_units.4.refs_1_, bf16[256,512]{1,0:T(8,128)(2,1)S(1)} %collective-permute-done.12.refs_2_, ...), custom_call_target="tpu_custom_call" | custom-call | tf_op jit(solution)/shard_map/down/pallas_call | solution.py:91
  49.2 0.1 collective-permute-done.16.refs_1_
  49.3 0.7 down.5
  50.0 1.6 %collective-permute-start.17 = (bf16[72,1792]{1,0:T(8,128)(2,1)S(1)}, bf16[72,1792]{1,0:T(8,128)(2,1)S(1)}, u32[]{:S(2)}, u32[]{:S(2)}) collective-permute-start(bf16[72,1792]{1,0:T(8,128)(2,1)S(1)} %down.5), channel_id=1, source_target_pairs={{0,2},{2,0},{4,6},{6,4},{8,10},{10,8},{12,14},{14,12},{1,3},{3,1},... | collective-permute-start | bytes 774152 | tf_op jit(solution)/shard_map/ppermute | solution.py:425
  51.6 0.5 collective-permute-start.15
  52.1 1.5 %collective-permute-start.14 = (bf16[72,1792]{1,0:T(8,128)(2,1)S(1)}, bf16[72,1792]{1,0:T(8,128)(2,1)S(1)}, u32[]{:S(2)}, u32[]{:S(2)}) collective-permute-start(bf16[72,1792]{1,0:T(8,128)(2,1)S(1)} %get-tuple-element.61), channel_id=1, source_target_pairs={{0,2},{2,0},{4,6},{6,4},{8,10},{10,8},{12,14},{14,12},{1,3},{3,1},... | collective-permute-start | bytes 774152 | tf_op jit(solution)/shard_map/ppermute | solution.py:425
  53.6 5.5 %collective-permute-done.17.back_ref = bf16[72,1792]{1,0:T(8,128)(2,1)S(1)} collective-permute-done((bf16[72,1792]{1,0:T(8,128)(2,1)S(1)}, bf16[72,1792]{1,0:T(8,128)(2,1)S(1)}, u32[]{:S(2)}, u32[]{:S(2)}) %collective-permute-start.17) | collective-permute-done | bytes 258080 | tf_op jit(solution)/shard_map/ppermute | solution.py:425
  59.1 0.4 combine.6
  59.6 1.6 %collective-permute-start.19 = (bf16[96,896]{1,0:T(8,128)(2,1)S(1)}, bf16[96,896]{1,0:T(8,128)(2,1)S(1)}, u32[]{:S(2)}, u32[]{:S(2)}) collective-permute-start(bf16[96,896]{1,0:T(8,128)(2,1)S(1)} %get-tuple-element.66), channel_id=1, source_target_pairs={{0,4},{2,6},{4,0},{6,2},{8,12},{10,14},{12,8},{14,10},{1,5},{3,7},... | collective-permute-start | bytes 516104 | tf_op jit(solution)/shard_map/ppermute | solution.py:425
  61.2 0.5 collective-permute-start.18
  61.7 1.5 %collective-permute-start.11 = (bf16[72,1792]{1,0:T(8,128)(2,1)S(1)}, bf16[72,1792]{1,0:T(8,128)(2,1)S(1)}, u32[]{:S(2)}, u32[]{:S(2)}) collective-permute-start(bf16[72,1792]{1,0:T(8,128)(2,1)S(1)} %get-tuple-element.57), channel_id=1, source_target_pairs={{0,2},{2,0},{4,6},{6,4},{8,10},{10,8},{12,14},{14,12},{1,3},{3,1},... | collective-permute-start | bytes 774152 | tf_op jit(solution)/shard_map/ppermute | solution.py:425
  63.2 1.4 %collective-permute-done.15.back_ref = bf16[72,1792]{1,0:T(8,128)(2,1)S(1)} collective-permute-done((bf16[72,1792]{1,0:T(8,128)(2,1)S(1)}, bf16[72,1792]{1,0:T(8,128)(2,1)S(1)}, u32[]{:S(2)}, u32[]{:S(2)}) %collective-permute-start.15) | collective-permute-done | bytes 258080 | tf_op jit(solution)/shard_map/ppermute | solution.py:425
  64.6 2.1 %collective-permute-done.19.refs_0_ = bf16[96,896]{1,0:T(8,128)(2,1)S(1)} collective-permute-done((bf16[96,896]{1,0:T(8,128)(2,1)S(1)}, bf16[96,896]{1,0:T(8,128)(2,1)S(1)}, u32[]{:S(2)}, u32[]{:S(2)}) %collective-permute-start.19) | collective-permute-done | bytes 172064 | tf_op jit(solution)/shard_map/ppermute | solution.py:425
  66.8 0.4 combine.7
  67.2 7.6 %collective-permute-start.20 = (bf16[96,896]{1,0:T(8,128)(2,1)S(1)}, bf16[96,896]{1,0:T(8,128)(2,1)S(1)}, u32[]{:S(2)}, u32[]{:S(2)}) collective-permute-start(bf16[96,896]{1,0:T(8,128)(2,1)S(1)} %combine.7), channel_id=1, source_target_pairs={{0,12},{2,14},{4,8},{6,10},{8,4},{10,6},{12,0},{14,2},{1,13},{3,15... | collective-permute-start | bytes 516104 | tf_op jit(solution)/shard_map/ppermute | solution.py:425
  74.8 0.4 combine.8
  75.2 1.4 %collective-permute-start.21 = (bf16[96,896]{1,0:T(8,128)(2,1)S(1)}, bf16[96,896]{1,0:T(8,128)(2,1)S(1)}, u32[]{:S(2)}, u32[]{:S(2)}) collective-permute-start(bf16[96,896]{1,0:T(8,128)(2,1)S(1)} %combine.8), channel_id=1, source_target_pairs={{0,12},{2,14},{4,8},{6,10},{8,4},{10,6},{12,0},{14,2},{1,13},{3,15... | collective-permute-start | bytes 516104 | tf_op jit(solution)/shard_map/ppermute | solution.py:425
  76.6 0.0 collective-permute-done.14.back_ref
  76.6 0.5 combine.9
  77.1 1.2 %collective-permute-start.22 = (bf16[96,896]{1,0:T(8,128)(2,1)S(1)}, bf16[96,896]{1,0:T(8,128)(2,1)S(1)}, u32[]{:S(2)}, u32[]{:S(2)}) collective-permute-start(bf16[96,896]{1,0:T(8,128)(2,1)S(1)} %get-tuple-element.72), channel_id=1, source_target_pairs={{0,4},{2,6},{4,0},{6,2},{8,12},{10,14},{12,8},{14,10},{1,5},{3,7},... | collective-permute-start | bytes 516104 | tf_op jit(solution)/shard_map/ppermute | solution.py:425
  78.3 0.9 %collective-permute-start.23 = (bf16[96,896]{1,0:T(8,128)(2,1)S(1)}, bf16[96,896]{1,0:T(8,128)(2,1)S(1)}, u32[]{:S(2)}, u32[]{:S(2)}) collective-permute-start(bf16[96,896]{1,0:T(8,128)(2,1)S(1)} %get-tuple-element.77), channel_id=1, source_target_pairs={{0,4},{2,6},{4,0},{6,2},{8,12},{10,14},{12,8},{14,10},{1,5},{3,7},... | collective-permute-start | bytes 516104 | tf_op jit(solution)/shard_map/ppermute | solution.py:425
  79.2 0.9 %collective-permute-done.20.refs_0_ = bf16[96,896]{1,0:T(8,128)(2,1)S(1)} collective-permute-done((bf16[96,896]{1,0:T(8,128)(2,1)S(1)}, bf16[96,896]{1,0:T(8,128)(2,1)S(1)}, u32[]{:S(2)}, u32[]{:S(2)}) %collective-permute-start.20) | collective-permute-done | bytes 172064 | tf_op jit(solution)/shard_map/ppermute | solution.py:425
  80.1 0.4 combine.10.refs_0_
  80.6 3.8 %collective-permute-done.21.refs_0_ = bf16[96,896]{1,0:T(8,128)(2,1)S(1)} collective-permute-done((bf16[96,896]{1,0:T(8,128)(2,1)S(1)}, bf16[96,896]{1,0:T(8,128)(2,1)S(1)}, u32[]{:S(2)}, u32[]{:S(2)}) %collective-permute-start.21) | collective-permute-done | bytes 172064 | tf_op jit(solution)/shard_map/ppermute | solution.py:425
  84.4 0.4 combine.11.refs_1_
  84.8 1.5 %collective-permute-done.22.refs_2_ = bf16[96,896]{1,0:T(8,128)(2,1)S(1)} collective-permute-done((bf16[96,896]{1,0:T(8,128)(2,1)S(1)}, bf16[96,896]{1,0:T(8,128)(2,1)S(1)}, u32[]{:S(2)}, u32[]{:S(2)}) %collective-permute-start.22) | collective-permute-done | bytes 172064 | tf_op jit(solution)/shard_map/ppermute | solution.py:425
  86.3 3.0 %collective-permute-done.23.refs_3_ = bf16[96,896]{1,0:T(8,128)(2,1)S(1)} collective-permute-done((bf16[96,896]{1,0:T(8,128)(2,1)S(1)}, bf16[96,896]{1,0:T(8,128)(2,1)S(1)}, u32[]{:S(2)}, u32[]{:S(2)}) %collective-permute-start.23) | collective-permute-done | bytes 172064 | tf_op jit(solution)/shard_map/ppermute | solution.py:425
  89.3 0.8 add_last.1
  (18 shorter events, 0.0 us)
Async XLA Ops:
  0.6 9.0 %copy-start.3 = (bf16[4,256,576]{1,2,0:T(8,128)(2,1)S(1)}, bf16[4,256,576]{1,2,0:T(8,128)(2,1)}, u32[]{:S(2)}) copy-start(bf16[4,256,576]{1,2,0:T(8,128)(2,1)} %param.11) | copy-start | bytes 3538948
  0.6 9.0 %copy-start.4 = (bf16[4,32,576]{2,1,0:T(8,128)(2,1)S(1)}, bf16[4,32,576]{2,1,0:T(8,128)(2,1)}, u32[]{:S(2)}) copy-start(bf16[4,32,576]{2,1,0:T(8,128)(2,1)} %query_ref) | copy-start | bytes 442372
  0.7 9.0 %copy-start.5 = (s32[32]{0:T(128)S(1)}, s32[32]{0:T(128)}, u32[]{:S(2)}) copy-start(s32[32]{0:T(128)} %param.12) | copy-start | bytes 388
  0.7 9.0 %copy-start.6 = (s32[32]{0:T(128)S(1)}, s32[32]{0:T(128)}, u32[]{:S(2)}) copy-start(s32[32]{0:T(128)} %param.13) | copy-start | bytes 388
  2.4 12.4 %collective-permute-start.2 = (bf16[512,1792]{1,0:T(8,128)(2,1)S(1)}, bf16[512,1792]{1,0:T(8,128)(2,1)S(1)}, u32[]{:S(2)}, u32[]{:S(2)}) collective-permute-start(bf16[512,1792]{1,0:T(8,128)(2,1)S(1)} %get-tuple-element.44), channel_id=1, source_target_pairs={{0,1},{1,0},{2,3},{3,2},{4,5},{5,4},{6,7},{7,6},{8,9},{9,8},{10,11... | collective-permute-start | bytes 5505032 | tf_op jit(solution)/shard_map/ppermute | solution.py:429
  3.0 11.8 %collective-permute-start = (bf16[96,1920]{1,0:T(8,128)(2,1)S(1)}, bf16[96,1920]{1,0:T(8,128)(2,1)S(1)}, u32[]{:S(2)}, u32[]{:S(2)}) collective-permute-start(bf16[96,1920]{1,0:T(8,128)(2,1)S(1)} %get-tuple-element.40.refs_0_.wide_ref), channel_id=1, source_target_pairs={{0,4},{2,6},{4,0},{6,2},{8,12},{10,14},{12,8},{14,10},{1,5},{3,7},... | collective-permute-start | bytes 1105928 | tf_op jit(solution)/shard_map/ppermute | solution.py:425
  5.6 8.3 %collective-permute-start.1 = (bf16[72,1792]{1,0:T(8,128)(2,1)S(1)}, bf16[72,1792]{1,0:T(8,128)(2,1)S(1)}, u32[]{:S(2)}, u32[]{:S(2)}) collective-permute-start(bf16[72,1792]{1,0:T(8,128)(2,1)S(1)} %get-tuple-element.42), channel_id=1, source_target_pairs={{0,2},{2,0},{4,6},{6,4},{8,10},{10,8},{12,14},{14,12},{1,3},{3,1},... | collective-permute-start | bytes 774152 | tf_op jit(solution)/shard_map/ppermute | solution.py:425
  7.1 17.9 %collective-permute-start.3 = (bf16[96,1920]{1,0:T(8,128)(2,1)S(1)}, bf16[96,1920]{1,0:T(8,128)(2,1)S(1)}, u32[]{:S(2)}, u32[]{:S(2)}) collective-permute-start(bf16[96,1920]{1,0:T(8,128)(2,1)S(1)} %get-tuple-element.40.refs_0_.wide_ref), channel_id=1, source_target_pairs={{0,12},{2,14},{4,8},{6,10},{8,4},{10,6},{12,0},{14,2},{1,13},{3,15... | collective-permute-start | bytes 1105928 | tf_op jit(solution)/shard_map/ppermute | solution.py:425
  15.3 11.5 %collective-permute-start.4 = (bf16[72,1792]{1,0:T(8,128)(2,1)S(1)}, bf16[72,1792]{1,0:T(8,128)(2,1)S(1)}, u32[]{:S(2)}, u32[]{:S(2)}) collective-permute-start(bf16[72,1792]{1,0:T(8,128)(2,1)S(1)} %cross_rows.3), channel_id=1, source_target_pairs={{0,2},{2,0},{4,6},{6,4},{8,10},{10,8},{12,14},{14,12},{1,3},{3,1},... | collective-permute-start | bytes 774152 | tf_op jit(solution)/shard_map/ppermute | solution.py:425
  25.0 10.1 %collective-permute-start.6 = (bf16[96,1920]{1,0:T(8,128)(2,1)S(1)}, bf16[96,1920]{1,0:T(8,128)(2,1)S(1)}, u32[]{:S(2)}, u32[]{:S(2)}) collective-permute-start(bf16[96,1920]{1,0:T(8,128)(2,1)S(1)} %collective-permute-done.3.wide_ref.refs_2_), channel_id=1, source_target_pairs={{0,4},{2,6},{4,0},{6,2},{8,12},{10,14},{12,8},{14,10},{1,5},{3,7},... | collective-permute-start | bytes 1105928 | tf_op jit(solution)/shard_map/ppermute | solution.py:425
  27.4 7.7 %collective-permute-start.7 = (bf16[72,1792]{1,0:T(8,128)(2,1)S(1)}, bf16[72,1792]{1,0:T(8,128)(2,1)S(1)}, u32[]{:S(2)}, u32[]{:S(2)}) collective-permute-start(bf16[72,1792]{1,0:T(8,128)(2,1)S(1)} %cross_rows.4), channel_id=1, source_target_pairs={{0,2},{2,0},{4,6},{6,4},{8,10},{10,8},{12,14},{14,12},{1,3},{3,1},... | collective-permute-start | bytes 774152 | tf_op jit(solution)/shard_map/ppermute | solution.py:425
  28.0 9.4 %collective-permute-start.5 = (bf16[368,1792]{1,0:T(8,128)(2,1)S(1)}, bf16[368,1792]{1,0:T(8,128)(2,1)S(1)}, u32[]{:S(2)}, u32[]{:S(2)}) collective-permute-start(bf16[368,1792]{1,0:T(8,128)(2,1)S(1)} %pack_rows.2.near_ref), channel_id=1, source_target_pairs={{0,1},{1,0},{2,3},{3,2},{4,5},{5,4},{6,7},{7,6},{8,9},{9,8},{10,11... | collective-permute-start | bytes 3956744 | tf_op jit(solution)/shard_map/ppermute | solution.py:429
  35.2 6.7 %collective-permute-start.10 = (bf16[256,1792]{1,0:T(8,128)(2,1)S(1)}, bf16[256,1792]{1,0:T(8,128)(2,1)S(1)}, u32[]{:S(2)}, u32[]{:S(2)}) collective-permute-start(bf16[256,1792]{1,0:T(8,128)(2,1)S(1)} %pack_rows.3.near_ref), channel_id=1, source_target_pairs={{0,1},{1,0},{2,3},{3,2},{4,5},{5,4},{6,7},{7,6},{8,9},{9,8},{10,11... | collective-permute-start | bytes 2752520 | tf_op jit(solution)/shard_map/ppermute | solution.py:429
  35.2 2.2 %copy-start.1 = (bf16[1,3584,512]{2,1,0:T(8,128)(2,1)S(1)}, bf16[1,3584,512]{2,1,0:T(8,128)(2,1)}, u32[]{:S(2)}) copy-start(bf16[1,3584,512]{2,1,0:T(8,128)(2,1)} %param.17) | copy-start | bytes 11010052
  35.3 3.2 %copy-start.2 = (bf16[1,3584,512]{2,1,0:T(8,128)(2,1)S(1)}, bf16[1,3584,512]{2,1,0:T(8,128)(2,1)}, u32[]{:S(2)}) copy-start(bf16[1,3584,512]{2,1,0:T(8,128)(2,1)} %param.18) | copy-start | bytes 11010052
  35.8 8.7 %collective-permute-start.9 = (bf16[72,1792]{1,0:T(8,128)(2,1)S(1)}, bf16[72,1792]{1,0:T(8,128)(2,1)S(1)}, u32[]{:S(2)}, u32[]{:S(2)}) collective-permute-start(bf16[72,1792]{1,0:T(8,128)(2,1)S(1)} %cross_rows.5), channel_id=1, source_target_pairs={{0,2},{2,0},{4,6},{6,4},{8,10},{10,8},{12,14},{14,12},{1,3},{3,1},... | collective-permute-start | bytes 774152 | tf_op jit(solution)/shard_map/ppermute | solution.py:425
  41.3 3.7 %collective-permute-start.8 = (bf16[368,512]{1,0:T(8,128)(2,1)S(1)}, bf16[368,512]{1,0:T(8,128)(2,1)S(1)}, u32[]{:S(2)}, u32[]{:S(2)}) collective-permute-start(bf16[368,512]{1,0:T(8,128)(2,1)S(1)} %hidden_units.3.refs_3_), channel_id=1, source_target_pairs={{0,1},{1,0},{2,3},{3,2},{4,5},{5,4},{6,7},{7,6},{8,9},{9,8},{10,11... | collective-permute-start | bytes 1130504 | tf_op jit(solution)/shard_map/ppermute | solution.py:429
  41.9 3.1 %copy-start = (bf16[1,512,3584]{2,1,0:T(8,128)(2,1)S(1)}, bf16[1,512,3584]{2,1,0:T(8,128)(2,1)}, u32[]{:S(2)}) copy-start(bf16[1,512,3584]{2,1,0:T(8,128)(2,1)} %refs_2_.1) | copy-start | bytes 11010052
  44.5 2.1 %collective-permute-start.13 = (bf16[72,1792]{1,0:T(8,128)(2,1)S(1)}, bf16[72,1792]{1,0:T(8,128)(2,1)S(1)}, u32[]{:S(2)}, u32[]{:S(2)}) collective-permute-start(bf16[72,1792]{1,0:T(8,128)(2,1)S(1)} %collective-permute-done.9.near_ref), channel_id=1, source_target_pairs={{0,1},{1,0},{2,3},{3,2},{4,5},{5,4},{6,7},{7,6},{8,9},{9,8},{10,11... | collective-permute-start | bytes 774152 | tf_op jit(solution)/shard_map/ppermute | solution.py:429
  44.5 3.6 %collective-permute-start.12 = (bf16[256,512]{1,0:T(8,128)(2,1)S(1)}, bf16[256,512]{1,0:T(8,128)(2,1)S(1)}, u32[]{:S(2)}, u32[]{:S(2)}) collective-permute-start(bf16[256,512]{1,0:T(8,128)(2,1)S(1)} %hidden_units.4.refs_1_), channel_id=1, source_target_pairs={{0,1},{1,0},{2,3},{3,2},{4,5},{5,4},{6,7},{7,6},{8,9},{9,8},{10,11... | collective-permute-start | bytes 786440 | tf_op jit(solution)/shard_map/ppermute | solution.py:429
  47.9 1.3 %collective-permute-start.16 = (bf16[72,512]{1,0:T(8,128)(2,1)S(1)}, bf16[72,512]{1,0:T(8,128)(2,1)S(1)}, u32[]{:S(2)}, u32[]{:S(2)}) collective-permute-start(bf16[72,512]{1,0:T(8,128)(2,1)S(1)} %hidden_units.5.refs_0_), channel_id=1, source_target_pairs={{0,1},{1,0},{2,3},{3,2},{4,5},{5,4},{6,7},{7,6},{8,9},{9,8},{10,11... | collective-permute-start | bytes 221192 | tf_op jit(solution)/shard_map/ppermute | solution.py:429
  50.0 9.1 %collective-permute-start.17 = (bf16[72,1792]{1,0:T(8,128)(2,1)S(1)}, bf16[72,1792]{1,0:T(8,128)(2,1)S(1)}, u32[]{:S(2)}, u32[]{:S(2)}) collective-permute-start(bf16[72,1792]{1,0:T(8,128)(2,1)S(1)} %down.5), channel_id=1, source_target_pairs={{0,2},{2,0},{4,6},{6,4},{8,10},{10,8},{12,14},{14,12},{1,3},{3,1},... | collective-permute-start | bytes 774152 | tf_op jit(solution)/shard_map/ppermute | solution.py:425
  51.6 13.0 %collective-permute-start.15 = (bf16[72,1792]{1,0:T(8,128)(2,1)S(1)}, bf16[72,1792]{1,0:T(8,128)(2,1)S(1)}, u32[]{:S(2)}, u32[]{:S(2)}) collective-permute-start(bf16[72,1792]{1,0:T(8,128)(2,1)S(1)} %get-tuple-element.63), channel_id=1, source_target_pairs={{0,2},{2,0},{4,6},{6,4},{8,10},{10,8},{12,14},{14,12},{1,3},{3,1},... | collective-permute-start | bytes 774152 | tf_op jit(solution)/shard_map/ppermute | solution.py:425
  52.1 24.5 %collective-permute-start.14 = (bf16[72,1792]{1,0:T(8,128)(2,1)S(1)}, bf16[72,1792]{1,0:T(8,128)(2,1)S(1)}, u32[]{:S(2)}, u32[]{:S(2)}) collective-permute-start(bf16[72,1792]{1,0:T(8,128)(2,1)S(1)} %get-tuple-element.61), channel_id=1, source_target_pairs={{0,2},{2,0},{4,6},{6,4},{8,10},{10,8},{12,14},{14,12},{1,3},{3,1},... | collective-permute-start | bytes 774152 | tf_op jit(solution)/shard_map/ppermute | solution.py:425
  59.6 7.2 %collective-permute-start.19 = (bf16[96,896]{1,0:T(8,128)(2,1)S(1)}, bf16[96,896]{1,0:T(8,128)(2,1)S(1)}, u32[]{:S(2)}, u32[]{:S(2)}) collective-permute-start(bf16[96,896]{1,0:T(8,128)(2,1)S(1)} %get-tuple-element.66), channel_id=1, source_target_pairs={{0,4},{2,6},{4,0},{6,2},{8,12},{10,14},{12,8},{14,10},{1,5},{3,7},... | collective-permute-start | bytes 516104 | tf_op jit(solution)/shard_map/ppermute | solution.py:425
  61.2 13.6 %collective-permute-start.18 = (bf16[96,896]{1,0:T(8,128)(2,1)S(1)}, bf16[96,896]{1,0:T(8,128)(2,1)S(1)}, u32[]{:S(2)}, u32[]{:S(2)}) collective-permute-start(bf16[96,896]{1,0:T(8,128)(2,1)S(1)} %get-tuple-element.68), channel_id=1, source_target_pairs={{0,4},{2,6},{4,0},{6,2},{8,12},{10,14},{12,8},{14,10},{1,5},{3,7},... | collective-permute-start | bytes 516104 | tf_op jit(solution)/shard_map/ppermute | solution.py:425
  61.7 17.6 %collective-permute-start.11 = (bf16[72,1792]{1,0:T(8,128)(2,1)S(1)}, bf16[72,1792]{1,0:T(8,128)(2,1)S(1)}, u32[]{:S(2)}, u32[]{:S(2)}) collective-permute-start(bf16[72,1792]{1,0:T(8,128)(2,1)S(1)} %get-tuple-element.57), channel_id=1, source_target_pairs={{0,2},{2,0},{4,6},{6,4},{8,10},{10,8},{12,14},{14,12},{1,3},{3,1},... | collective-permute-start | bytes 774152 | tf_op jit(solution)/shard_map/ppermute | solution.py:425
  67.2 13.0 %collective-permute-start.20 = (bf16[96,896]{1,0:T(8,128)(2,1)S(1)}, bf16[96,896]{1,0:T(8,128)(2,1)S(1)}, u32[]{:S(2)}, u32[]{:S(2)}) collective-permute-start(bf16[96,896]{1,0:T(8,128)(2,1)S(1)} %combine.7), channel_id=1, source_target_pairs={{0,12},{2,14},{4,8},{6,10},{8,4},{10,6},{12,0},{14,2},{1,13},{3,15... | collective-permute-start | bytes 516104 | tf_op jit(solution)/shard_map/ppermute | solution.py:425
  75.2 9.2 %collective-permute-start.21 = (bf16[96,896]{1,0:T(8,128)(2,1)S(1)}, bf16[96,896]{1,0:T(8,128)(2,1)S(1)}, u32[]{:S(2)}, u32[]{:S(2)}) collective-permute-start(bf16[96,896]{1,0:T(8,128)(2,1)S(1)} %combine.8), channel_id=1, source_target_pairs={{0,12},{2,14},{4,8},{6,10},{8,4},{10,6},{12,0},{14,2},{1,13},{3,15... | collective-permute-start | bytes 516104 | tf_op jit(solution)/shard_map/ppermute | solution.py:425
  77.1 9.2 %collective-permute-start.22 = (bf16[96,896]{1,0:T(8,128)(2,1)S(1)}, bf16[96,896]{1,0:T(8,128)(2,1)S(1)}, u32[]{:S(2)}, u32[]{:S(2)}) collective-permute-start(bf16[96,896]{1,0:T(8,128)(2,1)S(1)} %get-tuple-element.72), channel_id=1, source_target_pairs={{0,4},{2,6},{4,0},{6,2},{8,12},{10,14},{12,8},{14,10},{1,5},{3,7},... | collective-permute-start | bytes 516104 | tf_op jit(solution)/shard_map/ppermute | solution.py:425
  78.3 11.0 %collective-permute-start.23 = (bf16[96,896]{1,0:T(8,128)(2,1)S(1)}, bf16[96,896]{1,0:T(8,128)(2,1)S(1)}, u32[]{:S(2)}, u32[]{:S(2)}) collective-permute-start(bf16[96,896]{1,0:T(8,128)(2,1)S(1)} %get-tuple-element.77), channel_id=1, source_target_pairs={{0,4},{2,6},{4,0},{6,2},{8,12},{10,14},{12,8},{14,10},{1,5},{3,7},... | collective-permute-start | bytes 516104 | tf_op jit(solution)/shard_map/ppermute | solution.py:425

commit v7 on v6

--- a/solution.py
+++ b/solution.py
@@ -264,10 +264,15 @@
         out_ref[start : start + ref.shape[0], :] = ref[:, : out_ref.shape[1]]
 
 
-def pack(blocks, half):
+def pack(blocks, half, hint=0):
     starts, rows = row_starts(blocks)
     return call(
-        functools.partial(pack_kernel, starts), blocks, ((rows, half),), 0, "pack_rows"
+        functools.partial(pack_kernel, starts),
+        blocks,
+        ((rows, half),),
+        0,
+        "pack_rows",
+        hint=hint,
     )[0]
 
 
@@ -441,22 +446,22 @@
     wide, cross, down_away = prepare(
         tokens, w_down, expert_ids, gate_weights, role_count, capacity
     )
-    wide_mirror = swap(wide, mirror)
     wide_pair = swap(wide, pair)
     cross_in = swap(cross, row)
     w_gate, w_up = w_gate[0], w_up[0]
     down_other = swap_core(down_away)
     attended = attend(after(q_lat, wide), latent_cache, lengths, placement)
+    wide_mirror = swap(after(wide, attended), mirror)
     cross_in = after(cross_in, attended)
     wide_pair = after(wide_pair, cross_in, down_other)
     cross_pair = cross_rows(wide_pair, role_count, capacity)
     cross_pair_in = swap(cross_pair, row)
     wide_mirror = after(wide_mirror, cross_pair)
     wide_far = swap(wide_mirror, pair)
-    wide_mirror_ready = after(wide_mirror, cross_pair_in)
-    cross_mirror = cross_rows(wide_mirror_ready, role_count, capacity)
+    cross_mirror = cross_rows(wide_mirror, role_count, capacity)
     cross_mirror_in = swap(cross_mirror, row)
-    near_first = pack((wide, wide_pair, after(wide_mirror, cross_mirror), cross_in), half)
+    cross_pair_in = after(cross_pair_in, cross_mirror)
+    near_first = pack((after(wide, cross_pair_in), wide_pair, wide_mirror, cross_in), half)
     far_first = swap_core(near_first)
     wide_far = after(wide_far, near_first)
     cross_mirror_in = after(cross_mirror_in, wide_far)

time: 90.2 us -> 88.1 us (0.977)
  starting transfers between devices: 32.6 us -> 27.7 us
  waiting for transfers between devices: 37 us -> 38.8 us
  local copies, waits for them, and re-layouts: 1.04 us -> 2.06 us
    ppermute x17, starting transfers between devices: 30.8 us -> 25.9 us  [swap(): return lax.ppermute(array, 'role', pairs)]
    ppermute x17, waiting for transfers between devices: 36.9 us -> 38.7 us  [swap(): return lax.ppermute(array, 'role', pairs)]
    unnamed x14, local copies, waits for them, and re-layouts: 1.04 us -> 2.06 us
where the time goes in v7:
time: 88.1 us; the launch traced here: 87.9 us
  waiting for transfers between devices  38.8 us (44%)
  starting transfers between devices  27.7 us (31%)
  Pallas kernels  18.5 us (21%)
  local copies, waits for them, and re-layouts  2.06 us (2%)
    ppermute x17, waiting for transfers between devices, swap(): return lax.ppermute(array, 'role', pairs)  38.7 us
    ppermute x17, starting transfers between devices, swap(): return lax.ppermute(array, 'role', pairs)  25.9 us
    pallas_call x18, Pallas kernels, call(): pl.pallas_call(kernel, in_specs=[place] * len(operands), out_specs=[place...  14.7 us
    unnamed x14, local copies, waits for them, and re-layouts  2.06 us
    pallas_call x1, Pallas kernels, attend(): pl.pallas_call(attend_kernel, out_shape=jax.ShapeDtypeStruct((slot_count,...  2.06 us
    ppermute x7, starting transfers between devices, swap_core(): return lax.ppermute(array, 'tp', [(0, 1), (1, 0)])  1.81 us
    pallas_call x1, Pallas kernels, prepare(): pl.pallas_call(functools.partial(prepare_kernel, expert_count), in_specs=...  1.77 us
  transfers between devices with their start and end apart: 24, of which 13 were waited for; matrix products, arithmetic and copies ran while one was open for 0% of the time, Pallas kernels for 17%

profile of v7, /device:TPU:0, one launch (start us, length us, event | category | flops | bytes accessed | tf_op | source)
XLA Modules:
  0.0 87.9 jit_solution(11278649326858689348)
XLA Ops:
  0.7 1.8 %prepare.1 = (bf16[96,1920]{1,0:T(8,128)(2,1)S(1)}, bf16[72,1792]{1,0:T(8,128)(2,1)S(1)}, bf16[512,1792]{1,0:T(8,128)(2,1)S(1)}) custom-call(bf16[96,1792]{1,0:T(8,128)(2,1)} %tokens_hbm.1, bf16[1,512,3584]{2,1,0:T(8,128)(2,1)} %refs_2_.1, s32[4,96]{1,0:T(4,128)} %bitcast.16, f32[4,96]{1,0:T(4,128)} %bitcast.17), custom_call_target="tpu_custom_call" | custom-call | tf_op jit(solution)/shard_map/prepare/pallas_call | solution.py:212
  2.4 0.5 collective-permute-start.2
  3.0 2.6 %collective-permute-start = (bf16[96,1920]{1,0:T(8,128)(2,1)S(1)}, bf16[96,1920]{1,0:T(8,128)(2,1)S(1)}, u32[]{:S(2)}, u32[]{:S(2)}) collective-permute-start(bf16[96,1920]{1,0:T(8,128)(2,1)S(1)} %get-tuple-element.50.refs_0_.wide_ref), channel_id=1, source_target_pairs={{0,4},{2,6},{4,0},{6,2},{8,12},{10,14},{12,8},{14,10},{1,5},{3,7},... | collective-permute-start | bytes 1105928 | tf_op jit(solution)/shard_map/ppermute | solution.py:430
  5.6 1.5 %collective-permute-start.1 = (bf16[72,1792]{1,0:T(8,128)(2,1)S(1)}, bf16[72,1792]{1,0:T(8,128)(2,1)S(1)}, u32[]{:S(2)}, u32[]{:S(2)}) collective-permute-start(bf16[72,1792]{1,0:T(8,128)(2,1)S(1)} %get-tuple-element.43), channel_id=1, source_target_pairs={{0,2},{2,0},{4,6},{6,4},{8,10},{10,8},{12,14},{14,12},{1,3},{3,1},... | collective-permute-start | bytes 774152 | tf_op jit(solution)/shard_map/ppermute | solution.py:430
  7.2 2.1 %attend.1 = bf16[4,32,512]{2,1,0:T(8,128)(2,1)} custom-call(bf16[4,32,576]{2,1,0:T(8,128)(2,1)S(1)} %copy-done.4, bf16[4,576,256]{2,1,0:T(8,128)(2,1)S(1)} %bitcast.13, s32[1,32]{1,0:T(1,128)S(1)} %bitcast.14, s32[1,32]{1,0:T(1,128)S(1)} %bitcast.15), custom_call_target="tpu_custom_call" | custom-call | tf_op jit(solution)/shard_map/attend/pallas_call | solution.py:373
  9.2 2.5 %collective-permute-start.3 = (bf16[96,1920]{1,0:T(8,128)(2,1)S(1)}, bf16[96,1920]{1,0:T(8,128)(2,1)S(1)}, u32[]{:S(2)}, u32[]{:S(2)}) collective-permute-start(bf16[96,1920]{1,0:T(8,128)(2,1)S(1)} %get-tuple-element.50.refs_0_.wide_ref), channel_id=1, source_target_pairs={{0,12},{2,14},{4,8},{6,10},{8,4},{10,6},{12,0},{14,2},{1,13},{3,15... | collective-permute-start | bytes 1105928 | tf_op jit(solution)/shard_map/ppermute | solution.py:430
  11.7 2.2 %collective-permute-done.1.refs_3_ = bf16[72,1792]{1,0:T(8,128)(2,1)S(1)} collective-permute-done((bf16[72,1792]{1,0:T(8,128)(2,1)S(1)}, bf16[72,1792]{1,0:T(8,128)(2,1)S(1)}, u32[]{:S(2)}, u32[]{:S(2)}) %collective-permute-start.1) | collective-permute-done | bytes 258080 | tf_op jit(solution)/shard_map/ppermute | solution.py:430
  13.9 0.9 %collective-permute-done.wide_ref.refs_1_ = bf16[96,1920]{1,0:T(8,128)(2,1)S(1)} collective-permute-done((bf16[96,1920]{1,0:T(8,128)(2,1)S(1)}, bf16[96,1920]{1,0:T(8,128)(2,1)S(1)}, u32[]{:S(2)}, u32[]{:S(2)}) %collective-permute-start) | collective-permute-done | bytes 368672 | tf_op jit(solution)/shard_map/ppermute | solution.py:430
  14.8 0.0 collective-permute-done.2.refs_6_.refs_4_.refs_3_
  14.8 0.5 cross_rows.3
  15.3 1.8 %collective-permute-start.4 = (bf16[72,1792]{1,0:T(8,128)(2,1)S(1)}, bf16[72,1792]{1,0:T(8,128)(2,1)S(1)}, u32[]{:S(2)}, u32[]{:S(2)}) collective-permute-start(bf16[72,1792]{1,0:T(8,128)(2,1)S(1)} %cross_rows.3), channel_id=1, source_target_pairs={{0,2},{2,0},{4,6},{6,4},{8,10},{10,8},{12,14},{14,12},{1,3},{3,1},... | collective-permute-start | bytes 774152 | tf_op jit(solution)/shard_map/ppermute | solution.py:430
  17.1 7.9 %collective-permute-done.3.wide_ref.refs_2_ = bf16[96,1920]{1,0:T(8,128)(2,1)S(1)} collective-permute-done((bf16[96,1920]{1,0:T(8,128)(2,1)S(1)}, bf16[96,1920]{1,0:T(8,128)(2,1)S(1)}, u32[]{:S(2)}, u32[]{:S(2)}) %collective-permute-start.3) | collective-permute-done | bytes 368672 | tf_op jit(solution)/shard_map/ppermute | solution.py:430
  25.0 3.9 %collective-permute-start.6 = (bf16[96,1920]{1,0:T(8,128)(2,1)S(1)}, bf16[96,1920]{1,0:T(8,128)(2,1)S(1)}, u32[]{:S(2)}, u32[]{:S(2)}) collective-permute-start(bf16[96,1920]{1,0:T(8,128)(2,1)S(1)} %collective-permute-done.3.wide_ref.refs_2_), channel_id=1, source_target_pairs={{0,4},{2,6},{4,0},{6,2},{8,12},{10,14},{12,8},{14,10},{1,5},{3,7},... | collective-permute-start | bytes 1105928 | tf_op jit(solution)/shard_map/ppermute | solution.py:430
  28.9 0.5 cross_rows.4
  29.4 0.6 collective-permute-start.7
  30.0 0.1 pack_rows.2.near_ref
  30.1 0.1 collective-permute-start.5
  30.2 6.8 %collective-permute-done.6.refs_0_.wide_ref = bf16[96,1920]{1,0:T(8,128)(2,1)S(1)} collective-permute-done((bf16[96,1920]{1,0:T(8,128)(2,1)S(1)}, bf16[96,1920]{1,0:T(8,128)(2,1)S(1)}, u32[]{:S(2)}, u32[]{:S(2)}) %collective-permute-start.6) | collective-permute-done | bytes 368672 | tf_op jit(solution)/shard_map/ppermute | solution.py:430
  37.0 0.1 pack_rows.3.near_ref
  37.0 0.1 collective-permute-start.10
  37.1 0.0 copy-start.1
  37.1 0.0 copy-start.2
  37.2 0.5 cross_rows.5
  37.7 0.6 collective-permute-start.9
  38.3 0.9 %copy-done.1 = bf16[1,3584,512]{2,1,0:T(8,128)(2,1)S(1)} copy-done((bf16[1,3584,512]{2,1,0:T(8,128)(2,1)S(1)}, bf16[1,3584,512]{2,1,0:T(8,128)(2,1)}, u32[]{:S(2)}) %copy-start.1) | copy-done | bytes 3670040
  39.2 1.1 %copy-done.2 = bf16[1,3584,512]{2,1,0:T(8,128)(2,1)S(1)} copy-done((bf16[1,3584,512]{2,1,0:T(8,128)(2,1)S(1)}, bf16[1,3584,512]{2,1,0:T(8,128)(2,1)}, u32[]{:S(2)}) %copy-start.2) | copy-done | bytes 3670040
  40.3 2.9 %hidden_units.3.refs_3_ = bf16[368,512]{1,0:T(8,128)(2,1)S(1)} custom-call(bf16[368,1792]{1,0:T(8,128)(2,1)S(1)} %pack_rows.2.near_ref, bf16[368,1792]{1,0:T(8,128)(2,1)S(1)} %collective-permute-done.5.far_ref, bf16[3584,512]{1,0:T(8,128)(2,1)S(1)} %bitcast.7, bf16[3584,512]{1,0:T(8,128)(2,1)S(1)} %bitcast.10), custom_call_target="tpu_custom_call" | custom-call | tf_op jit(solution)/shard_map/hidden_units/pallas_call | solution.py:91
  43.2 0.6 collective-permute-start.8
  43.7 2.1 %hidden_units.4.refs_1_ = bf16[256,512]{1,0:T(8,128)(2,1)S(1)} custom-call(bf16[256,1792]{1,0:T(8,128)(2,1)S(1)} %pack_rows.3.near_ref, bf16[256,1792]{1,0:T(8,128)(2,1)S(1)} %collective-permute-done.10.far_ref, bf16[3584,512]{1,0:T(8,128)(2,1)S(1)} %bitcast.8, bf16[3584,512]{1,0:T(8,128)(2,1)S(1)} %bitcast.11), custom_call_target="tpu_custom_call" | custom-call | tf_op jit(solution)/shard_map/hidden_units/pallas_call | solution.py:91
  45.8 0.5 collective-permute-done.9.near_ref
  46.3 0.5 collective-permute-start.12
  46.9 0.0 collective-permute-done.8.refs_4_
  46.9 1.5 %down.3 = (f32[96,1792]{1,0:T(8,128)S(1)}, f32[96,1792]{1,0:T(8,128)S(1)}, f32[96,1792]{1,0:T(8,128)S(1)}, bf16[72,1792]{1,0:T(8,128)(2,1)S(1)}) custom-call(bf16[96,1920]{1,0:T(8,128)(2,1)S(1)} %get-tuple-element.50.refs_0_.wide_ref, bf16[96,1920]{1,0:T(8,128)(2,1)S(1)} %collective-permute-done.wide_ref.refs_1_, ...), custom_call_target="tpu_custom_call" | custom-call | tf_op jit(solution)/shard_map/down/pallas_call | solution.py:91
  48.4 0.0 collective-permute-done.13.far_ref
  48.4 1.4 %hidden_units.5.refs_0_ = bf16[72,512]{1,0:T(8,128)(2,1)S(1)} custom-call(bf16[72,1792]{1,0:T(8,128)(2,1)S(1)} %collective-permute-done.9.near_ref, bf16[72,1792]{1,0:T(8,128)(2,1)S(1)} %collective-permute-done.13.far_ref, bf16[3584,512]{1,0:T(8,128)(2,1)S(1)} %bitcast.9, bf16[3584,512]{1,0:T(8,128)(2,1)S(1)} %bitcast.12), custom_call_target="tpu_custom_call" | custom-call | tf_op jit(solution)/shard_map/hidden_units/pallas_call | solution.py:91
  49.8 0.1 collective-permute-start.16
  49.9 1.1 %down.4 = (f32[96,1792]{1,0:T(8,128)S(1)}, bf16[72,1792]{1,0:T(8,128)(2,1)S(1)}, bf16[72,1792]{1,0:T(8,128)(2,1)S(1)}) custom-call(bf16[96,1920]{1,0:T(8,128)(2,1)S(1)} %collective-permute-done.6.refs_0_.wide_ref, bf16[256,512]{1,0:T(8,128)(2,1)S(1)} %hidden_units.4.refs_1_, bf16[256,512]{1,0:T(8,128)(2,1)S(1)} %collective-permute-done.12.refs_2_, ...), custom_call_target="tpu_custom_call" | custom-call | tf_op jit(solution)/shard_map/down/pallas_call | solution.py:91
  51.0 0.1 collective-permute-done.16.refs_1_
  51.2 0.7 down.5
  51.9 0.6 collective-permute-start.17
  52.5 1.5 %collective-permute-start.15 = (bf16[72,1792]{1,0:T(8,128)(2,1)S(1)}, bf16[72,1792]{1,0:T(8,128)(2,1)S(1)}, u32[]{:S(2)}, u32[]{:S(2)}) collective-permute-start(bf16[72,1792]{1,0:T(8,128)(2,1)S(1)} %get-tuple-element.65), channel_id=1, source_target_pairs={{0,2},{2,0},{4,6},{6,4},{8,10},{10,8},{12,14},{14,12},{1,3},{3,1},... | collective-permute-start | bytes 774152 | tf_op jit(solution)/shard_map/ppermute | solution.py:430
  54.0 0.5 collective-permute-start.14
  54.5 6.5 %collective-permute-done.17.back_ref = bf16[72,1792]{1,0:T(8,128)(2,1)S(1)} collective-permute-done((bf16[72,1792]{1,0:T(8,128)(2,1)S(1)}, bf16[72,1792]{1,0:T(8,128)(2,1)S(1)}, u32[]{:S(2)}, u32[]{:S(2)}) %collective-permute-start.17) | collective-permute-done | bytes 258080 | tf_op jit(solution)/shard_map/ppermute | solution.py:430
  61.0 0.4 combine.6
  61.4 1.8 %collective-permute-start.19 = (bf16[96,896]{1,0:T(8,128)(2,1)S(1)}, bf16[96,896]{1,0:T(8,128)(2,1)S(1)}, u32[]{:S(2)}, u32[]{:S(2)}) collective-permute-start(bf16[96,896]{1,0:T(8,128)(2,1)S(1)} %get-tuple-element.68), channel_id=1, source_target_pairs={{0,4},{2,6},{4,0},{6,2},{8,12},{10,14},{12,8},{14,10},{1,5},{3,7},... | collective-permute-start | bytes 516104 | tf_op jit(solution)/shard_map/ppermute | solution.py:430
  63.3 0.3 collective-permute-start.18
  63.5 0.5 collective-permute-start.11
  64.1 2.5 %collective-permute-done.15.back_ref = bf16[72,1792]{1,0:T(8,128)(2,1)S(1)} collective-permute-done((bf16[72,1792]{1,0:T(8,128)(2,1)S(1)}, bf16[72,1792]{1,0:T(8,128)(2,1)S(1)}, u32[]{:S(2)}, u32[]{:S(2)}) %collective-permute-start.15) | collective-permute-done | bytes 258080 | tf_op jit(solution)/shard_map/ppermute | solution.py:430
  66.5 2.1 %collective-permute-done.19.refs_0_ = bf16[96,896]{1,0:T(8,128)(2,1)S(1)} collective-permute-done((bf16[96,896]{1,0:T(8,128)(2,1)S(1)}, bf16[96,896]{1,0:T(8,128)(2,1)S(1)}, u32[]{:S(2)}, u32[]{:S(2)}) %collective-permute-start.19) | collective-permute-done | bytes 172064 | tf_op jit(solution)/shard_map/ppermute | solution.py:430
  68.7 0.4 combine.7
  69.1 2.4 %collective-permute-start.20 = (bf16[96,896]{1,0:T(8,128)(2,1)S(1)}, bf16[96,896]{1,0:T(8,128)(2,1)S(1)}, u32[]{:S(2)}, u32[]{:S(2)}) collective-permute-start(bf16[96,896]{1,0:T(8,128)(2,1)S(1)} %combine.7), channel_id=1, source_target_pairs={{0,12},{2,14},{4,8},{6,10},{8,4},{10,6},{12,0},{14,2},{1,13},{3,15... | collective-permute-start | bytes 516104 | tf_op jit(solution)/shard_map/ppermute | solution.py:430
  71.5 0.0 collective-permute-done.18.refs_0_
  71.5 0.4 combine.8
  71.9 2.7 %collective-permute-start.21 = (bf16[96,896]{1,0:T(8,128)(2,1)S(1)}, bf16[96,896]{1,0:T(8,128)(2,1)S(1)}, u32[]{:S(2)}, u32[]{:S(2)}) collective-permute-start(bf16[96,896]{1,0:T(8,128)(2,1)S(1)} %combine.8), channel_id=1, source_target_pairs={{0,12},{2,14},{4,8},{6,10},{8,4},{10,6},{12,0},{14,2},{1,13},{3,15... | collective-permute-start | bytes 516104 | tf_op jit(solution)/shard_map/ppermute | solution.py:430
  74.6 0.5 combine.9
  75.0 1.6 %collective-permute-start.22 = (bf16[96,896]{1,0:T(8,128)(2,1)S(1)}, bf16[96,896]{1,0:T(8,128)(2,1)S(1)}, u32[]{:S(2)}, u32[]{:S(2)}) collective-permute-start(bf16[96,896]{1,0:T(8,128)(2,1)S(1)} %get-tuple-element.74), channel_id=1, source_target_pairs={{0,4},{2,6},{4,0},{6,2},{8,12},{10,14},{12,8},{14,10},{1,5},{3,7},... | collective-permute-start | bytes 516104 | tf_op jit(solution)/shard_map/ppermute | solution.py:430
  76.7 0.4 collective-permute-start.23
  77.1 1.2 %collective-permute-done.20.refs_0_ = bf16[96,896]{1,0:T(8,128)(2,1)S(1)} collective-permute-done((bf16[96,896]{1,0:T(8,128)(2,1)S(1)}, bf16[96,896]{1,0:T(8,128)(2,1)S(1)}, u32[]{:S(2)}, u32[]{:S(2)}) %collective-permute-start.20) | collective-permute-done | bytes 172064 | tf_op jit(solution)/shard_map/ppermute | solution.py:430
  78.3 0.4 combine.10.refs_0_
  78.7 3.3 %collective-permute-done.21.refs_0_ = bf16[96,896]{1,0:T(8,128)(2,1)S(1)} collective-permute-done((bf16[96,896]{1,0:T(8,128)(2,1)S(1)}, bf16[96,896]{1,0:T(8,128)(2,1)S(1)}, u32[]{:S(2)}, u32[]{:S(2)}) %collective-permute-start.21) | collective-permute-done | bytes 172064 | tf_op jit(solution)/shard_map/ppermute | solution.py:430
  82.0 0.4 combine.11.refs_1_
  82.4 1.7 %collective-permute-done.22.refs_2_ = bf16[96,896]{1,0:T(8,128)(2,1)S(1)} collective-permute-done((bf16[96,896]{1,0:T(8,128)(2,1)S(1)}, bf16[96,896]{1,0:T(8,128)(2,1)S(1)}, u32[]{:S(2)}, u32[]{:S(2)}) %collective-permute-start.22) | collective-permute-done | bytes 172064 | tf_op jit(solution)/shard_map/ppermute | solution.py:430
  84.1 3.1 %collective-permute-done.23.refs_3_ = bf16[96,896]{1,0:T(8,128)(2,1)S(1)} collective-permute-done((bf16[96,896]{1,0:T(8,128)(2,1)S(1)}, bf16[96,896]{1,0:T(8,128)(2,1)S(1)}, u32[]{:S(2)}, u32[]{:S(2)}) %collective-permute-start.23) | collective-permute-done | bytes 172064 | tf_op jit(solution)/shard_map/ppermute | solution.py:430
  87.1 0.8 add_last.1
  (18 shorter events, 0.0 us)
Async XLA Ops:
  0.6 6.5 %copy-start.3 = (bf16[4,256,576]{1,2,0:T(8,128)(2,1)S(1)}, bf16[4,256,576]{1,2,0:T(8,128)(2,1)}, u32[]{:S(2)}) copy-start(bf16[4,256,576]{1,2,0:T(8,128)(2,1)} %param.11) | copy-start | bytes 3538948
  0.6 6.5 %copy-start.4 = (bf16[4,32,576]{2,1,0:T(8,128)(2,1)S(1)}, bf16[4,32,576]{2,1,0:T(8,128)(2,1)}, u32[]{:S(2)}) copy-start(bf16[4,32,576]{2,1,0:T(8,128)(2,1)} %query_ref) | copy-start | bytes 442372
  0.7 6.5 %copy-start.5 = (s32[32]{0:T(128)S(1)}, s32[32]{0:T(128)}, u32[]{:S(2)}) copy-start(s32[32]{0:T(128)} %param.12) | copy-start | bytes 388
  0.7 6.5 %copy-start.6 = (s32[32]{0:T(128)S(1)}, s32[32]{0:T(128)}, u32[]{:S(2)}) copy-start(s32[32]{0:T(128)} %param.13) | copy-start | bytes 388
  2.4 12.4 %collective-permute-start.2 = (bf16[512,1792]{1,0:T(8,128)(2,1)S(1)}, bf16[512,1792]{1,0:T(8,128)(2,1)S(1)}, u32[]{:S(2)}, u32[]{:S(2)}) collective-permute-start(bf16[512,1792]{1,0:T(8,128)(2,1)S(1)} %get-tuple-element.45), channel_id=1, source_target_pairs={{0,1},{1,0},{2,3},{3,2},{4,5},{5,4},{6,7},{7,6},{8,9},{9,8},{10,11... | collective-permute-start | bytes 5505032 | tf_op jit(solution)/shard_map/ppermute | solution.py:434
  3.0 11.8 %collective-permute-start = (bf16[96,1920]{1,0:T(8,128)(2,1)S(1)}, bf16[96,1920]{1,0:T(8,128)(2,1)S(1)}, u32[]{:S(2)}, u32[]{:S(2)}) collective-permute-start(bf16[96,1920]{1,0:T(8,128)(2,1)S(1)} %get-tuple-element.50.refs_0_.wide_ref), channel_id=1, source_target_pairs={{0,4},{2,6},{4,0},{6,2},{8,12},{10,14},{12,8},{14,10},{1,5},{3,7},... | collective-permute-start | bytes 1105928 | tf_op jit(solution)/shard_map/ppermute | solution.py:430
  5.6 8.3 %collective-permute-start.1 = (bf16[72,1792]{1,0:T(8,128)(2,1)S(1)}, bf16[72,1792]{1,0:T(8,128)(2,1)S(1)}, u32[]{:S(2)}, u32[]{:S(2)}) collective-permute-start(bf16[72,1792]{1,0:T(8,128)(2,1)S(1)} %get-tuple-element.43), channel_id=1, source_target_pairs={{0,2},{2,0},{4,6},{6,4},{8,10},{10,8},{12,14},{14,12},{1,3},{3,1},... | collective-permute-start | bytes 774152 | tf_op jit(solution)/shard_map/ppermute | solution.py:430
  9.2 15.8 %collective-permute-start.3 = (bf16[96,1920]{1,0:T(8,128)(2,1)S(1)}, bf16[96,1920]{1,0:T(8,128)(2,1)S(1)}, u32[]{:S(2)}, u32[]{:S(2)}) collective-permute-start(bf16[96,1920]{1,0:T(8,128)(2,1)S(1)} %get-tuple-element.50.refs_0_.wide_ref), channel_id=1, source_target_pairs={{0,12},{2,14},{4,8},{6,10},{8,4},{10,6},{12,0},{14,2},{1,13},{3,15... | collective-permute-start | bytes 1105928 | tf_op jit(solution)/shard_map/ppermute | solution.py:430
  15.3 14.7 %collective-permute-start.4 = (bf16[72,1792]{1,0:T(8,128)(2,1)S(1)}, bf16[72,1792]{1,0:T(8,128)(2,1)S(1)}, u32[]{:S(2)}, u32[]{:S(2)}) collective-permute-start(bf16[72,1792]{1,0:T(8,128)(2,1)S(1)} %cross_rows.3), channel_id=1, source_target_pairs={{0,2},{2,0},{4,6},{6,4},{8,10},{10,8},{12,14},{14,12},{1,3},{3,1},... | collective-permute-start | bytes 774152 | tf_op jit(solution)/shard_map/ppermute | solution.py:430
  25.0 12.0 %collective-permute-start.6 = (bf16[96,1920]{1,0:T(8,128)(2,1)S(1)}, bf16[96,1920]{1,0:T(8,128)(2,1)S(1)}, u32[]{:S(2)}, u32[]{:S(2)}) collective-permute-start(bf16[96,1920]{1,0:T(8,128)(2,1)S(1)} %collective-permute-done.3.wide_ref.refs_2_), channel_id=1, source_target_pairs={{0,4},{2,6},{4,0},{6,2},{8,12},{10,14},{12,8},{14,10},{1,5},{3,7},... | collective-permute-start | bytes 1105928 | tf_op jit(solution)/shard_map/ppermute | solution.py:430
  29.4 7.6 %collective-permute-start.7 = (bf16[72,1792]{1,0:T(8,128)(2,1)S(1)}, bf16[72,1792]{1,0:T(8,128)(2,1)S(1)}, u32[]{:S(2)}, u32[]{:S(2)}) collective-permute-start(bf16[72,1792]{1,0:T(8,128)(2,1)S(1)} %cross_rows.4), channel_id=1, source_target_pairs={{0,2},{2,0},{4,6},{6,4},{8,10},{10,8},{12,14},{14,12},{1,3},{3,1},... | collective-permute-start | bytes 774152 | tf_op jit(solution)/shard_map/ppermute | solution.py:430
  30.1 8.2 %collective-permute-start.5 = (bf16[368,1792]{1,0:T(8,128)(2,1)S(1)}, bf16[368,1792]{1,0:T(8,128)(2,1)S(1)}, u32[]{:S(2)}, u32[]{:S(2)}) collective-permute-start(bf16[368,1792]{1,0:T(8,128)(2,1)S(1)} %pack_rows.2.near_ref), channel_id=1, source_target_pairs={{0,1},{1,0},{2,3},{3,2},{4,5},{5,4},{6,7},{7,6},{8,9},{9,8},{10,11... | collective-permute-start | bytes 3956744 | tf_op jit(solution)/shard_map/ppermute | solution.py:434
  37.0 6.7 %collective-permute-start.10 = (bf16[256,1792]{1,0:T(8,128)(2,1)S(1)}, bf16[256,1792]{1,0:T(8,128)(2,1)S(1)}, u32[]{:S(2)}, u32[]{:S(2)}) collective-permute-start(bf16[256,1792]{1,0:T(8,128)(2,1)S(1)} %pack_rows.3.near_ref), channel_id=1, source_target_pairs={{0,1},{1,0},{2,3},{3,2},{4,5},{5,4},{6,7},{7,6},{8,9},{9,8},{10,11... | collective-permute-start | bytes 2752520 | tf_op jit(solution)/shard_map/ppermute | solution.py:434
  37.1 2.0 %copy-start.1 = (bf16[1,3584,512]{2,1,0:T(8,128)(2,1)S(1)}, bf16[1,3584,512]{2,1,0:T(8,128)(2,1)}, u32[]{:S(2)}) copy-start(bf16[1,3584,512]{2,1,0:T(8,128)(2,1)} %param.17) | copy-start | bytes 11010052
  37.1 3.2 %copy-start.2 = (bf16[1,3584,512]{2,1,0:T(8,128)(2,1)S(1)}, bf16[1,3584,512]{2,1,0:T(8,128)(2,1)}, u32[]{:S(2)}) copy-start(bf16[1,3584,512]{2,1,0:T(8,128)(2,1)} %param.18) | copy-start | bytes 11010052
  37.7 8.7 %collective-permute-start.9 = (bf16[72,1792]{1,0:T(8,128)(2,1)S(1)}, bf16[72,1792]{1,0:T(8,128)(2,1)S(1)}, u32[]{:S(2)}, u32[]{:S(2)}) collective-permute-start(bf16[72,1792]{1,0:T(8,128)(2,1)S(1)} %cross_rows.5), channel_id=1, source_target_pairs={{0,2},{2,0},{4,6},{6,4},{8,10},{10,8},{12,14},{14,12},{1,3},{3,1},... | collective-permute-start | bytes 774152 | tf_op jit(solution)/shard_map/ppermute | solution.py:430
  43.2 3.7 %collective-permute-start.8 = (bf16[368,512]{1,0:T(8,128)(2,1)S(1)}, bf16[368,512]{1,0:T(8,128)(2,1)S(1)}, u32[]{:S(2)}, u32[]{:S(2)}) collective-permute-start(bf16[368,512]{1,0:T(8,128)(2,1)S(1)} %hidden_units.3.refs_3_), channel_id=1, source_target_pairs={{0,1},{1,0},{2,3},{3,2},{4,5},{5,4},{6,7},{7,6},{8,9},{9,8},{10,11... | collective-permute-start | bytes 1130504 | tf_op jit(solution)/shard_map/ppermute | solution.py:434
  43.7 3.1 %copy-start = (bf16[1,512,3584]{2,1,0:T(8,128)(2,1)S(1)}, bf16[1,512,3584]{2,1,0:T(8,128)(2,1)}, u32[]{:S(2)}) copy-start(bf16[1,512,3584]{2,1,0:T(8,128)(2,1)} %refs_2_.1) | copy-start | bytes 11010052
  46.3 2.1 %collective-permute-start.13 = (bf16[72,1792]{1,0:T(8,128)(2,1)S(1)}, bf16[72,1792]{1,0:T(8,128)(2,1)S(1)}, u32[]{:S(2)}, u32[]{:S(2)}) collective-permute-start(bf16[72,1792]{1,0:T(8,128)(2,1)S(1)} %collective-permute-done.9.near_ref), channel_id=1, source_target_pairs={{0,1},{1,0},{2,3},{3,2},{4,5},{5,4},{6,7},{7,6},{8,9},{9,8},{10,11... | collective-permute-start | bytes 774152 | tf_op jit(solution)/shard_map/ppermute | solution.py:434
  46.3 3.6 %collective-permute-start.12 = (bf16[256,512]{1,0:T(8,128)(2,1)S(1)}, bf16[256,512]{1,0:T(8,128)(2,1)S(1)}, u32[]{:S(2)}, u32[]{:S(2)}) collective-permute-start(bf16[256,512]{1,0:T(8,128)(2,1)S(1)} %hidden_units.4.refs_1_), channel_id=1, source_target_pairs={{0,1},{1,0},{2,3},{3,2},{4,5},{5,4},{6,7},{7,6},{8,9},{9,8},{10,11... | collective-permute-start | bytes 786440 | tf_op jit(solution)/shard_map/ppermute | solution.py:434
  49.8 1.3 %collective-permute-start.16 = (bf16[72,512]{1,0:T(8,128)(2,1)S(1)}, bf16[72,512]{1,0:T(8,128)(2,1)S(1)}, u32[]{:S(2)}, u32[]{:S(2)}) collective-permute-start(bf16[72,512]{1,0:T(8,128)(2,1)S(1)} %hidden_units.5.refs_0_), channel_id=1, source_target_pairs={{0,1},{1,0},{2,3},{3,2},{4,5},{5,4},{6,7},{7,6},{8,9},{9,8},{10,11... | collective-permute-start | bytes 221192 | tf_op jit(solution)/shard_map/ppermute | solution.py:434
  51.9 9.1 %collective-permute-start.17 = (bf16[72,1792]{1,0:T(8,128)(2,1)S(1)}, bf16[72,1792]{1,0:T(8,128)(2,1)S(1)}, u32[]{:S(2)}, u32[]{:S(2)}) collective-permute-start(bf16[72,1792]{1,0:T(8,128)(2,1)S(1)} %down.5), channel_id=1, source_target_pairs={{0,2},{2,0},{4,6},{6,4},{8,10},{10,8},{12,14},{14,12},{1,3},{3,1},... | collective-permute-start | bytes 774152 | tf_op jit(solution)/shard_map/ppermute | solution.py:430
  52.5 14.1 %collective-permute-start.15 = (bf16[72,1792]{1,0:T(8,128)(2,1)S(1)}, bf16[72,1792]{1,0:T(8,128)(2,1)S(1)}, u32[]{:S(2)}, u32[]{:S(2)}) collective-permute-start(bf16[72,1792]{1,0:T(8,128)(2,1)S(1)} %get-tuple-element.65), channel_id=1, source_target_pairs={{0,2},{2,0},{4,6},{6,4},{8,10},{10,8},{12,14},{14,12},{1,3},{3,1},... | collective-permute-start | bytes 774152 | tf_op jit(solution)/shard_map/ppermute | solution.py:430
  54.0 20.6 %collective-permute-start.14 = (bf16[72,1792]{1,0:T(8,128)(2,1)S(1)}, bf16[72,1792]{1,0:T(8,128)(2,1)S(1)}, u32[]{:S(2)}, u32[]{:S(2)}) collective-permute-start(bf16[72,1792]{1,0:T(8,128)(2,1)S(1)} %get-tuple-element.63), channel_id=1, source_target_pairs={{0,2},{2,0},{4,6},{6,4},{8,10},{10,8},{12,14},{14,12},{1,3},{3,1},... | collective-permute-start | bytes 774152 | tf_op jit(solution)/shard_map/ppermute | solution.py:430
  61.4 7.2 %collective-permute-start.19 = (bf16[96,896]{1,0:T(8,128)(2,1)S(1)}, bf16[96,896]{1,0:T(8,128)(2,1)S(1)}, u32[]{:S(2)}, u32[]{:S(2)}) collective-permute-start(bf16[96,896]{1,0:T(8,128)(2,1)S(1)} %get-tuple-element.68), channel_id=1, source_target_pairs={{0,4},{2,6},{4,0},{6,2},{8,12},{10,14},{12,8},{14,10},{1,5},{3,7},... | collective-permute-start | bytes 516104 | tf_op jit(solution)/shard_map/ppermute | solution.py:430
  63.3 8.2 %collective-permute-start.18 = (bf16[96,896]{1,0:T(8,128)(2,1)S(1)}, bf16[96,896]{1,0:T(8,128)(2,1)S(1)}, u32[]{:S(2)}, u32[]{:S(2)}) collective-permute-start(bf16[96,896]{1,0:T(8,128)(2,1)S(1)} %get-tuple-element.70), channel_id=1, source_target_pairs={{0,4},{2,6},{4,0},{6,2},{8,12},{10,14},{12,8},{14,10},{1,5},{3,7},... | collective-permute-start | bytes 516104 | tf_op jit(solution)/shard_map/ppermute | solution.py:430
  63.5 13.6 %collective-permute-start.11 = (bf16[72,1792]{1,0:T(8,128)(2,1)S(1)}, bf16[72,1792]{1,0:T(8,128)(2,1)S(1)}, u32[]{:S(2)}, u32[]{:S(2)}) collective-permute-start(bf16[72,1792]{1,0:T(8,128)(2,1)S(1)} %get-tuple-element.59), channel_id=1, source_target_pairs={{0,2},{2,0},{4,6},{6,4},{8,10},{10,8},{12,14},{14,12},{1,3},{3,1},... | collective-permute-start | bytes 774152 | tf_op jit(solution)/shard_map/ppermute | solution.py:430
  69.1 9.2 %collective-permute-start.20 = (bf16[96,896]{1,0:T(8,128)(2,1)S(1)}, bf16[96,896]{1,0:T(8,128)(2,1)S(1)}, u32[]{:S(2)}, u32[]{:S(2)}) collective-permute-start(bf16[96,896]{1,0:T(8,128)(2,1)S(1)} %combine.7), channel_id=1, source_target_pairs={{0,12},{2,14},{4,8},{6,10},{8,4},{10,6},{12,0},{14,2},{1,13},{3,15... | collective-permute-start | bytes 516104 | tf_op jit(solution)/shard_map/ppermute | solution.py:430
  71.9 10.1 %collective-permute-start.21 = (bf16[96,896]{1,0:T(8,128)(2,1)S(1)}, bf16[96,896]{1,0:T(8,128)(2,1)S(1)}, u32[]{:S(2)}, u32[]{:S(2)}) collective-permute-start(bf16[96,896]{1,0:T(8,128)(2,1)S(1)} %combine.8), channel_id=1, source_target_pairs={{0,12},{2,14},{4,8},{6,10},{8,4},{10,6},{12,0},{14,2},{1,13},{3,15... | collective-permute-start | bytes 516104 | tf_op jit(solution)/shard_map/ppermute | solution.py:430
  75.0 9.0 %collective-permute-start.22 = (bf16[96,896]{1,0:T(8,128)(2,1)S(1)}, bf16[96,896]{1,0:T(8,128)(2,1)S(1)}, u32[]{:S(2)}, u32[]{:S(2)}) collective-permute-start(bf16[96,896]{1,0:T(8,128)(2,1)S(1)} %get-tuple-element.74), channel_id=1, source_target_pairs={{0,4},{2,6},{4,0},{6,2},{8,12},{10,14},{12,8},{14,10},{1,5},{3,7},... | collective-permute-start | bytes 516104 | tf_op jit(solution)/shard_map/ppermute | solution.py:430
  76.7 10.4 %collective-permute-start.23 = (bf16[96,896]{1,0:T(8,128)(2,1)S(1)}, bf16[96,896]{1,0:T(8,128)(2,1)S(1)}, u32[]{:S(2)}, u32[]{:S(2)}) collective-permute-start(bf16[96,896]{1,0:T(8,128)(2,1)S(1)} %get-tuple-element.79), channel_id=1, source_target_pairs={{0,4},{2,6},{4,0},{6,2},{8,12},{10,14},{12,8},{14,10},{1,5},{3,7},... | collective-permute-start | bytes 516104 | tf_op jit(solution)/shard_map/ppermute | solution.py:430

commit v8 on v7

--- a/solution.py
+++ b/solution.py
@@ -379,7 +379,38 @@
     )(q_lat, latent_cache.transpose(0, 2, 1), lengths[None, :], placement[None, :])
 
 
-def combine_kernel(expert_count, first, sum_count, wide_ref, own_ref, back_ref, *refs):
+def last_down_kernel(own_ref, other_ref, down_ref, down_other_ref, *outs):
+    half = down_other_ref.shape[1]
+    base = pl.multiple_of(lax.axis_index("tp") * half, LANES)
+    start = 0
+    for out_ref in outs:
+        for first in range(0, out_ref.shape[1], 256):
+            width = min(256, out_ref.shape[1] - first)
+            column = start + first
+            result = jnp.dot(
+                own_ref[...],
+                down_ref[0, :, pl.ds(pl.multiple_of(base + column, LANES), width)],
+                preferred_element_type=jnp.float32,
+            ) + jnp.dot(
+                other_ref[...],
+                down_other_ref[:, column : column + width],
+                preferred_element_type=jnp.float32,
+            )
+            out_ref[:, first : first + width] = result[: out_ref.shape[0]].astype(jnp.bfloat16)
+        start += out_ref.shape[1]
+
+
+def last_down(hidden, hidden_other, w_down, down_other, capacity, widths):
+    return call(
+        last_down_kernel,
+        (hidden, hidden_other, w_down, down_other),
+        tuple((capacity, width) for width in widths),
+        0,
+        "last_down",
+    )
+
+
+def combine_kernel(expert_count, first, shift, sum_count, wide_ref, own_ref, back_ref, *refs):
     sums, outs = refs[:sum_count], refs[sum_count:]
     half = own_ref.shape[1]
     other = lax.axis_index("role") ^ 1
@@ -389,7 +420,11 @@
     for out_ref in outs:
         for column in range(0, out_ref.shape[1], width):
             columns = slice(first + column, first + column + width)
-            spread = jnp.dot(slots, back_ref[:, columns], preferred_element_type=jnp.float32)
+            spread = jnp.dot(
+                slots,
+                back_ref[:, columns.start - shift : columns.stop - shift],
+                preferred_element_type=jnp.float32,
+            )
             result = own_ref[:, columns] + gate * spread
             for ref in sums:
                 result = result + ref[:, column : column + width].astype(jnp.float32)
@@ -397,15 +432,18 @@
         first += out_ref.shape[1]
 
 
-def combine(wide, own, back, sums, expert_count, first, widths, dtype=jnp.bfloat16):
+def combine(
+    wide, own, back, sums, expert_count, first, widths, dtype=jnp.bfloat16, shift=0, hint=0
+):
     rows = own.shape[0]
     return call(
-        functools.partial(combine_kernel, expert_count, first, len(sums)),
+        functools.partial(combine_kernel, expert_count, first, shift, len(sums)),
         (wide, own, back, *sums),
         tuple((rows, width) for width in widths),
         0,
         "combine",
         types=(dtype,) * len(widths),
+        hint=hint,
     )
 
 
@@ -495,22 +533,34 @@
         (wide_far,), 2, hidden_second, hidden_second_other, *down_weights, capacity, role_count
     )
     hidden_third_other = after(hidden_third_other, own_far)
-    (back_far,) = down(
-        (), 1, hidden_third, hidden_third_other, *down_weights, capacity, role_count
-    )
-    back_far = swap(back_far, row)
+    split = half // 2
+    widths = (split, half - split)
+    back_far_left, back_far_right = last_down(
+        hidden_third, hidden_third_other, *down_weights, capacity, widths
+    )
+    back_far_left = swap(back_far_left, row)
+    back_far_right = swap(back_far_right, row)
     back_mirror = swap(back_mirror, row)
     back_pair = swap(back_pair, row)
     back_own = swap(back_own, row)
 
-    split = half // 2
-    widths = (split, half - split)
-    sum_far_left, sum_far_right = combine(
-        wide_far, own_far, back_far, (), role_count, 0, widths
+    (sum_far_left,) = combine(
+        wide_far, own_far, back_far_left, (), role_count, 0, widths[:1]
     )
     from_far_left = swap(sum_far_left, pair)
+    back_far_right = after(back_far_right, sum_far_left)
+    (sum_far_right,) = combine(
+        wide_far,
+        own_far,
+        back_far_right,
+        (),
+        role_count,
+        split,
+        widths[1:],
+        shift=split,
+    )
     from_far_right = swap(sum_far_right, pair)
-    back_mirror = after(back_mirror, sum_far_left)
+    back_mirror = after(back_mirror, sum_far_right)
     from_far_left = after(from_far_left, back_mirror)
     (sum_mirror_left,) = combine(
         wide_mirror, own_mirror, back_mirror, (from_far_left,), role_count, 0, widths[:1]

time: 88.1 us -> 86.3 us (0.980)
  waiting for transfers between devices: 38.8 us -> 34.7 us
  starting transfers between devices: 27.7 us -> 29.6 us
    ppermute x17 -> x18, waiting for transfers between devices: 38.7 us -> 34.6 us  [swap(): return lax.ppermute(array, 'role', pairs)]
    ppermute x17 -> x18, starting transfers between devices: 25.9 us -> 27.8 us  [swap(): return lax.ppermute(array, 'role', pairs)]
    pallas_call x18 -> x19, Pallas kernels: 14.7 us -> 15.1 us  [call(): pl.pallas_call(kernel, in_specs=[place] * len(operands), out_specs=[place...]
  transfers between devices with their start and end apart: 24 -> 25, of which waited for: 13 -> 14; matrix products, arithmetic and copies ran while one was open for 0% -> 0% of each run, Pallas kernels for 17% -> 18%
where the time goes in v8:
time: 86.3 us; the launch traced here: 86.1 us
  waiting for transfers between devices  34.7 us (40%)
  starting transfers between devices  29.6 us (34%)
  Pallas kernels  18.9 us (22%)
  local copies, waits for them, and re-layouts  2.06 us (2%)
  between operations  0.88 us (1%)
    ppermute x18, waiting for transfers between devices, swap(): return lax.ppermute(array, 'role', pairs)  34.6 us
    ppermute x18, starting transfers between devices, swap(): return lax.ppermute(array, 'role', pairs)  27.8 us
    pallas_call x19, Pallas kernels, call(): pl.pallas_call(kernel, in_specs=[place] * len(operands), out_specs=[place...  15.1 us
    unnamed x14, local copies, waits for them, and re-layouts  2.06 us
    pallas_call x1, Pallas kernels, attend(): pl.pallas_call(attend_kernel, out_shape=jax.ShapeDtypeStruct((slot_count,...  2.06 us
    ppermute x7, starting transfers between devices, swap_core(): return lax.ppermute(array, 'tp', [(0, 1), (1, 0)])  1.8 us
    pallas_call x1, Pallas kernels, prepare(): pl.pallas_call(functools.partial(prepare_kernel, expert_count), in_specs=...  1.77 us
  transfers between devices with their start and end apart: 25, of which 14 were waited for; matrix products, arithmetic and copies ran while one was open for 0% of the time, Pallas kernels for 18%

profile of v8, /device:TPU:0, one launch (start us, length us, event | category | flops | bytes accessed | tf_op | source)
XLA Modules:
  0.0 86.1 jit_solution(2879307114045519804)
XLA Ops:
  0.7 1.8 %prepare.1 = (bf16[96,1920]{1,0:T(8,128)(2,1)S(1)}, bf16[72,1792]{1,0:T(8,128)(2,1)S(1)}, bf16[512,1792]{1,0:T(8,128)(2,1)S(1)}) custom-call(bf16[96,1792]{1,0:T(8,128)(2,1)} %tokens_hbm.1, bf16[1,512,3584]{2,1,0:T(8,128)(2,1)} %down_ref.1, s32[4,96]{1,0:T(4,128)} %bitcast.16, f32[4,96]{1,0:T(4,128)} %bitcast.17), custom_call_target="tpu_custom_call" | custom-call | tf_op jit(solution)/shard_map/prepare/pallas_call | solution.py:212
  2.4 0.5 collective-permute-start.2
  3.0 2.6 %collective-permute-start = (bf16[96,1920]{1,0:T(8,128)(2,1)S(1)}, bf16[96,1920]{1,0:T(8,128)(2,1)S(1)}, u32[]{:S(2)}, u32[]{:S(2)}) collective-permute-start(bf16[96,1920]{1,0:T(8,128)(2,1)S(1)} %get-tuple-element.51.refs_0_.wide_ref), channel_id=1, source_target_pairs={{0,4},{2,6},{4,0},{6,2},{8,12},{10,14},{12,8},{14,10},{1,5},{3,7},... | collective-permute-start | bytes 1105928 | tf_op jit(solution)/shard_map/ppermute | solution.py:468
  5.6 1.5 %collective-permute-start.1 = (bf16[72,1792]{1,0:T(8,128)(2,1)S(1)}, bf16[72,1792]{1,0:T(8,128)(2,1)S(1)}, u32[]{:S(2)}, u32[]{:S(2)}) collective-permute-start(bf16[72,1792]{1,0:T(8,128)(2,1)S(1)} %get-tuple-element.44), channel_id=1, source_target_pairs={{0,2},{2,0},{4,6},{6,4},{8,10},{10,8},{12,14},{14,12},{1,3},{3,1},... | collective-permute-start | bytes 774152 | tf_op jit(solution)/shard_map/ppermute | solution.py:468
  7.2 2.1 %attend.1 = bf16[4,32,512]{2,1,0:T(8,128)(2,1)} custom-call(bf16[4,32,576]{2,1,0:T(8,128)(2,1)S(1)} %copy-done.4, bf16[4,576,256]{2,1,0:T(8,128)(2,1)S(1)} %bitcast.13, s32[1,32]{1,0:T(1,128)S(1)} %bitcast.14, s32[1,32]{1,0:T(1,128)S(1)} %bitcast.15), custom_call_target="tpu_custom_call" | custom-call | tf_op jit(solution)/shard_map/attend/pallas_call | solution.py:373
  9.2 2.5 %collective-permute-start.3 = (bf16[96,1920]{1,0:T(8,128)(2,1)S(1)}, bf16[96,1920]{1,0:T(8,128)(2,1)S(1)}, u32[]{:S(2)}, u32[]{:S(2)}) collective-permute-start(bf16[96,1920]{1,0:T(8,128)(2,1)S(1)} %get-tuple-element.51.refs_0_.wide_ref), channel_id=1, source_target_pairs={{0,12},{2,14},{4,8},{6,10},{8,4},{10,6},{12,0},{14,2},{1,13},{3,15... | collective-permute-start | bytes 1105928 | tf_op jit(solution)/shard_map/ppermute | solution.py:468
  11.7 2.2 %collective-permute-done.1.refs_3_ = bf16[72,1792]{1,0:T(8,128)(2,1)S(1)} collective-permute-done((bf16[72,1792]{1,0:T(8,128)(2,1)S(1)}, bf16[72,1792]{1,0:T(8,128)(2,1)S(1)}, u32[]{:S(2)}, u32[]{:S(2)}) %collective-permute-start.1) | collective-permute-done | bytes 258080 | tf_op jit(solution)/shard_map/ppermute | solution.py:468
  13.9 0.9 %collective-permute-done.wide_ref.refs_1_ = bf16[96,1920]{1,0:T(8,128)(2,1)S(1)} collective-permute-done((bf16[96,1920]{1,0:T(8,128)(2,1)S(1)}, bf16[96,1920]{1,0:T(8,128)(2,1)S(1)}, u32[]{:S(2)}, u32[]{:S(2)}) %collective-permute-start) | collective-permute-done | bytes 368672 | tf_op jit(solution)/shard_map/ppermute | solution.py:468
  14.8 0.0 collective-permute-done.2.refs_6_.refs_4_.down_other_ref
  14.8 0.5 cross_rows.3
  15.3 1.8 %collective-permute-start.4 = (bf16[72,1792]{1,0:T(8,128)(2,1)S(1)}, bf16[72,1792]{1,0:T(8,128)(2,1)S(1)}, u32[]{:S(2)}, u32[]{:S(2)}) collective-permute-start(bf16[72,1792]{1,0:T(8,128)(2,1)S(1)} %cross_rows.3), channel_id=1, source_target_pairs={{0,2},{2,0},{4,6},{6,4},{8,10},{10,8},{12,14},{14,12},{1,3},{3,1},... | collective-permute-start | bytes 774152 | tf_op jit(solution)/shard_map/ppermute | solution.py:468
  17.1 7.9 %collective-permute-done.3.wide_ref.refs_2_ = bf16[96,1920]{1,0:T(8,128)(2,1)S(1)} collective-permute-done((bf16[96,1920]{1,0:T(8,128)(2,1)S(1)}, bf16[96,1920]{1,0:T(8,128)(2,1)S(1)}, u32[]{:S(2)}, u32[]{:S(2)}) %collective-permute-start.3) | collective-permute-done | bytes 368672 | tf_op jit(solution)/shard_map/ppermute | solution.py:468
  25.0 3.9 %collective-permute-start.6 = (bf16[96,1920]{1,0:T(8,128)(2,1)S(1)}, bf16[96,1920]{1,0:T(8,128)(2,1)S(1)}, u32[]{:S(2)}, u32[]{:S(2)}) collective-permute-start(bf16[96,1920]{1,0:T(8,128)(2,1)S(1)} %collective-permute-done.3.wide_ref.refs_2_), channel_id=1, source_target_pairs={{0,4},{2,6},{4,0},{6,2},{8,12},{10,14},{12,8},{14,10},{1,5},{3,7},... | collective-permute-start | bytes 1105928 | tf_op jit(solution)/shard_map/ppermute | solution.py:468
  28.9 0.5 cross_rows.4
  29.4 0.6 collective-permute-start.7
  30.0 0.1 pack_rows.2.near_ref
  30.1 0.1 collective-permute-start.5
  30.2 6.8 %collective-permute-done.6.refs_0_.wide_ref = bf16[96,1920]{1,0:T(8,128)(2,1)S(1)} collective-permute-done((bf16[96,1920]{1,0:T(8,128)(2,1)S(1)}, bf16[96,1920]{1,0:T(8,128)(2,1)S(1)}, u32[]{:S(2)}, u32[]{:S(2)}) %collective-permute-start.6) | collective-permute-done | bytes 368672 | tf_op jit(solution)/shard_map/ppermute | solution.py:468
  37.0 0.1 pack_rows.3.near_ref
  37.0 0.1 collective-permute-start.10
  37.1 0.0 copy-start.1
  37.1 0.0 copy-start.2
  37.2 0.5 cross_rows.5
  37.7 0.6 collective-permute-start.9
  38.3 0.9 %copy-done.1 = bf16[1,3584,512]{2,1,0:T(8,128)(2,1)S(1)} copy-done((bf16[1,3584,512]{2,1,0:T(8,128)(2,1)S(1)}, bf16[1,3584,512]{2,1,0:T(8,128)(2,1)}, u32[]{:S(2)}) %copy-start.1) | copy-done | bytes 3670040
  39.2 1.1 %copy-done.2 = bf16[1,3584,512]{2,1,0:T(8,128)(2,1)S(1)} copy-done((bf16[1,3584,512]{2,1,0:T(8,128)(2,1)S(1)}, bf16[1,3584,512]{2,1,0:T(8,128)(2,1)}, u32[]{:S(2)}) %copy-start.2) | copy-done | bytes 3670040
  40.3 2.9 %hidden_units.3.refs_3_ = bf16[368,512]{1,0:T(8,128)(2,1)S(1)} custom-call(bf16[368,1792]{1,0:T(8,128)(2,1)S(1)} %pack_rows.2.near_ref, bf16[368,1792]{1,0:T(8,128)(2,1)S(1)} %collective-permute-done.5.far_ref, bf16[3584,512]{1,0:T(8,128)(2,1)S(1)} %bitcast.7, bf16[3584,512]{1,0:T(8,128)(2,1)S(1)} %bitcast.10), custom_call_target="tpu_custom_call" | custom-call | tf_op jit(solution)/shard_map/hidden_units/pallas_call | solution.py:91
  43.2 0.6 collective-permute-start.8
  43.7 2.1 %hidden_units.4.refs_1_ = bf16[256,512]{1,0:T(8,128)(2,1)S(1)} custom-call(bf16[256,1792]{1,0:T(8,128)(2,1)S(1)} %pack_rows.3.near_ref, bf16[256,1792]{1,0:T(8,128)(2,1)S(1)} %collective-permute-done.10.far_ref, bf16[3584,512]{1,0:T(8,128)(2,1)S(1)} %bitcast.8, bf16[3584,512]{1,0:T(8,128)(2,1)S(1)} %bitcast.11), custom_call_target="tpu_custom_call" | custom-call | tf_op jit(solution)/shard_map/hidden_units/pallas_call | solution.py:91
  45.8 0.5 collective-permute-done.9.near_ref
  46.3 0.5 collective-permute-start.12
  46.9 1.5 %down.2 = (f32[96,1792]{1,0:T(8,128)S(1)}, f32[96,1792]{1,0:T(8,128)S(1)}, f32[96,1792]{1,0:T(8,128)S(1)}, bf16[72,1792]{1,0:T(8,128)(2,1)S(1)}) custom-call(bf16[96,1920]{1,0:T(8,128)(2,1)S(1)} %get-tuple-element.51.refs_0_.wide_ref, bf16[96,1920]{1,0:T(8,128)(2,1)S(1)} %collective-permute-done.wide_ref.refs_1_, ...), custom_call_target="tpu_custom_call" | custom-call | tf_op jit(solution)/shard_map/down/pallas_call | solution.py:91
  48.4 1.4 %hidden_units.5.own_ref = bf16[72,512]{1,0:T(8,128)(2,1)S(1)} custom-call(bf16[72,1792]{1,0:T(8,128)(2,1)S(1)} %collective-permute-done.9.near_ref, bf16[72,1792]{1,0:T(8,128)(2,1)S(1)} %collective-permute-done.13.far_ref, bf16[3584,512]{1,0:T(8,128)(2,1)S(1)} %bitcast.9, bf16[3584,512]{1,0:T(8,128)(2,1)S(1)} %bitcast.12), custom_call_target="tpu_custom_call" | custom-call | tf_op jit(solution)/shard_map/hidden_units/pallas_call | solution.py:91
  49.8 0.1 collective-permute-start.16
  49.9 1.1 %down.3 = (f32[96,1792]{1,0:T(8,128)S(1)}, bf16[72,1792]{1,0:T(8,128)(2,1)S(1)}, bf16[72,1792]{1,0:T(8,128)(2,1)S(1)}) custom-call(bf16[96,1920]{1,0:T(8,128)(2,1)S(1)} %collective-permute-done.6.refs_0_.wide_ref, bf16[256,512]{1,0:T(8,128)(2,1)S(1)} %hidden_units.4.refs_1_, bf16[256,512]{1,0:T(8,128)(2,1)S(1)} %collective-permute-done.12.refs_2_, ...), custom_call_target="tpu_custom_call" | custom-call | tf_op jit(solution)/shard_map/down/pallas_call | solution.py:91
  51.1 0.1 collective-permute-done.16.other_ref
  51.2 0.7 last_down.1
  51.9 0.6 collective-permute-start.18
  52.5 1.5 %collective-permute-start.17 = (bf16[72,896]{1,0:T(8,128)(2,1)S(1)}, bf16[72,896]{1,0:T(8,128)(2,1)S(1)}, u32[]{:S(2)}, u32[]{:S(2)}) collective-permute-start(bf16[72,896]{1,0:T(8,128)(2,1)S(1)} %get-tuple-element.69), channel_id=1, source_target_pairs={{0,2},{2,0},{4,6},{6,4},{8,10},{10,8},{12,14},{14,12},{1,3},{3,1},... | collective-permute-start | bytes 387080 | tf_op jit(solution)/shard_map/ppermute | solution.py:468
  54.0 0.5 collective-permute-start.15
  54.5 1.5 %collective-permute-start.14 = (bf16[72,1792]{1,0:T(8,128)(2,1)S(1)}, bf16[72,1792]{1,0:T(8,128)(2,1)S(1)}, u32[]{:S(2)}, u32[]{:S(2)}) collective-permute-start(bf16[72,1792]{1,0:T(8,128)(2,1)S(1)} %get-tuple-element.64), channel_id=1, source_target_pairs={{0,2},{2,0},{4,6},{6,4},{8,10},{10,8},{12,14},{14,12},{1,3},{3,1},... | collective-permute-start | bytes 774152 | tf_op jit(solution)/shard_map/ppermute | solution.py:468
  56.0 2.2 %collective-permute-done.18.back_ref = bf16[72,896]{1,0:T(8,128)(2,1)S(1)} collective-permute-done((bf16[72,896]{1,0:T(8,128)(2,1)S(1)}, bf16[72,896]{1,0:T(8,128)(2,1)S(1)}, u32[]{:S(2)}, u32[]{:S(2)}) %collective-permute-start.18) | collective-permute-done | bytes 129056 | tf_op jit(solution)/shard_map/ppermute | solution.py:468
  58.2 0.4 combine.7
  58.6 1.8 %collective-permute-start.20 = (bf16[96,896]{1,0:T(8,128)(2,1)S(1)}, bf16[96,896]{1,0:T(8,128)(2,1)S(1)}, u32[]{:S(2)}, u32[]{:S(2)}) collective-permute-start(bf16[96,896]{1,0:T(8,128)(2,1)S(1)} %combine.7), channel_id=1, source_target_pairs={{0,4},{2,6},{4,0},{6,2},{8,12},{10,14},{12,8},{14,10},{1,5},{3,7},... | collective-permute-start | bytes 516104 | tf_op jit(solution)/shard_map/ppermute | solution.py:468
  60.5 0.5 collective-permute-done.17.back_ref
  61.0 0.4 combine.8
  61.4 1.8 %collective-permute-start.19 = (bf16[96,896]{1,0:T(8,128)(2,1)S(1)}, bf16[96,896]{1,0:T(8,128)(2,1)S(1)}, u32[]{:S(2)}, u32[]{:S(2)}) collective-permute-start(bf16[96,896]{1,0:T(8,128)(2,1)S(1)} %combine.8), channel_id=1, source_target_pairs={{0,4},{2,6},{4,0},{6,2},{8,12},{10,14},{12,8},{14,10},{1,5},{3,7},... | collective-permute-start | bytes 516104 | tf_op jit(solution)/shard_map/ppermute | solution.py:468
  63.2 0.5 collective-permute-start.11
  63.7 2.8 %collective-permute-done.15.back_ref = bf16[72,1792]{1,0:T(8,128)(2,1)S(1)} collective-permute-done((bf16[72,1792]{1,0:T(8,128)(2,1)S(1)}, bf16[72,1792]{1,0:T(8,128)(2,1)S(1)}, u32[]{:S(2)}, u32[]{:S(2)}) %collective-permute-start.15) | collective-permute-done | bytes 258080 | tf_op jit(solution)/shard_map/ppermute | solution.py:468
  66.5 0.4 combine.9
  66.9 2.4 %collective-permute-start.21 = (bf16[96,896]{1,0:T(8,128)(2,1)S(1)}, bf16[96,896]{1,0:T(8,128)(2,1)S(1)}, u32[]{:S(2)}, u32[]{:S(2)}) collective-permute-start(bf16[96,896]{1,0:T(8,128)(2,1)S(1)} %combine.9), channel_id=1, source_target_pairs={{0,12},{2,14},{4,8},{6,10},{8,4},{10,6},{12,0},{14,2},{1,13},{3,15... | collective-permute-start | bytes 516104 | tf_op jit(solution)/shard_map/ppermute | solution.py:468
  69.3 0.4 combine.10
  69.7 1.6 %collective-permute-start.22 = (bf16[96,896]{1,0:T(8,128)(2,1)S(1)}, bf16[96,896]{1,0:T(8,128)(2,1)S(1)}, u32[]{:S(2)}, u32[]{:S(2)}) collective-permute-start(bf16[96,896]{1,0:T(8,128)(2,1)S(1)} %combine.10), channel_id=1, source_target_pairs={{0,12},{2,14},{4,8},{6,10},{8,4},{10,6},{12,0},{14,2},{1,13},{3,15... | collective-permute-start | bytes 516104 | tf_op jit(solution)/shard_map/ppermute | solution.py:468
  71.3 0.7 collective-permute-done.14.back_ref
  72.0 0.4 combine.11
  72.5 1.8 %collective-permute-start.23 = (bf16[96,896]{1,0:T(8,128)(2,1)S(1)}, bf16[96,896]{1,0:T(8,128)(2,1)S(1)}, u32[]{:S(2)}, u32[]{:S(2)}) collective-permute-start(bf16[96,896]{1,0:T(8,128)(2,1)S(1)} %get-tuple-element.76), channel_id=1, source_target_pairs={{0,4},{2,6},{4,0},{6,2},{8,12},{10,14},{12,8},{14,10},{1,5},{3,7},... | collective-permute-start | bytes 516104 | tf_op jit(solution)/shard_map/ppermute | solution.py:468
  74.3 0.3 collective-permute-start.24
  74.6 2.4 %collective-permute-done.11.back_ref = bf16[72,1792]{1,0:T(8,128)(2,1)S(1)} collective-permute-done((bf16[72,1792]{1,0:T(8,128)(2,1)S(1)}, bf16[72,1792]{1,0:T(8,128)(2,1)S(1)}, u32[]{:S(2)}, u32[]{:S(2)}) %collective-permute-start.11) | collective-permute-done | bytes 258080 | tf_op jit(solution)/shard_map/ppermute | solution.py:468
  77.0 0.4 combine.12.refs_0_
  77.4 1.8 %collective-permute-done.22.refs_0_ = bf16[96,896]{1,0:T(8,128)(2,1)S(1)} collective-permute-done((bf16[96,896]{1,0:T(8,128)(2,1)S(1)}, bf16[96,896]{1,0:T(8,128)(2,1)S(1)}, u32[]{:S(2)}, u32[]{:S(2)}) %collective-permute-start.22) | collective-permute-done | bytes 172064 | tf_op jit(solution)/shard_map/ppermute | solution.py:468
  79.2 0.4 combine.13.refs_1_
  79.6 2.1 %collective-permute-done.23.refs_2_ = bf16[96,896]{1,0:T(8,128)(2,1)S(1)} collective-permute-done((bf16[96,896]{1,0:T(8,128)(2,1)S(1)}, bf16[96,896]{1,0:T(8,128)(2,1)S(1)}, u32[]{:S(2)}, u32[]{:S(2)}) %collective-permute-start.23) | collective-permute-done | bytes 172064 | tf_op jit(solution)/shard_map/ppermute | solution.py:468
  81.7 3.6 %collective-permute-done.24.refs_3_ = bf16[96,896]{1,0:T(8,128)(2,1)S(1)} collective-permute-done((bf16[96,896]{1,0:T(8,128)(2,1)S(1)}, bf16[96,896]{1,0:T(8,128)(2,1)S(1)}, u32[]{:S(2)}, u32[]{:S(2)}) %collective-permute-start.24) | collective-permute-done | bytes 172064 | tf_op jit(solution)/shard_map/ppermute | solution.py:468
  85.3 0.8 add_last.1
  (21 shorter events, 0.0 us)
Async XLA Ops:
  0.6 6.5 %copy-start.3 = (bf16[4,256,576]{1,2,0:T(8,128)(2,1)S(1)}, bf16[4,256,576]{1,2,0:T(8,128)(2,1)}, u32[]{:S(2)}) copy-start(bf16[4,256,576]{1,2,0:T(8,128)(2,1)} %param.11) | copy-start | bytes 3538948
  0.6 6.5 %copy-start.4 = (bf16[4,32,576]{2,1,0:T(8,128)(2,1)S(1)}, bf16[4,32,576]{2,1,0:T(8,128)(2,1)}, u32[]{:S(2)}) copy-start(bf16[4,32,576]{2,1,0:T(8,128)(2,1)} %query_ref) | copy-start | bytes 442372
  0.7 6.5 %copy-start.5 = (s32[32]{0:T(128)S(1)}, s32[32]{0:T(128)}, u32[]{:S(2)}) copy-start(s32[32]{0:T(128)} %param.12) | copy-start | bytes 388
  0.7 6.5 %copy-start.6 = (s32[32]{0:T(128)S(1)}, s32[32]{0:T(128)}, u32[]{:S(2)}) copy-start(s32[32]{0:T(128)} %param.13) | copy-start | bytes 388
  2.4 12.4 %collective-permute-start.2 = (bf16[512,1792]{1,0:T(8,128)(2,1)S(1)}, bf16[512,1792]{1,0:T(8,128)(2,1)S(1)}, u32[]{:S(2)}, u32[]{:S(2)}) collective-permute-start(bf16[512,1792]{1,0:T(8,128)(2,1)S(1)} %get-tuple-element.46), channel_id=1, source_target_pairs={{0,1},{1,0},{2,3},{3,2},{4,5},{5,4},{6,7},{7,6},{8,9},{9,8},{10,11... | collective-permute-start | bytes 5505032 | tf_op jit(solution)/shard_map/ppermute | solution.py:472
  3.0 11.8 %collective-permute-start = (bf16[96,1920]{1,0:T(8,128)(2,1)S(1)}, bf16[96,1920]{1,0:T(8,128)(2,1)S(1)}, u32[]{:S(2)}, u32[]{:S(2)}) collective-permute-start(bf16[96,1920]{1,0:T(8,128)(2,1)S(1)} %get-tuple-element.51.refs_0_.wide_ref), channel_id=1, source_target_pairs={{0,4},{2,6},{4,0},{6,2},{8,12},{10,14},{12,8},{14,10},{1,5},{3,7},... | collective-permute-start | bytes 1105928 | tf_op jit(solution)/shard_map/ppermute | solution.py:468
  5.6 8.3 %collective-permute-start.1 = (bf16[72,1792]{1,0:T(8,128)(2,1)S(1)}, bf16[72,1792]{1,0:T(8,128)(2,1)S(1)}, u32[]{:S(2)}, u32[]{:S(2)}) collective-permute-start(bf16[72,1792]{1,0:T(8,128)(2,1)S(1)} %get-tuple-element.44), channel_id=1, source_target_pairs={{0,2},{2,0},{4,6},{6,4},{8,10},{10,8},{12,14},{14,12},{1,3},{3,1},... | collective-permute-start | bytes 774152 | tf_op jit(solution)/shard_map/ppermute | solution.py:468
  9.2 15.8 %collective-permute-start.3 = (bf16[96,1920]{1,0:T(8,128)(2,1)S(1)}, bf16[96,1920]{1,0:T(8,128)(2,1)S(1)}, u32[]{:S(2)}, u32[]{:S(2)}) collective-permute-start(bf16[96,1920]{1,0:T(8,128)(2,1)S(1)} %get-tuple-element.51.refs_0_.wide_ref), channel_id=1, source_target_pairs={{0,12},{2,14},{4,8},{6,10},{8,4},{10,6},{12,0},{14,2},{1,13},{3,15... | collective-permute-start | bytes 1105928 | tf_op jit(solution)/shard_map/ppermute | solution.py:468
  15.3 14.7 %collective-permute-start.4 = (bf16[72,1792]{1,0:T(8,128)(2,1)S(1)}, bf16[72,1792]{1,0:T(8,128)(2,1)S(1)}, u32[]{:S(2)}, u32[]{:S(2)}) collective-permute-start(bf16[72,1792]{1,0:T(8,128)(2,1)S(1)} %cross_rows.3), channel_id=1, source_target_pairs={{0,2},{2,0},{4,6},{6,4},{8,10},{10,8},{12,14},{14,12},{1,3},{3,1},... | collective-permute-start | bytes 774152 | tf_op jit(solution)/shard_map/ppermute | solution.py:468
  25.0 12.0 %collective-permute-start.6 = (bf16[96,1920]{1,0:T(8,128)(2,1)S(1)}, bf16[96,1920]{1,0:T(8,128)(2,1)S(1)}, u32[]{:S(2)}, u32[]{:S(2)}) collective-permute-start(bf16[96,1920]{1,0:T(8,128)(2,1)S(1)} %collective-permute-done.3.wide_ref.refs_2_), channel_id=1, source_target_pairs={{0,4},{2,6},{4,0},{6,2},{8,12},{10,14},{12,8},{14,10},{1,5},{3,7},... | collective-permute-start | bytes 1105928 | tf_op jit(solution)/shard_map/ppermute | solution.py:468
  29.4 7.6 %collective-permute-start.7 = (bf16[72,1792]{1,0:T(8,128)(2,1)S(1)}, bf16[72,1792]{1,0:T(8,128)(2,1)S(1)}, u32[]{:S(2)}, u32[]{:S(2)}) collective-permute-start(bf16[72,1792]{1,0:T(8,128)(2,1)S(1)} %cross_rows.4), channel_id=1, source_target_pairs={{0,2},{2,0},{4,6},{6,4},{8,10},{10,8},{12,14},{14,12},{1,3},{3,1},... | collective-permute-start | bytes 774152 | tf_op jit(solution)/shard_map/ppermute | solution.py:468
  30.1 8.2 %collective-permute-start.5 = (bf16[368,1792]{1,0:T(8,128)(2,1)S(1)}, bf16[368,1792]{1,0:T(8,128)(2,1)S(1)}, u32[]{:S(2)}, u32[]{:S(2)}) collective-permute-start(bf16[368,1792]{1,0:T(8,128)(2,1)S(1)} %pack_rows.2.near_ref), channel_id=1, source_target_pairs={{0,1},{1,0},{2,3},{3,2},{4,5},{5,4},{6,7},{7,6},{8,9},{9,8},{10,11... | collective-permute-start | bytes 3956744 | tf_op jit(solution)/shard_map/ppermute | solution.py:472
  37.0 6.7 %collective-permute-start.10 = (bf16[256,1792]{1,0:T(8,128)(2,1)S(1)}, bf16[256,1792]{1,0:T(8,128)(2,1)S(1)}, u32[]{:S(2)}, u32[]{:S(2)}) collective-permute-start(bf16[256,1792]{1,0:T(8,128)(2,1)S(1)} %pack_rows.3.near_ref), channel_id=1, source_target_pairs={{0,1},{1,0},{2,3},{3,2},{4,5},{5,4},{6,7},{7,6},{8,9},{9,8},{10,11... | collective-permute-start | bytes 2752520 | tf_op jit(solution)/shard_map/ppermute | solution.py:472
  37.1 2.0 %copy-start.1 = (bf16[1,3584,512]{2,1,0:T(8,128)(2,1)S(1)}, bf16[1,3584,512]{2,1,0:T(8,128)(2,1)}, u32[]{:S(2)}) copy-start(bf16[1,3584,512]{2,1,0:T(8,128)(2,1)} %param.17) | copy-start | bytes 11010052
  37.1 3.2 %copy-start.2 = (bf16[1,3584,512]{2,1,0:T(8,128)(2,1)S(1)}, bf16[1,3584,512]{2,1,0:T(8,128)(2,1)}, u32[]{:S(2)}) copy-start(bf16[1,3584,512]{2,1,0:T(8,128)(2,1)} %param.18) | copy-start | bytes 11010052
  37.7 8.7 %collective-permute-start.9 = (bf16[72,1792]{1,0:T(8,128)(2,1)S(1)}, bf16[72,1792]{1,0:T(8,128)(2,1)S(1)}, u32[]{:S(2)}, u32[]{:S(2)}) collective-permute-start(bf16[72,1792]{1,0:T(8,128)(2,1)S(1)} %cross_rows.5), channel_id=1, source_target_pairs={{0,2},{2,0},{4,6},{6,4},{8,10},{10,8},{12,14},{14,12},{1,3},{3,1},... | collective-permute-start | bytes 774152 | tf_op jit(solution)/shard_map/ppermute | solution.py:468
  43.2 3.7 %collective-permute-start.8 = (bf16[368,512]{1,0:T(8,128)(2,1)S(1)}, bf16[368,512]{1,0:T(8,128)(2,1)S(1)}, u32[]{:S(2)}, u32[]{:S(2)}) collective-permute-start(bf16[368,512]{1,0:T(8,128)(2,1)S(1)} %hidden_units.3.refs_3_), channel_id=1, source_target_pairs={{0,1},{1,0},{2,3},{3,2},{4,5},{5,4},{6,7},{7,6},{8,9},{9,8},{10,11... | collective-permute-start | bytes 1130504 | tf_op jit(solution)/shard_map/ppermute | solution.py:472
  43.7 3.1 %copy-start = (bf16[1,512,3584]{2,1,0:T(8,128)(2,1)S(1)}, bf16[1,512,3584]{2,1,0:T(8,128)(2,1)}, u32[]{:S(2)}) copy-start(bf16[1,512,3584]{2,1,0:T(8,128)(2,1)} %down_ref.1) | copy-start | bytes 11010052
  46.3 2.1 %collective-permute-start.13 = (bf16[72,1792]{1,0:T(8,128)(2,1)S(1)}, bf16[72,1792]{1,0:T(8,128)(2,1)S(1)}, u32[]{:S(2)}, u32[]{:S(2)}) collective-permute-start(bf16[72,1792]{1,0:T(8,128)(2,1)S(1)} %collective-permute-done.9.near_ref), channel_id=1, source_target_pairs={{0,1},{1,0},{2,3},{3,2},{4,5},{5,4},{6,7},{7,6},{8,9},{9,8},{10,11... | collective-permute-start | bytes 774152 | tf_op jit(solution)/shard_map/ppermute | solution.py:472
  46.3 3.6 %collective-permute-start.12 = (bf16[256,512]{1,0:T(8,128)(2,1)S(1)}, bf16[256,512]{1,0:T(8,128)(2,1)S(1)}, u32[]{:S(2)}, u32[]{:S(2)}) collective-permute-start(bf16[256,512]{1,0:T(8,128)(2,1)S(1)} %hidden_units.4.refs_1_), channel_id=1, source_target_pairs={{0,1},{1,0},{2,3},{3,2},{4,5},{5,4},{6,7},{7,6},{8,9},{9,8},{10,11... | collective-permute-start | bytes 786440 | tf_op jit(solution)/shard_map/ppermute | solution.py:472
  49.8 1.3 %collective-permute-start.16 = (bf16[72,512]{1,0:T(8,128)(2,1)S(1)}, bf16[72,512]{1,0:T(8,128)(2,1)S(1)}, u32[]{:S(2)}, u32[]{:S(2)}) collective-permute-start(bf16[72,512]{1,0:T(8,128)(2,1)S(1)} %hidden_units.5.own_ref), channel_id=1, source_target_pairs={{0,1},{1,0},{2,3},{3,2},{4,5},{5,4},{6,7},{7,6},{8,9},{9,8},{10,11... | collective-permute-start | bytes 221192 | tf_op jit(solution)/shard_map/ppermute | solution.py:472
  51.9 6.4 %collective-permute-start.18 = (bf16[72,896]{1,0:T(8,128)(2,1)S(1)}, bf16[72,896]{1,0:T(8,128)(2,1)S(1)}, u32[]{:S(2)}, u32[]{:S(2)}) collective-permute-start(bf16[72,896]{1,0:T(8,128)(2,1)S(1)} %get-tuple-element.70), channel_id=1, source_target_pairs={{0,2},{2,0},{4,6},{6,4},{8,10},{10,8},{12,14},{14,12},{1,3},{3,1},... | collective-permute-start | bytes 387080 | tf_op jit(solution)/shard_map/ppermute | solution.py:468
  52.5 8.5 %collective-permute-start.17 = (bf16[72,896]{1,0:T(8,128)(2,1)S(1)}, bf16[72,896]{1,0:T(8,128)(2,1)S(1)}, u32[]{:S(2)}, u32[]{:S(2)}) collective-permute-start(bf16[72,896]{1,0:T(8,128)(2,1)S(1)} %get-tuple-element.69), channel_id=1, source_target_pairs={{0,2},{2,0},{4,6},{6,4},{8,10},{10,8},{12,14},{14,12},{1,3},{3,1},... | collective-permute-start | bytes 387080 | tf_op jit(solution)/shard_map/ppermute | solution.py:468
  54.0 12.5 %collective-permute-start.15 = (bf16[72,1792]{1,0:T(8,128)(2,1)S(1)}, bf16[72,1792]{1,0:T(8,128)(2,1)S(1)}, u32[]{:S(2)}, u32[]{:S(2)}) collective-permute-start(bf16[72,1792]{1,0:T(8,128)(2,1)S(1)} %get-tuple-element.66), channel_id=1, source_target_pairs={{0,2},{2,0},{4,6},{6,4},{8,10},{10,8},{12,14},{14,12},{1,3},{3,1},... | collective-permute-start | bytes 774152 | tf_op jit(solution)/shard_map/ppermute | solution.py:468
  54.5 17.6 %collective-permute-start.14 = (bf16[72,1792]{1,0:T(8,128)(2,1)S(1)}, bf16[72,1792]{1,0:T(8,128)(2,1)S(1)}, u32[]{:S(2)}, u32[]{:S(2)}) collective-permute-start(bf16[72,1792]{1,0:T(8,128)(2,1)S(1)} %get-tuple-element.64), channel_id=1, source_target_pairs={{0,2},{2,0},{4,6},{6,4},{8,10},{10,8},{12,14},{14,12},{1,3},{3,1},... | collective-permute-start | bytes 774152 | tf_op jit(solution)/shard_map/ppermute | solution.py:468
  58.6 7.9 %collective-permute-start.20 = (bf16[96,896]{1,0:T(8,128)(2,1)S(1)}, bf16[96,896]{1,0:T(8,128)(2,1)S(1)}, u32[]{:S(2)}, u32[]{:S(2)}) collective-permute-start(bf16[96,896]{1,0:T(8,128)(2,1)S(1)} %combine.7), channel_id=1, source_target_pairs={{0,4},{2,6},{4,0},{6,2},{8,12},{10,14},{12,8},{14,10},{1,5},{3,7},... | collective-permute-start | bytes 516104 | tf_op jit(solution)/shard_map/ppermute | solution.py:468
  61.4 7.9 %collective-permute-start.19 = (bf16[96,896]{1,0:T(8,128)(2,1)S(1)}, bf16[96,896]{1,0:T(8,128)(2,1)S(1)}, u32[]{:S(2)}, u32[]{:S(2)}) collective-permute-start(bf16[96,896]{1,0:T(8,128)(2,1)S(1)} %combine.8), channel_id=1, source_target_pairs={{0,4},{2,6},{4,0},{6,2},{8,12},{10,14},{12,8},{14,10},{1,5},{3,7},... | collective-permute-start | bytes 516104 | tf_op jit(solution)/shard_map/ppermute | solution.py:468
  63.2 13.8 %collective-permute-start.11 = (bf16[72,1792]{1,0:T(8,128)(2,1)S(1)}, bf16[72,1792]{1,0:T(8,128)(2,1)S(1)}, u32[]{:S(2)}, u32[]{:S(2)}) collective-permute-start(bf16[72,1792]{1,0:T(8,128)(2,1)S(1)} %get-tuple-element.60), channel_id=1, source_target_pairs={{0,2},{2,0},{4,6},{6,4},{8,10},{10,8},{12,14},{14,12},{1,3},{3,1},... | collective-permute-start | bytes 774152 | tf_op jit(solution)/shard_map/ppermute | solution.py:468
  66.9 10.1 %collective-permute-start.21 = (bf16[96,896]{1,0:T(8,128)(2,1)S(1)}, bf16[96,896]{1,0:T(8,128)(2,1)S(1)}, u32[]{:S(2)}, u32[]{:S(2)}) collective-permute-start(bf16[96,896]{1,0:T(8,128)(2,1)S(1)} %combine.9), channel_id=1, source_target_pairs={{0,12},{2,14},{4,8},{6,10},{8,4},{10,6},{12,0},{14,2},{1,13},{3,15... | collective-permute-start | bytes 516104 | tf_op jit(solution)/shard_map/ppermute | solution.py:468
  69.7 9.5 %collective-permute-start.22 = (bf16[96,896]{1,0:T(8,128)(2,1)S(1)}, bf16[96,896]{1,0:T(8,128)(2,1)S(1)}, u32[]{:S(2)}, u32[]{:S(2)}) collective-permute-start(bf16[96,896]{1,0:T(8,128)(2,1)S(1)} %combine.10), channel_id=1, source_target_pairs={{0,12},{2,14},{4,8},{6,10},{8,4},{10,6},{12,0},{14,2},{1,13},{3,15... | collective-permute-start | bytes 516104 | tf_op jit(solution)/shard_map/ppermute | solution.py:468
  72.5 9.2 %collective-permute-start.23 = (bf16[96,896]{1,0:T(8,128)(2,1)S(1)}, bf16[96,896]{1,0:T(8,128)(2,1)S(1)}, u32[]{:S(2)}, u32[]{:S(2)}) collective-permute-start(bf16[96,896]{1,0:T(8,128)(2,1)S(1)} %get-tuple-element.76), channel_id=1, source_target_pairs={{0,4},{2,6},{4,0},{6,2},{8,12},{10,14},{12,8},{14,10},{1,5},{3,7},... | collective-permute-start | bytes 516104 | tf_op jit(solution)/shard_map/ppermute | solution.py:468
  74.3 11.0 %collective-permute-start.24 = (bf16[96,896]{1,0:T(8,128)(2,1)S(1)}, bf16[96,896]{1,0:T(8,128)(2,1)S(1)}, u32[]{:S(2)}, u32[]{:S(2)}) collective-permute-start(bf16[96,896]{1,0:T(8,128)(2,1)S(1)} %get-tuple-element.81), channel_id=1, source_target_pairs={{0,4},{2,6},{4,0},{6,2},{8,12},{10,14},{12,8},{14,10},{1,5},{3,7},... | collective-permute-start | bytes 516104 | tf_op jit(solution)/shard_map/ppermute | solution.py:468

commit v9 on v8

--- a/solution.py
+++ b/solution.py
@@ -264,11 +264,11 @@
         out_ref[start : start + ref.shape[0], :] = ref[:, : out_ref.shape[1]]
 
 
-def pack(blocks, half, hint=0):
+def pack(blocks, half, kept=(), hint=0):
     starts, rows = row_starts(blocks)
     return call(
         functools.partial(pack_kernel, starts),
-        blocks,
+        (*blocks, *kept),
         ((rows, half),),
         0,
         "pack_rows",
@@ -484,12 +484,12 @@
     wide, cross, down_away = prepare(
         tokens, w_down, expert_ids, gate_weights, role_count, capacity
     )
+    wide_mirror = swap(wide, mirror)
     wide_pair = swap(wide, pair)
     cross_in = swap(cross, row)
     w_gate, w_up = w_gate[0], w_up[0]
     down_other = swap_core(down_away)
     attended = attend(after(q_lat, wide), latent_cache, lengths, placement)
-    wide_mirror = swap(after(wide, attended), mirror)
     cross_in = after(cross_in, attended)
     wide_pair = after(wide_pair, cross_in, down_other)
     cross_pair = cross_rows(wide_pair, role_count, capacity)
@@ -499,7 +499,7 @@
     cross_mirror = cross_rows(wide_mirror, role_count, capacity)
     cross_mirror_in = swap(cross_mirror, row)
     cross_pair_in = after(cross_pair_in, cross_mirror)
-    near_first = pack((after(wide, cross_pair_in), wide_pair, wide_mirror, cross_in), half)
+    near_first = pack((after(wide, cross_pair_in), wide_pair, wide_mirror, cross_in), half, (w_gate, w_up))
     far_first = swap_core(near_first)
     wide_far = after(wide_far, near_first)
     cross_mirror_in = after(cross_mirror_in, wide_far)

time: 86.3 us -> 84.7 us (0.981)
  waiting for transfers between devices: 34.7 us -> 32.7 us
  local copies, waits for them, and re-layouts: 2.06 us -> 3.33 us
  starting transfers between devices: 29.6 us -> 28.6 us
    ppermute x18, waiting for transfers between devices: 34.6 us -> 32.6 us  [swap(): return lax.ppermute(array, 'role', pairs)]
    unnamed x14 -> x16, local copies, waits for them, and re-layouts: 2.06 us -> 3.33 us
  transfers between devices with their start and end apart: 25 -> 25, of which waited for: 14 -> 13; matrix products, arithmetic and copies ran while one was open for 0% -> 0% of each run, Pallas kernels for 18% -> 19%
where the time goes in v9:
time: 84.7 us; the launch traced here: 84.5 us
  waiting for transfers between devices  32.7 us (39%)
  starting transfers between devices  28.6 us (34%)
  Pallas kernels  19 us (22%)
  local copies, waits for them, and re-layouts  3.33 us (4%)
  between operations  0.88 us (1%)
    ppermute x18, waiting for transfers between devices, swap(): return lax.ppermute(array, 'role', pairs)  32.6 us
    ppermute x18, starting transfers between devices, swap(): return lax.ppermute(array, 'role', pairs)  26.9 us
    pallas_call x19, Pallas kernels, call(): pl.pallas_call(kernel, in_specs=[place] * len(operands), out_specs=[place...  15.1 us
    unnamed x16, local copies, waits for them, and re-layouts  3.33 us
    pallas_call x1, Pallas kernels, attend(): pl.pallas_call(attend_kernel, out_shape=jax.ShapeDtypeStruct((slot_count,...  2.05 us
    pallas_call x1, Pallas kernels, prepare(): pl.pallas_call(functools.partial(prepare_kernel, expert_count), in_specs=...  1.82 us
    ppermute x7, starting transfers between devices, swap_core(): return lax.ppermute(array, 'tp', [(0, 1), (1, 0)])  1.7 us
  transfers between devices with their start and end apart: 25, of which 13 were waited for; matrix products, arithmetic and copies ran while one was open for 0% of the time, Pallas kernels for 19%

profile of v9, /device:TPU:0, one launch (start us, length us, event | category | flops | bytes accessed | tf_op | source)
XLA Modules:
  0.0 84.5 jit_solution(15819087704882040471)
XLA Ops:
  0.7 1.8 %prepare.1 = (bf16[96,1920]{1,0:T(8,128)(2,1)S(1)}, bf16[72,1792]{1,0:T(8,128)(2,1)S(1)}, bf16[512,1792]{1,0:T(8,128)(2,1)S(1)}) custom-call(bf16[96,1792]{1,0:T(8,128)(2,1)} %tokens_hbm.1, bf16[1,512,3584]{2,1,0:T(8,128)(2,1)} %down_ref.1, s32[4,96]{1,0:T(4,128)} %bitcast.18, f32[4,96]{1,0:T(4,128)} %bitcast.19), custom_call_target="tpu_custom_call" | custom-call | tf_op jit(solution)/shard_map/prepare/pallas_call | solution.py:212
  2.5 0.5 collective-permute-start.2
  3.0 2.6 %collective-permute-start = (bf16[96,1920]{1,0:T(8,128)(2,1)S(1)}, bf16[96,1920]{1,0:T(8,128)(2,1)S(1)}, u32[]{:S(2)}, u32[]{:S(2)}) collective-permute-start(bf16[96,1920]{1,0:T(8,128)(2,1)S(1)} %get-tuple-element.49.refs_0_.wide_ref), channel_id=1, source_target_pairs={{0,4},{2,6},{4,0},{6,2},{8,12},{10,14},{12,8},{14,10},{1,5},{3,7},... | collective-permute-start | bytes 1105928 | tf_op jit(solution)/shard_map/ppermute | solution.py:468
  5.7 1.5 %collective-permute-start.1 = (bf16[72,1792]{1,0:T(8,128)(2,1)S(1)}, bf16[72,1792]{1,0:T(8,128)(2,1)S(1)}, u32[]{:S(2)}, u32[]{:S(2)}) collective-permute-start(bf16[72,1792]{1,0:T(8,128)(2,1)S(1)} %get-tuple-element.43), channel_id=1, source_target_pairs={{0,2},{2,0},{4,6},{6,4},{8,10},{10,8},{12,14},{14,12},{1,3},{3,1},... | collective-permute-start | bytes 774152 | tf_op jit(solution)/shard_map/ppermute | solution.py:468
  7.2 2.5 %collective-permute-start.3 = (bf16[96,1920]{1,0:T(8,128)(2,1)S(1)}, bf16[96,1920]{1,0:T(8,128)(2,1)S(1)}, u32[]{:S(2)}, u32[]{:S(2)}) collective-permute-start(bf16[96,1920]{1,0:T(8,128)(2,1)S(1)} %get-tuple-element.49.refs_0_.wide_ref), channel_id=1, source_target_pairs={{0,12},{2,14},{4,8},{6,10},{8,4},{10,6},{12,0},{14,2},{1,13},{3,15... | collective-permute-start | bytes 1105928 | tf_op jit(solution)/shard_map/ppermute | solution.py:468
  9.7 1.3 %copy-done.4 = bf16[4,256,576]{1,2,0:T(8,128)(2,1)S(1)} copy-done((bf16[4,256,576]{1,2,0:T(8,128)(2,1)S(1)}, bf16[4,256,576]{1,2,0:T(8,128)(2,1)}, u32[]{:S(2)}) %copy-start.4) | copy-done | bytes 1179672
  10.9 2.0 %attend.1 = bf16[4,32,512]{2,1,0:T(8,128)(2,1)} custom-call(bf16[4,32,576]{2,1,0:T(8,128)(2,1)S(1)} %copy-done.5, bf16[4,576,256]{2,1,0:T(8,128)(2,1)S(1)} %bitcast.15, s32[1,32]{1,0:T(1,128)S(1)} %bitcast.16, s32[1,32]{1,0:T(1,128)S(1)} %bitcast.17), custom_call_target="tpu_custom_call" | custom-call | tf_op jit(solution)/shard_map/attend/pallas_call | solution.py:373
  13.0 1.0 %collective-permute-done.1.refs_3_ = bf16[72,1792]{1,0:T(8,128)(2,1)S(1)} collective-permute-done((bf16[72,1792]{1,0:T(8,128)(2,1)S(1)}, bf16[72,1792]{1,0:T(8,128)(2,1)S(1)}, u32[]{:S(2)}, u32[]{:S(2)}) %collective-permute-start.1) | collective-permute-done | bytes 258080 | tf_op jit(solution)/shard_map/ppermute | solution.py:468
  14.0 0.9 %collective-permute-done.wide_ref.refs_1_ = bf16[96,1920]{1,0:T(8,128)(2,1)S(1)} collective-permute-done((bf16[96,1920]{1,0:T(8,128)(2,1)S(1)}, bf16[96,1920]{1,0:T(8,128)(2,1)S(1)}, u32[]{:S(2)}, u32[]{:S(2)}) %collective-permute-start) | collective-permute-done | bytes 368672 | tf_op jit(solution)/shard_map/ppermute | solution.py:468
  14.9 0.5 cross_rows.3
  15.4 1.8 %collective-permute-start.4 = (bf16[72,1792]{1,0:T(8,128)(2,1)S(1)}, bf16[72,1792]{1,0:T(8,128)(2,1)S(1)}, u32[]{:S(2)}, u32[]{:S(2)}) collective-permute-start(bf16[72,1792]{1,0:T(8,128)(2,1)S(1)} %cross_rows.3), channel_id=1, source_target_pairs={{0,2},{2,0},{4,6},{6,4},{8,10},{10,8},{12,14},{14,12},{1,3},{3,1},... | collective-permute-start | bytes 774152 | tf_op jit(solution)/shard_map/ppermute | solution.py:468
  17.1 7.9 %collective-permute-done.3.wide_ref.refs_2_ = bf16[96,1920]{1,0:T(8,128)(2,1)S(1)} collective-permute-done((bf16[96,1920]{1,0:T(8,128)(2,1)S(1)}, bf16[96,1920]{1,0:T(8,128)(2,1)S(1)}, u32[]{:S(2)}, u32[]{:S(2)}) %collective-permute-start.3) | collective-permute-done | bytes 368672 | tf_op jit(solution)/shard_map/ppermute | solution.py:468
  25.1 1.8 %collective-permute-start.6 = (bf16[96,1920]{1,0:T(8,128)(2,1)S(1)}, bf16[96,1920]{1,0:T(8,128)(2,1)S(1)}, u32[]{:S(2)}, u32[]{:S(2)}) collective-permute-start(bf16[96,1920]{1,0:T(8,128)(2,1)S(1)} %collective-permute-done.3.wide_ref.refs_2_), channel_id=1, source_target_pairs={{0,4},{2,6},{4,0},{6,2},{8,12},{10,14},{12,8},{14,10},{1,5},{3,7},... | collective-permute-start | bytes 1105928 | tf_op jit(solution)/shard_map/ppermute | solution.py:468
  26.9 0.5 cross_rows.4
  27.4 0.6 collective-permute-start.7
  28.0 2.0 %copy-done.1 = bf16[1,3584,512]{2,1,0:T(8,128)(2,1)S(1)} copy-done((bf16[1,3584,512]{2,1,0:T(8,128)(2,1)S(1)}, bf16[1,3584,512]{2,1,0:T(8,128)(2,1)}, u32[]{:S(2)}) %copy-start.1) | copy-done | bytes 3670040
  30.0 0.1 pack_rows.2.near_ref
  30.1 0.1 collective-permute-start.5
  30.2 5.0 %collective-permute-done.6.refs_0_.wide_ref = bf16[96,1920]{1,0:T(8,128)(2,1)S(1)} collective-permute-done((bf16[96,1920]{1,0:T(8,128)(2,1)S(1)}, bf16[96,1920]{1,0:T(8,128)(2,1)S(1)}, u32[]{:S(2)}, u32[]{:S(2)}) %collective-permute-start.6) | collective-permute-done | bytes 368672 | tf_op jit(solution)/shard_map/ppermute | solution.py:468
  35.2 0.0 collective-permute-done.7.refs_2_
  35.2 0.1 pack_rows.3.near_ref
  35.2 0.1 collective-permute-start.10
  35.3 0.0 copy-start.2
  35.3 0.5 cross_rows.5
  35.8 1.6 %collective-permute-start.9 = (bf16[72,1792]{1,0:T(8,128)(2,1)S(1)}, bf16[72,1792]{1,0:T(8,128)(2,1)S(1)}, u32[]{:S(2)}, u32[]{:S(2)}) collective-permute-start(bf16[72,1792]{1,0:T(8,128)(2,1)S(1)} %cross_rows.5), channel_id=1, source_target_pairs={{0,2},{2,0},{4,6},{6,4},{8,10},{10,8},{12,14},{14,12},{1,3},{3,1},... | collective-permute-start | bytes 774152 | tf_op jit(solution)/shard_map/ppermute | solution.py:468
  37.4 2.9 %hidden_units.3.refs_3_ = bf16[368,512]{1,0:T(8,128)(2,1)S(1)} custom-call(bf16[368,1792]{1,0:T(8,128)(2,1)S(1)} %pack_rows.2.near_ref, bf16[368,1792]{1,0:T(8,128)(2,1)S(1)} %collective-permute-done.5.far_ref, bf16[3584,512]{1,0:T(8,128)(2,1)S(1)} %bitcast.8, bf16[3584,512]{1,0:T(8,128)(2,1)S(1)} %bitcast.12), custom_call_target="tpu_custom_call" | custom-call | tf_op jit(solution)/shard_map/hidden_units/pallas_call | solution.py:91
  40.3 0.5 collective-permute-start.8
  40.8 2.1 %hidden_units.4.refs_1_ = bf16[256,512]{1,0:T(8,128)(2,1)S(1)} custom-call(bf16[256,1792]{1,0:T(8,128)(2,1)S(1)} %pack_rows.3.near_ref, bf16[256,1792]{1,0:T(8,128)(2,1)S(1)} %collective-permute-done.10.far_ref, bf16[3584,512]{1,0:T(8,128)(2,1)S(1)} %bitcast.9, bf16[3584,512]{1,0:T(8,128)(2,1)S(1)} %bitcast.13), custom_call_target="tpu_custom_call" | custom-call | tf_op jit(solution)/shard_map/hidden_units/pallas_call | solution.py:91
  42.9 1.6 %collective-permute-done.9.near_ref = bf16[72,1792]{1,0:T(8,128)(2,1)S(1)} collective-permute-done((bf16[72,1792]{1,0:T(8,128)(2,1)S(1)}, bf16[72,1792]{1,0:T(8,128)(2,1)S(1)}, u32[]{:S(2)}, u32[]{:S(2)}) %collective-permute-start.9) | collective-permute-done | bytes 258080 | tf_op jit(solution)/shard_map/ppermute | solution.py:468
  44.5 0.5 collective-permute-start.12
  45.0 0.0 collective-permute-done.8.refs_4_
  45.0 1.5 %down.2 = (f32[96,1792]{1,0:T(8,128)S(1)}, f32[96,1792]{1,0:T(8,128)S(1)}, f32[96,1792]{1,0:T(8,128)S(1)}, bf16[72,1792]{1,0:T(8,128)(2,1)S(1)}) custom-call(bf16[96,1920]{1,0:T(8,128)(2,1)S(1)} %get-tuple-element.49.refs_0_.wide_ref, bf16[96,1920]{1,0:T(8,128)(2,1)S(1)} %collective-permute-done.wide_ref.refs_1_, ...), custom_call_target="tpu_custom_call" | custom-call | tf_op jit(solution)/shard_map/down/pallas_call | solution.py:91
  46.6 1.4 %hidden_units.5.own_ref = bf16[72,512]{1,0:T(8,128)(2,1)S(1)} custom-call(bf16[72,1792]{1,0:T(8,128)(2,1)S(1)} %collective-permute-done.9.near_ref, bf16[72,1792]{1,0:T(8,128)(2,1)S(1)} %collective-permute-done.13.far_ref, bf16[3584,512]{1,0:T(8,128)(2,1)S(1)} %bitcast.10, bf16[3584,512]{1,0:T(8,128)(2,1)S(1)} %bitcast.14), custom_call_target="tpu_custom_call" | custom-call | tf_op jit(solution)/shard_map/hidden_units/pallas_call | solution.py:91
  48.0 0.1 collective-permute-start.16
  48.1 1.1 %down.3 = (f32[96,1792]{1,0:T(8,128)S(1)}, bf16[72,1792]{1,0:T(8,128)(2,1)S(1)}, bf16[72,1792]{1,0:T(8,128)(2,1)S(1)}) custom-call(bf16[96,1920]{1,0:T(8,128)(2,1)S(1)} %collective-permute-done.6.refs_0_.wide_ref, bf16[256,512]{1,0:T(8,128)(2,1)S(1)} %hidden_units.4.refs_1_, bf16[256,512]{1,0:T(8,128)(2,1)S(1)} %collective-permute-done.12.refs_2_, ...), custom_call_target="tpu_custom_call" | custom-call | tf_op jit(solution)/shard_map/down/pallas_call | solution.py:91
  49.2 0.1 collective-permute-done.16.other_ref
  49.3 0.7 last_down.1
  50.0 1.6 %collective-permute-start.18 = (bf16[72,896]{1,0:T(8,128)(2,1)S(1)}, bf16[72,896]{1,0:T(8,128)(2,1)S(1)}, u32[]{:S(2)}, u32[]{:S(2)}) collective-permute-start(bf16[72,896]{1,0:T(8,128)(2,1)S(1)} %get-tuple-element.68), channel_id=1, source_target_pairs={{0,2},{2,0},{4,6},{6,4},{8,10},{10,8},{12,14},{14,12},{1,3},{3,1},... | collective-permute-start | bytes 387080 | tf_op jit(solution)/shard_map/ppermute | solution.py:468
  51.6 0.5 collective-permute-start.17
  52.2 1.5 %collective-permute-start.15 = (bf16[72,1792]{1,0:T(8,128)(2,1)S(1)}, bf16[72,1792]{1,0:T(8,128)(2,1)S(1)}, u32[]{:S(2)}, u32[]{:S(2)}) collective-permute-start(bf16[72,1792]{1,0:T(8,128)(2,1)S(1)} %get-tuple-element.64), channel_id=1, source_target_pairs={{0,2},{2,0},{4,6},{6,4},{8,10},{10,8},{12,14},{14,12},{1,3},{3,1},... | collective-permute-start | bytes 774152 | tf_op jit(solution)/shard_map/ppermute | solution.py:468
  53.7 0.5 collective-permute-start.14
  54.2 2.2 %collective-permute-done.18.back_ref = bf16[72,896]{1,0:T(8,128)(2,1)S(1)} collective-permute-done((bf16[72,896]{1,0:T(8,128)(2,1)S(1)}, bf16[72,896]{1,0:T(8,128)(2,1)S(1)}, u32[]{:S(2)}, u32[]{:S(2)}) %collective-permute-start.18) | collective-permute-done | bytes 129056 | tf_op jit(solution)/shard_map/ppermute | solution.py:468
  56.4 0.4 combine.7
  56.8 1.6 %collective-permute-start.20 = (bf16[96,896]{1,0:T(8,128)(2,1)S(1)}, bf16[96,896]{1,0:T(8,128)(2,1)S(1)}, u32[]{:S(2)}, u32[]{:S(2)}) collective-permute-start(bf16[96,896]{1,0:T(8,128)(2,1)S(1)} %combine.7), channel_id=1, source_target_pairs={{0,4},{2,6},{4,0},{6,2},{8,12},{10,14},{12,8},{14,10},{1,5},{3,7},... | collective-permute-start | bytes 516104 | tf_op jit(solution)/shard_map/ppermute | solution.py:468
  58.4 0.7 collective-permute-done.17.back_ref
  59.2 0.4 combine.8
  59.6 1.6 %collective-permute-start.19 = (bf16[96,896]{1,0:T(8,128)(2,1)S(1)}, bf16[96,896]{1,0:T(8,128)(2,1)S(1)}, u32[]{:S(2)}, u32[]{:S(2)}) collective-permute-start(bf16[96,896]{1,0:T(8,128)(2,1)S(1)} %combine.8), channel_id=1, source_target_pairs={{0,4},{2,6},{4,0},{6,2},{8,12},{10,14},{12,8},{14,10},{1,5},{3,7},... | collective-permute-start | bytes 516104 | tf_op jit(solution)/shard_map/ppermute | solution.py:468
  61.2 0.3 collective-permute-start.11
  61.5 3.2 %collective-permute-done.15.back_ref = bf16[72,1792]{1,0:T(8,128)(2,1)S(1)} collective-permute-done((bf16[72,1792]{1,0:T(8,128)(2,1)S(1)}, bf16[72,1792]{1,0:T(8,128)(2,1)S(1)}, u32[]{:S(2)}, u32[]{:S(2)}) %collective-permute-start.15) | collective-permute-done | bytes 258080 | tf_op jit(solution)/shard_map/ppermute | solution.py:468
  64.7 0.4 combine.9
  65.1 3.9 %collective-permute-start.21 = (bf16[96,896]{1,0:T(8,128)(2,1)S(1)}, bf16[96,896]{1,0:T(8,128)(2,1)S(1)}, u32[]{:S(2)}, u32[]{:S(2)}) collective-permute-start(bf16[96,896]{1,0:T(8,128)(2,1)S(1)} %combine.9), channel_id=1, source_target_pairs={{0,12},{2,14},{4,8},{6,10},{8,4},{10,6},{12,0},{14,2},{1,13},{3,15... | collective-permute-start | bytes 516104 | tf_op jit(solution)/shard_map/ppermute | solution.py:468
  69.0 0.0 collective-permute-done.19.refs_0_
  69.0 0.4 combine.10
  69.4 0.9 %collective-permute-start.22 = (bf16[96,896]{1,0:T(8,128)(2,1)S(1)}, bf16[96,896]{1,0:T(8,128)(2,1)S(1)}, u32[]{:S(2)}, u32[]{:S(2)}) collective-permute-start(bf16[96,896]{1,0:T(8,128)(2,1)S(1)} %combine.10), channel_id=1, source_target_pairs={{0,12},{2,14},{4,8},{6,10},{8,4},{10,6},{12,0},{14,2},{1,13},{3,15... | collective-permute-start | bytes 516104 | tf_op jit(solution)/shard_map/ppermute | solution.py:468
  70.3 0.5 combine.11
  70.7 1.5 %collective-permute-start.23 = (bf16[96,896]{1,0:T(8,128)(2,1)S(1)}, bf16[96,896]{1,0:T(8,128)(2,1)S(1)}, u32[]{:S(2)}, u32[]{:S(2)}) collective-permute-start(bf16[96,896]{1,0:T(8,128)(2,1)S(1)} %get-tuple-element.74), channel_id=1, source_target_pairs={{0,4},{2,6},{4,0},{6,2},{8,12},{10,14},{12,8},{14,10},{1,5},{3,7},... | collective-permute-start | bytes 516104 | tf_op jit(solution)/shard_map/ppermute | solution.py:468
  72.3 0.5 collective-permute-start.24
  72.8 2.4 %collective-permute-done.11.back_ref = bf16[72,1792]{1,0:T(8,128)(2,1)S(1)} collective-permute-done((bf16[72,1792]{1,0:T(8,128)(2,1)S(1)}, bf16[72,1792]{1,0:T(8,128)(2,1)S(1)}, u32[]{:S(2)}, u32[]{:S(2)}) %collective-permute-start.11) | collective-permute-done | bytes 258080 | tf_op jit(solution)/shard_map/ppermute | solution.py:468
  75.2 0.4 combine.12.refs_0_
  75.6 2.8 %collective-permute-done.22.refs_0_ = bf16[96,896]{1,0:T(8,128)(2,1)S(1)} collective-permute-done((bf16[96,896]{1,0:T(8,128)(2,1)S(1)}, bf16[96,896]{1,0:T(8,128)(2,1)S(1)}, u32[]{:S(2)}, u32[]{:S(2)}) %collective-permute-start.22) | collective-permute-done | bytes 172064 | tf_op jit(solution)/shard_map/ppermute | solution.py:468
  78.5 0.4 combine.13.refs_1_
  78.9 2.2 %collective-permute-done.23.refs_2_ = bf16[96,896]{1,0:T(8,128)(2,1)S(1)} collective-permute-done((bf16[96,896]{1,0:T(8,128)(2,1)S(1)}, bf16[96,896]{1,0:T(8,128)(2,1)S(1)}, u32[]{:S(2)}, u32[]{:S(2)}) %collective-permute-start.23) | collective-permute-done | bytes 172064 | tf_op jit(solution)/shard_map/ppermute | solution.py:468
  81.1 2.6 %collective-permute-done.24.refs_3_ = bf16[96,896]{1,0:T(8,128)(2,1)S(1)} collective-permute-done((bf16[96,896]{1,0:T(8,128)(2,1)S(1)}, bf16[96,896]{1,0:T(8,128)(2,1)S(1)}, u32[]{:S(2)}, u32[]{:S(2)}) %collective-permute-start.24) | collective-permute-done | bytes 172064 | tf_op jit(solution)/shard_map/ppermute | solution.py:468
  83.7 0.8 add_last.1
  (23 shorter events, 0.1 us)
Async XLA Ops:
  0.6 9.0 %copy-start.5 = (bf16[4,32,576]{2,1,0:T(8,128)(2,1)S(1)}, bf16[4,32,576]{2,1,0:T(8,128)(2,1)}, u32[]{:S(2)}) copy-start(bf16[4,32,576]{2,1,0:T(8,128)(2,1)} %query_ref) | copy-start | bytes 442372
  0.6 9.0 %copy-start.6 = (s32[32]{0:T(128)S(1)}, s32[32]{0:T(128)}, u32[]{:S(2)}) copy-start(s32[32]{0:T(128)} %param.12) | copy-start | bytes 388
  0.7 9.0 %copy-start.7 = (s32[32]{0:T(128)S(1)}, s32[32]{0:T(128)}, u32[]{:S(2)}) copy-start(s32[32]{0:T(128)} %param.13) | copy-start | bytes 388
  0.7 27.3 %copy-start = (bf16[1,3584,512]{2,1,0:T(8,128)(2,1)S(1)}, bf16[1,3584,512]{2,1,0:T(8,128)(2,1)}, u32[]{:S(2)}) copy-start(bf16[1,3584,512]{2,1,0:T(8,128)(2,1)} %param.17) | copy-start | bytes 11010052
  2.5 12.4 %collective-permute-start.2 = (bf16[512,1792]{1,0:T(8,128)(2,1)S(1)}, bf16[512,1792]{1,0:T(8,128)(2,1)S(1)}, u32[]{:S(2)}, u32[]{:S(2)}) collective-permute-start(bf16[512,1792]{1,0:T(8,128)(2,1)S(1)} %get-tuple-element.45), channel_id=1, source_target_pairs={{0,1},{1,0},{2,3},{3,2},{4,5},{5,4},{6,7},{7,6},{8,9},{9,8},{10,11... | collective-permute-start | bytes 5505032 | tf_op jit(solution)/shard_map/ppermute | solution.py:472
  3.0 11.8 %collective-permute-start = (bf16[96,1920]{1,0:T(8,128)(2,1)S(1)}, bf16[96,1920]{1,0:T(8,128)(2,1)S(1)}, u32[]{:S(2)}, u32[]{:S(2)}) collective-permute-start(bf16[96,1920]{1,0:T(8,128)(2,1)S(1)} %get-tuple-element.49.refs_0_.wide_ref), channel_id=1, source_target_pairs={{0,4},{2,6},{4,0},{6,2},{8,12},{10,14},{12,8},{14,10},{1,5},{3,7},... | collective-permute-start | bytes 1105928 | tf_op jit(solution)/shard_map/ppermute | solution.py:468
  5.7 8.3 %collective-permute-start.1 = (bf16[72,1792]{1,0:T(8,128)(2,1)S(1)}, bf16[72,1792]{1,0:T(8,128)(2,1)S(1)}, u32[]{:S(2)}, u32[]{:S(2)}) collective-permute-start(bf16[72,1792]{1,0:T(8,128)(2,1)S(1)} %get-tuple-element.43), channel_id=1, source_target_pairs={{0,2},{2,0},{4,6},{6,4},{8,10},{10,8},{12,14},{14,12},{1,3},{3,1},... | collective-permute-start | bytes 774152 | tf_op jit(solution)/shard_map/ppermute | solution.py:468
  7.2 17.9 %collective-permute-start.3 = (bf16[96,1920]{1,0:T(8,128)(2,1)S(1)}, bf16[96,1920]{1,0:T(8,128)(2,1)S(1)}, u32[]{:S(2)}, u32[]{:S(2)}) collective-permute-start(bf16[96,1920]{1,0:T(8,128)(2,1)S(1)} %get-tuple-element.49.refs_0_.wide_ref), channel_id=1, source_target_pairs={{0,12},{2,14},{4,8},{6,10},{8,4},{10,6},{12,0},{14,2},{1,13},{3,15... | collective-permute-start | bytes 1105928 | tf_op jit(solution)/shard_map/ppermute | solution.py:468
  9.7 1.3 %copy-start.4 = (bf16[4,256,576]{1,2,0:T(8,128)(2,1)S(1)}, bf16[4,256,576]{1,2,0:T(8,128)(2,1)}, u32[]{:S(2)}) copy-start(bf16[4,256,576]{1,2,0:T(8,128)(2,1)} %param.11) | copy-start | bytes 3538948
  15.4 12.6 %collective-permute-start.4 = (bf16[72,1792]{1,0:T(8,128)(2,1)S(1)}, bf16[72,1792]{1,0:T(8,128)(2,1)S(1)}, u32[]{:S(2)}, u32[]{:S(2)}) collective-permute-start(bf16[72,1792]{1,0:T(8,128)(2,1)S(1)} %cross_rows.3), channel_id=1, source_target_pairs={{0,2},{2,0},{4,6},{6,4},{8,10},{10,8},{12,14},{14,12},{1,3},{3,1},... | collective-permute-start | bytes 774152 | tf_op jit(solution)/shard_map/ppermute | solution.py:468
  25.1 10.1 %collective-permute-start.6 = (bf16[96,1920]{1,0:T(8,128)(2,1)S(1)}, bf16[96,1920]{1,0:T(8,128)(2,1)S(1)}, u32[]{:S(2)}, u32[]{:S(2)}) collective-permute-start(bf16[96,1920]{1,0:T(8,128)(2,1)S(1)} %collective-permute-done.3.wide_ref.refs_2_), channel_id=1, source_target_pairs={{0,4},{2,6},{4,0},{6,2},{8,12},{10,14},{12,8},{14,10},{1,5},{3,7},... | collective-permute-start | bytes 1105928 | tf_op jit(solution)/shard_map/ppermute | solution.py:468
  27.4 7.8 %collective-permute-start.7 = (bf16[72,1792]{1,0:T(8,128)(2,1)S(1)}, bf16[72,1792]{1,0:T(8,128)(2,1)S(1)}, u32[]{:S(2)}, u32[]{:S(2)}) collective-permute-start(bf16[72,1792]{1,0:T(8,128)(2,1)S(1)} %cross_rows.4), channel_id=1, source_target_pairs={{0,2},{2,0},{4,6},{6,4},{8,10},{10,8},{12,14},{14,12},{1,3},{3,1},... | collective-permute-start | bytes 774152 | tf_op jit(solution)/shard_map/ppermute | solution.py:468
  28.0 2.0 %copy-start.1 = (bf16[1,3584,512]{2,1,0:T(8,128)(2,1)S(1)}, bf16[1,3584,512]{2,1,0:T(8,128)(2,1)}, u32[]{:S(2)}) copy-start(bf16[1,3584,512]{2,1,0:T(8,128)(2,1)} %param.18) | copy-start | bytes 11010052
  30.1 7.3 %collective-permute-start.5 = (bf16[368,1792]{1,0:T(8,128)(2,1)S(1)}, bf16[368,1792]{1,0:T(8,128)(2,1)S(1)}, u32[]{:S(2)}, u32[]{:S(2)}) collective-permute-start(bf16[368,1792]{1,0:T(8,128)(2,1)S(1)} %pack_rows.2.near_ref), channel_id=1, source_target_pairs={{0,1},{1,0},{2,3},{3,2},{4,5},{5,4},{6,7},{7,6},{8,9},{9,8},{10,11... | collective-permute-start | bytes 3956744 | tf_op jit(solution)/shard_map/ppermute | solution.py:472
  35.2 5.6 %collective-permute-start.10 = (bf16[256,1792]{1,0:T(8,128)(2,1)S(1)}, bf16[256,1792]{1,0:T(8,128)(2,1)S(1)}, u32[]{:S(2)}, u32[]{:S(2)}) collective-permute-start(bf16[256,1792]{1,0:T(8,128)(2,1)S(1)} %pack_rows.3.near_ref), channel_id=1, source_target_pairs={{0,1},{1,0},{2,3},{3,2},{4,5},{5,4},{6,7},{7,6},{8,9},{9,8},{10,11... | collective-permute-start | bytes 2752520 | tf_op jit(solution)/shard_map/ppermute | solution.py:472
  35.3 2.1 %copy-start.2 = (bf16[1,3584,512]{2,1,0:T(8,128)(2,1)S(1)}, bf16[1,3584,512]{2,1,0:T(8,128)(2,1)}, u32[]{:S(2)}) copy-start(bf16[1,3584,512]{2,1,0:T(8,128)(2,1)} %param.18) | copy-start | bytes 11010052
  35.8 8.7 %collective-permute-start.9 = (bf16[72,1792]{1,0:T(8,128)(2,1)S(1)}, bf16[72,1792]{1,0:T(8,128)(2,1)S(1)}, u32[]{:S(2)}, u32[]{:S(2)}) collective-permute-start(bf16[72,1792]{1,0:T(8,128)(2,1)S(1)} %cross_rows.5), channel_id=1, source_target_pairs={{0,2},{2,0},{4,6},{6,4},{8,10},{10,8},{12,14},{14,12},{1,3},{3,1},... | collective-permute-start | bytes 774152 | tf_op jit(solution)/shard_map/ppermute | solution.py:468
  40.3 4.7 %collective-permute-start.8 = (bf16[368,512]{1,0:T(8,128)(2,1)S(1)}, bf16[368,512]{1,0:T(8,128)(2,1)S(1)}, u32[]{:S(2)}, u32[]{:S(2)}) collective-permute-start(bf16[368,512]{1,0:T(8,128)(2,1)S(1)} %hidden_units.3.refs_3_), channel_id=1, source_target_pairs={{0,1},{1,0},{2,3},{3,2},{4,5},{5,4},{6,7},{7,6},{8,9},{9,8},{10,11... | collective-permute-start | bytes 1130504 | tf_op jit(solution)/shard_map/ppermute | solution.py:472
  40.8 4.2 %copy-start.3 = (bf16[1,512,3584]{2,1,0:T(8,128)(2,1)S(1)}, bf16[1,512,3584]{2,1,0:T(8,128)(2,1)}, u32[]{:S(2)}) copy-start(bf16[1,512,3584]{2,1,0:T(8,128)(2,1)} %down_ref.1) | copy-start | bytes 11010052
  44.5 2.1 %collective-permute-start.13 = (bf16[72,1792]{1,0:T(8,128)(2,1)S(1)}, bf16[72,1792]{1,0:T(8,128)(2,1)S(1)}, u32[]{:S(2)}, u32[]{:S(2)}) collective-permute-start(bf16[72,1792]{1,0:T(8,128)(2,1)S(1)} %collective-permute-done.9.near_ref), channel_id=1, source_target_pairs={{0,1},{1,0},{2,3},{3,2},{4,5},{5,4},{6,7},{7,6},{8,9},{9,8},{10,11... | collective-permute-start | bytes 774152 | tf_op jit(solution)/shard_map/ppermute | solution.py:472
  44.5 3.6 %collective-permute-start.12 = (bf16[256,512]{1,0:T(8,128)(2,1)S(1)}, bf16[256,512]{1,0:T(8,128)(2,1)S(1)}, u32[]{:S(2)}, u32[]{:S(2)}) collective-permute-start(bf16[256,512]{1,0:T(8,128)(2,1)S(1)} %hidden_units.4.refs_1_), channel_id=1, source_target_pairs={{0,1},{1,0},{2,3},{3,2},{4,5},{5,4},{6,7},{7,6},{8,9},{9,8},{10,11... | collective-permute-start | bytes 786440 | tf_op jit(solution)/shard_map/ppermute | solution.py:472
  48.0 1.3 %collective-permute-start.16 = (bf16[72,512]{1,0:T(8,128)(2,1)S(1)}, bf16[72,512]{1,0:T(8,128)(2,1)S(1)}, u32[]{:S(2)}, u32[]{:S(2)}) collective-permute-start(bf16[72,512]{1,0:T(8,128)(2,1)S(1)} %hidden_units.5.own_ref), channel_id=1, source_target_pairs={{0,1},{1,0},{2,3},{3,2},{4,5},{5,4},{6,7},{7,6},{8,9},{9,8},{10,11... | collective-permute-start | bytes 221192 | tf_op jit(solution)/shard_map/ppermute | solution.py:472
  50.0 6.4 %collective-permute-start.18 = (bf16[72,896]{1,0:T(8,128)(2,1)S(1)}, bf16[72,896]{1,0:T(8,128)(2,1)S(1)}, u32[]{:S(2)}, u32[]{:S(2)}) collective-permute-start(bf16[72,896]{1,0:T(8,128)(2,1)S(1)} %get-tuple-element.68), channel_id=1, source_target_pairs={{0,2},{2,0},{4,6},{6,4},{8,10},{10,8},{12,14},{14,12},{1,3},{3,1},... | collective-permute-start | bytes 387080 | tf_op jit(solution)/shard_map/ppermute | solution.py:468
  51.6 7.5 %collective-permute-start.17 = (bf16[72,896]{1,0:T(8,128)(2,1)S(1)}, bf16[72,896]{1,0:T(8,128)(2,1)S(1)}, u32[]{:S(2)}, u32[]{:S(2)}) collective-permute-start(bf16[72,896]{1,0:T(8,128)(2,1)S(1)} %get-tuple-element.67), channel_id=1, source_target_pairs={{0,2},{2,0},{4,6},{6,4},{8,10},{10,8},{12,14},{14,12},{1,3},{3,1},... | collective-permute-start | bytes 387080 | tf_op jit(solution)/shard_map/ppermute | solution.py:468
  52.2 12.5 %collective-permute-start.15 = (bf16[72,1792]{1,0:T(8,128)(2,1)S(1)}, bf16[72,1792]{1,0:T(8,128)(2,1)S(1)}, u32[]{:S(2)}, u32[]{:S(2)}) collective-permute-start(bf16[72,1792]{1,0:T(8,128)(2,1)S(1)} %get-tuple-element.64), channel_id=1, source_target_pairs={{0,2},{2,0},{4,6},{6,4},{8,10},{10,8},{12,14},{14,12},{1,3},{3,1},... | collective-permute-start | bytes 774152 | tf_op jit(solution)/shard_map/ppermute | solution.py:468
  53.7 16.6 %collective-permute-start.14 = (bf16[72,1792]{1,0:T(8,128)(2,1)S(1)}, bf16[72,1792]{1,0:T(8,128)(2,1)S(1)}, u32[]{:S(2)}, u32[]{:S(2)}) collective-permute-start(bf16[72,1792]{1,0:T(8,128)(2,1)S(1)} %get-tuple-element.62), channel_id=1, source_target_pairs={{0,2},{2,0},{4,6},{6,4},{8,10},{10,8},{12,14},{14,12},{1,3},{3,1},... | collective-permute-start | bytes 774152 | tf_op jit(solution)/shard_map/ppermute | solution.py:468
  56.8 7.9 %collective-permute-start.20 = (bf16[96,896]{1,0:T(8,128)(2,1)S(1)}, bf16[96,896]{1,0:T(8,128)(2,1)S(1)}, u32[]{:S(2)}, u32[]{:S(2)}) collective-permute-start(bf16[96,896]{1,0:T(8,128)(2,1)S(1)} %combine.7), channel_id=1, source_target_pairs={{0,4},{2,6},{4,0},{6,2},{8,12},{10,14},{12,8},{14,10},{1,5},{3,7},... | collective-permute-start | bytes 516104 | tf_op jit(solution)/shard_map/ppermute | solution.py:468
  59.6 9.4 %collective-permute-start.19 = (bf16[96,896]{1,0:T(8,128)(2,1)S(1)}, bf16[96,896]{1,0:T(8,128)(2,1)S(1)}, u32[]{:S(2)}, u32[]{:S(2)}) collective-permute-start(bf16[96,896]{1,0:T(8,128)(2,1)S(1)} %combine.8), channel_id=1, source_target_pairs={{0,4},{2,6},{4,0},{6,2},{8,12},{10,14},{12,8},{14,10},{1,5},{3,7},... | collective-permute-start | bytes 516104 | tf_op jit(solution)/shard_map/ppermute | solution.py:468
  61.2 14.0 %collective-permute-start.11 = (bf16[72,1792]{1,0:T(8,128)(2,1)S(1)}, bf16[72,1792]{1,0:T(8,128)(2,1)S(1)}, u32[]{:S(2)}, u32[]{:S(2)}) collective-permute-start(bf16[72,1792]{1,0:T(8,128)(2,1)S(1)} %get-tuple-element.58), channel_id=1, source_target_pairs={{0,2},{2,0},{4,6},{6,4},{8,10},{10,8},{12,14},{14,12},{1,3},{3,1},... | collective-permute-start | bytes 774152 | tf_op jit(solution)/shard_map/ppermute | solution.py:468
  65.1 10.1 %collective-permute-start.21 = (bf16[96,896]{1,0:T(8,128)(2,1)S(1)}, bf16[96,896]{1,0:T(8,128)(2,1)S(1)}, u32[]{:S(2)}, u32[]{:S(2)}) collective-permute-start(bf16[96,896]{1,0:T(8,128)(2,1)S(1)} %combine.9), channel_id=1, source_target_pairs={{0,12},{2,14},{4,8},{6,10},{8,4},{10,6},{12,0},{14,2},{1,13},{3,15... | collective-permute-start | bytes 516104 | tf_op jit(solution)/shard_map/ppermute | solution.py:468
  69.4 9.0 %collective-permute-start.22 = (bf16[96,896]{1,0:T(8,128)(2,1)S(1)}, bf16[96,896]{1,0:T(8,128)(2,1)S(1)}, u32[]{:S(2)}, u32[]{:S(2)}) collective-permute-start(bf16[96,896]{1,0:T(8,128)(2,1)S(1)} %combine.10), channel_id=1, source_target_pairs={{0,12},{2,14},{4,8},{6,10},{8,4},{10,6},{12,0},{14,2},{1,13},{3,15... | collective-permute-start | bytes 516104 | tf_op jit(solution)/shard_map/ppermute | solution.py:468
  70.7 10.3 %collective-permute-start.23 = (bf16[96,896]{1,0:T(8,128)(2,1)S(1)}, bf16[96,896]{1,0:T(8,128)(2,1)S(1)}, u32[]{:S(2)}, u32[]{:S(2)}) collective-permute-start(bf16[96,896]{1,0:T(8,128)(2,1)S(1)} %get-tuple-element.74), channel_id=1, source_target_pairs={{0,4},{2,6},{4,0},{6,2},{8,12},{10,14},{12,8},{14,10},{1,5},{3,7},... | collective-permute-start | bytes 516104 | tf_op jit(solution)/shard_map/ppermute | solution.py:468
  72.3 11.4 %collective-permute-start.24 = (bf16[96,896]{1,0:T(8,128)(2,1)S(1)}, bf16[96,896]{1,0:T(8,128)(2,1)S(1)}, u32[]{:S(2)}, u32[]{:S(2)}) collective-permute-start(bf16[96,896]{1,0:T(8,128)(2,1)S(1)} %get-tuple-element.79), channel_id=1, source_target_pairs={{0,4},{2,6},{4,0},{6,2},{8,12},{10,14},{12,8},{14,10},{1,5},{3,7},... | collective-permute-start | bytes 516104 | tf_op jit(solution)/shard_map/ppermute | solution.py:468

commit v10 on v9

--- a/solution.py
+++ b/solution.py
@@ -491,19 +491,21 @@
     down_other = swap_core(down_away)
     attended = attend(after(q_lat, wide), latent_cache, lengths, placement)
     cross_in = after(cross_in, attended)
-    wide_pair = after(wide_pair, cross_in, down_other)
-    cross_pair = cross_rows(wide_pair, role_count, capacity)
-    cross_pair_in = swap(cross_pair, row)
-    wide_mirror = after(wide_mirror, cross_pair)
+    wide_mirror = after(wide_mirror, cross_in, down_other)
     wide_far = swap(wide_mirror, pair)
     cross_mirror = cross_rows(wide_mirror, role_count, capacity)
     cross_mirror_in = swap(cross_mirror, row)
-    cross_pair_in = after(cross_pair_in, cross_mirror)
-    near_first = pack((after(wide, cross_pair_in), wide_pair, wide_mirror, cross_in), half, (w_gate, w_up))
+    wide_pair = after(wide_pair, cross_mirror)
+    cross_pair = cross_rows(wide_pair, role_count, capacity)
+    cross_pair_in = swap(cross_pair, row)
+    near_first = pack(
+        (after(wide, cross_pair), wide_pair, wide_mirror, cross_in), half, (w_gate, w_up)
+    )
     far_first = swap_core(near_first)
-    wide_far = after(wide_far, near_first)
-    cross_mirror_in = after(cross_mirror_in, wide_far)
+    cross_mirror_in = after(cross_mirror_in, near_first)
     wide_far = after(wide_far, cross_mirror_in)
+    cross_pair_in = after(cross_pair_in, wide_far)
+    wide_far = after(wide_far, cross_pair_in)
     cross_far = cross_rows(wide_far, role_count, capacity, 10**10)
     cross_far_in = swap(cross_far, row)
     near_second = pack((wide_far, cross_pair_in, cross_mirror_in), half)

time: 84.7 us -> 87.5 us (1.033)
  starting transfers between devices: 28.6 us -> 31.3 us
    ppermute x18, starting transfers between devices: 26.9 us -> 29.6 us  [swap(): return lax.ppermute(array, 'role', pairs)]
  transfers between devices with their start and end apart: 25 -> 25, of which waited for: 13 -> 14; matrix products, arithmetic and copies ran while one was open for 0% -> 0% of each run, Pallas kernels for 19% -> 18%
where the time goes in v10:
time: 87.5 us; the launch traced here: 87.3 us
  waiting for transfers between devices  32.7 us (37%)
  starting transfers between devices  31.3 us (36%)
  Pallas kernels  19 us (22%)
  local copies, waits for them, and re-layouts  3.33 us (4%)
  between operations  0.89 us (1%)
    ppermute x18, waiting for transfers between devices, swap(): return lax.ppermute(array, 'role', pairs)  32.6 us
    ppermute x18, starting transfers between devices, swap(): return lax.ppermute(array, 'role', pairs)  29.6 us
    pallas_call x19, Pallas kernels, call(): pl.pallas_call(kernel, in_specs=[place] * len(operands), out_specs=[place...  15.1 us
    unnamed x16, local copies, waits for them, and re-layouts  3.33 us
    pallas_call x1, Pallas kernels, attend(): pl.pallas_call(attend_kernel, out_shape=jax.ShapeDtypeStruct((slot_count,...  2.05 us
    pallas_call x1, Pallas kernels, prepare(): pl.pallas_call(functools.partial(prepare_kernel, expert_count), in_specs=...  1.82 us
  transfers between devices with their start and end apart: 25, of which 14 were waited for; matrix products, arithmetic and copies ran while one was open for 0% of the time, Pallas kernels for 18%

profile of v10, /device:TPU:0, one launch (start us, length us, event | category | flops | bytes accessed | tf_op | source)
XLA Modules:
  0.0 87.3 jit_solution(15423972149080047282)
XLA Ops:
  0.7 1.8 %prepare.1 = (bf16[96,1920]{1,0:T(8,128)(2,1)S(1)}, bf16[72,1792]{1,0:T(8,128)(2,1)S(1)}, bf16[512,1792]{1,0:T(8,128)(2,1)S(1)}) custom-call(bf16[96,1792]{1,0:T(8,128)(2,1)} %tokens_hbm.1, bf16[1,512,3584]{2,1,0:T(8,128)(2,1)} %down_ref.1, s32[4,96]{1,0:T(4,128)} %bitcast.18, f32[4,96]{1,0:T(4,128)} %bitcast.19), custom_call_target="tpu_custom_call" | custom-call | tf_op jit(solution)/shard_map/prepare/pallas_call | solution.py:212
  2.5 0.5 collective-permute-start.3
  3.0 4.7 %collective-permute-start.1 = (bf16[96,1920]{1,0:T(8,128)(2,1)S(1)}, bf16[96,1920]{1,0:T(8,128)(2,1)S(1)}, u32[]{:S(2)}, u32[]{:S(2)}) collective-permute-start(bf16[96,1920]{1,0:T(8,128)(2,1)S(1)} %get-tuple-element.48.refs_0_.wide_ref), channel_id=1, source_target_pairs={{0,12},{2,14},{4,8},{6,10},{8,4},{10,6},{12,0},{14,2},{1,13},{3,15... | collective-permute-start | bytes 1105928 | tf_op jit(solution)/shard_map/ppermute | solution.py:468
  7.7 1.5 %collective-permute-start.2 = (bf16[72,1792]{1,0:T(8,128)(2,1)S(1)}, bf16[72,1792]{1,0:T(8,128)(2,1)S(1)}, u32[]{:S(2)}, u32[]{:S(2)}) collective-permute-start(bf16[72,1792]{1,0:T(8,128)(2,1)S(1)} %get-tuple-element.43), channel_id=1, source_target_pairs={{0,2},{2,0},{4,6},{6,4},{8,10},{10,8},{12,14},{14,12},{1,3},{3,1},... | collective-permute-start | bytes 774152 | tf_op jit(solution)/shard_map/ppermute | solution.py:468
  9.2 0.0 copy-start.4
  9.2 1.3 %copy-done.4 = bf16[4,256,576]{1,2,0:T(8,128)(2,1)S(1)} copy-done((bf16[4,256,576]{1,2,0:T(8,128)(2,1)S(1)}, bf16[4,256,576]{1,2,0:T(8,128)(2,1)}, u32[]{:S(2)}) %copy-start.4) | copy-done | bytes 1179672
  10.5 2.0 %attend.1 = bf16[4,32,512]{2,1,0:T(8,128)(2,1)} custom-call(bf16[4,32,576]{2,1,0:T(8,128)(2,1)S(1)} %copy-done.5, bf16[4,576,256]{2,1,0:T(8,128)(2,1)S(1)} %bitcast.15, s32[1,32]{1,0:T(1,128)S(1)} %bitcast.16, s32[1,32]{1,0:T(1,128)S(1)} %bitcast.17), custom_call_target="tpu_custom_call" | custom-call | tf_op jit(solution)/shard_map/attend/pallas_call | solution.py:373
  12.6 3.4 %collective-permute-done.2.refs_3_ = bf16[72,1792]{1,0:T(8,128)(2,1)S(1)} collective-permute-done((bf16[72,1792]{1,0:T(8,128)(2,1)S(1)}, bf16[72,1792]{1,0:T(8,128)(2,1)S(1)}, u32[]{:S(2)}, u32[]{:S(2)}) %collective-permute-start.2) | collective-permute-done | bytes 258080 | tf_op jit(solution)/shard_map/ppermute | solution.py:468
  16.0 1.2 %collective-permute-done.1.wide_ref.refs_2_ = bf16[96,1920]{1,0:T(8,128)(2,1)S(1)} collective-permute-done((bf16[96,1920]{1,0:T(8,128)(2,1)S(1)}, bf16[96,1920]{1,0:T(8,128)(2,1)S(1)}, u32[]{:S(2)}, u32[]{:S(2)}) %collective-permute-start.1) | collective-permute-done | bytes 368672 | tf_op jit(solution)/shard_map/ppermute | solution.py:468
  17.2 7.3 %collective-permute-start.5 = (bf16[96,1920]{1,0:T(8,128)(2,1)S(1)}, bf16[96,1920]{1,0:T(8,128)(2,1)S(1)}, u32[]{:S(2)}, u32[]{:S(2)}) collective-permute-start(bf16[96,1920]{1,0:T(8,128)(2,1)S(1)} %collective-permute-done.1.wide_ref.refs_2_), channel_id=1, source_target_pairs={{0,4},{2,6},{4,0},{6,2},{8,12},{10,14},{12,8},{14,10},{1,5},{3,7},... | collective-permute-start | bytes 1105928 | tf_op jit(solution)/shard_map/ppermute | solution.py:468
  24.5 0.5 cross_rows.3
  25.0 1.6 %collective-permute-start.6 = (bf16[72,1792]{1,0:T(8,128)(2,1)S(1)}, bf16[72,1792]{1,0:T(8,128)(2,1)S(1)}, u32[]{:S(2)}, u32[]{:S(2)}) collective-permute-start(bf16[72,1792]{1,0:T(8,128)(2,1)S(1)} %cross_rows.3), channel_id=1, source_target_pairs={{0,2},{2,0},{4,6},{6,4},{8,10},{10,8},{12,14},{14,12},{1,3},{3,1},... | collective-permute-start | bytes 774152 | tf_op jit(solution)/shard_map/ppermute | solution.py:468
  26.6 0.5 cross_rows.4
  27.2 0.5 collective-permute-start.7
  27.7 2.0 %copy-done.1 = bf16[1,3584,512]{2,1,0:T(8,128)(2,1)S(1)} copy-done((bf16[1,3584,512]{2,1,0:T(8,128)(2,1)S(1)}, bf16[1,3584,512]{2,1,0:T(8,128)(2,1)}, u32[]{:S(2)}) %copy-start.1) | copy-done | bytes 3670040
  29.8 0.1 pack_rows.2.near_ref
  29.9 0.1 collective-permute-start.4
  29.9 4.3 %collective-permute-done.6.refs_2_ = bf16[72,1792]{1,0:T(8,128)(2,1)S(1)} collective-permute-done((bf16[72,1792]{1,0:T(8,128)(2,1)S(1)}, bf16[72,1792]{1,0:T(8,128)(2,1)S(1)}, u32[]{:S(2)}, u32[]{:S(2)}) %collective-permute-start.6) | collective-permute-done | bytes 258080 | tf_op jit(solution)/shard_map/ppermute | solution.py:468
  34.3 0.0 collective-permute-done.5.refs_0_.wide_ref
  34.3 3.9 %collective-permute-done.7.refs_1_ = bf16[72,1792]{1,0:T(8,128)(2,1)S(1)} collective-permute-done((bf16[72,1792]{1,0:T(8,128)(2,1)S(1)}, bf16[72,1792]{1,0:T(8,128)(2,1)S(1)}, u32[]{:S(2)}, u32[]{:S(2)}) %collective-permute-start.7) | collective-permute-done | bytes 258080 | tf_op jit(solution)/shard_map/ppermute | solution.py:468
  38.1 0.1 pack_rows.3.near_ref
  38.2 0.1 collective-permute-start.10
  38.3 0.0 copy-start.2
  38.3 0.5 cross_rows.5
  38.8 1.6 %collective-permute-start.9 = (bf16[72,1792]{1,0:T(8,128)(2,1)S(1)}, bf16[72,1792]{1,0:T(8,128)(2,1)S(1)}, u32[]{:S(2)}, u32[]{:S(2)}) collective-permute-start(bf16[72,1792]{1,0:T(8,128)(2,1)S(1)} %cross_rows.5), channel_id=1, source_target_pairs={{0,2},{2,0},{4,6},{6,4},{8,10},{10,8},{12,14},{14,12},{1,3},{3,1},... | collective-permute-start | bytes 774152 | tf_op jit(solution)/shard_map/ppermute | solution.py:468
  40.4 2.9 %hidden_units.3.refs_3_ = bf16[368,512]{1,0:T(8,128)(2,1)S(1)} custom-call(bf16[368,1792]{1,0:T(8,128)(2,1)S(1)} %pack_rows.2.near_ref, bf16[368,1792]{1,0:T(8,128)(2,1)S(1)} %collective-permute-done.4.far_ref, bf16[3584,512]{1,0:T(8,128)(2,1)S(1)} %bitcast.8, bf16[3584,512]{1,0:T(8,128)(2,1)S(1)} %bitcast.12), custom_call_target="tpu_custom_call" | custom-call | tf_op jit(solution)/shard_map/hidden_units/pallas_call | solution.py:91
  43.3 0.5 collective-permute-start.8
  43.8 2.1 %hidden_units.4.refs_1_ = bf16[256,512]{1,0:T(8,128)(2,1)S(1)} custom-call(bf16[256,1792]{1,0:T(8,128)(2,1)S(1)} %pack_rows.3.near_ref, bf16[256,1792]{1,0:T(8,128)(2,1)S(1)} %collective-permute-done.10.far_ref, bf16[3584,512]{1,0:T(8,128)(2,1)S(1)} %bitcast.9, bf16[3584,512]{1,0:T(8,128)(2,1)S(1)} %bitcast.13), custom_call_target="tpu_custom_call" | custom-call | tf_op jit(solution)/shard_map/hidden_units/pallas_call | solution.py:91
  45.9 1.6 %collective-permute-done.9.near_ref = bf16[72,1792]{1,0:T(8,128)(2,1)S(1)} collective-permute-done((bf16[72,1792]{1,0:T(8,128)(2,1)S(1)}, bf16[72,1792]{1,0:T(8,128)(2,1)S(1)}, u32[]{:S(2)}, u32[]{:S(2)}) %collective-permute-start.9) | collective-permute-done | bytes 258080 | tf_op jit(solution)/shard_map/ppermute | solution.py:468
  47.5 0.0 collective-permute-start.13
  47.5 0.5 collective-permute-start.12
  48.0 1.5 %down.2 = (f32[96,1792]{1,0:T(8,128)S(1)}, f32[96,1792]{1,0:T(8,128)S(1)}, f32[96,1792]{1,0:T(8,128)S(1)}, bf16[72,1792]{1,0:T(8,128)(2,1)S(1)}) custom-call(bf16[96,1920]{1,0:T(8,128)(2,1)S(1)} %get-tuple-element.48.refs_0_.wide_ref, bf16[96,1920]{1,0:T(8,128)(2,1)S(1)} %collective-permute-done.wide_ref.refs_1_, ...), custom_call_target="tpu_custom_call" | custom-call | tf_op jit(solution)/shard_map/down/pallas_call | solution.py:91
  49.6 1.4 %hidden_units.5.own_ref = bf16[72,512]{1,0:T(8,128)(2,1)S(1)} custom-call(bf16[72,1792]{1,0:T(8,128)(2,1)S(1)} %collective-permute-done.9.near_ref, bf16[72,1792]{1,0:T(8,128)(2,1)S(1)} %collective-permute-done.13.far_ref, bf16[3584,512]{1,0:T(8,128)(2,1)S(1)} %bitcast.10, bf16[3584,512]{1,0:T(8,128)(2,1)S(1)} %bitcast.14), custom_call_target="tpu_custom_call" | custom-call | tf_op jit(solution)/shard_map/hidden_units/pallas_call | solution.py:91
  51.0 0.1 collective-permute-start.16
  51.1 1.1 %down.3 = (f32[96,1792]{1,0:T(8,128)S(1)}, bf16[72,1792]{1,0:T(8,128)(2,1)S(1)}, bf16[72,1792]{1,0:T(8,128)(2,1)S(1)}) custom-call(bf16[96,1920]{1,0:T(8,128)(2,1)S(1)} %collective-permute-done.5.refs_0_.wide_ref, bf16[256,512]{1,0:T(8,128)(2,1)S(1)} %hidden_units.4.refs_1_, bf16[256,512]{1,0:T(8,128)(2,1)S(1)} %collective-permute-done.12.refs_2_, ...), custom_call_target="tpu_custom_call" | custom-call | tf_op jit(solution)/shard_map/down/pallas_call | solution.py:91
  52.2 0.1 collective-permute-done.16.other_ref
  52.3 0.7 last_down.1
  53.0 1.6 %collective-permute-start.18 = (bf16[72,896]{1,0:T(8,128)(2,1)S(1)}, bf16[72,896]{1,0:T(8,128)(2,1)S(1)}, u32[]{:S(2)}, u32[]{:S(2)}) collective-permute-start(bf16[72,896]{1,0:T(8,128)(2,1)S(1)} %get-tuple-element.68), channel_id=1, source_target_pairs={{0,2},{2,0},{4,6},{6,4},{8,10},{10,8},{12,14},{14,12},{1,3},{3,1},... | collective-permute-start | bytes 387080 | tf_op jit(solution)/shard_map/ppermute | solution.py:468
  54.6 0.5 collective-permute-start.17
  55.1 1.5 %collective-permute-start.15 = (bf16[72,1792]{1,0:T(8,128)(2,1)S(1)}, bf16[72,1792]{1,0:T(8,128)(2,1)S(1)}, u32[]{:S(2)}, u32[]{:S(2)}) collective-permute-start(bf16[72,1792]{1,0:T(8,128)(2,1)S(1)} %get-tuple-element.64), channel_id=1, source_target_pairs={{0,2},{2,0},{4,6},{6,4},{8,10},{10,8},{12,14},{14,12},{1,3},{3,1},... | collective-permute-start | bytes 774152 | tf_op jit(solution)/shard_map/ppermute | solution.py:468
  56.7 0.5 collective-permute-start.14
  57.2 2.2 %collective-permute-done.18.back_ref = bf16[72,896]{1,0:T(8,128)(2,1)S(1)} collective-permute-done((bf16[72,896]{1,0:T(8,128)(2,1)S(1)}, bf16[72,896]{1,0:T(8,128)(2,1)S(1)}, u32[]{:S(2)}, u32[]{:S(2)}) %collective-permute-start.18) | collective-permute-done | bytes 129056 | tf_op jit(solution)/shard_map/ppermute | solution.py:468
  59.4 0.4 combine.7
  59.8 0.4 collective-permute-start.20
  60.1 2.0 %collective-permute-done.17.back_ref = bf16[72,896]{1,0:T(8,128)(2,1)S(1)} collective-permute-done((bf16[72,896]{1,0:T(8,128)(2,1)S(1)}, bf16[72,896]{1,0:T(8,128)(2,1)S(1)}, u32[]{:S(2)}, u32[]{:S(2)}) %collective-permute-start.17) | collective-permute-done | bytes 129056 | tf_op jit(solution)/shard_map/ppermute | solution.py:468
  62.1 0.4 combine.8
  62.5 0.4 collective-permute-start.19
  62.9 1.5 %collective-permute-start.11 = (bf16[72,1792]{1,0:T(8,128)(2,1)S(1)}, bf16[72,1792]{1,0:T(8,128)(2,1)S(1)}, u32[]{:S(2)}, u32[]{:S(2)}) collective-permute-start(bf16[72,1792]{1,0:T(8,128)(2,1)S(1)} %get-tuple-element.58), channel_id=1, source_target_pairs={{0,2},{2,0},{4,6},{6,4},{8,10},{10,8},{12,14},{14,12},{1,3},{3,1},... | collective-permute-start | bytes 774152 | tf_op jit(solution)/shard_map/ppermute | solution.py:468
  64.4 3.2 %collective-permute-done.15.back_ref = bf16[72,1792]{1,0:T(8,128)(2,1)S(1)} collective-permute-done((bf16[72,1792]{1,0:T(8,128)(2,1)S(1)}, bf16[72,1792]{1,0:T(8,128)(2,1)S(1)}, u32[]{:S(2)}, u32[]{:S(2)}) %collective-permute-start.15) | collective-permute-done | bytes 258080 | tf_op jit(solution)/shard_map/ppermute | solution.py:468
  67.7 0.4 combine.9
  68.1 2.5 %collective-permute-start.21 = (bf16[96,896]{1,0:T(8,128)(2,1)S(1)}, bf16[96,896]{1,0:T(8,128)(2,1)S(1)}, u32[]{:S(2)}, u32[]{:S(2)}) collective-permute-start(bf16[96,896]{1,0:T(8,128)(2,1)S(1)} %combine.9), channel_id=1, source_target_pairs={{0,12},{2,14},{4,8},{6,10},{8,4},{10,6},{12,0},{14,2},{1,13},{3,15... | collective-permute-start | bytes 516104 | tf_op jit(solution)/shard_map/ppermute | solution.py:468
  70.6 0.4 combine.10
  71.0 1.4 %collective-permute-start.22 = (bf16[96,896]{1,0:T(8,128)(2,1)S(1)}, bf16[96,896]{1,0:T(8,128)(2,1)S(1)}, u32[]{:S(2)}, u32[]{:S(2)}) collective-permute-start(bf16[96,896]{1,0:T(8,128)(2,1)S(1)} %combine.10), channel_id=1, source_target_pairs={{0,12},{2,14},{4,8},{6,10},{8,4},{10,6},{12,0},{14,2},{1,13},{3,15... | collective-permute-start | bytes 516104 | tf_op jit(solution)/shard_map/ppermute | solution.py:468
  72.4 0.7 collective-permute-done.14.back_ref
  73.2 0.4 combine.11
  73.7 0.4 collective-permute-start.23
  74.0 1.7 %collective-permute-start.24 = (bf16[96,896]{1,0:T(8,128)(2,1)S(1)}, bf16[96,896]{1,0:T(8,128)(2,1)S(1)}, u32[]{:S(2)}, u32[]{:S(2)}) collective-permute-start(bf16[96,896]{1,0:T(8,128)(2,1)S(1)} %get-tuple-element.79), channel_id=1, source_target_pairs={{0,4},{2,6},{4,0},{6,2},{8,12},{10,14},{12,8},{14,10},{1,5},{3,7},... | collective-permute-start | bytes 516104 | tf_op jit(solution)/shard_map/ppermute | solution.py:468
  75.7 2.4 %collective-permute-done.11.back_ref = bf16[72,1792]{1,0:T(8,128)(2,1)S(1)} collective-permute-done((bf16[72,1792]{1,0:T(8,128)(2,1)S(1)}, bf16[72,1792]{1,0:T(8,128)(2,1)S(1)}, u32[]{:S(2)}, u32[]{:S(2)}) %collective-permute-start.11) | collective-permute-done | bytes 258080 | tf_op jit(solution)/shard_map/ppermute | solution.py:468
  78.2 0.4 combine.12.refs_0_
  78.6 1.6 %collective-permute-done.22.refs_0_ = bf16[96,896]{1,0:T(8,128)(2,1)S(1)} collective-permute-done((bf16[96,896]{1,0:T(8,128)(2,1)S(1)}, bf16[96,896]{1,0:T(8,128)(2,1)S(1)}, u32[]{:S(2)}, u32[]{:S(2)}) %collective-permute-start.22) | collective-permute-done | bytes 172064 | tf_op jit(solution)/shard_map/ppermute | solution.py:468
  80.2 0.4 combine.13.refs_1_
  80.6 2.2 %collective-permute-done.23.refs_2_ = bf16[96,896]{1,0:T(8,128)(2,1)S(1)} collective-permute-done((bf16[96,896]{1,0:T(8,128)(2,1)S(1)}, bf16[96,896]{1,0:T(8,128)(2,1)S(1)}, u32[]{:S(2)}, u32[]{:S(2)}) %collective-permute-start.23) | collective-permute-done | bytes 172064 | tf_op jit(solution)/shard_map/ppermute | solution.py:468
  82.9 3.6 %collective-permute-done.24.refs_3_ = bf16[96,896]{1,0:T(8,128)(2,1)S(1)} collective-permute-done((bf16[96,896]{1,0:T(8,128)(2,1)S(1)}, bf16[96,896]{1,0:T(8,128)(2,1)S(1)}, u32[]{:S(2)}, u32[]{:S(2)}) %collective-permute-start.24) | collective-permute-done | bytes 172064 | tf_op jit(solution)/shard_map/ppermute | solution.py:468
  86.5 0.8 add_last.1
  (23 shorter events, 0.1 us)
Async XLA Ops:
  0.6 8.6 %copy-start.5 = (bf16[4,32,576]{2,1,0:T(8,128)(2,1)S(1)}, bf16[4,32,576]{2,1,0:T(8,128)(2,1)}, u32[]{:S(2)}) copy-start(bf16[4,32,576]{2,1,0:T(8,128)(2,1)} %query_ref) | copy-start | bytes 442372
  0.6 8.6 %copy-start.6 = (s32[32]{0:T(128)S(1)}, s32[32]{0:T(128)}, u32[]{:S(2)}) copy-start(s32[32]{0:T(128)} %param.12) | copy-start | bytes 388
  0.7 8.6 %copy-start.7 = (s32[32]{0:T(128)S(1)}, s32[32]{0:T(128)}, u32[]{:S(2)}) copy-start(s32[32]{0:T(128)} %param.13) | copy-start | bytes 388
  0.7 27.1 %copy-start = (bf16[1,3584,512]{2,1,0:T(8,128)(2,1)S(1)}, bf16[1,3584,512]{2,1,0:T(8,128)(2,1)}, u32[]{:S(2)}) copy-start(bf16[1,3584,512]{2,1,0:T(8,128)(2,1)} %param.17) | copy-start | bytes 11010052
  2.5 14.7 %collective-permute-start.3 = (bf16[512,1792]{1,0:T(8,128)(2,1)S(1)}, bf16[512,1792]{1,0:T(8,128)(2,1)S(1)}, u32[]{:S(2)}, u32[]{:S(2)}) collective-permute-start(bf16[512,1792]{1,0:T(8,128)(2,1)S(1)} %get-tuple-element.45), channel_id=1, source_target_pairs={{0,1},{1,0},{2,3},{3,2},{4,5},{5,4},{6,7},{7,6},{8,9},{9,8},{10,11... | collective-permute-start | bytes 5505032 | tf_op jit(solution)/shard_map/ppermute | solution.py:472
  3.0 14.2 %collective-permute-start.1 = (bf16[96,1920]{1,0:T(8,128)(2,1)S(1)}, bf16[96,1920]{1,0:T(8,128)(2,1)S(1)}, u32[]{:S(2)}, u32[]{:S(2)}) collective-permute-start(bf16[96,1920]{1,0:T(8,128)(2,1)S(1)} %get-tuple-element.48.refs_0_.wide_ref), channel_id=1, source_target_pairs={{0,12},{2,14},{4,8},{6,10},{8,4},{10,6},{12,0},{14,2},{1,13},{3,15... | collective-permute-start | bytes 1105928 | tf_op jit(solution)/shard_map/ppermute | solution.py:468
  7.7 8.3 %collective-permute-start.2 = (bf16[72,1792]{1,0:T(8,128)(2,1)S(1)}, bf16[72,1792]{1,0:T(8,128)(2,1)S(1)}, u32[]{:S(2)}, u32[]{:S(2)}) collective-permute-start(bf16[72,1792]{1,0:T(8,128)(2,1)S(1)} %get-tuple-element.43), channel_id=1, source_target_pairs={{0,2},{2,0},{4,6},{6,4},{8,10},{10,8},{12,14},{14,12},{1,3},{3,1},... | collective-permute-start | bytes 774152 | tf_op jit(solution)/shard_map/ppermute | solution.py:468
  9.2 17.4 %collective-permute-start = (bf16[96,1920]{1,0:T(8,128)(2,1)S(1)}, bf16[96,1920]{1,0:T(8,128)(2,1)S(1)}, u32[]{:S(2)}, u32[]{:S(2)}) collective-permute-start(bf16[96,1920]{1,0:T(8,128)(2,1)S(1)} %get-tuple-element.48.refs_0_.wide_ref), channel_id=1, source_target_pairs={{0,4},{2,6},{4,0},{6,2},{8,12},{10,14},{12,8},{14,10},{1,5},{3,7},... | collective-permute-start | bytes 1105928 | tf_op jit(solution)/shard_map/ppermute | solution.py:468
  9.2 1.3 %copy-start.4 = (bf16[4,256,576]{1,2,0:T(8,128)(2,1)S(1)}, bf16[4,256,576]{1,2,0:T(8,128)(2,1)}, u32[]{:S(2)}) copy-start(bf16[4,256,576]{1,2,0:T(8,128)(2,1)} %param.11) | copy-start | bytes 3538948
  17.2 17.0 %collective-permute-start.5 = (bf16[96,1920]{1,0:T(8,128)(2,1)S(1)}, bf16[96,1920]{1,0:T(8,128)(2,1)S(1)}, u32[]{:S(2)}, u32[]{:S(2)}) collective-permute-start(bf16[96,1920]{1,0:T(8,128)(2,1)S(1)} %collective-permute-done.1.wide_ref.refs_2_), channel_id=1, source_target_pairs={{0,4},{2,6},{4,0},{6,2},{8,12},{10,14},{12,8},{14,10},{1,5},{3,7},... | collective-permute-start | bytes 1105928 | tf_op jit(solution)/shard_map/ppermute | solution.py:468
  25.0 9.2 %collective-permute-start.6 = (bf16[72,1792]{1,0:T(8,128)(2,1)S(1)}, bf16[72,1792]{1,0:T(8,128)(2,1)S(1)}, u32[]{:S(2)}, u32[]{:S(2)}) collective-permute-start(bf16[72,1792]{1,0:T(8,128)(2,1)S(1)} %cross_rows.3), channel_id=1, source_target_pairs={{0,2},{2,0},{4,6},{6,4},{8,10},{10,8},{12,14},{14,12},{1,3},{3,1},... | collective-permute-start | bytes 774152 | tf_op jit(solution)/shard_map/ppermute | solution.py:468
  27.2 11.0 %collective-permute-start.7 = (bf16[72,1792]{1,0:T(8,128)(2,1)S(1)}, bf16[72,1792]{1,0:T(8,128)(2,1)S(1)}, u32[]{:S(2)}, u32[]{:S(2)}) collective-permute-start(bf16[72,1792]{1,0:T(8,128)(2,1)S(1)} %cross_rows.4), channel_id=1, source_target_pairs={{0,2},{2,0},{4,6},{6,4},{8,10},{10,8},{12,14},{14,12},{1,3},{3,1},... | collective-permute-start | bytes 774152 | tf_op jit(solution)/shard_map/ppermute | solution.py:468
  27.7 2.0 %copy-start.1 = (bf16[1,3584,512]{2,1,0:T(8,128)(2,1)S(1)}, bf16[1,3584,512]{2,1,0:T(8,128)(2,1)}, u32[]{:S(2)}) copy-start(bf16[1,3584,512]{2,1,0:T(8,128)(2,1)} %param.18) | copy-start | bytes 11010052
  29.9 10.6 %collective-permute-start.4 = (bf16[368,1792]{1,0:T(8,128)(2,1)S(1)}, bf16[368,1792]{1,0:T(8,128)(2,1)S(1)}, u32[]{:S(2)}, u32[]{:S(2)}) collective-permute-start(bf16[368,1792]{1,0:T(8,128)(2,1)S(1)} %pack_rows.2.near_ref), channel_id=1, source_target_pairs={{0,1},{1,0},{2,3},{3,2},{4,5},{5,4},{6,7},{7,6},{8,9},{9,8},{10,11... | collective-permute-start | bytes 3956744 | tf_op jit(solution)/shard_map/ppermute | solution.py:472
  38.2 5.6 %collective-permute-start.10 = (bf16[256,1792]{1,0:T(8,128)(2,1)S(1)}, bf16[256,1792]{1,0:T(8,128)(2,1)S(1)}, u32[]{:S(2)}, u32[]{:S(2)}) collective-permute-start(bf16[256,1792]{1,0:T(8,128)(2,1)S(1)} %pack_rows.3.near_ref), channel_id=1, source_target_pairs={{0,1},{1,0},{2,3},{3,2},{4,5},{5,4},{6,7},{7,6},{8,9},{9,8},{10,11... | collective-permute-start | bytes 2752520 | tf_op jit(solution)/shard_map/ppermute | solution.py:472
  38.3 2.1 %copy-start.2 = (bf16[1,3584,512]{2,1,0:T(8,128)(2,1)S(1)}, bf16[1,3584,512]{2,1,0:T(8,128)(2,1)}, u32[]{:S(2)}) copy-start(bf16[1,3584,512]{2,1,0:T(8,128)(2,1)} %param.18) | copy-start | bytes 11010052
  38.8 8.7 %collective-permute-start.9 = (bf16[72,1792]{1,0:T(8,128)(2,1)S(1)}, bf16[72,1792]{1,0:T(8,128)(2,1)S(1)}, u32[]{:S(2)}, u32[]{:S(2)}) collective-permute-start(bf16[72,1792]{1,0:T(8,128)(2,1)S(1)} %cross_rows.5), channel_id=1, source_target_pairs={{0,2},{2,0},{4,6},{6,4},{8,10},{10,8},{12,14},{14,12},{1,3},{3,1},... | collective-permute-start | bytes 774152 | tf_op jit(solution)/shard_map/ppermute | solution.py:468
  43.3 4.7 %collective-permute-start.8 = (bf16[368,512]{1,0:T(8,128)(2,1)S(1)}, bf16[368,512]{1,0:T(8,128)(2,1)S(1)}, u32[]{:S(2)}, u32[]{:S(2)}) collective-permute-start(bf16[368,512]{1,0:T(8,128)(2,1)S(1)} %hidden_units.3.refs_3_), channel_id=1, source_target_pairs={{0,1},{1,0},{2,3},{3,2},{4,5},{5,4},{6,7},{7,6},{8,9},{9,8},{10,11... | collective-permute-start | bytes 1130504 | tf_op jit(solution)/shard_map/ppermute | solution.py:472
  43.8 4.2 %copy-start.3 = (bf16[1,512,3584]{2,1,0:T(8,128)(2,1)S(1)}, bf16[1,512,3584]{2,1,0:T(8,128)(2,1)}, u32[]{:S(2)}) copy-start(bf16[1,512,3584]{2,1,0:T(8,128)(2,1)} %down_ref.1) | copy-start | bytes 11010052
  47.5 2.1 %collective-permute-start.13 = (bf16[72,1792]{1,0:T(8,128)(2,1)S(1)}, bf16[72,1792]{1,0:T(8,128)(2,1)S(1)}, u32[]{:S(2)}, u32[]{:S(2)}) collective-permute-start(bf16[72,1792]{1,0:T(8,128)(2,1)S(1)} %collective-permute-done.9.near_ref), channel_id=1, source_target_pairs={{0,1},{1,0},{2,3},{3,2},{4,5},{5,4},{6,7},{7,6},{8,9},{9,8},{10,11... | collective-permute-start | bytes 774152 | tf_op jit(solution)/shard_map/ppermute | solution.py:472
  47.5 3.6 %collective-permute-start.12 = (bf16[256,512]{1,0:T(8,128)(2,1)S(1)}, bf16[256,512]{1,0:T(8,128)(2,1)S(1)}, u32[]{:S(2)}, u32[]{:S(2)}) collective-permute-start(bf16[256,512]{1,0:T(8,128)(2,1)S(1)} %hidden_units.4.refs_1_), channel_id=1, source_target_pairs={{0,1},{1,0},{2,3},{3,2},{4,5},{5,4},{6,7},{7,6},{8,9},{9,8},{10,11... | collective-permute-start | bytes 786440 | tf_op jit(solution)/shard_map/ppermute | solution.py:472
  51.0 1.3 %collective-permute-start.16 = (bf16[72,512]{1,0:T(8,128)(2,1)S(1)}, bf16[72,512]{1,0:T(8,128)(2,1)S(1)}, u32[]{:S(2)}, u32[]{:S(2)}) collective-permute-start(bf16[72,512]{1,0:T(8,128)(2,1)S(1)} %hidden_units.5.own_ref), channel_id=1, source_target_pairs={{0,1},{1,0},{2,3},{3,2},{4,5},{5,4},{6,7},{7,6},{8,9},{9,8},{10,11... | collective-permute-start | bytes 221192 | tf_op jit(solution)/shard_map/ppermute | solution.py:472
  53.0 6.4 %collective-permute-start.18 = (bf16[72,896]{1,0:T(8,128)(2,1)S(1)}, bf16[72,896]{1,0:T(8,128)(2,1)S(1)}, u32[]{:S(2)}, u32[]{:S(2)}) collective-permute-start(bf16[72,896]{1,0:T(8,128)(2,1)S(1)} %get-tuple-element.68), channel_id=1, source_target_pairs={{0,2},{2,0},{4,6},{6,4},{8,10},{10,8},{12,14},{14,12},{1,3},{3,1},... | collective-permute-start | bytes 387080 | tf_op jit(solution)/shard_map/ppermute | solution.py:468
  54.6 7.5 %collective-permute-start.17 = (bf16[72,896]{1,0:T(8,128)(2,1)S(1)}, bf16[72,896]{1,0:T(8,128)(2,1)S(1)}, u32[]{:S(2)}, u32[]{:S(2)}) collective-permute-start(bf16[72,896]{1,0:T(8,128)(2,1)S(1)} %get-tuple-element.67), channel_id=1, source_target_pairs={{0,2},{2,0},{4,6},{6,4},{8,10},{10,8},{12,14},{14,12},{1,3},{3,1},... | collective-permute-start | bytes 387080 | tf_op jit(solution)/shard_map/ppermute | solution.py:468
  55.1 12.5 %collective-permute-start.15 = (bf16[72,1792]{1,0:T(8,128)(2,1)S(1)}, bf16[72,1792]{1,0:T(8,128)(2,1)S(1)}, u32[]{:S(2)}, u32[]{:S(2)}) collective-permute-start(bf16[72,1792]{1,0:T(8,128)(2,1)S(1)} %get-tuple-element.64), channel_id=1, source_target_pairs={{0,2},{2,0},{4,6},{6,4},{8,10},{10,8},{12,14},{14,12},{1,3},{3,1},... | collective-permute-start | bytes 774152 | tf_op jit(solution)/shard_map/ppermute | solution.py:468
  56.7 16.5 %collective-permute-start.14 = (bf16[72,1792]{1,0:T(8,128)(2,1)S(1)}, bf16[72,1792]{1,0:T(8,128)(2,1)S(1)}, u32[]{:S(2)}, u32[]{:S(2)}) collective-permute-start(bf16[72,1792]{1,0:T(8,128)(2,1)S(1)} %get-tuple-element.62), channel_id=1, source_target_pairs={{0,2},{2,0},{4,6},{6,4},{8,10},{10,8},{12,14},{14,12},{1,3},{3,1},... | collective-permute-start | bytes 774152 | tf_op jit(solution)/shard_map/ppermute | solution.py:468
  59.8 7.9 %collective-permute-start.20 = (bf16[96,896]{1,0:T(8,128)(2,1)S(1)}, bf16[96,896]{1,0:T(8,128)(2,1)S(1)}, u32[]{:S(2)}, u32[]{:S(2)}) collective-permute-start(bf16[96,896]{1,0:T(8,128)(2,1)S(1)} %combine.7), channel_id=1, source_target_pairs={{0,4},{2,6},{4,0},{6,2},{8,12},{10,14},{12,8},{14,10},{1,5},{3,7},... | collective-permute-start | bytes 516104 | tf_op jit(solution)/shard_map/ppermute | solution.py:468
  62.5 8.1 %collective-permute-start.19 = (bf16[96,896]{1,0:T(8,128)(2,1)S(1)}, bf16[96,896]{1,0:T(8,128)(2,1)S(1)}, u32[]{:S(2)}, u32[]{:S(2)}) collective-permute-start(bf16[96,896]{1,0:T(8,128)(2,1)S(1)} %combine.8), channel_id=1, source_target_pairs={{0,4},{2,6},{4,0},{6,2},{8,12},{10,14},{12,8},{14,10},{1,5},{3,7},... | collective-permute-start | bytes 516104 | tf_op jit(solution)/shard_map/ppermute | solution.py:468
  62.9 15.3 %collective-permute-start.11 = (bf16[72,1792]{1,0:T(8,128)(2,1)S(1)}, bf16[72,1792]{1,0:T(8,128)(2,1)S(1)}, u32[]{:S(2)}, u32[]{:S(2)}) collective-permute-start(bf16[72,1792]{1,0:T(8,128)(2,1)S(1)} %get-tuple-element.58), channel_id=1, source_target_pairs={{0,2},{2,0},{4,6},{6,4},{8,10},{10,8},{12,14},{14,12},{1,3},{3,1},... | collective-permute-start | bytes 774152 | tf_op jit(solution)/shard_map/ppermute | solution.py:468
  68.1 10.1 %collective-permute-start.21 = (bf16[96,896]{1,0:T(8,128)(2,1)S(1)}, bf16[96,896]{1,0:T(8,128)(2,1)S(1)}, u32[]{:S(2)}, u32[]{:S(2)}) collective-permute-start(bf16[96,896]{1,0:T(8,128)(2,1)S(1)} %combine.9), channel_id=1, source_target_pairs={{0,12},{2,14},{4,8},{6,10},{8,4},{10,6},{12,0},{14,2},{1,13},{3,15... | collective-permute-start | bytes 516104 | tf_op jit(solution)/shard_map/ppermute | solution.py:468
  71.0 9.2 %collective-permute-start.22 = (bf16[96,896]{1,0:T(8,128)(2,1)S(1)}, bf16[96,896]{1,0:T(8,128)(2,1)S(1)}, u32[]{:S(2)}, u32[]{:S(2)}) collective-permute-start(bf16[96,896]{1,0:T(8,128)(2,1)S(1)} %combine.10), channel_id=1, source_target_pairs={{0,12},{2,14},{4,8},{6,10},{8,4},{10,6},{12,0},{14,2},{1,13},{3,15... | collective-permute-start | bytes 516104 | tf_op jit(solution)/shard_map/ppermute | solution.py:468
  73.7 9.2 %collective-permute-start.23 = (bf16[96,896]{1,0:T(8,128)(2,1)S(1)}, bf16[96,896]{1,0:T(8,128)(2,1)S(1)}, u32[]{:S(2)}, u32[]{:S(2)}) collective-permute-start(bf16[96,896]{1,0:T(8,128)(2,1)S(1)} %get-tuple-element.74), channel_id=1, source_target_pairs={{0,4},{2,6},{4,0},{6,2},{8,12},{10,14},{12,8},{14,10},{1,5},{3,7},... | collective-permute-start | bytes 516104 | tf_op jit(solution)/shard_map/ppermute | solution.py:468
  74.0 12.5 %collective-permute-start.24 = (bf16[96,896]{1,0:T(8,128)(2,1)S(1)}, bf16[96,896]{1,0:T(8,128)(2,1)S(1)}, u32[]{:S(2)}, u32[]{:S(2)}) collective-permute-start(bf16[96,896]{1,0:T(8,128)(2,1)S(1)} %get-tuple-element.79), channel_id=1, source_target_pairs={{0,4},{2,6},{4,0},{6,2},{8,12},{10,14},{12,8},{14,10},{1,5},{3,7},... | collective-permute-start | bytes 516104 | tf_op jit(solution)/shard_map/ppermute | solution.py:468

commit v11 on v9

--- a/solution.py
+++ b/solution.py
@@ -488,10 +488,10 @@
     wide_pair = swap(wide, pair)
     cross_in = swap(cross, row)
     w_gate, w_up = w_gate[0], w_up[0]
-    down_other = swap_core(down_away)
     attended = attend(after(q_lat, wide), latent_cache, lengths, placement)
     cross_in = after(cross_in, attended)
-    wide_pair = after(wide_pair, cross_in, down_other)
+    down_other = swap_core(after(down_away, attended))
+    wide_pair = after(wide_pair, cross_in)
     cross_pair = cross_rows(wide_pair, role_count, capacity)
     cross_pair_in = swap(cross_pair, row)
     wide_mirror = after(wide_mirror, cross_pair)

time: 84.7 us -> 84.7 us (level)
  no operation moved by 1% of the time
where the time goes in v11:
time: 84.7 us; the launch traced here: 84.5 us
  waiting for transfers between devices  32.8 us (39%)
  starting transfers between devices  28.5 us (34%)
  Pallas kernels  19 us (22%)
  local copies, waits for them, and re-layouts  3.33 us (4%)
  between operations  0.89 us (1%)
    ppermute x18, waiting for transfers between devices, swap(): return lax.ppermute(array, 'role', pairs)  32.7 us
    ppermute x18, starting transfers between devices, swap(): return lax.ppermute(array, 'role', pairs)  27.3 us
    pallas_call x19, Pallas kernels, call(): pl.pallas_call(kernel, in_specs=[place] * len(operands), out_specs=[place...  15.1 us
    unnamed x16, local copies, waits for them, and re-layouts  3.33 us
    pallas_call x1, Pallas kernels, attend(): pl.pallas_call(attend_kernel, out_shape=jax.ShapeDtypeStruct((slot_count,...  2.05 us
    pallas_call x1, Pallas kernels, prepare(): pl.pallas_call(functools.partial(prepare_kernel, expert_count), in_specs=...  1.82 us
  transfers between devices with their start and end apart: 25, of which 13 were waited for; matrix products, arithmetic and copies ran while one was open for 0% of the time, Pallas kernels for 19%

profile of v11, /device:TPU:0, one launch (start us, length us, event | category | flops | bytes accessed | tf_op | source)
XLA Modules:
  0.0 84.5 jit_solution(5649751125738507158)
XLA Ops:
  0.7 1.8 %prepare.1 = (bf16[96,1920]{1,0:T(8,128)(2,1)S(1)}, bf16[72,1792]{1,0:T(8,128)(2,1)S(1)}, bf16[512,1792]{1,0:T(8,128)(2,1)S(1)}) custom-call(bf16[96,1792]{1,0:T(8,128)(2,1)} %tokens_hbm.1, bf16[1,512,3584]{2,1,0:T(8,128)(2,1)} %down_ref.1, s32[4,96]{1,0:T(4,128)} %bitcast.18, f32[4,96]{1,0:T(4,128)} %bitcast.19), custom_call_target="tpu_custom_call" | custom-call | tf_op jit(solution)/shard_map/prepare/pallas_call | solution.py:212
  2.5 3.1 %collective-permute-start = (bf16[96,1920]{1,0:T(8,128)(2,1)S(1)}, bf16[96,1920]{1,0:T(8,128)(2,1)S(1)}, u32[]{:S(2)}, u32[]{:S(2)}) collective-permute-start(bf16[96,1920]{1,0:T(8,128)(2,1)S(1)} %get-tuple-element.49.refs_0_.wide_ref), channel_id=1, source_target_pairs={{0,4},{2,6},{4,0},{6,2},{8,12},{10,14},{12,8},{14,10},{1,5},{3,7},... | collective-permute-start | bytes 1105928 | tf_op jit(solution)/shard_map/ppermute | solution.py:468
  5.6 1.5 %collective-permute-start.1 = (bf16[72,1792]{1,0:T(8,128)(2,1)S(1)}, bf16[72,1792]{1,0:T(8,128)(2,1)S(1)}, u32[]{:S(2)}, u32[]{:S(2)}) collective-permute-start(bf16[72,1792]{1,0:T(8,128)(2,1)S(1)} %get-tuple-element.44), channel_id=1, source_target_pairs={{0,2},{2,0},{4,6},{6,4},{8,10},{10,8},{12,14},{14,12},{1,3},{3,1},... | collective-permute-start | bytes 774152 | tf_op jit(solution)/shard_map/ppermute | solution.py:468
  7.1 2.5 %collective-permute-start.2 = (bf16[96,1920]{1,0:T(8,128)(2,1)S(1)}, bf16[96,1920]{1,0:T(8,128)(2,1)S(1)}, u32[]{:S(2)}, u32[]{:S(2)}) collective-permute-start(bf16[96,1920]{1,0:T(8,128)(2,1)S(1)} %get-tuple-element.49.refs_0_.wide_ref), channel_id=1, source_target_pairs={{0,12},{2,14},{4,8},{6,10},{8,4},{10,6},{12,0},{14,2},{1,13},{3,15... | collective-permute-start | bytes 1105928 | tf_op jit(solution)/shard_map/ppermute | solution.py:468
  9.6 1.3 %copy-done.4 = bf16[4,256,576]{1,2,0:T(8,128)(2,1)S(1)} copy-done((bf16[4,256,576]{1,2,0:T(8,128)(2,1)S(1)}, bf16[4,256,576]{1,2,0:T(8,128)(2,1)}, u32[]{:S(2)}) %copy-start.4) | copy-done | bytes 1179672
  10.9 2.0 %attend.1 = bf16[4,32,512]{2,1,0:T(8,128)(2,1)} custom-call(bf16[4,32,576]{2,1,0:T(8,128)(2,1)S(1)} %copy-done.5, bf16[4,576,256]{2,1,0:T(8,128)(2,1)S(1)} %bitcast.15, s32[1,32]{1,0:T(1,128)S(1)} %bitcast.16, s32[1,32]{1,0:T(1,128)S(1)} %bitcast.17), custom_call_target="tpu_custom_call" | custom-call | tf_op jit(solution)/shard_map/attend/pallas_call | solution.py:373
  12.9 0.4 collective-permute-done.1.refs_3_
  13.3 1.3 %collective-permute-done.wide_ref.refs_1_ = bf16[96,1920]{1,0:T(8,128)(2,1)S(1)} collective-permute-done((bf16[96,1920]{1,0:T(8,128)(2,1)S(1)}, bf16[96,1920]{1,0:T(8,128)(2,1)S(1)}, u32[]{:S(2)}, u32[]{:S(2)}) %collective-permute-start) | collective-permute-done | bytes 368672 | tf_op jit(solution)/shard_map/ppermute | solution.py:468
  14.6 0.5 cross_rows.3
  15.1 1.6 %collective-permute-start.3 = (bf16[72,1792]{1,0:T(8,128)(2,1)S(1)}, bf16[72,1792]{1,0:T(8,128)(2,1)S(1)}, u32[]{:S(2)}, u32[]{:S(2)}) collective-permute-start(bf16[72,1792]{1,0:T(8,128)(2,1)S(1)} %cross_rows.3), channel_id=1, source_target_pairs={{0,2},{2,0},{4,6},{6,4},{8,10},{10,8},{12,14},{14,12},{1,3},{3,1},... | collective-permute-start | bytes 774152 | tf_op jit(solution)/shard_map/ppermute | solution.py:468
  16.7 0.0 collective-permute-start.10
  16.7 7.7 %collective-permute-done.2.wide_ref.refs_2_ = bf16[96,1920]{1,0:T(8,128)(2,1)S(1)} collective-permute-done((bf16[96,1920]{1,0:T(8,128)(2,1)S(1)}, bf16[96,1920]{1,0:T(8,128)(2,1)S(1)}, u32[]{:S(2)}, u32[]{:S(2)}) %collective-permute-start.2) | collective-permute-done | bytes 368672 | tf_op jit(solution)/shard_map/ppermute | solution.py:468
  24.4 1.8 %collective-permute-start.5 = (bf16[96,1920]{1,0:T(8,128)(2,1)S(1)}, bf16[96,1920]{1,0:T(8,128)(2,1)S(1)}, u32[]{:S(2)}, u32[]{:S(2)}) collective-permute-start(bf16[96,1920]{1,0:T(8,128)(2,1)S(1)} %collective-permute-done.2.wide_ref.refs_2_), channel_id=1, source_target_pairs={{0,4},{2,6},{4,0},{6,2},{8,12},{10,14},{12,8},{14,10},{1,5},{3,7},... | collective-permute-start | bytes 1105928 | tf_op jit(solution)/shard_map/ppermute | solution.py:468
  26.2 0.5 cross_rows.4
  26.7 0.6 collective-permute-start.6
  27.3 0.0 collective-permute-done.3.refs_1_
  27.3 2.0 %copy-done.1 = bf16[1,3584,512]{2,1,0:T(8,128)(2,1)S(1)} copy-done((bf16[1,3584,512]{2,1,0:T(8,128)(2,1)S(1)}, bf16[1,3584,512]{2,1,0:T(8,128)(2,1)}, u32[]{:S(2)}) %copy-start.1) | copy-done | bytes 3670040
  29.3 0.1 pack_rows.2.near_ref
  29.4 0.1 collective-permute-start.4
  29.5 4.3 %collective-permute-done.5.refs_0_.wide_ref = bf16[96,1920]{1,0:T(8,128)(2,1)S(1)} collective-permute-done((bf16[96,1920]{1,0:T(8,128)(2,1)S(1)}, bf16[96,1920]{1,0:T(8,128)(2,1)S(1)}, u32[]{:S(2)}, u32[]{:S(2)}) %collective-permute-start.5) | collective-permute-done | bytes 368672 | tf_op jit(solution)/shard_map/ppermute | solution.py:468
  33.8 0.0 collective-permute-done.6.refs_2_
  33.8 0.1 pack_rows.3.near_ref
  33.8 0.1 collective-permute-start.9
  33.9 0.0 copy-start.2
  33.9 0.5 cross_rows.5
  34.5 1.6 %collective-permute-start.8 = (bf16[72,1792]{1,0:T(8,128)(2,1)S(1)}, bf16[72,1792]{1,0:T(8,128)(2,1)S(1)}, u32[]{:S(2)}, u32[]{:S(2)}) collective-permute-start(bf16[72,1792]{1,0:T(8,128)(2,1)S(1)} %cross_rows.5), channel_id=1, source_target_pairs={{0,2},{2,0},{4,6},{6,4},{8,10},{10,8},{12,14},{14,12},{1,3},{3,1},... | collective-permute-start | bytes 774152 | tf_op jit(solution)/shard_map/ppermute | solution.py:468
  36.1 2.9 %hidden_units.3.refs_3_ = bf16[368,512]{1,0:T(8,128)(2,1)S(1)} custom-call(bf16[368,1792]{1,0:T(8,128)(2,1)S(1)} %pack_rows.2.near_ref, bf16[368,1792]{1,0:T(8,128)(2,1)S(1)} %collective-permute-done.4.far_ref, bf16[3584,512]{1,0:T(8,128)(2,1)S(1)} %bitcast.8, bf16[3584,512]{1,0:T(8,128)(2,1)S(1)} %bitcast.12), custom_call_target="tpu_custom_call" | custom-call | tf_op jit(solution)/shard_map/hidden_units/pallas_call | solution.py:91
  39.0 0.5 collective-permute-start.7
  39.4 2.1 %hidden_units.4.refs_1_ = bf16[256,512]{1,0:T(8,128)(2,1)S(1)} custom-call(bf16[256,1792]{1,0:T(8,128)(2,1)S(1)} %pack_rows.3.near_ref, bf16[256,1792]{1,0:T(8,128)(2,1)S(1)} %collective-permute-done.9.far_ref, bf16[3584,512]{1,0:T(8,128)(2,1)S(1)} %bitcast.9, bf16[3584,512]{1,0:T(8,128)(2,1)S(1)} %bitcast.13), custom_call_target="tpu_custom_call" | custom-call | tf_op jit(solution)/shard_map/hidden_units/pallas_call | solution.py:91
  41.5 1.6 %collective-permute-done.8.near_ref = bf16[72,1792]{1,0:T(8,128)(2,1)S(1)} collective-permute-done((bf16[72,1792]{1,0:T(8,128)(2,1)S(1)}, bf16[72,1792]{1,0:T(8,128)(2,1)S(1)}, u32[]{:S(2)}, u32[]{:S(2)}) %collective-permute-start.8) | collective-permute-done | bytes 258080 | tf_op jit(solution)/shard_map/ppermute | solution.py:468
  43.1 0.0 collective-permute-start.13
  43.1 0.5 collective-permute-start.12
  43.6 1.5 %down.2 = (f32[96,1792]{1,0:T(8,128)S(1)}, f32[96,1792]{1,0:T(8,128)S(1)}, f32[96,1792]{1,0:T(8,128)S(1)}, bf16[72,1792]{1,0:T(8,128)(2,1)S(1)}) custom-call(bf16[96,1920]{1,0:T(8,128)(2,1)S(1)} %get-tuple-element.49.refs_0_.wide_ref, bf16[96,1920]{1,0:T(8,128)(2,1)S(1)} %collective-permute-done.wide_ref.refs_1_, ...), custom_call_target="tpu_custom_call" | custom-call | tf_op jit(solution)/shard_map/down/pallas_call | solution.py:91
  45.2 1.4 %hidden_units.5.own_ref = bf16[72,512]{1,0:T(8,128)(2,1)S(1)} custom-call(bf16[72,1792]{1,0:T(8,128)(2,1)S(1)} %collective-permute-done.8.near_ref, bf16[72,1792]{1,0:T(8,128)(2,1)S(1)} %collective-permute-done.13.far_ref, bf16[3584,512]{1,0:T(8,128)(2,1)S(1)} %bitcast.10, bf16[3584,512]{1,0:T(8,128)(2,1)S(1)} %bitcast.14), custom_call_target="tpu_custom_call" | custom-call | tf_op jit(solution)/shard_map/hidden_units/pallas_call | solution.py:91
  46.6 0.1 collective-permute-start.16
  46.7 1.1 %down.3 = (f32[96,1792]{1,0:T(8,128)S(1)}, bf16[72,1792]{1,0:T(8,128)(2,1)S(1)}, bf16[72,1792]{1,0:T(8,128)(2,1)S(1)}) custom-call(bf16[96,1920]{1,0:T(8,128)(2,1)S(1)} %collective-permute-done.5.refs_0_.wide_ref, bf16[256,512]{1,0:T(8,128)(2,1)S(1)} %hidden_units.4.refs_1_, bf16[256,512]{1,0:T(8,128)(2,1)S(1)} %collective-permute-done.12.refs_2_, ...), custom_call_target="tpu_custom_call" | custom-call | tf_op jit(solution)/shard_map/down/pallas_call | solution.py:91
  47.8 0.1 collective-permute-done.16.other_ref
  48.0 0.7 last_down.1
  48.7 1.6 %collective-permute-start.18 = (bf16[72,896]{1,0:T(8,128)(2,1)S(1)}, bf16[72,896]{1,0:T(8,128)(2,1)S(1)}, u32[]{:S(2)}, u32[]{:S(2)}) collective-permute-start(bf16[72,896]{1,0:T(8,128)(2,1)S(1)} %get-tuple-element.70), channel_id=1, source_target_pairs={{0,2},{2,0},{4,6},{6,4},{8,10},{10,8},{12,14},{14,12},{1,3},{3,1},... | collective-permute-start | bytes 387080 | tf_op jit(solution)/shard_map/ppermute | solution.py:468
  50.3 0.5 collective-permute-start.17
  50.8 1.5 %collective-permute-start.15 = (bf16[72,1792]{1,0:T(8,128)(2,1)S(1)}, bf16[72,1792]{1,0:T(8,128)(2,1)S(1)}, u32[]{:S(2)}, u32[]{:S(2)}) collective-permute-start(bf16[72,1792]{1,0:T(8,128)(2,1)S(1)} %get-tuple-element.66), channel_id=1, source_target_pairs={{0,2},{2,0},{4,6},{6,4},{8,10},{10,8},{12,14},{14,12},{1,3},{3,1},... | collective-permute-start | bytes 774152 | tf_op jit(solution)/shard_map/ppermute | solution.py:468
  52.3 0.5 collective-permute-start.14
  52.8 2.2 %collective-permute-done.18.back_ref = bf16[72,896]{1,0:T(8,128)(2,1)S(1)} collective-permute-done((bf16[72,896]{1,0:T(8,128)(2,1)S(1)}, bf16[72,896]{1,0:T(8,128)(2,1)S(1)}, u32[]{:S(2)}, u32[]{:S(2)}) %collective-permute-start.18) | collective-permute-done | bytes 129056 | tf_op jit(solution)/shard_map/ppermute | solution.py:468
  55.0 0.4 combine.7
  55.4 0.4 collective-permute-start.20
  55.9 1.9 %collective-permute-done.17.back_ref = bf16[72,896]{1,0:T(8,128)(2,1)S(1)} collective-permute-done((bf16[72,896]{1,0:T(8,128)(2,1)S(1)}, bf16[72,896]{1,0:T(8,128)(2,1)S(1)}, u32[]{:S(2)}, u32[]{:S(2)}) %collective-permute-start.17) | collective-permute-done | bytes 129056 | tf_op jit(solution)/shard_map/ppermute | solution.py:468
  57.8 0.4 combine.8
  58.2 0.4 collective-permute-start.19
  58.6 1.4 %collective-permute-start.11 = (bf16[72,1792]{1,0:T(8,128)(2,1)S(1)}, bf16[72,1792]{1,0:T(8,128)(2,1)S(1)}, u32[]{:S(2)}, u32[]{:S(2)}) collective-permute-start(bf16[72,1792]{1,0:T(8,128)(2,1)S(1)} %get-tuple-element.60), channel_id=1, source_target_pairs={{0,2},{2,0},{4,6},{6,4},{8,10},{10,8},{12,14},{14,12},{1,3},{3,1},... | collective-permute-start | bytes 774152 | tf_op jit(solution)/shard_map/ppermute | solution.py:468
  60.1 3.2 %collective-permute-done.15.back_ref = bf16[72,1792]{1,0:T(8,128)(2,1)S(1)} collective-permute-done((bf16[72,1792]{1,0:T(8,128)(2,1)S(1)}, bf16[72,1792]{1,0:T(8,128)(2,1)S(1)}, u32[]{:S(2)}, u32[]{:S(2)}) %collective-permute-start.15) | collective-permute-done | bytes 258080 | tf_op jit(solution)/shard_map/ppermute | solution.py:468
  63.3 0.4 combine.9
  63.7 5.3 %collective-permute-start.21 = (bf16[96,896]{1,0:T(8,128)(2,1)S(1)}, bf16[96,896]{1,0:T(8,128)(2,1)S(1)}, u32[]{:S(2)}, u32[]{:S(2)}) collective-permute-start(bf16[96,896]{1,0:T(8,128)(2,1)S(1)} %combine.9), channel_id=1, source_target_pairs={{0,12},{2,14},{4,8},{6,10},{8,4},{10,6},{12,0},{14,2},{1,13},{3,15... | collective-permute-start | bytes 516104 | tf_op jit(solution)/shard_map/ppermute | solution.py:468
  69.0 0.4 combine.10
  69.4 0.9 %collective-permute-start.22 = (bf16[96,896]{1,0:T(8,128)(2,1)S(1)}, bf16[96,896]{1,0:T(8,128)(2,1)S(1)}, u32[]{:S(2)}, u32[]{:S(2)}) collective-permute-start(bf16[96,896]{1,0:T(8,128)(2,1)S(1)} %combine.10), channel_id=1, source_target_pairs={{0,12},{2,14},{4,8},{6,10},{8,4},{10,6},{12,0},{14,2},{1,13},{3,15... | collective-permute-start | bytes 516104 | tf_op jit(solution)/shard_map/ppermute | solution.py:468
  70.3 0.5 combine.11
  70.7 0.1 collective-permute-start.23
  70.8 2.0 %collective-permute-start.24 = (bf16[96,896]{1,0:T(8,128)(2,1)S(1)}, bf16[96,896]{1,0:T(8,128)(2,1)S(1)}, u32[]{:S(2)}, u32[]{:S(2)}) collective-permute-start(bf16[96,896]{1,0:T(8,128)(2,1)S(1)} %get-tuple-element.81), channel_id=1, source_target_pairs={{0,4},{2,6},{4,0},{6,2},{8,12},{10,14},{12,8},{14,10},{1,5},{3,7},... | collective-permute-start | bytes 516104 | tf_op jit(solution)/shard_map/ppermute | solution.py:468
  72.8 1.0 %collective-permute-done.11.back_ref = bf16[72,1792]{1,0:T(8,128)(2,1)S(1)} collective-permute-done((bf16[72,1792]{1,0:T(8,128)(2,1)S(1)}, bf16[72,1792]{1,0:T(8,128)(2,1)S(1)}, u32[]{:S(2)}, u32[]{:S(2)}) %collective-permute-start.11) | collective-permute-done | bytes 258080 | tf_op jit(solution)/shard_map/ppermute | solution.py:468
  73.8 0.4 combine.12.refs_0_
  74.2 4.2 %collective-permute-done.22.refs_0_ = bf16[96,896]{1,0:T(8,128)(2,1)S(1)} collective-permute-done((bf16[96,896]{1,0:T(8,128)(2,1)S(1)}, bf16[96,896]{1,0:T(8,128)(2,1)S(1)}, u32[]{:S(2)}, u32[]{:S(2)}) %collective-permute-start.22) | collective-permute-done | bytes 172064 | tf_op jit(solution)/shard_map/ppermute | solution.py:468
  78.4 0.4 combine.13.refs_1_
  78.8 2.2 %collective-permute-done.23.refs_2_ = bf16[96,896]{1,0:T(8,128)(2,1)S(1)} collective-permute-done((bf16[96,896]{1,0:T(8,128)(2,1)S(1)}, bf16[96,896]{1,0:T(8,128)(2,1)S(1)}, u32[]{:S(2)}, u32[]{:S(2)}) %collective-permute-start.23) | collective-permute-done | bytes 172064 | tf_op jit(solution)/shard_map/ppermute | solution.py:468
  81.1 2.6 %collective-permute-done.24.refs_3_ = bf16[96,896]{1,0:T(8,128)(2,1)S(1)} collective-permute-done((bf16[96,896]{1,0:T(8,128)(2,1)S(1)}, bf16[96,896]{1,0:T(8,128)(2,1)S(1)}, u32[]{:S(2)}, u32[]{:S(2)}) %collective-permute-start.24) | collective-permute-done | bytes 172064 | tf_op jit(solution)/shard_map/ppermute | solution.py:468
  83.7 0.8 add_last.1
  (23 shorter events, 0.1 us)
Async XLA Ops:
  0.6 9.0 %copy-start.5 = (bf16[4,32,576]{2,1,0:T(8,128)(2,1)S(1)}, bf16[4,32,576]{2,1,0:T(8,128)(2,1)}, u32[]{:S(2)}) copy-start(bf16[4,32,576]{2,1,0:T(8,128)(2,1)} %query_ref) | copy-start | bytes 442372
  0.6 8.9 %copy-start.6 = (s32[32]{0:T(128)S(1)}, s32[32]{0:T(128)}, u32[]{:S(2)}) copy-start(s32[32]{0:T(128)} %param.12) | copy-start | bytes 388
  0.7 8.9 %copy-start.7 = (s32[32]{0:T(128)S(1)}, s32[32]{0:T(128)}, u32[]{:S(2)}) copy-start(s32[32]{0:T(128)} %param.13) | copy-start | bytes 388
  0.7 26.6 %copy-start = (bf16[1,3584,512]{2,1,0:T(8,128)(2,1)S(1)}, bf16[1,3584,512]{2,1,0:T(8,128)(2,1)}, u32[]{:S(2)}) copy-start(bf16[1,3584,512]{2,1,0:T(8,128)(2,1)} %param.17) | copy-start | bytes 11010052
  2.5 12.1 %collective-permute-start = (bf16[96,1920]{1,0:T(8,128)(2,1)S(1)}, bf16[96,1920]{1,0:T(8,128)(2,1)S(1)}, u32[]{:S(2)}, u32[]{:S(2)}) collective-permute-start(bf16[96,1920]{1,0:T(8,128)(2,1)S(1)} %get-tuple-element.49.refs_0_.wide_ref), channel_id=1, source_target_pairs={{0,4},{2,6},{4,0},{6,2},{8,12},{10,14},{12,8},{14,10},{1,5},{3,7},... | collective-permute-start | bytes 1105928 | tf_op jit(solution)/shard_map/ppermute | solution.py:468
  5.6 7.7 %collective-permute-start.1 = (bf16[72,1792]{1,0:T(8,128)(2,1)S(1)}, bf16[72,1792]{1,0:T(8,128)(2,1)S(1)}, u32[]{:S(2)}, u32[]{:S(2)}) collective-permute-start(bf16[72,1792]{1,0:T(8,128)(2,1)S(1)} %get-tuple-element.44), channel_id=1, source_target_pairs={{0,2},{2,0},{4,6},{6,4},{8,10},{10,8},{12,14},{14,12},{1,3},{3,1},... | collective-permute-start | bytes 774152 | tf_op jit(solution)/shard_map/ppermute | solution.py:468
  7.1 17.3 %collective-permute-start.2 = (bf16[96,1920]{1,0:T(8,128)(2,1)S(1)}, bf16[96,1920]{1,0:T(8,128)(2,1)S(1)}, u32[]{:S(2)}, u32[]{:S(2)}) collective-permute-start(bf16[96,1920]{1,0:T(8,128)(2,1)S(1)} %get-tuple-element.49.refs_0_.wide_ref), channel_id=1, source_target_pairs={{0,12},{2,14},{4,8},{6,10},{8,4},{10,6},{12,0},{14,2},{1,13},{3,15... | collective-permute-start | bytes 1105928 | tf_op jit(solution)/shard_map/ppermute | solution.py:468
  9.6 1.3 %copy-start.4 = (bf16[4,256,576]{1,2,0:T(8,128)(2,1)S(1)}, bf16[4,256,576]{1,2,0:T(8,128)(2,1)}, u32[]{:S(2)}) copy-start(bf16[4,256,576]{1,2,0:T(8,128)(2,1)} %param.11) | copy-start | bytes 3538948
  15.1 12.2 %collective-permute-start.3 = (bf16[72,1792]{1,0:T(8,128)(2,1)S(1)}, bf16[72,1792]{1,0:T(8,128)(2,1)S(1)}, u32[]{:S(2)}, u32[]{:S(2)}) collective-permute-start(bf16[72,1792]{1,0:T(8,128)(2,1)S(1)} %cross_rows.3), channel_id=1, source_target_pairs={{0,2},{2,0},{4,6},{6,4},{8,10},{10,8},{12,14},{14,12},{1,3},{3,1},... | collective-permute-start | bytes 774152 | tf_op jit(solution)/shard_map/ppermute | solution.py:468
  16.7 26.9 %collective-permute-start.10 = (bf16[512,1792]{1,0:T(8,128)(2,1)S(1)}, bf16[512,1792]{1,0:T(8,128)(2,1)S(1)}, u32[]{:S(2)}, u32[]{:S(2)}) collective-permute-start(bf16[512,1792]{1,0:T(8,128)(2,1)S(1)} %get-tuple-element.58), channel_id=1, source_target_pairs={{0,1},{1,0},{2,3},{3,2},{4,5},{5,4},{6,7},{7,6},{8,9},{9,8},{10,11... | collective-permute-start | bytes 5505032 | tf_op jit(solution)/shard_map/ppermute | solution.py:472
  24.4 9.4 %collective-permute-start.5 = (bf16[96,1920]{1,0:T(8,128)(2,1)S(1)}, bf16[96,1920]{1,0:T(8,128)(2,1)S(1)}, u32[]{:S(2)}, u32[]{:S(2)}) collective-permute-start(bf16[96,1920]{1,0:T(8,128)(2,1)S(1)} %collective-permute-done.2.wide_ref.refs_2_), channel_id=1, source_target_pairs={{0,4},{2,6},{4,0},{6,2},{8,12},{10,14},{12,8},{14,10},{1,5},{3,7},... | collective-permute-start | bytes 1105928 | tf_op jit(solution)/shard_map/ppermute | solution.py:468
  26.7 7.1 %collective-permute-start.6 = (bf16[72,1792]{1,0:T(8,128)(2,1)S(1)}, bf16[72,1792]{1,0:T(8,128)(2,1)S(1)}, u32[]{:S(2)}, u32[]{:S(2)}) collective-permute-start(bf16[72,1792]{1,0:T(8,128)(2,1)S(1)} %cross_rows.4), channel_id=1, source_target_pairs={{0,2},{2,0},{4,6},{6,4},{8,10},{10,8},{12,14},{14,12},{1,3},{3,1},... | collective-permute-start | bytes 774152 | tf_op jit(solution)/shard_map/ppermute | solution.py:468
  27.3 2.0 %copy-start.1 = (bf16[1,3584,512]{2,1,0:T(8,128)(2,1)S(1)}, bf16[1,3584,512]{2,1,0:T(8,128)(2,1)}, u32[]{:S(2)}) copy-start(bf16[1,3584,512]{2,1,0:T(8,128)(2,1)} %param.18) | copy-start | bytes 11010052
  29.4 6.6 %collective-permute-start.4 = (bf16[368,1792]{1,0:T(8,128)(2,1)S(1)}, bf16[368,1792]{1,0:T(8,128)(2,1)S(1)}, u32[]{:S(2)}, u32[]{:S(2)}) collective-permute-start(bf16[368,1792]{1,0:T(8,128)(2,1)S(1)} %pack_rows.2.near_ref), channel_id=1, source_target_pairs={{0,1},{1,0},{2,3},{3,2},{4,5},{5,4},{6,7},{7,6},{8,9},{9,8},{10,11... | collective-permute-start | bytes 3956744 | tf_op jit(solution)/shard_map/ppermute | solution.py:472
  33.8 5.6 %collective-permute-start.9 = (bf16[256,1792]{1,0:T(8,128)(2,1)S(1)}, bf16[256,1792]{1,0:T(8,128)(2,1)S(1)}, u32[]{:S(2)}, u32[]{:S(2)}) collective-permute-start(bf16[256,1792]{1,0:T(8,128)(2,1)S(1)} %pack_rows.3.near_ref), channel_id=1, source_target_pairs={{0,1},{1,0},{2,3},{3,2},{4,5},{5,4},{6,7},{7,6},{8,9},{9,8},{10,11... | collective-permute-start | bytes 2752520 | tf_op jit(solution)/shard_map/ppermute | solution.py:472
  33.9 2.1 %copy-start.2 = (bf16[1,3584,512]{2,1,0:T(8,128)(2,1)S(1)}, bf16[1,3584,512]{2,1,0:T(8,128)(2,1)}, u32[]{:S(2)}) copy-start(bf16[1,3584,512]{2,1,0:T(8,128)(2,1)} %param.18) | copy-start | bytes 11010052
  34.5 8.7 %collective-permute-start.8 = (bf16[72,1792]{1,0:T(8,128)(2,1)S(1)}, bf16[72,1792]{1,0:T(8,128)(2,1)S(1)}, u32[]{:S(2)}, u32[]{:S(2)}) collective-permute-start(bf16[72,1792]{1,0:T(8,128)(2,1)S(1)} %cross_rows.5), channel_id=1, source_target_pairs={{0,2},{2,0},{4,6},{6,4},{8,10},{10,8},{12,14},{14,12},{1,3},{3,1},... | collective-permute-start | bytes 774152 | tf_op jit(solution)/shard_map/ppermute | solution.py:468
  39.0 4.7 %collective-permute-start.7 = (bf16[368,512]{1,0:T(8,128)(2,1)S(1)}, bf16[368,512]{1,0:T(8,128)(2,1)S(1)}, u32[]{:S(2)}, u32[]{:S(2)}) collective-permute-start(bf16[368,512]{1,0:T(8,128)(2,1)S(1)} %hidden_units.3.refs_3_), channel_id=1, source_target_pairs={{0,1},{1,0},{2,3},{3,2},{4,5},{5,4},{6,7},{7,6},{8,9},{9,8},{10,11... | collective-permute-start | bytes 1130504 | tf_op jit(solution)/shard_map/ppermute | solution.py:472
  39.4 4.2 %copy-start.3 = (bf16[1,512,3584]{2,1,0:T(8,128)(2,1)S(1)}, bf16[1,512,3584]{2,1,0:T(8,128)(2,1)}, u32[]{:S(2)}) copy-start(bf16[1,512,3584]{2,1,0:T(8,128)(2,1)} %down_ref.1) | copy-start | bytes 11010052
  43.1 2.1 %collective-permute-start.13 = (bf16[72,1792]{1,0:T(8,128)(2,1)S(1)}, bf16[72,1792]{1,0:T(8,128)(2,1)S(1)}, u32[]{:S(2)}, u32[]{:S(2)}) collective-permute-start(bf16[72,1792]{1,0:T(8,128)(2,1)S(1)} %collective-permute-done.8.near_ref), channel_id=1, source_target_pairs={{0,1},{1,0},{2,3},{3,2},{4,5},{5,4},{6,7},{7,6},{8,9},{9,8},{10,11... | collective-permute-start | bytes 774152 | tf_op jit(solution)/shard_map/ppermute | solution.py:472
  43.1 3.6 %collective-permute-start.12 = (bf16[256,512]{1,0:T(8,128)(2,1)S(1)}, bf16[256,512]{1,0:T(8,128)(2,1)S(1)}, u32[]{:S(2)}, u32[]{:S(2)}) collective-permute-start(bf16[256,512]{1,0:T(8,128)(2,1)S(1)} %hidden_units.4.refs_1_), channel_id=1, source_target_pairs={{0,1},{1,0},{2,3},{3,2},{4,5},{5,4},{6,7},{7,6},{8,9},{9,8},{10,11... | collective-permute-start | bytes 786440 | tf_op jit(solution)/shard_map/ppermute | solution.py:472
  46.6 1.3 %collective-permute-start.16 = (bf16[72,512]{1,0:T(8,128)(2,1)S(1)}, bf16[72,512]{1,0:T(8,128)(2,1)S(1)}, u32[]{:S(2)}, u32[]{:S(2)}) collective-permute-start(bf16[72,512]{1,0:T(8,128)(2,1)S(1)} %hidden_units.5.own_ref), channel_id=1, source_target_pairs={{0,1},{1,0},{2,3},{3,2},{4,5},{5,4},{6,7},{7,6},{8,9},{9,8},{10,11... | collective-permute-start | bytes 221192 | tf_op jit(solution)/shard_map/ppermute | solution.py:472
  48.7 6.4 %collective-permute-start.18 = (bf16[72,896]{1,0:T(8,128)(2,1)S(1)}, bf16[72,896]{1,0:T(8,128)(2,1)S(1)}, u32[]{:S(2)}, u32[]{:S(2)}) collective-permute-start(bf16[72,896]{1,0:T(8,128)(2,1)S(1)} %get-tuple-element.70), channel_id=1, source_target_pairs={{0,2},{2,0},{4,6},{6,4},{8,10},{10,8},{12,14},{14,12},{1,3},{3,1},... | collective-permute-start | bytes 387080 | tf_op jit(solution)/shard_map/ppermute | solution.py:468
  50.3 7.5 %collective-permute-start.17 = (bf16[72,896]{1,0:T(8,128)(2,1)S(1)}, bf16[72,896]{1,0:T(8,128)(2,1)S(1)}, u32[]{:S(2)}, u32[]{:S(2)}) collective-permute-start(bf16[72,896]{1,0:T(8,128)(2,1)S(1)} %get-tuple-element.69), channel_id=1, source_target_pairs={{0,2},{2,0},{4,6},{6,4},{8,10},{10,8},{12,14},{14,12},{1,3},{3,1},... | collective-permute-start | bytes 387080 | tf_op jit(solution)/shard_map/ppermute | solution.py:468
  50.8 12.5 %collective-permute-start.15 = (bf16[72,1792]{1,0:T(8,128)(2,1)S(1)}, bf16[72,1792]{1,0:T(8,128)(2,1)S(1)}, u32[]{:S(2)}, u32[]{:S(2)}) collective-permute-start(bf16[72,1792]{1,0:T(8,128)(2,1)S(1)} %get-tuple-element.66), channel_id=1, source_target_pairs={{0,2},{2,0},{4,6},{6,4},{8,10},{10,8},{12,14},{14,12},{1,3},{3,1},... | collective-permute-start | bytes 774152 | tf_op jit(solution)/shard_map/ppermute | solution.py:468
  52.3 18.0 %collective-permute-start.14 = (bf16[72,1792]{1,0:T(8,128)(2,1)S(1)}, bf16[72,1792]{1,0:T(8,128)(2,1)S(1)}, u32[]{:S(2)}, u32[]{:S(2)}) collective-permute-start(bf16[72,1792]{1,0:T(8,128)(2,1)S(1)} %get-tuple-element.64), channel_id=1, source_target_pairs={{0,2},{2,0},{4,6},{6,4},{8,10},{10,8},{12,14},{14,12},{1,3},{3,1},... | collective-permute-start | bytes 774152 | tf_op jit(solution)/shard_map/ppermute | solution.py:468
  55.4 7.9 %collective-permute-start.20 = (bf16[96,896]{1,0:T(8,128)(2,1)S(1)}, bf16[96,896]{1,0:T(8,128)(2,1)S(1)}, u32[]{:S(2)}, u32[]{:S(2)}) collective-permute-start(bf16[96,896]{1,0:T(8,128)(2,1)S(1)} %combine.7), channel_id=1, source_target_pairs={{0,4},{2,6},{4,0},{6,2},{8,12},{10,14},{12,8},{14,10},{1,5},{3,7},... | collective-permute-start | bytes 516104 | tf_op jit(solution)/shard_map/ppermute | solution.py:468
  58.2 10.8 %collective-permute-start.19 = (bf16[96,896]{1,0:T(8,128)(2,1)S(1)}, bf16[96,896]{1,0:T(8,128)(2,1)S(1)}, u32[]{:S(2)}, u32[]{:S(2)}) collective-permute-start(bf16[96,896]{1,0:T(8,128)(2,1)S(1)} %combine.8), channel_id=1, source_target_pairs={{0,4},{2,6},{4,0},{6,2},{8,12},{10,14},{12,8},{14,10},{1,5},{3,7},... | collective-permute-start | bytes 516104 | tf_op jit(solution)/shard_map/ppermute | solution.py:468
  58.6 15.2 %collective-permute-start.11 = (bf16[72,1792]{1,0:T(8,128)(2,1)S(1)}, bf16[72,1792]{1,0:T(8,128)(2,1)S(1)}, u32[]{:S(2)}, u32[]{:S(2)}) collective-permute-start(bf16[72,1792]{1,0:T(8,128)(2,1)S(1)} %get-tuple-element.60), channel_id=1, source_target_pairs={{0,2},{2,0},{4,6},{6,4},{8,10},{10,8},{12,14},{14,12},{1,3},{3,1},... | collective-permute-start | bytes 774152 | tf_op jit(solution)/shard_map/ppermute | solution.py:468
  63.7 10.1 %collective-permute-start.21 = (bf16[96,896]{1,0:T(8,128)(2,1)S(1)}, bf16[96,896]{1,0:T(8,128)(2,1)S(1)}, u32[]{:S(2)}, u32[]{:S(2)}) collective-permute-start(bf16[96,896]{1,0:T(8,128)(2,1)S(1)} %combine.9), channel_id=1, source_target_pairs={{0,12},{2,14},{4,8},{6,10},{8,4},{10,6},{12,0},{14,2},{1,13},{3,15... | collective-permute-start | bytes 516104 | tf_op jit(solution)/shard_map/ppermute | solution.py:468
  69.4 9.0 %collective-permute-start.22 = (bf16[96,896]{1,0:T(8,128)(2,1)S(1)}, bf16[96,896]{1,0:T(8,128)(2,1)S(1)}, u32[]{:S(2)}, u32[]{:S(2)}) collective-permute-start(bf16[96,896]{1,0:T(8,128)(2,1)S(1)} %combine.10), channel_id=1, source_target_pairs={{0,12},{2,14},{4,8},{6,10},{8,4},{10,6},{12,0},{14,2},{1,13},{3,15... | collective-permute-start | bytes 516104 | tf_op jit(solution)/shard_map/ppermute | solution.py:468
  70.7 10.3 %collective-permute-start.23 = (bf16[96,896]{1,0:T(8,128)(2,1)S(1)}, bf16[96,896]{1,0:T(8,128)(2,1)S(1)}, u32[]{:S(2)}, u32[]{:S(2)}) collective-permute-start(bf16[96,896]{1,0:T(8,128)(2,1)S(1)} %get-tuple-element.76), channel_id=1, source_target_pairs={{0,4},{2,6},{4,0},{6,2},{8,12},{10,14},{12,8},{14,10},{1,5},{3,7},... | collective-permute-start | bytes 516104 | tf_op jit(solution)/shard_map/ppermute | solution.py:468
  70.8 12.9 %collective-permute-start.24 = (bf16[96,896]{1,0:T(8,128)(2,1)S(1)}, bf16[96,896]{1,0:T(8,128)(2,1)S(1)}, u32[]{:S(2)}, u32[]{:S(2)}) collective-permute-start(bf16[96,896]{1,0:T(8,128)(2,1)S(1)} %get-tuple-element.81), channel_id=1, source_target_pairs={{0,4},{2,6},{4,0},{6,2},{8,12},{10,14},{12,8},{14,10},{1,5},{3,7},... | collective-permute-start | bytes 516104 | tf_op jit(solution)/shard_map/ppermute | solution.py:468

commit v12 on v11

--- a/solution.py
+++ b/solution.py
@@ -147,12 +147,10 @@
 def prepare_kernel(
     expert_count,
     tokens_hbm,
-    down_hbm,
     ids_hbm,
     gates_hbm,
     wide_ref,
     cross_ref,
-    away_ref,
     ids_ref,
     gates_ref,
     sems,
@@ -166,9 +164,6 @@
     for part in first:
         part.start()
     copy.start()
-    sibling = pl.multiple_of((1 - lax.axis_index("tp")) * half, LANES)
-    away = pltpu.make_async_copy(down_hbm.at[0, :, pl.ds(sibling, half)], away_ref, sems.at[1])
-    away.start()
     for part in first:
         part.wait()
     piece_rows = round_up(3 * expert_count, 16)
@@ -198,20 +193,18 @@
     copy.wait()
     gate = decode_gate(turned, lax.axis_index("role") ^ 1, expert_count)
     cross_ref[...] = compact(gate, wide_ref[:, :half], cross_ref.shape[0])
-    away.wait()
-
-
-def prepare(tokens, w_down, expert_ids, gate_weights, expert_count, capacity):
+
+
+def prepare(tokens, expert_ids, gate_weights, expert_count, capacity):
     rows, half = tokens.shape
     shapes = [
         (rows, half + LANES),
         (capacity, half),
-        (w_down.shape[1], half),
     ]
     whole = pl.BlockSpec(memory_space=pltpu.VMEM)
     return pl.pallas_call(
         functools.partial(prepare_kernel, expert_count),
-        in_specs=[pl.BlockSpec(memory_space=pltpu.HBM)] * 4,
+        in_specs=[pl.BlockSpec(memory_space=pltpu.HBM)] * 3,
         out_specs=[whole] * len(shapes),
         out_shape=[pltpu.VMEM(shape, jnp.bfloat16) for shape in shapes],
         scratch_shapes=[
@@ -224,7 +217,6 @@
         cost_estimate=pl.CostEstimate(flops=0, bytes_accessed=0, transcendentals=0),
     )(
         pltpu.with_memory_space_constraint(tokens, pltpu.HBM),
-        pltpu.with_memory_space_constraint(w_down, pltpu.HBM),
         pltpu.with_memory_space_constraint(expert_ids.T, pltpu.HBM),
         pltpu.with_memory_space_constraint(gate_weights.T, pltpu.HBM),
     )
@@ -345,7 +337,13 @@
     )
 
 
-def attend_kernel(query_ref, latent_ref, lengths_ref, placement_ref, out_ref):
+def attend_kernel(
+    query_ref, latent_ref, lengths_ref, placement_ref, down_hbm, out_ref, away_ref, sem
+):
+    half = away_ref.shape[1]
+    sibling = pl.multiple_of((1 - lax.axis_index("tp")) * half, LANES)
+    away = pltpu.make_async_copy(down_hbm.at[0, :, pl.ds(sibling, half)], away_ref, sem)
+    away.start()
     slot_count, head_count, _ = query_ref.shape
     rank, context = out_ref.shape[2], latent_ref.shape[2]
     first = lax.axis_index("role") * slot_count
@@ -366,17 +364,31 @@
             (((1,), (1,)), ((), ())),
             preferred_element_type=jnp.float32,
         ).astype(jnp.bfloat16)
-
-
-def attend(q_lat, latent_cache, lengths, placement):
+    away.wait()
+
+
+def attend(q_lat, latent_cache, lengths, placement, w_down):
     slot_count, head_count, _ = q_lat.shape
+    place = pl.BlockSpec(memory_space=pltpu.VMEM)
     return pl.pallas_call(
         attend_kernel,
-        out_shape=jax.ShapeDtypeStruct((slot_count, head_count, KV_RANK), jnp.bfloat16),
+        in_specs=[place] * 4 + [pl.BlockSpec(memory_space=pltpu.HBM)],
+        out_specs=[place] * 2,
+        out_shape=[
+            jax.ShapeDtypeStruct((slot_count, head_count, KV_RANK), jnp.bfloat16),
+            pltpu.VMEM((w_down.shape[1], w_down.shape[2] // 2), jnp.bfloat16),
+        ],
+        scratch_shapes=[pltpu.SemaphoreType.DMA],
         name="attend",
         compiler_params=pltpu.CompilerParams(vmem_limit_bytes=VMEM_LIMIT),
         cost_estimate=pl.CostEstimate(flops=0, bytes_accessed=0, transcendentals=0),
-    )(q_lat, latent_cache.transpose(0, 2, 1), lengths[None, :], placement[None, :])
+    )(
+        q_lat,
+        latent_cache.transpose(0, 2, 1),
+        lengths[None, :],
+        placement[None, :],
+        pltpu.with_memory_space_constraint(w_down, pltpu.HBM),
+    )
 
 
 def last_down_kernel(own_ref, other_ref, down_ref, down_other_ref, *outs):
@@ -481,14 +493,16 @@
     capacity = 3 * token_count * route_count // (2 * role_count)
     pair, mirror, row = 2, 6, 1
 
-    wide, cross, down_away = prepare(
-        tokens, w_down, expert_ids, gate_weights, role_count, capacity
+    wide, cross = prepare(
+        tokens, expert_ids, gate_weights, role_count, capacity
     )
     wide_mirror = swap(wide, mirror)
     wide_pair = swap(wide, pair)
     cross_in = swap(cross, row)
     w_gate, w_up = w_gate[0], w_up[0]
-    attended = attend(after(q_lat, wide), latent_cache, lengths, placement)
+    attended, down_away = attend(
+        after(q_lat, wide), latent_cache, lengths, placement, w_down
+    )
     cross_in = after(cross_in, attended)
     down_other = swap_core(after(down_away, attended))
     wide_pair = after(wide_pair, cross_in)

time: 84.7 us -> 84.5 us (level)
  waiting for transfers between devices: 32.8 us -> 30.4 us
  local copies, waits for them, and re-layouts: 3.33 us -> 5.55 us
  starting transfers between devices: 28.5 us -> 27.5 us
  Pallas kernels: 19 us -> 19.9 us
    ppermute x18, waiting for transfers between devices: 32.7 us -> 30.2 us  [swap(): return lax.ppermute(array, 'role', pairs)]
    unnamed x16, local copies, waits for them, and re-layouts: 3.33 us -> 5.55 us
    pallas_call x1, Pallas kernels: 2.05 us -> 3.26 us  [attend(): pl.pallas_call(attend_kernel, in_specs=[place] * 4 + [pl.BlockSpec(memory...]
    ppermute x18, starting transfers between devices: 27.3 us -> 26.3 us  [swap(): return lax.ppermute(array, 'role', pairs)]
  transfers between devices with their start and end apart: 25 -> 25, of which waited for: 13 -> 11; matrix products, arithmetic and copies ran while one was open for 0% -> 0% of each run, Pallas kernels for 19% -> 20%
where the time goes in v12:
time: 84.5 us; the launch traced here: 84.2 us
  waiting for transfers between devices  30.4 us (36%)
  starting transfers between devices  27.5 us (33%)
  Pallas kernels  19.9 us (24%)
  local copies, waits for them, and re-layouts  5.55 us (7%)
  between operations  0.87 us (1%)
    ppermute x18, waiting for transfers between devices, swap(): return lax.ppermute(array, 'role', pairs)  30.2 us
    ppermute x18, starting transfers between devices, swap(): return lax.ppermute(array, 'role', pairs)  26.3 us
    pallas_call x19, Pallas kernels, call(): pl.pallas_call(kernel, in_specs=[place] * len(operands), out_specs=[place...  15.1 us
    unnamed x16, local copies, waits for them, and re-layouts  5.55 us
    pallas_call x1, Pallas kernels, attend(): pl.pallas_call(attend_kernel, in_specs=[place] * 4 + [pl.BlockSpec(memory...  3.26 us
  transfers between devices with their start and end apart: 25, of which 11 were waited for; matrix products, arithmetic and copies ran while one was open for 0% of the time, Pallas kernels for 20%

profile of v12, /device:TPU:0, one launch (start us, length us, event | category | flops | bytes accessed | tf_op | source)
XLA Modules:
  0.0 84.2 jit_solution(367836954300935979)
XLA Ops:
  0.6 1.6 %prepare.1 = (bf16[96,1920]{1,0:T(8,128)(2,1)S(1)}, bf16[72,1792]{1,0:T(8,128)(2,1)S(1)}) custom-call(bf16[96,1792]{1,0:T(8,128)(2,1)} %tokens_hbm.1, s32[4,96]{1,0:T(4,128)} %bitcast.18, f32[4,96]{1,0:T(4,128)} %bitcast.19), custom_call_target="tpu_custom_call" | custom-call | tf_op jit(solution)/shard_map/prepare/pallas_call | solution.py:205
  2.2 3.1 %collective-permute-start = (bf16[96,1920]{1,0:T(8,128)(2,1)S(1)}, bf16[96,1920]{1,0:T(8,128)(2,1)S(1)}, u32[]{:S(2)}, u32[]{:S(2)}) collective-permute-start(bf16[96,1920]{1,0:T(8,128)(2,1)S(1)} %get-tuple-element.51.refs_0_.wide_ref), channel_id=1, source_target_pairs={{0,4},{2,6},{4,0},{6,2},{8,12},{10,14},{12,8},{14,10},{1,5},{3,7},... | collective-permute-start | bytes 1105928 | tf_op jit(solution)/shard_map/ppermute | solution.py:480
  5.3 1.5 %collective-permute-start.1 = (bf16[72,1792]{1,0:T(8,128)(2,1)S(1)}, bf16[72,1792]{1,0:T(8,128)(2,1)S(1)}, u32[]{:S(2)}, u32[]{:S(2)}) collective-permute-start(bf16[72,1792]{1,0:T(8,128)(2,1)S(1)} %get-tuple-element.46), channel_id=1, source_target_pairs={{0,2},{2,0},{4,6},{6,4},{8,10},{10,8},{12,14},{14,12},{1,3},{3,1},... | collective-permute-start | bytes 774152 | tf_op jit(solution)/shard_map/ppermute | solution.py:480
  6.8 2.5 %collective-permute-start.2 = (bf16[96,1920]{1,0:T(8,128)(2,1)S(1)}, bf16[96,1920]{1,0:T(8,128)(2,1)S(1)}, u32[]{:S(2)}, u32[]{:S(2)}) collective-permute-start(bf16[96,1920]{1,0:T(8,128)(2,1)S(1)} %get-tuple-element.51.refs_0_.wide_ref), channel_id=1, source_target_pairs={{0,12},{2,14},{4,8},{6,10},{8,4},{10,6},{12,0},{14,2},{1,13},{3,15... | collective-permute-start | bytes 1105928 | tf_op jit(solution)/shard_map/ppermute | solution.py:480
  9.3 1.3 %copy-done.4 = bf16[4,256,576]{1,2,0:T(8,128)(2,1)S(1)} copy-done((bf16[4,256,576]{1,2,0:T(8,128)(2,1)S(1)}, bf16[4,256,576]{1,2,0:T(8,128)(2,1)}, u32[]{:S(2)}) %copy-start.4) | copy-done | bytes 1179672
  10.6 0.9 %copy-done.5 = bf16[4,32,576]{2,1,0:T(8,128)(2,1)S(1)} copy-done((bf16[4,32,576]{2,1,0:T(8,128)(2,1)S(1)}, bf16[4,32,576]{2,1,0:T(8,128)(2,1)}, u32[]{:S(2)}) %copy-start.5) | copy-done | bytes 147480
  11.5 0.7 copy-done.6
  12.1 0.7 copy-done.7
  12.8 3.3 %attend.1 = (bf16[4,32,512]{2,1,0:T(8,128)(2,1)}, bf16[512,1792]{1,0:T(8,128)(2,1)S(1)}) custom-call(bf16[4,32,576]{2,1,0:T(8,128)(2,1)S(1)} %copy-done.5, bf16[4,576,256]{2,1,0:T(8,128)(2,1)S(1)} %bitcast.15, s32[1,32]{1,0:T(1,128)S(1)} %bitcast.16, s32[1,32]{1,0:T(1,128)S(1)} %bitcast.17, bf16[1,512,3584]{2,1,0:T(8,128)(2,1)} %down_ref.1), custom_call_target="tpu_custom_call" | custom-call | tf_op jit(solution)/shard_map/attend/pallas_call | solution.py:373
  16.1 0.0 collective-permute-done.wide_ref.refs_1_
  16.1 0.5 cross_rows.3
  16.6 0.6 collective-permute-start.3
  17.2 0.0 collective-permute-start.10
  17.2 6.9 %collective-permute-done.2.wide_ref.refs_2_ = bf16[96,1920]{1,0:T(8,128)(2,1)S(1)} collective-permute-done((bf16[96,1920]{1,0:T(8,128)(2,1)S(1)}, bf16[96,1920]{1,0:T(8,128)(2,1)S(1)}, u32[]{:S(2)}, u32[]{:S(2)}) %collective-permute-start.2) | collective-permute-done | bytes 368672 | tf_op jit(solution)/shard_map/ppermute | solution.py:480
  24.1 1.8 %collective-permute-start.5 = (bf16[96,1920]{1,0:T(8,128)(2,1)S(1)}, bf16[96,1920]{1,0:T(8,128)(2,1)S(1)}, u32[]{:S(2)}, u32[]{:S(2)}) collective-permute-start(bf16[96,1920]{1,0:T(8,128)(2,1)S(1)} %collective-permute-done.2.wide_ref.refs_2_), channel_id=1, source_target_pairs={{0,4},{2,6},{4,0},{6,2},{8,12},{10,14},{12,8},{14,10},{1,5},{3,7},... | collective-permute-start | bytes 1105928 | tf_op jit(solution)/shard_map/ppermute | solution.py:480
  25.9 0.5 cross_rows.4
  26.4 0.6 collective-permute-start.6
  27.0 2.0 %copy-done.1 = bf16[1,3584,512]{2,1,0:T(8,128)(2,1)S(1)} copy-done((bf16[1,3584,512]{2,1,0:T(8,128)(2,1)S(1)}, bf16[1,3584,512]{2,1,0:T(8,128)(2,1)}, u32[]{:S(2)}) %copy-start.1) | copy-done | bytes 3670040
  29.0 0.1 pack_rows.2.near_ref
  29.1 0.1 collective-permute-start.4
  29.2 4.3 %collective-permute-done.5.refs_0_.wide_ref = bf16[96,1920]{1,0:T(8,128)(2,1)S(1)} collective-permute-done((bf16[96,1920]{1,0:T(8,128)(2,1)S(1)}, bf16[96,1920]{1,0:T(8,128)(2,1)S(1)}, u32[]{:S(2)}, u32[]{:S(2)}) %collective-permute-start.5) | collective-permute-done | bytes 368672 | tf_op jit(solution)/shard_map/ppermute | solution.py:480
  33.5 0.1 pack_rows.3.near_ref
  33.5 0.1 collective-permute-start.9
  33.6 0.0 copy-start.2
  33.6 0.5 cross_rows.5
  34.1 1.6 %collective-permute-start.8 = (bf16[72,1792]{1,0:T(8,128)(2,1)S(1)}, bf16[72,1792]{1,0:T(8,128)(2,1)S(1)}, u32[]{:S(2)}, u32[]{:S(2)}) collective-permute-start(bf16[72,1792]{1,0:T(8,128)(2,1)S(1)} %cross_rows.5), channel_id=1, source_target_pairs={{0,2},{2,0},{4,6},{6,4},{8,10},{10,8},{12,14},{14,12},{1,3},{3,1},... | collective-permute-start | bytes 774152 | tf_op jit(solution)/shard_map/ppermute | solution.py:480
  35.7 2.9 %hidden_units.3.refs_3_ = bf16[368,512]{1,0:T(8,128)(2,1)S(1)} custom-call(bf16[368,1792]{1,0:T(8,128)(2,1)S(1)} %pack_rows.2.near_ref, bf16[368,1792]{1,0:T(8,128)(2,1)S(1)} %collective-permute-done.4.far_ref, bf16[3584,512]{1,0:T(8,128)(2,1)S(1)} %bitcast.8, bf16[3584,512]{1,0:T(8,128)(2,1)S(1)} %bitcast.12), custom_call_target="tpu_custom_call" | custom-call | tf_op jit(solution)/shard_map/hidden_units/pallas_call | solution.py:91
  38.6 0.5 collective-permute-start.7
  39.1 2.1 %hidden_units.4.refs_1_ = bf16[256,512]{1,0:T(8,128)(2,1)S(1)} custom-call(bf16[256,1792]{1,0:T(8,128)(2,1)S(1)} %pack_rows.3.near_ref, bf16[256,1792]{1,0:T(8,128)(2,1)S(1)} %collective-permute-done.9.far_ref, bf16[3584,512]{1,0:T(8,128)(2,1)S(1)} %bitcast.9, bf16[3584,512]{1,0:T(8,128)(2,1)S(1)} %bitcast.13), custom_call_target="tpu_custom_call" | custom-call | tf_op jit(solution)/shard_map/hidden_units/pallas_call | solution.py:91
  41.2 1.6 %collective-permute-done.8.near_ref = bf16[72,1792]{1,0:T(8,128)(2,1)S(1)} collective-permute-done((bf16[72,1792]{1,0:T(8,128)(2,1)S(1)}, bf16[72,1792]{1,0:T(8,128)(2,1)S(1)}, u32[]{:S(2)}, u32[]{:S(2)}) %collective-permute-start.8) | collective-permute-done | bytes 258080 | tf_op jit(solution)/shard_map/ppermute | solution.py:480
  42.8 0.5 collective-permute-start.12
  43.3 1.5 %down.2 = (f32[96,1792]{1,0:T(8,128)S(1)}, f32[96,1792]{1,0:T(8,128)S(1)}, f32[96,1792]{1,0:T(8,128)S(1)}, bf16[72,1792]{1,0:T(8,128)(2,1)S(1)}) custom-call(bf16[96,1920]{1,0:T(8,128)(2,1)S(1)} %get-tuple-element.51.refs_0_.wide_ref, bf16[96,1920]{1,0:T(8,128)(2,1)S(1)} %collective-permute-done.wide_ref.refs_1_, ...), custom_call_target="tpu_custom_call" | custom-call | tf_op jit(solution)/shard_map/down/pallas_call | solution.py:91
  44.9 1.4 %hidden_units.5.own_ref = bf16[72,512]{1,0:T(8,128)(2,1)S(1)} custom-call(bf16[72,1792]{1,0:T(8,128)(2,1)S(1)} %collective-permute-done.8.near_ref, bf16[72,1792]{1,0:T(8,128)(2,1)S(1)} %collective-permute-done.13.far_ref, bf16[3584,512]{1,0:T(8,128)(2,1)S(1)} %bitcast.10, bf16[3584,512]{1,0:T(8,128)(2,1)S(1)} %bitcast.14), custom_call_target="tpu_custom_call" | custom-call | tf_op jit(solution)/shard_map/hidden_units/pallas_call | solution.py:91
  46.3 0.1 collective-permute-start.16
  46.4 1.1 %down.3 = (f32[96,1792]{1,0:T(8,128)S(1)}, bf16[72,1792]{1,0:T(8,128)(2,1)S(1)}, bf16[72,1792]{1,0:T(8,128)(2,1)S(1)}) custom-call(bf16[96,1920]{1,0:T(8,128)(2,1)S(1)} %collective-permute-done.5.refs_0_.wide_ref, bf16[256,512]{1,0:T(8,128)(2,1)S(1)} %hidden_units.4.refs_1_, bf16[256,512]{1,0:T(8,128)(2,1)S(1)} %collective-permute-done.12.refs_2_, ...), custom_call_target="tpu_custom_call" | custom-call | tf_op jit(solution)/shard_map/down/pallas_call | solution.py:91
  47.5 0.1 collective-permute-done.16.other_ref
  47.7 0.7 last_down.1
  48.4 1.6 %collective-permute-start.18 = (bf16[72,896]{1,0:T(8,128)(2,1)S(1)}, bf16[72,896]{1,0:T(8,128)(2,1)S(1)}, u32[]{:S(2)}, u32[]{:S(2)}) collective-permute-start(bf16[72,896]{1,0:T(8,128)(2,1)S(1)} %get-tuple-element.72), channel_id=1, source_target_pairs={{0,2},{2,0},{4,6},{6,4},{8,10},{10,8},{12,14},{14,12},{1,3},{3,1},... | collective-permute-start | bytes 387080 | tf_op jit(solution)/shard_map/ppermute | solution.py:480
  50.0 0.5 collective-permute-start.17
  50.5 1.5 %collective-permute-start.15 = (bf16[72,1792]{1,0:T(8,128)(2,1)S(1)}, bf16[72,1792]{1,0:T(8,128)(2,1)S(1)}, u32[]{:S(2)}, u32[]{:S(2)}) collective-permute-start(bf16[72,1792]{1,0:T(8,128)(2,1)S(1)} %get-tuple-element.68), channel_id=1, source_target_pairs={{0,2},{2,0},{4,6},{6,4},{8,10},{10,8},{12,14},{14,12},{1,3},{3,1},... | collective-permute-start | bytes 774152 | tf_op jit(solution)/shard_map/ppermute | solution.py:480
  52.0 0.5 collective-permute-start.14
  52.5 2.2 %collective-permute-done.18.back_ref = bf16[72,896]{1,0:T(8,128)(2,1)S(1)} collective-permute-done((bf16[72,896]{1,0:T(8,128)(2,1)S(1)}, bf16[72,896]{1,0:T(8,128)(2,1)S(1)}, u32[]{:S(2)}, u32[]{:S(2)}) %collective-permute-start.18) | collective-permute-done | bytes 129056 | tf_op jit(solution)/shard_map/ppermute | solution.py:480
  54.7 0.4 combine.7
  55.1 0.5 collective-permute-start.20
  55.6 1.9 %collective-permute-done.17.back_ref = bf16[72,896]{1,0:T(8,128)(2,1)S(1)} collective-permute-done((bf16[72,896]{1,0:T(8,128)(2,1)S(1)}, bf16[72,896]{1,0:T(8,128)(2,1)S(1)}, u32[]{:S(2)}, u32[]{:S(2)}) %collective-permute-start.17) | collective-permute-done | bytes 129056 | tf_op jit(solution)/shard_map/ppermute | solution.py:480
  57.5 0.4 combine.8
  57.9 0.5 collective-permute-start.19
  58.3 1.4 %collective-permute-start.11 = (bf16[72,1792]{1,0:T(8,128)(2,1)S(1)}, bf16[72,1792]{1,0:T(8,128)(2,1)S(1)}, u32[]{:S(2)}, u32[]{:S(2)}) collective-permute-start(bf16[72,1792]{1,0:T(8,128)(2,1)S(1)} %get-tuple-element.62), channel_id=1, source_target_pairs={{0,2},{2,0},{4,6},{6,4},{8,10},{10,8},{12,14},{14,12},{1,3},{3,1},... | collective-permute-start | bytes 774152 | tf_op jit(solution)/shard_map/ppermute | solution.py:480
  59.8 3.2 %collective-permute-done.15.back_ref = bf16[72,1792]{1,0:T(8,128)(2,1)S(1)} collective-permute-done((bf16[72,1792]{1,0:T(8,128)(2,1)S(1)}, bf16[72,1792]{1,0:T(8,128)(2,1)S(1)}, u32[]{:S(2)}, u32[]{:S(2)}) %collective-permute-start.15) | collective-permute-done | bytes 258080 | tf_op jit(solution)/shard_map/ppermute | solution.py:480
  63.0 0.4 combine.9
  63.4 5.3 %collective-permute-start.21 = (bf16[96,896]{1,0:T(8,128)(2,1)S(1)}, bf16[96,896]{1,0:T(8,128)(2,1)S(1)}, u32[]{:S(2)}, u32[]{:S(2)}) collective-permute-start(bf16[96,896]{1,0:T(8,128)(2,1)S(1)} %combine.9), channel_id=1, source_target_pairs={{0,12},{2,14},{4,8},{6,10},{8,4},{10,6},{12,0},{14,2},{1,13},{3,15... | collective-permute-start | bytes 516104 | tf_op jit(solution)/shard_map/ppermute | solution.py:480
  68.7 0.4 combine.10
  69.1 0.9 %collective-permute-start.22 = (bf16[96,896]{1,0:T(8,128)(2,1)S(1)}, bf16[96,896]{1,0:T(8,128)(2,1)S(1)}, u32[]{:S(2)}, u32[]{:S(2)}) collective-permute-start(bf16[96,896]{1,0:T(8,128)(2,1)S(1)} %combine.10), channel_id=1, source_target_pairs={{0,12},{2,14},{4,8},{6,10},{8,4},{10,6},{12,0},{14,2},{1,13},{3,15... | collective-permute-start | bytes 516104 | tf_op jit(solution)/shard_map/ppermute | solution.py:480
  70.0 0.5 combine.11
  70.4 0.1 collective-permute-start.23
  70.5 2.0 %collective-permute-start.24 = (bf16[96,896]{1,0:T(8,128)(2,1)S(1)}, bf16[96,896]{1,0:T(8,128)(2,1)S(1)}, u32[]{:S(2)}, u32[]{:S(2)}) collective-permute-start(bf16[96,896]{1,0:T(8,128)(2,1)S(1)} %get-tuple-element.83), channel_id=1, source_target_pairs={{0,4},{2,6},{4,0},{6,2},{8,12},{10,14},{12,8},{14,10},{1,5},{3,7},... | collective-permute-start | bytes 516104 | tf_op jit(solution)/shard_map/ppermute | solution.py:480
  72.5 1.0 %collective-permute-done.11.back_ref = bf16[72,1792]{1,0:T(8,128)(2,1)S(1)} collective-permute-done((bf16[72,1792]{1,0:T(8,128)(2,1)S(1)}, bf16[72,1792]{1,0:T(8,128)(2,1)S(1)}, u32[]{:S(2)}, u32[]{:S(2)}) %collective-permute-start.11) | collective-permute-done | bytes 258080 | tf_op jit(solution)/shard_map/ppermute | solution.py:480
  73.5 0.0 collective-permute-done.21.refs_0_
  73.5 0.4 combine.12.refs_0_
  73.9 4.2 %collective-permute-done.22.refs_0_ = bf16[96,896]{1,0:T(8,128)(2,1)S(1)} collective-permute-done((bf16[96,896]{1,0:T(8,128)(2,1)S(1)}, bf16[96,896]{1,0:T(8,128)(2,1)S(1)}, u32[]{:S(2)}, u32[]{:S(2)}) %collective-permute-start.22) | collective-permute-done | bytes 172064 | tf_op jit(solution)/shard_map/ppermute | solution.py:480
  78.1 0.4 combine.13.refs_1_
  78.5 2.2 %collective-permute-done.23.refs_2_ = bf16[96,896]{1,0:T(8,128)(2,1)S(1)} collective-permute-done((bf16[96,896]{1,0:T(8,128)(2,1)S(1)}, bf16[96,896]{1,0:T(8,128)(2,1)S(1)}, u32[]{:S(2)}, u32[]{:S(2)}) %collective-permute-start.23) | collective-permute-done | bytes 172064 | tf_op jit(solution)/shard_map/ppermute | solution.py:480
  80.8 2.6 %collective-permute-done.24.refs_3_ = bf16[96,896]{1,0:T(8,128)(2,1)S(1)} collective-permute-done((bf16[96,896]{1,0:T(8,128)(2,1)S(1)}, bf16[96,896]{1,0:T(8,128)(2,1)S(1)}, u32[]{:S(2)}, u32[]{:S(2)}) %collective-permute-start.24) | collective-permute-done | bytes 172064 | tf_op jit(solution)/shard_map/ppermute | solution.py:480
  83.4 0.8 add_last.1
  (23 shorter events, 0.1 us)
Async XLA Ops:
  2.2 13.9 %collective-permute-start = (bf16[96,1920]{1,0:T(8,128)(2,1)S(1)}, bf16[96,1920]{1,0:T(8,128)(2,1)S(1)}, u32[]{:S(2)}, u32[]{:S(2)}) collective-permute-start(bf16[96,1920]{1,0:T(8,128)(2,1)S(1)} %get-tuple-element.51.refs_0_.wide_ref), channel_id=1, source_target_pairs={{0,4},{2,6},{4,0},{6,2},{8,12},{10,14},{12,8},{14,10},{1,5},{3,7},... | collective-permute-start | bytes 1105928 | tf_op jit(solution)/shard_map/ppermute | solution.py:480
  5.3 10.8 %collective-permute-start.1 = (bf16[72,1792]{1,0:T(8,128)(2,1)S(1)}, bf16[72,1792]{1,0:T(8,128)(2,1)S(1)}, u32[]{:S(2)}, u32[]{:S(2)}) collective-permute-start(bf16[72,1792]{1,0:T(8,128)(2,1)S(1)} %get-tuple-element.46), channel_id=1, source_target_pairs={{0,2},{2,0},{4,6},{6,4},{8,10},{10,8},{12,14},{14,12},{1,3},{3,1},... | collective-permute-start | bytes 774152 | tf_op jit(solution)/shard_map/ppermute | solution.py:480
  6.8 17.3 %collective-permute-start.2 = (bf16[96,1920]{1,0:T(8,128)(2,1)S(1)}, bf16[96,1920]{1,0:T(8,128)(2,1)S(1)}, u32[]{:S(2)}, u32[]{:S(2)}) collective-permute-start(bf16[96,1920]{1,0:T(8,128)(2,1)S(1)} %get-tuple-element.51.refs_0_.wide_ref), channel_id=1, source_target_pairs={{0,12},{2,14},{4,8},{6,10},{8,4},{10,6},{12,0},{14,2},{1,13},{3,15... | collective-permute-start | bytes 1105928 | tf_op jit(solution)/shard_map/ppermute | solution.py:480
  9.3 1.3 %copy-start.4 = (bf16[4,256,576]{1,2,0:T(8,128)(2,1)S(1)}, bf16[4,256,576]{1,2,0:T(8,128)(2,1)}, u32[]{:S(2)}) copy-start(bf16[4,256,576]{1,2,0:T(8,128)(2,1)} %param.11) | copy-start | bytes 3538948
  10.6 0.9 %copy-start.5 = (bf16[4,32,576]{2,1,0:T(8,128)(2,1)S(1)}, bf16[4,32,576]{2,1,0:T(8,128)(2,1)}, u32[]{:S(2)}) copy-start(bf16[4,32,576]{2,1,0:T(8,128)(2,1)} %query_ref) | copy-start | bytes 442372
  11.5 0.7 copy-start.6
  12.1 0.7 copy-start.7
  12.8 14.2 %copy-start = (bf16[1,3584,512]{2,1,0:T(8,128)(2,1)S(1)}, bf16[1,3584,512]{2,1,0:T(8,128)(2,1)}, u32[]{:S(2)}) copy-start(bf16[1,3584,512]{2,1,0:T(8,128)(2,1)} %param.17) | copy-start | bytes 11010052
  16.6 10.4 %collective-permute-start.3 = (bf16[72,1792]{1,0:T(8,128)(2,1)S(1)}, bf16[72,1792]{1,0:T(8,128)(2,1)S(1)}, u32[]{:S(2)}, u32[]{:S(2)}) collective-permute-start(bf16[72,1792]{1,0:T(8,128)(2,1)S(1)} %cross_rows.3), channel_id=1, source_target_pairs={{0,2},{2,0},{4,6},{6,4},{8,10},{10,8},{12,14},{14,12},{1,3},{3,1},... | collective-permute-start | bytes 774152 | tf_op jit(solution)/shard_map/ppermute | solution.py:480
  17.2 26.2 %collective-permute-start.10 = (bf16[512,1792]{1,0:T(8,128)(2,1)S(1)}, bf16[512,1792]{1,0:T(8,128)(2,1)S(1)}, u32[]{:S(2)}, u32[]{:S(2)}) collective-permute-start(bf16[512,1792]{1,0:T(8,128)(2,1)S(1)} %get-tuple-element.60), channel_id=1, source_target_pairs={{0,1},{1,0},{2,3},{3,2},{4,5},{5,4},{6,7},{7,6},{8,9},{9,8},{10,11... | collective-permute-start | bytes 5505032 | tf_op jit(solution)/shard_map/ppermute | solution.py:484
  24.1 9.4 %collective-permute-start.5 = (bf16[96,1920]{1,0:T(8,128)(2,1)S(1)}, bf16[96,1920]{1,0:T(8,128)(2,1)S(1)}, u32[]{:S(2)}, u32[]{:S(2)}) collective-permute-start(bf16[96,1920]{1,0:T(8,128)(2,1)S(1)} %collective-permute-done.2.wide_ref.refs_2_), channel_id=1, source_target_pairs={{0,4},{2,6},{4,0},{6,2},{8,12},{10,14},{12,8},{14,10},{1,5},{3,7},... | collective-permute-start | bytes 1105928 | tf_op jit(solution)/shard_map/ppermute | solution.py:480
  26.4 7.0 %collective-permute-start.6 = (bf16[72,1792]{1,0:T(8,128)(2,1)S(1)}, bf16[72,1792]{1,0:T(8,128)(2,1)S(1)}, u32[]{:S(2)}, u32[]{:S(2)}) collective-permute-start(bf16[72,1792]{1,0:T(8,128)(2,1)S(1)} %cross_rows.4), channel_id=1, source_target_pairs={{0,2},{2,0},{4,6},{6,4},{8,10},{10,8},{12,14},{14,12},{1,3},{3,1},... | collective-permute-start | bytes 774152 | tf_op jit(solution)/shard_map/ppermute | solution.py:480
  27.0 2.0 %copy-start.1 = (bf16[1,3584,512]{2,1,0:T(8,128)(2,1)S(1)}, bf16[1,3584,512]{2,1,0:T(8,128)(2,1)}, u32[]{:S(2)}) copy-start(bf16[1,3584,512]{2,1,0:T(8,128)(2,1)} %param.18) | copy-start | bytes 11010052
  29.1 6.6 %collective-permute-start.4 = (bf16[368,1792]{1,0:T(8,128)(2,1)S(1)}, bf16[368,1792]{1,0:T(8,128)(2,1)S(1)}, u32[]{:S(2)}, u32[]{:S(2)}) collective-permute-start(bf16[368,1792]{1,0:T(8,128)(2,1)S(1)} %pack_rows.2.near_ref), channel_id=1, source_target_pairs={{0,1},{1,0},{2,3},{3,2},{4,5},{5,4},{6,7},{7,6},{8,9},{9,8},{10,11... | collective-permute-start | bytes 3956744 | tf_op jit(solution)/shard_map/ppermute | solution.py:484
  33.5 5.6 %collective-permute-start.9 = (bf16[256,1792]{1,0:T(8,128)(2,1)S(1)}, bf16[256,1792]{1,0:T(8,128)(2,1)S(1)}, u32[]{:S(2)}, u32[]{:S(2)}) collective-permute-start(bf16[256,1792]{1,0:T(8,128)(2,1)S(1)} %pack_rows.3.near_ref), channel_id=1, source_target_pairs={{0,1},{1,0},{2,3},{3,2},{4,5},{5,4},{6,7},{7,6},{8,9},{9,8},{10,11... | collective-permute-start | bytes 2752520 | tf_op jit(solution)/shard_map/ppermute | solution.py:484
  33.6 2.1 %copy-start.2 = (bf16[1,3584,512]{2,1,0:T(8,128)(2,1)S(1)}, bf16[1,3584,512]{2,1,0:T(8,128)(2,1)}, u32[]{:S(2)}) copy-start(bf16[1,3584,512]{2,1,0:T(8,128)(2,1)} %param.18) | copy-start | bytes 11010052
  34.1 8.7 %collective-permute-start.8 = (bf16[72,1792]{1,0:T(8,128)(2,1)S(1)}, bf16[72,1792]{1,0:T(8,128)(2,1)S(1)}, u32[]{:S(2)}, u32[]{:S(2)}) collective-permute-start(bf16[72,1792]{1,0:T(8,128)(2,1)S(1)} %cross_rows.5), channel_id=1, source_target_pairs={{0,2},{2,0},{4,6},{6,4},{8,10},{10,8},{12,14},{14,12},{1,3},{3,1},... | collective-permute-start | bytes 774152 | tf_op jit(solution)/shard_map/ppermute | solution.py:480
  38.6 4.7 %collective-permute-start.7 = (bf16[368,512]{1,0:T(8,128)(2,1)S(1)}, bf16[368,512]{1,0:T(8,128)(2,1)S(1)}, u32[]{:S(2)}, u32[]{:S(2)}) collective-permute-start(bf16[368,512]{1,0:T(8,128)(2,1)S(1)} %hidden_units.3.refs_3_), channel_id=1, source_target_pairs={{0,1},{1,0},{2,3},{3,2},{4,5},{5,4},{6,7},{7,6},{8,9},{9,8},{10,11... | collective-permute-start | bytes 1130504 | tf_op jit(solution)/shard_map/ppermute | solution.py:484
  39.1 4.2 %copy-start.3 = (bf16[1,512,3584]{2,1,0:T(8,128)(2,1)S(1)}, bf16[1,512,3584]{2,1,0:T(8,128)(2,1)}, u32[]{:S(2)}) copy-start(bf16[1,512,3584]{2,1,0:T(8,128)(2,1)} %down_ref.1) | copy-start | bytes 11010052
  42.8 2.1 %collective-permute-start.13 = (bf16[72,1792]{1,0:T(8,128)(2,1)S(1)}, bf16[72,1792]{1,0:T(8,128)(2,1)S(1)}, u32[]{:S(2)}, u32[]{:S(2)}) collective-permute-start(bf16[72,1792]{1,0:T(8,128)(2,1)S(1)} %collective-permute-done.8.near_ref), channel_id=1, source_target_pairs={{0,1},{1,0},{2,3},{3,2},{4,5},{5,4},{6,7},{7,6},{8,9},{9,8},{10,11... | collective-permute-start | bytes 774152 | tf_op jit(solution)/shard_map/ppermute | solution.py:484
  42.8 3.6 %collective-permute-start.12 = (bf16[256,512]{1,0:T(8,128)(2,1)S(1)}, bf16[256,512]{1,0:T(8,128)(2,1)S(1)}, u32[]{:S(2)}, u32[]{:S(2)}) collective-permute-start(bf16[256,512]{1,0:T(8,128)(2,1)S(1)} %hidden_units.4.refs_1_), channel_id=1, source_target_pairs={{0,1},{1,0},{2,3},{3,2},{4,5},{5,4},{6,7},{7,6},{8,9},{9,8},{10,11... | collective-permute-start | bytes 786440 | tf_op jit(solution)/shard_map/ppermute | solution.py:484
  46.3 1.3 %collective-permute-start.16 = (bf16[72,512]{1,0:T(8,128)(2,1)S(1)}, bf16[72,512]{1,0:T(8,128)(2,1)S(1)}, u32[]{:S(2)}, u32[]{:S(2)}) collective-permute-start(bf16[72,512]{1,0:T(8,128)(2,1)S(1)} %hidden_units.5.own_ref), channel_id=1, source_target_pairs={{0,1},{1,0},{2,3},{3,2},{4,5},{5,4},{6,7},{7,6},{8,9},{9,8},{10,11... | collective-permute-start | bytes 221192 | tf_op jit(solution)/shard_map/ppermute | solution.py:484
  48.4 6.4 %collective-permute-start.18 = (bf16[72,896]{1,0:T(8,128)(2,1)S(1)}, bf16[72,896]{1,0:T(8,128)(2,1)S(1)}, u32[]{:S(2)}, u32[]{:S(2)}) collective-permute-start(bf16[72,896]{1,0:T(8,128)(2,1)S(1)} %get-tuple-element.72), channel_id=1, source_target_pairs={{0,2},{2,0},{4,6},{6,4},{8,10},{10,8},{12,14},{14,12},{1,3},{3,1},... | collective-permute-start | bytes 387080 | tf_op jit(solution)/shard_map/ppermute | solution.py:480
  50.0 7.5 %collective-permute-start.17 = (bf16[72,896]{1,0:T(8,128)(2,1)S(1)}, bf16[72,896]{1,0:T(8,128)(2,1)S(1)}, u32[]{:S(2)}, u32[]{:S(2)}) collective-permute-start(bf16[72,896]{1,0:T(8,128)(2,1)S(1)} %get-tuple-element.71), channel_id=1, source_target_pairs={{0,2},{2,0},{4,6},{6,4},{8,10},{10,8},{12,14},{14,12},{1,3},{3,1},... | collective-permute-start | bytes 387080 | tf_op jit(solution)/shard_map/ppermute | solution.py:480
  50.5 12.5 %collective-permute-start.15 = (bf16[72,1792]{1,0:T(8,128)(2,1)S(1)}, bf16[72,1792]{1,0:T(8,128)(2,1)S(1)}, u32[]{:S(2)}, u32[]{:S(2)}) collective-permute-start(bf16[72,1792]{1,0:T(8,128)(2,1)S(1)} %get-tuple-element.68), channel_id=1, source_target_pairs={{0,2},{2,0},{4,6},{6,4},{8,10},{10,8},{12,14},{14,12},{1,3},{3,1},... | collective-permute-start | bytes 774152 | tf_op jit(solution)/shard_map/ppermute | solution.py:480
  52.0 18.0 %collective-permute-start.14 = (bf16[72,1792]{1,0:T(8,128)(2,1)S(1)}, bf16[72,1792]{1,0:T(8,128)(2,1)S(1)}, u32[]{:S(2)}, u32[]{:S(2)}) collective-permute-start(bf16[72,1792]{1,0:T(8,128)(2,1)S(1)} %get-tuple-element.66), channel_id=1, source_target_pairs={{0,2},{2,0},{4,6},{6,4},{8,10},{10,8},{12,14},{14,12},{1,3},{3,1},... | collective-permute-start | bytes 774152 | tf_op jit(solution)/shard_map/ppermute | solution.py:480
  55.1 7.9 %collective-permute-start.20 = (bf16[96,896]{1,0:T(8,128)(2,1)S(1)}, bf16[96,896]{1,0:T(8,128)(2,1)S(1)}, u32[]{:S(2)}, u32[]{:S(2)}) collective-permute-start(bf16[96,896]{1,0:T(8,128)(2,1)S(1)} %combine.7), channel_id=1, source_target_pairs={{0,4},{2,6},{4,0},{6,2},{8,12},{10,14},{12,8},{14,10},{1,5},{3,7},... | collective-permute-start | bytes 516104 | tf_op jit(solution)/shard_map/ppermute | solution.py:480
  57.9 10.8 %collective-permute-start.19 = (bf16[96,896]{1,0:T(8,128)(2,1)S(1)}, bf16[96,896]{1,0:T(8,128)(2,1)S(1)}, u32[]{:S(2)}, u32[]{:S(2)}) collective-permute-start(bf16[96,896]{1,0:T(8,128)(2,1)S(1)} %combine.8), channel_id=1, source_target_pairs={{0,4},{2,6},{4,0},{6,2},{8,12},{10,14},{12,8},{14,10},{1,5},{3,7},... | collective-permute-start | bytes 516104 | tf_op jit(solution)/shard_map/ppermute | solution.py:480
  58.3 15.2 %collective-permute-start.11 = (bf16[72,1792]{1,0:T(8,128)(2,1)S(1)}, bf16[72,1792]{1,0:T(8,128)(2,1)S(1)}, u32[]{:S(2)}, u32[]{:S(2)}) collective-permute-start(bf16[72,1792]{1,0:T(8,128)(2,1)S(1)} %get-tuple-element.62), channel_id=1, source_target_pairs={{0,2},{2,0},{4,6},{6,4},{8,10},{10,8},{12,14},{14,12},{1,3},{3,1},... | collective-permute-start | bytes 774152 | tf_op jit(solution)/shard_map/ppermute | solution.py:480
  63.4 10.1 %collective-permute-start.21 = (bf16[96,896]{1,0:T(8,128)(2,1)S(1)}, bf16[96,896]{1,0:T(8,128)(2,1)S(1)}, u32[]{:S(2)}, u32[]{:S(2)}) collective-permute-start(bf16[96,896]{1,0:T(8,128)(2,1)S(1)} %combine.9), channel_id=1, source_target_pairs={{0,12},{2,14},{4,8},{6,10},{8,4},{10,6},{12,0},{14,2},{1,13},{3,15... | collective-permute-start | bytes 516104 | tf_op jit(solution)/shard_map/ppermute | solution.py:480
  69.1 9.0 %collective-permute-start.22 = (bf16[96,896]{1,0:T(8,128)(2,1)S(1)}, bf16[96,896]{1,0:T(8,128)(2,1)S(1)}, u32[]{:S(2)}, u32[]{:S(2)}) collective-permute-start(bf16[96,896]{1,0:T(8,128)(2,1)S(1)} %combine.10), channel_id=1, source_target_pairs={{0,12},{2,14},{4,8},{6,10},{8,4},{10,6},{12,0},{14,2},{1,13},{3,15... | collective-permute-start | bytes 516104 | tf_op jit(solution)/shard_map/ppermute | solution.py:480
  70.4 10.3 %collective-permute-start.23 = (bf16[96,896]{1,0:T(8,128)(2,1)S(1)}, bf16[96,896]{1,0:T(8,128)(2,1)S(1)}, u32[]{:S(2)}, u32[]{:S(2)}) collective-permute-start(bf16[96,896]{1,0:T(8,128)(2,1)S(1)} %get-tuple-element.78), channel_id=1, source_target_pairs={{0,4},{2,6},{4,0},{6,2},{8,12},{10,14},{12,8},{14,10},{1,5},{3,7},... | collective-permute-start | bytes 516104 | tf_op jit(solution)/shard_map/ppermute | solution.py:480
  70.5 12.9 %collective-permute-start.24 = (bf16[96,896]{1,0:T(8,128)(2,1)S(1)}, bf16[96,896]{1,0:T(8,128)(2,1)S(1)}, u32[]{:S(2)}, u32[]{:S(2)}) collective-permute-start(bf16[96,896]{1,0:T(8,128)(2,1)S(1)} %get-tuple-element.83), channel_id=1, source_target_pairs={{0,4},{2,6},{4,0},{6,2},{8,12},{10,14},{12,8},{14,10},{1,5},{3,7},... | collective-permute-start | bytes 516104 | tf_op jit(solution)/shard_map/ppermute | solution.py:480
